TPU v7x, 32 devices: a whole 2x2x4 slice. The times are simulated.
32 devices in a mesh: dp: 16 (over z, y, core), mp: 2 (over x).
Axes of the slice: x: 2, y: 2, z: 4, core: 2. Of those that a mesh axis runs over, the one named last changes fastest.
Arguments:
- patches: bfloat16 [256, 49, 768], P(('dp', 'mp')), may hold values from -6 to 6
- token_valid: int32 [256, 49], P(('dp', 'mp')), may hold values from 0 to 1, as said below
- ln1_gain: float32 [768], replicated, may hold values from 0.5 to 1.5
- ln1_shift: float32 [768], replicated, may hold values from -2.5 to 2.5
- qkv_weight: bfloat16 [768, 3, 768], P(None, None, 'mp'), may hold values from -0.21875 to 0.21875
- qv_bias: float32 [2, 768], P(None, 'mp'), may hold values from -2.5 to 2.5
- bias_table: float32 [169, 24], P(None, 'mp'), may hold values from -3 to 3
- proj_weight: bfloat16 [768, 768], P('mp'), may hold values from -1 to 1
- proj_bias: float32 [768], replicated, may hold values from -2.5 to 2.5
- ln2_gain: float32 [768], replicated, may hold values from 0.5 to 1.5
- ln2_shift: float32 [768], replicated, may hold values from -2.5 to 2.5
- fc1_weight: bfloat16 [768, 3072], P(None, 'mp'), may hold values from -0.21875 to 0.21875
- fc1_bias: float32 [3072], P('mp'), may hold values from -2.5 to 2.5
- fc2_weight: bfloat16 [3072, 768], P('mp'), may hold values from -0.109375 to 0.109375
- fc2_bias: float32 [768], replicated, may hold values from -2.5 to 2.5
- cotangent: bfloat16 [256, 49, 768], P(('dp', 'mp')), may hold values from -6 to 6
Outputs:
- output: bfloat16 [256, 49, 768], P(('dp', 'mp'))
- g_patches: bfloat16 [256, 49, 768], P(('dp', 'mp'))
- g_ln1_gain: float32 [768], replicated
- g_ln1_shift: float32 [768], replicated
- g_qkv_weight: float32 [768, 3, 768], P(None, None, 'mp')
- g_qv_bias: float32 [2, 768], P(None, 'mp')
- g_bias_table: float32 [169, 24], P(None, 'mp')
- g_proj_weight: float32 [768, 768], P('mp')
- g_proj_bias: float32 [768], replicated
- g_ln2_gain: float32 [768], replicated
- g_ln2_shift: float32 [768], replicated
- g_fc1_weight: float32 [768, 3072], P(None, 'mp')
- g_fc1_bias: float32 [3072], P('mp')
- g_fc2_weight: float32 [3072, 768], P('mp')
- g_fc2_bias: float32 [768], replicated
Inputs may be any that keep to these rules, and one draw needn't show every extreme that they name: `token_valid`: in each window the valid patches fill the top-left rows and columns of its 7 x 7 grid, at least 3 x 3 of them; the first patch is always valid.
All inputs are finite; a program needn't handle non-finite values.
Results may differ from a plain program's by a relative error of at most 0.02.
Values may be sent and summed in bfloat16 or wider, within the bound.
No kernel may reach another device: no remote copies, remote signals or barrier semaphores. Data moves between devices by JAX's collectives and lax.ppermute only.
A program may use at most 192 MiB of HBM per device.

v0:
```python
import jax
import jax.numpy as jnp
from jax import lax
from jax.sharding import PartitionSpec as P

HEAD = 32
WSIDE = 7
WIN = 49
REL = 169


HIGH = lax.Precision.HIGHEST
CONTRACT_ROWS = (((0,), (0,)), ((), ()))
CONTRACT_LAST = (((1,), (1,)), ((), ()))


def layer_norm(row_data, gain, shift):
    row_mean = jnp.mean(row_data, axis=-1, keepdims=True)
    centred = row_data - row_mean
    variance = jnp.mean(centred * centred, axis=-1, keepdims=True)
    return centred * lax.rsqrt(variance + 1e-05) * gain + shift


def layer_norm_back(row_data, gain, shift, upstream):
    _, pullback = jax.vjp(layer_norm, row_data, gain, shift)
    return pullback(upstream)


def gelu_exact(values):
    return jax.nn.gelu(values, approximate=False)


def relative_onehot():
    places = jnp.arange(WIN, dtype=jnp.int32)
    row_pos = places // WSIDE
    col_pos = places % WSIDE
    row_delta = row_pos[:, None] - row_pos[None, :] + (WSIDE - 1)
    col_delta = col_pos[:, None] - col_pos[None, :] + (WSIDE - 1)
    flat_index = (row_delta * (2 * WSIDE - 1) + col_delta).reshape(WIN * WIN)
    return (flat_index[:, None] == jnp.arange(REL, dtype=jnp.int32)[None, :]).astype(jnp.float32)


def project(row_data, weight, bias):
    packed = jnp.einsum("rc,cjd->rjd", row_data, weight, preferred_element_type=jnp.float32)
    queries = (packed[:, 0] + bias[0]).astype(jnp.bfloat16)
    key_vecs = packed[:, 1].astype(jnp.bfloat16)
    values = (packed[:, 2] + bias[1]).astype(jnp.bfloat16)
    return (queries, key_vecs, values)


def split_heads(row_data):
    return row_data.reshape(row_data.shape[0] // WIN, WIN, row_data.shape[1] // HEAD, HEAD)


def position_bias(rel_table, onehot):
    flat_bias = jnp.dot(onehot, rel_table, precision=HIGH)
    return flat_bias.T.reshape(rel_table.shape[1], WIN, WIN)


def attend(queries, key_vecs, values, rel_table, onehot, allowed):
    query_heads = split_heads(queries)
    key_heads = split_heads(key_vecs)
    value_heads = split_heads(values)
    scores = jnp.einsum(
        "bqhd,bkhd->bhqk", query_heads, key_heads, preferred_element_type=jnp.float32
    ) * HEAD ** (-0.5)
    scores = scores + position_bias(rel_table, onehot)[None]
    scores = jnp.where(allowed[:, None, None, :], scores, -1000000000.0)
    attn_prob = jax.nn.softmax(scores, axis=-1)
    mixed_rows = jnp.einsum(
        "bhqk,bkhd->bqhd",
        attn_prob.astype(jnp.bfloat16),
        value_heads,
        preferred_element_type=jnp.float32,
    )
    return (attn_prob, mixed_rows.astype(jnp.bfloat16).reshape(queries.shape))


def attend_back(queries, key_vecs, values, attn_prob, grad_mixed, onehot):
    query_heads = split_heads(queries)
    key_heads = split_heads(key_vecs)
    value_heads = split_heads(values)
    grad_heads = split_heads(grad_mixed)
    scaling = HEAD ** (-0.5)
    grad_prob = jnp.einsum(
        "bqhd,bkhd->bhqk", grad_heads, value_heads, preferred_element_type=jnp.float32
    )
    grad_values = jnp.einsum(
        "bhqk,bqhd->bkhd",
        attn_prob.astype(jnp.bfloat16),
        grad_heads,
        preferred_element_type=jnp.float32,
    ).astype(jnp.bfloat16)
    grad_scores = (
        attn_prob * (grad_prob - jnp.sum(attn_prob * grad_prob, axis=-1, keepdims=True))
    ).astype(jnp.bfloat16)
    grad_query = (
        jnp.einsum("bhqk,bkhd->bqhd", grad_scores, key_heads, preferred_element_type=jnp.float32)
        * scaling
    ).astype(jnp.bfloat16)
    grad_keys = (
        jnp.einsum("bhqk,bqhd->bkhd", grad_scores, query_heads, preferred_element_type=jnp.float32)
        * scaling
    ).astype(jnp.bfloat16)
    grad_bias = jnp.sum(grad_scores, axis=0, dtype=jnp.float32)
    head_count = grad_bias.shape[0]
    grad_table = jnp.dot(onehot.T, grad_bias.reshape(head_count, WIN * WIN).T, precision=HIGH)
    row_shape = queries.shape
    packed = jnp.stack(
        (
            grad_query.reshape(row_shape),
            grad_keys.reshape(row_shape),
            grad_values.reshape(row_shape),
        ),
        axis=1,
    )
    grad_qv = jnp.stack(
        (
            jnp.sum(packed[:, 0], axis=0, dtype=jnp.float32),
            jnp.sum(packed[:, 2], axis=0, dtype=jnp.float32),
        )
    )
    return (packed, grad_qv, grad_table)


def mlp_back(normed_in, pre_act, hidden, upstream, down_weight):
    grad_hidden = lax.dot_general(
        upstream, down_weight, CONTRACT_LAST, preferred_element_type=jnp.float32
    )
    _, pullback = jax.vjp(gelu_exact, pre_act)
    grad_pre = pullback(grad_hidden)[0].astype(jnp.bfloat16)
    grad_down = lax.dot_general(hidden, upstream, CONTRACT_ROWS, preferred_element_type=jnp.float32)
    grad_up = lax.dot_general(
        normed_in, grad_pre, CONTRACT_ROWS, preferred_element_type=jnp.float32
    )
    grad_upb = jnp.sum(grad_pre, axis=0, dtype=jnp.float32)
    return (grad_pre, grad_up, grad_upb, grad_down)


def shards(
    patches,
    token_valid,
    ln1_gain,
    ln1_shift,
    qkv_weight,
    qv_bias,
    bias_table,
    proj_weight,
    proj_bias,
    ln2_gain,
    ln2_shift,
    fc1_weight,
    fc1_bias,
    fc2_weight,
    fc2_bias,
    cotangent,
):
    windows_own = patches.shape[0]
    features = patches.shape[2]
    own_rows = windows_own * WIN
    inputs = patches.astype(jnp.float32).reshape(own_rows, features)
    upstream = cotangent.reshape(own_rows, features)
    upstream_f = upstream.astype(jnp.float32)
    onehot = relative_onehot()
    normed = layer_norm(inputs, ln1_gain, ln1_shift).astype(jnp.bfloat16)
    gathered, flag_rows = (
        lax.all_gather(normed.reshape(windows_own, WIN, features), "mp", axis=0, tiled=True),
        lax.all_gather(token_valid.astype(jnp.bfloat16), "mp", axis=0, tiled=True),
    )
    group_rows = gathered.shape[0] * WIN
    normed_all = gathered.reshape(group_rows, features)
    allowed = flag_rows > 0.5
    queries, key_vecs, values = project(normed_all, qkv_weight, qv_bias)
    attn_prob, mixed_rows = attend(queries, key_vecs, values, bias_table, onehot, allowed)
    middle = (
        inputs
        + lax.psum_scatter(
            jnp.dot(mixed_rows, proj_weight, preferred_element_type=jnp.float32).astype(
                jnp.bfloat16
            ),
            "mp",
            scatter_dimension=0,
            tiled=True,
        ).astype(jnp.float32)
        + proj_bias
    )
    normed_mid = layer_norm(middle, ln2_gain, ln2_shift).astype(jnp.bfloat16)
    normed_mid_all = lax.all_gather(normed_mid, "mp", axis=0, tiled=True)
    hidden = gelu_exact(
        jnp.dot(normed_mid_all, fc1_weight, preferred_element_type=jnp.float32) + fc1_bias
    ).astype(jnp.bfloat16)
    output = (
        middle
        + lax.psum_scatter(
            jnp.dot(hidden, fc2_weight, preferred_element_type=jnp.float32).astype(jnp.bfloat16),
            "mp",
            scatter_dimension=0,
            tiled=True,
        ).astype(jnp.float32)
        + fc2_bias
    )
    mid_back = lax.all_gather(normed_mid, "mp", axis=0, tiled=True)
    pre_back = jnp.dot(mid_back, fc1_weight, preferred_element_type=jnp.float32) + fc1_bias
    hidden_back = gelu_exact(pre_back).astype(jnp.bfloat16)
    upstream_all = lax.all_gather(upstream, "mp", axis=0, tiled=True)
    grad_pre, grad_up, grad_upb, grad_down = mlp_back(
        mid_back, pre_back, hidden_back, upstream_all, fc2_weight
    )
    grad_mid = lax.psum_scatter(
        lax.dot_general(
            grad_pre, fc1_weight, CONTRACT_LAST, preferred_element_type=jnp.float32
        ).astype(jnp.bfloat16),
        "mp",
        scatter_dimension=0,
        tiled=True,
    ).astype(jnp.float32)
    middle_add, grad_g2, grad_s2 = layer_norm_back(middle, ln2_gain, ln2_shift, grad_mid)
    dmiddle = upstream_f + middle_add
    grad_branch = dmiddle.astype(jnp.bfloat16)
    branch_all = lax.all_gather(grad_branch, "mp", axis=0, tiled=True)
    normed_back = lax.all_gather(normed, "mp", axis=0, tiled=True)
    queries_back, keys_back, values_back = project(normed_back, qkv_weight, qv_bias)
    prob_back, mixed_back = attend(
        queries_back, keys_back, values_back, bias_table, onehot, allowed
    )
    grad_mixed = lax.dot_general(
        branch_all, proj_weight, CONTRACT_LAST, preferred_element_type=jnp.float32
    ).astype(jnp.bfloat16)
    grad_proj = lax.dot_general(
        mixed_back, branch_all, CONTRACT_ROWS, preferred_element_type=jnp.float32
    )
    packed, grad_qv, grad_table = attend_back(
        queries_back, keys_back, values_back, prob_back, grad_mixed, onehot
    )
    grad_qkv = jnp.einsum("rc,rjd->cjd", normed_back, packed, preferred_element_type=jnp.float32)
    grad_norm = lax.psum_scatter(
        jnp.einsum("rjd,cjd->rc", packed, qkv_weight, preferred_element_type=jnp.float32).astype(
            jnp.bfloat16
        ),
        "mp",
        scatter_dimension=0,
        tiled=True,
    ).astype(jnp.float32)
    sharded = (grad_qkv, grad_qv, grad_table, grad_proj, grad_up, grad_upb, grad_down)
    input_add, grad_g1, grad_s1 = layer_norm_back(inputs, ln1_gain, ln1_shift, grad_norm)
    grad_input = dmiddle + input_add
    summed = (
        lax.psum(sharded[0].astype(jnp.bfloat16), "dp").astype(jnp.float32),
        lax.psum(sharded[1].astype(jnp.bfloat16), "dp").astype(jnp.float32),
        lax.psum(sharded[2].astype(jnp.bfloat16), "dp").astype(jnp.float32),
        lax.psum(sharded[3].astype(jnp.bfloat16), "dp").astype(jnp.float32),
        lax.psum(sharded[4].astype(jnp.bfloat16), "dp").astype(jnp.float32),
        lax.psum(sharded[5].astype(jnp.bfloat16), "dp").astype(jnp.float32),
        lax.psum(sharded[6].astype(jnp.bfloat16), "dp").astype(jnp.float32),
    )
    totals = lax.psum(
        (grad_g1, grad_s1, jnp.sum(dmiddle, axis=0), grad_g2, grad_s2, jnp.sum(upstream_f, axis=0)),
        ("dp", "mp"),
    )
    return (
        output.astype(jnp.bfloat16).reshape(windows_own, WIN, features),
        grad_input.astype(jnp.bfloat16).reshape(windows_own, WIN, features),
        totals[0],
        totals[1],
        summed[0],
        summed[1],
        summed[2],
        summed[3],
        totals[2],
        totals[3],
        totals[4],
        summed[4],
        summed[5],
        summed[6],
        totals[5],
    )


def solution(mesh):
    placed = (
        P(("dp", "mp"), None, None),
        P(("dp", "mp"), None),
        P(),
        P(),
        P(None, None, "mp"),
        P(None, "mp"),
        P(None, "mp"),
        P("mp", None),
        P(),
        P(),
        P(),
        P(None, "mp"),
        P("mp"),
        P("mp", None),
        P(),
        P(("dp", "mp"), None, None),
    )
    return jax.shard_map(
        shards,
        mesh=mesh,
        in_specs=placed,
        out_specs=(
            P(("dp", "mp"), None, None),
            P(("dp", "mp"), None, None),
            P(),
            P(),
            P(None, None, "mp"),
            P(None, "mp"),
            P(None, "mp"),
            P("mp", None),
            P(),
            P(),
            P(),
            P(None, "mp"),
            P("mp"),
            P("mp", None),
            P(),
        ),
        check_vma=False,
    )
```

profile of v0, /device:TPU:0, one launch (start us, length us, event | category | flops | bytes accessed | tf_op | source)
XLA Modules:
  0.0 503.6 jit_solution(17690641825707956364)
XLA Ops:
  10.4 2.2 add_convert_fusion.9
  15.3 5.2 %all_gather.20 = bf16[16,49]{1,0:T(8,128)(2,1)S(1)} all-gather(bf16[8,49]{1,0:T(8,128)(2,1)S(1)} %convert_element_type.184), channel_id=1, replica_groups=mesh['dp'=16,'mp'=2] {'mp'}, dimensions={0}, use_global_device_ids=true | all-gather | bytes 2352 | tf_op jit(solution)/shard_map/all_gather | solution.py:168
  20.6 17.9 %all-gather.6.cloned.1.call-done = bf16[16,49,768]{2,0,1:T(8,128)(2,1)} async-done(((bf16[8,49,768]{2,0,1:T(8,128)(2,1)}), bf16[16,49,768]{2,0,1:T(8,128)(2,1)}) %all-gather.6.cloned.1.call-update) | async-done | bytes 1204240 | tf_op jit(solution)/shard_map/all_gather | solution.py:167
  38.5 2.7 copy.174
  41.2 2.3 reshape.298
  43.5 3.6 fusion.79
  49.6 2.8 copy.176
  52.4 4.6 squeeze.15
  58.3 3.4 convert_element_type.186
  61.8 2.8 copy.175
  64.6 4.7 squeeze.14
  69.3 2.5 add_convert_fusion.3
  74.2 2.9 fusion.75
  78.4 2.2 copy.183
  80.6 3.6 reshape.291
  84.2 3.2 convolution_convert_fusion.5
  88.9 2.5 reshape.289
  91.4 18.1 %reduce-scatter.5.cloned.1.call-done = bf16[392,768]{1,0:T(8,128)(2,1)} async-done(((bf16[784,768]{1,0:T(8,128)(2,1)}), bf16[392,768]{1,0:T(8,128)(2,1)}) %reduce-scatter.5.cloned.1.call-update) | async-done | bytes 602128 | tf_op jit(solution)/shard_map/reduce_scatter | solution.py:177
  109.6 2.7 fusion.72
  117.6 20.1 %all-gather.8.cloned.1.call-done = bf16[784,768]{1,0:T(8,128)(2,1)} async-done(((bf16[392,768]{1,0:T(8,128)(2,1)}), bf16[784,768]{1,0:T(8,128)(2,1)}) %all-gather.8.cloned.1.call-update) | async-done | bytes 1204240 | tf_op jit(solution)/shard_map/all_gather | solution.py:188
  137.6 6.2 %fusion.80 = f32[784,1536]{1,0:T(8,128)} fusion(bf16[784,768]{1,0:T(8,128)(2,1)} %all-gather.8.cloned.1.call-done, bf16[768,1536]{1,0:T(8,128)(2,1)} %param.27), kind=kOutput, calls=%fused_computation.156 | convolution fusion | flops 1849688064 | bytes 8380416 | tf_op jit(solution)/shard_map/dot_general | solution.py:190
  143.9 18.8 %all-gather.10.cloned.1.call-done = bf16[784,768]{1,0:T(8,128)(2,1)} async-done(((bf16[392,768]{1,0:T(8,128)(2,1)}), bf16[784,768]{1,0:T(8,128)(2,1)}) %all-gather.10.cloned.1.call-update) | async-done | bytes 1204240 | tf_op jit(solution)/shard_map/all_gather | solution.py:205
  162.7 15.6 %fusion.69 = (bf16[1536]{0:T(1024)(128)(2,1)S(1)}, bf16[784,1536]{1,0:T(8,128)(2,1)S(1)}, f32[784,1536]{1,0:T(8,128)}) fusion(f32[784,1536]{1,0:T(8,128)} %fusion.80, f32[1536]{0:T(1024)S(1)} %copy-done.36, bf16[784,768]{1,0:T(8,128)(2,1)} %all-gather.10.cloned.1.call-done, bf16[1536,768]{1,0:T(8,128)(2,1)S(1)} %copy-done), kind=kOutput, calls=%fused_computation.146 | convolution fusion | flops 1938799104 | bytes 15614976 | tf_op jit(solution)/shard_map/dot_general | solution.py:127
  179.8 3.1 convolution_convert_fusion.6
  182.9 5.0 multiply_convert_fusion.1
  189.4 3.1 convolution_convert_fusion.7
  192.9 3.6 fusion.55
  199.1 1.7 copy.186
  200.8 3.6 squeeze.16
  204.4 1.7 copy.190
  206.1 3.6 squeeze.17
  209.6 3.7 add_convert_fusion.2
  215.0 21.2 %reduce-scatter.7.cloned.1.call-done = bf16[392,768]{1,0:T(8,128)(2,1)} async-done(((bf16[784,768]{1,0:T(8,128)(2,1)}), bf16[392,768]{1,0:T(8,128)(2,1)}) %reduce-scatter.7.cloned.1.call-update) | async-done | bytes 602128 | tf_op jit(solution)/shard_map/reduce_scatter | solution.py:194
  236.2 2.6 fusion.71
  241.0 3.6 add_convert_fusion.1
  246.3 2.5 convert_element_type.202
  248.9 3.2 fusion.36
  252.1 4.5 fusion.76
  256.6 7.6 %all-gather.14.cloned.1.call-done = bf16[784,768]{1,0:T(8,128)(2,1)} async-done(((bf16[392,768]{1,0:T(8,128)(2,1)}), bf16[784,768]{1,0:T(8,128)(2,1)}) %all-gather.14.cloned.1.call-update) | async-done | bytes 1204240 | tf_op jit(solution)/shard_map/all_gather | solution.py:220
  264.2 2.9 convolution_convert_fusion.8
  268.5 3.6 reshape.294
  272.1 5.8 %multiply_reduce_fusion = (f32[16,12,49]{2,1,0:T(8,128)S(1)}, f32[16,12,49,49]{2,3,1,0:T(8,128)S(1)}) fusion(f32[16,12,49,49]{2,3,1,0:T(8,128)} %get-tuple-element.134, f32[16,12,49]{2,1,0:T(8,128)S(1)} %get-tuple-element.133, bf16[16,49,12,32]{1,0,3,2:T(8,128)(2,1)} %add_convert_fusion.1, bf16[16,49,12,32]{1,0,3,2:T(8,128)(2,1)} %reshape.294), kind=kOutput, calls=%fused_computation.5 | convolution fusion | flops 30877056 | bytes 4967424 | tf_op jit(solution)/shard_map/bqhd,bkhd->bhqk/dot_general | solution.py:85
  278.0 1.8 convert_reduce_fusion
  281.3 2.7 fusion.31
  284.0 2.7 fusion.77
  287.8 1.8 stack_reshape.9
  290.7 2.4 copy.198
  293.1 2.1 stack_reshape.10
  296.2 2.4 copy.201
  298.7 1.8 stack_reshape.11
  301.6 5.0 bitcast_convert_fusion
  306.7 3.8 fusion.29
  311.6 2.1 reshape.297
  313.7 6.2 %convolution_convert_fusion.1 = bf16[768,1536]{1,0:T(8,128)(2,1)} fusion(bf16[784,768]{1,0:T(8,128)(2,1)} %all-gather.8.cloned.1.call-done, bf16[784,1536]{1,0:T(8,128)(2,1)} %copy-done.48), kind=kOutput, calls=%fused_computation.30 | convolution fusion | flops 1850867712 | bytes 5971968 | tf_op jit(solution)/shard_map/dot_general | solution.py:133
  319.9 3.9 convolution_convert_fusion
  325.9 3.4 convolution_convert_fusion.2
  334.3 64.0 %all-reduce.1 = (bf16[2,384]{1,0:T(2,128)(2,1)S(1)}, bf16[169,12]{0,1:T(8,128)(2,1)S(1)}, bf16[1536]{0:T(1024)(128)(2,1)S(1)}) all-reduce(bf16[2,384]{1,0:T(2,128)(2,1)S(1)} %pad_maximum_fusion.3, bf16[169,12]{0,1:T(8,128)(2,1)S(1)} %fusion.57, bf16[1536]{0:T(1024)(128)(2,1)S(1)} %get-tuple-element.112), channel_id=1, replica_groups=mesh['dp'=16,'mp'=2] {'dp'}, use_global_device_ids=true, to_apply=%region_24.25 | all-reduce | flops 4332 | bytes 17328 | tf_op jit(solution)/shard_map/psum | solution.py:249
  401.8 1.8 fusion.53
  403.6 1.9 add_convert_fusion.5
  406.6 37.9 %all-reduce = (f32[768]{0:T(1024)}, f32[768]{0:T(1024)}, f32[768]{0:T(1024)}, f32[768]{0:T(1024)}, f32[768]{0:T(1024)}, /*index=5*/f32[768]{0:T(1024)}) all-reduce(f32[768]{0:T(1024)S(1)} %get-tuple-element.90, f32[768]{0:T(1024)S(1)} %get-tuple-element.95, ...), channel_id=1, replica_groups=mesh['dp'=16,'mp'=2] {'dp','mp'}, use_global_device_ids=true, to_apply=%region_18.19 | all-reduce | flops 4608 | bytes 36864 | tf_op jit(solution)/shard_map/psum | solution.py:256
  444.5 41.4 %all-reduce.5.cloned.1.call-done = (bf16[768,3,384]{2,0,1:T(8,128)(2,1)}, bf16[384,768]{1,0:T(8,128)(2,1)}, bf16[768,1536]{1,0:T(8,128)(2,1)}, bf16[1536,768]{1,0:T(8,128)(2,1)}) async-done(((bf16[768,3,384]{2,0,1:T(8,128)(2,1)}, bf16[384,768]{1,0:T(8,128)(2,1)}, bf16[768,1536]{1,0:T(8,128)(2,1)}, bf16[1536,768]{1,0:T(8,128)(2,1)}), (bf16[768,3,384]{2,0,1:T(8,128)(2,1)}, bf16[384,768]{1,0:T(8,128)(2,1)}, ...) | async-done | bytes 7077904 | tf_op jit(solution)/shard_map/psum | solution.py:248
  485.9 4.6 convert_element_type.231
  490.6 2.5 convert_element_type.234
  493.1 2.0 convert_element_type.219
  (194 shorter events, 52.3 us)
Async XLA Ops:
  7.2 155.5 %copy-start = (bf16[1536,768]{1,0:T(8,128)(2,1)S(1)}, bf16[1536,768]{1,0:T(8,128)(2,1)}, u32[]{:S(2)}) copy-start(bf16[1536,768]{1,0:T(8,128)(2,1)} %param.29) | copy-start | bytes 7077892
  7.2 5.4 %copy-start.41 = (f32[2,384]{1,0:T(2,128)S(1)}, f32[2,384]{1,0:T(2,128)}, u32[]{:S(2)}) copy-start(f32[2,384]{1,0:T(2,128)} %param.21) | copy-start | bytes 9220
  7.2 6.4 %copy-start.47 = (f32[169,12]{0,1:T(8,128)S(1)}, f32[169,12]{0,1:T(8,128)}, u32[]{:S(2)}) copy-start(f32[169,12]{0,1:T(8,128)} %param.22) | copy-start | bytes 24340
  7.2 31.3 %all-gather.6.cloned.1.call-start = ((), (), s32[]{:S(2)}) async-start(), calls=%async_computation.4 | async-start | bytes 1806336 | tf_op jit(solution)/shard_map/all_gather | solution.py:167
  8.6 6.6 %copy-start.40 = (s32[8,49]{1,0:T(8,128)S(1)}, s32[8,49]{1,0:T(8,128)}, u32[]{:S(2)}) copy-start(s32[8,49]{1,0:T(8,128)} %param.17) | copy-start | bytes 4708
  12.6 97.0 %reduce-scatter.5.cloned.1.call-start = ((), (), s32[]{:S(2)}) async-start(), calls=%async_computation.5 | async-start | bytes 1806336 | tf_op jit(solution)/shard_map/reduce_scatter | solution.py:177
  13.0 0.6 copy-start.34
  69.3 2.5 copy-start.10
  71.8 1.9 copy-start.6
  84.2 3.4 copy-start.8
  87.4 22.2 %copy-start.24 = (f32[768]{0:T(1024)S(1)}, f32[768]{0:T(1024)}, u32[]{:S(2)}) copy-start(f32[768]{0:T(1024)} %param.18) | copy-start | bytes 9220
  87.4 22.2 %copy-start.33 = (f32[768]{0:T(1024)S(1)}, f32[768]{0:T(1024)}, u32[]{:S(2)}) copy-start(f32[768]{0:T(1024)} %param.19) | copy-start | bytes 9220
  87.4 22.2 %copy-start.37 = (f32[768]{0:T(1024)S(1)}, f32[768]{0:T(1024)}, u32[]{:S(2)}) copy-start(f32[768]{0:T(1024)} %param.24) | copy-start | bytes 9220
  87.4 50.2 %all-gather.8.cloned.1.call-start = ((), (), s32[]{:S(2)}) async-start(), calls=%async_computation.6 | async-start | bytes 1806336 | tf_op jit(solution)/shard_map/all_gather | solution.py:188
  87.6 24.7 %copy-start.26 = (f32[392]{0:T(512)}, f32[392]{0:T(512)S(1)}, u32[]{:S(2)}) copy-start(f32[392]{0:T(512)S(1)} %div.84) | copy-start | bytes 4708
  88.8 23.4 %copy-start.31 = (f32[392]{0:T(512)}, f32[392]{0:T(512)S(1)}, u32[]{:S(2)}) copy-start(f32[392]{0:T(512)S(1)} %add.261) | copy-start | bytes 4708
  88.9 23.4 %copy-start.29 = (f32[392]{0:T(512)}, f32[392]{0:T(512)S(1)}, u32[]{:S(2)}) copy-start(f32[392]{0:T(512)S(1)} %rsqrt.27) | copy-start | bytes 4708
  91.4 21.9 %copy-start.28 = (f32[768]{0:T(1024)S(1)}, f32[768]{0:T(1024)}, u32[]{:S(2)}) copy-start(f32[768]{0:T(1024)} %param.25) | copy-start | bytes 9220
  91.4 21.9 %copy-start.38 = (f32[768]{0:T(1024)S(1)}, f32[768]{0:T(1024)}, u32[]{:S(2)}) copy-start(f32[768]{0:T(1024)} %param.26) | copy-start | bytes 9220
  112.2 1.1 copy-start.3
  114.4 48.3 %all-gather.10.cloned.1.call-start = ((), (), s32[]{:S(2)}) async-start(), calls=%async_computation.8 | async-start | bytes 1806336 | tf_op jit(solution)/shard_map/all_gather | solution.py:205
  116.7 76.2 %all-gather.12.cloned.1.call-start = ((), (), s32[]{:S(2)}) async-start(), calls=%async_computation.10 | async-start | bytes 1806336 | tf_op jit(solution)/shard_map/all_gather | solution.py:221
  117.3 45.4 %copy-start.36 = (f32[1536]{0:T(1024)S(1)}, f32[1536]{0:T(1024)}, u32[]{:S(2)}) copy-start(f32[1536]{0:T(1024)} %param.28) | copy-start | bytes 18436
  117.3 96.1 %reduce-scatter.9.cloned.1.call-start = ((), (), s32[]{:S(2)}) async-start(), calls=%async_computation.9 | async-start | bytes 1806336 | tf_op jit(solution)/shard_map/reduce_scatter | solution.py:209
  162.7 17.1 %copy-start.42 = (bf16[768,1536]{1,0:T(8,128)(2,1)S(1)}, bf16[768,1536]{1,0:T(8,128)(2,1)}, u32[]{:S(2)}) copy-start(bf16[768,1536]{1,0:T(8,128)(2,1)} %param.27) | copy-start | bytes 7077892
  178.3 1.4 copy-start.48
  182.9 53.4 %reduce-scatter.7.cloned.1.call-start = ((), (), s32[]{:S(2)}) async-start(), calls=%async_computation.7 | async-start | bytes 1806336 | tf_op jit(solution)/shard_map/reduce_scatter | solution.py:194
  187.9 1.4 copy-start.13
  192.4 71.7 %all-gather.14.cloned.1.call-start = ((), (), s32[]{:S(2)}) async-start(), calls=%async_computation.11 | async-start | bytes 1806336 | tf_op jit(solution)/shard_map/all_gather | solution.py:220
  196.5 2.6 copy-start.12
  209.6 3.7 copy-start.4
  209.6 26.6 %copy-start.39 = (f32[768]{0:T(1024)S(1)}, f32[768]{0:T(1024)}, u32[]{:S(2)}) copy-start(f32[768]{0:T(1024)} %param.30) | copy-start | bytes 9220
  215.0 24.9 %copy-start.9 = (bf16[392,768]{1,0:T(8,128)(2,1)S(1)}, bf16[392,768]{1,0:T(8,128)(2,1)}, u32[]{:S(2)}) copy-start(bf16[392,768]{1,0:T(8,128)(2,1)} %reshape.293) | copy-start | bytes 1806340
  238.9 1.0 copy-start.7
  241.0 159.2 %reduce-scatter.11.cloned.1.call-start = ((), (), s32[]{:S(2)}) async-start(), calls=%async_computation.12 | async-start | bytes 1806336 | tf_op jit(solution)/shard_map/reduce_scatter | solution.py:236
  252.0 12.2 %copy-start.46 = (bf16[384,768]{1,0:T(8,128)(2,1)S(1)}, bf16[384,768]{1,0:T(8,128)(2,1)}, u32[]{:S(2)}) copy-start(bf16[384,768]{1,0:T(8,128)(2,1)} %param.23) | copy-start | bytes 1769476
  272.1 5.9 %slice-start = ((s8[5505024]{0:T(1024)(128)(4,1)}), s8[4194304]{0:T(1024)(128)(4,1)S(1)}, s32[]{:S(2)}) async-start(s8[5505024]{0:T(1024)(128)(4,1)} %bitcast.79), calls=%async_computation.14 | async-start | bytes 8388608
  272.1 5.9 %slice-start.1 = ((s8[5505024]{0:T(1024)(128)(4,1)}), s8[1310720]{0:T(1024)(128)(4,1)S(1)}, s32[]{:S(2)}) async-start(s8[5505024]{0:T(1024)(128)(4,1)} %bitcast.79), calls=%async_computation.15 | async-start | bytes 2621440
  279.8 1.5 copy-start.5
  281.3 2.7 copy-start.18
  301.6 5.1 %copy-start.19 = (bf16[16,49,12,32]{1,0,3,2:T(8,128)(2,1)S(1)}, bf16[16,49,12,32]{1,0,3,2:T(8,128)(2,1)}, u32[]{:S(2)}) copy-start(bf16[16,49,12,32]{1,0,3,2:T(8,128)(2,1)} %add_convert_fusion.1) | copy-start | bytes 1806340
  306.6 179.3 %all-reduce.5.cloned.1.call-start = ((), (), s32[]{:S(2)}) async-start(), calls=%async_computation.13 | async-start | bytes 14155776 | tf_op jit(solution)/shard_map/psum | solution.py:248
  313.7 6.3 %copy-start.14 = (bf16[784,1536]{1,0:T(8,128)(2,1)S(1)}, bf16[784,1536]{1,0:T(8,128)(2,1)}, u32[]{:S(2)}) copy-start(bf16[784,1536]{1,0:T(8,128)(2,1)} %copy-done.13) | copy-start | bytes 7225348
  313.7 6.3 %copy-start.43 = (bf16[784,768]{1,0:T(8,128)(2,1)S(1)}, bf16[784,768]{1,0:T(8,128)(2,1)}, u32[]{:S(2)}) copy-start(bf16[784,768]{1,0:T(8,128)(2,1)} %all-gather.10.cloned.1.call-done) | copy-start | bytes 3612676
  319.9 3.9 copy-start.45
  323.9 1.6 copy-start.20
  323.9 1.6 copy-start.21
  323.9 1.6 copy-start.22
  323.9 2.0 copy-start.44
  329.3 1.1 copy-start.15
  330.4 3.0 copy-start.35
  330.5 69.7 %copy-start.2 = (f32[392,768]{1,0:T(8,128)S(1)}, f32[392,768]{1,0:T(8,128)}, u32[]{:S(2)}) copy-start(f32[392,768]{1,0:T(8,128)} %reshape.289) | copy-start | bytes 3612676
  330.5 69.7 %copy-start.25 = (f32[768]{0:T(1024)S(1)}, f32[768]{0:T(1024)}, u32[]{:S(2)}) copy-start(f32[768]{0:T(1024)} %param.18) | copy-start | bytes 9220
  330.5 69.7 %copy-start.27 = (f32[392]{0:T(512)S(1)}, f32[392]{0:T(512)}, u32[]{:S(2)}) copy-start(f32[392]{0:T(512)} %copy-done.26) | copy-start | bytes 4708
  331.9 69.9 %copy-start.32 = (f32[392]{0:T(512)S(1)}, f32[392]{0:T(512)}, u32[]{:S(2)}) copy-start(f32[392]{0:T(512)} %copy-done.31) | copy-start | bytes 4708
  331.9 69.9 %copy-start.30 = (f32[392]{0:T(512)S(1)}, f32[392]{0:T(512)}, u32[]{:S(2)}) copy-start(f32[392]{0:T(512)} %copy-done.29) | copy-start | bytes 4708
  400.2 3.4 copy-start.11
  485.9 4.7 copy-start.16
  490.6 2.6 copy-start.17
  493.1 3.2 copy-start.1
  493.1 2.0 copy-start.23
Sparse Core Ops, SparseCore 0:
  12.7 25.7 all-gather.5
  87.5 22.0 reduce-scatter.4
  114.5 23.0 all-gather.7
  139.6 23.0 all-gather.9
  164.7 23.0 all-gather.11
  189.9 22.0 reduce-scatter.8
  214.2 22.0 reduce-scatter.6
  241.1 23.0 all-gather.13
  306.7 22.0 reduce-scatter.10
  333.8 152.0 all-reduce.4
where the time goes:
time: 511 us; the launch traced here: 504 us
  waiting for transfers between devices  146 us (29%)
  blocking collectives  107 us (21%)
  local copies, waits for them, and re-layouts  91.4 us (18%)
  matrix products  86.4 us (17%)
  other arithmetic  56.4 us (11%)
  between operations  15.3 us (3%)
    psum x1, blocking collectives, shards(): lax.psum(sharded[1].astype(jnp.bfloat16), 'dp').astype(jnp.float32)  64 us
    psum x1, waiting for transfers between devices, shards(): lax.psum(sharded[0].astype(jnp.bfloat16), 'dp').astype(jnp.float32)  41.4 us
    psum x1, blocking collectives, shards(): lax.psum((grad_g1, grad_s1, jnp.sum(dmiddle, axis=0), grad_g2, grad_s2, j...  37.9 us
    reduce_scatter x1, waiting for transfers between devices, shards(): lax.psum_scatter(jnp.dot(hidden, fc2_weight, preferred_element_type=jnp.f...  21.2 us
    all_gather x1, waiting for transfers between devices, shards(): normed_mid_all = lax.all_gather(normed_mid, 'mp', axis=0, tiled=True)  20.1 us
    all_gather x1, waiting for transfers between devices, shards(): upstream_all = lax.all_gather(upstream, 'mp', axis=0, tiled=True)  18.8 us
    reduce_scatter x1, waiting for transfers between devices, shards(): lax.psum_scatter(jnp.dot(mixed_rows, proj_weight, preferred_element_type=...  18.1 us
    all_gather x1, waiting for transfers between devices, shards(): lax.all_gather(normed.reshape(windows_own, WIN, features), 'mp', axis=0,...  17.9 us
  transfers between devices with their start and end apart: 10, of which 7 were waited for; matrix products, arithmetic and copies ran while one was open for 22% of the time, Pallas kernels for 0%

commit v1 on v0

v1 whole, which is shorter than its diff:
```python
import functools

import jax
import jax.numpy as jnp
from jax import lax
from jax.experimental import pallas as pl
from jax.experimental.pallas import tpu as pltpu
from jax.sharding import PartitionSpec as P

HEAD = 32
WSIDE = 7
WIN = 49
REL = 169
SLOT = 64
GROUP = 4
LANES = 128
EPS = 1e-05
SCALING = HEAD ** (-0.5)
BF = jnp.bfloat16
F32 = jnp.float32
HIGH = lax.Precision.HIGHEST
VMEM_LIMIT = 28 * 1024 * 1024
ALL_VMEM = 58 * 1024 * 1024
BLOCK = 96
CORE, SIDE, LINE = 1, 2, 4

ROW_COL = (((1,), (0,)), ((), ()))
LAST_LAST = (((1,), (1,)), ((), ()))
ROWS_ROWS = (((0,), (0,)), ((), ()))


def mm(a, b, dims=ROW_COL):
    return lax.dot_general(a, b, dims, preferred_element_type=F32)


def norm_parts(rows):
    mean = jnp.mean(rows, axis=-1, keepdims=True)
    centred = rows - mean
    variance = jnp.mean(centred * centred, axis=-1, keepdims=True)
    inv = lax.rsqrt(variance + EPS)
    return centred * inv, inv


def norm_back(xhat, inv, gain, upstream):
    z = upstream * gain
    mean_z = jnp.mean(z, axis=-1, keepdims=True)
    mean_zx = jnp.mean(z * xhat, axis=-1, keepdims=True)
    return (z - mean_z - xhat * mean_zx) * inv


def head_masks():
    lane = lax.broadcasted_iota(jnp.int32, (SLOT, LANES), 1)
    return [jnp.where((lane >> 5) == h, 1.0, 0.0).astype(BF) for h in range(GROUP)]


def block_ones():
    row = lax.broadcasted_iota(jnp.int32, (GROUP * SLOT, GROUP * SLOT), 0)
    col = lax.broadcasted_iota(jnp.int32, (GROUP * SLOT, GROUP * SLOT), 1)
    return jnp.where((row >> 6) == (col >> 6), 1.0, 0.0).astype(BF)


def spread(tile, masks):
    return jnp.concatenate([tile * m for m in masks], axis=0)


def collect(full, masks_f):
    total = full[0:SLOT] * masks_f[0]
    for h in range(1, GROUP):
        total = total + full[h * SLOT : (h + 1) * SLOT] * masks_f[h]
    return total


def fill(scratch, rows):
    count = rows.shape[0]
    for g in range(scratch.shape[0]):
        scratch[g, 0:count, :] = rows[:, g * LANES : (g + 1) * LANES]
        scratch[g, count:, :] = jnp.zeros((scratch.shape[1] - count, LANES), rows.dtype)


def empty(scratch, count):
    return jnp.concatenate([scratch[g, 0:count, :] for g in range(scratch.shape[0])], axis=1).astype(BF)


def row_max(tile, low_half):
    low = jnp.max(jnp.where(low_half, tile, -3e38), axis=-1, keepdims=True)
    high = jnp.max(jnp.where(low_half, -3e38, tile), axis=-1, keepdims=True)
    return jnp.where(low_half, low, high)


def ds(start, size):
    unit = 384 if size % 384 == 0 else 48
    return pl.ds(pl.multiple_of(start, unit), size)


def each_block(me, *by_core):
    for c_rel, target in enumerate(by_core):
        for y_rel in range(2):
            for z_rel in range(4):
                yield target, y_rel, z_rel, (me & 1) ^ c_rel, ((me >> 1) & 1) ^ y_rel, (me >> 2) ^ z_rel


def line(ref):
    return ref[...].reshape(1, -1)


def begin(sems, *pairs):
    copies = [pltpu.make_async_copy(a, b, sems.at[i]) for i, (a, b) in enumerate(pairs)]
    for copy in copies:
        copy.start()
    return copies


def finish_all(copies):
    for copy in copies:
        copy.wait()


def attn_forward_kernel(windows, x_in, gain_ref, shift_ref, w_in, bias_ref, pos_ref, valid_ref,
                        prob_ref, q_ref, k_ref, v_ref, mixed_ref, normed_t_ref,
                        mask_s, q_s, k_s, v_s, mixed_s, x_ref, w_ref, in_sems):
    copies = begin(in_sems, (x_in, x_ref), *[(w_in.at[p], w_ref.at[p]) for p in range(3)])
    mask_s[...] = jnp.zeros(mask_s.shape, F32)
    for h in range(GROUP):
        mask_s[:, h * SLOT : h * SLOT + WIN] = valid_ref[...].astype(F32)
    masks = head_masks()
    ones = block_ones()
    low_half = lax.broadcasted_iota(jnp.int32, (SLOT, LANES), 1) < SLOT
    copies[0].wait()
    x = x_ref[...].astype(F32)
    rows = x.shape[0]
    groups = q_s.shape[0]
    xhat, _ = norm_parts(x)
    normed = (xhat * line(gain_ref) + line(shift_ref)).astype(BF)
    normed_t_ref[...] = normed.T
    for part, scratch in enumerate((q_s, k_s, v_s)):
        copies[1 + part].wait()
        got = mm(normed, w_ref[part])
        if part != 1:
            got = got + bias_ref[part // 2 : part // 2 + 1, :]
        fill(scratch, got.astype(BF).astype(F32))

    def window(w, carry):
        allowed = jnp.broadcast_to(mask_s[pl.ds(w, 1), :], (SLOT, GROUP * SLOT)) > 0.5
        for g in range(groups):
            cols = slice(g * LANES, (g + 1) * LANES)
            places = pl.ds(w, SLOT, stride=windows)
            q = q_s[g, places, :].astype(BF)
            k = k_s[g, places, :].astype(BF)
            v = v_s[g, places, :].astype(BF)
            q_ref[w, :, cols] = q
            k_ref[w, :, cols] = k
            v_ref[w, :, cols] = v
            scores = mm(q, spread(k, masks), LAST_LAST) * SCALING + pos_ref[g]
            scores = jnp.where(allowed, scores, -1000000000.0)
            top = jnp.concatenate([row_max(scores[:, :LANES], low_half), row_max(scores[:, LANES:], low_half)], axis=1)
            e = jnp.exp(scores - top)
            total = mm(e.astype(BF), ones)
            prob = (e / total).astype(BF)
            prob_ref[w, g] = prob
            mixed_s[g, places, :] = mm(prob, spread(v, masks))
        return carry

    lax.fori_loop(0, windows, window, 0, unroll=2)
    mixed_ref[...] = empty(mixed_s, rows)


def middle_kernel(x_ref, own_ref, peer_ref, bias_ref, gain_ref, shift_ref, middle_ref, nm_ref):
    middle = x_ref[...].astype(F32) + (own_ref[...].astype(F32) + peer_ref[...].astype(F32)) + line(bias_ref)
    middle_ref[...] = middle
    xhat, _ = norm_parts(middle)
    nm_ref[...] = (xhat * line(gain_ref) + line(shift_ref)).astype(BF)


def mlp_kernel(nm_ref, cot_ref, fc1_ref, b1_ref, fc2_ref, hid_ref, gpre_ref, out_ref, gmid_ref):
    hidden_size = fc1_ref.shape[1]
    features = fc1_ref.shape[0]
    step = 256 if hidden_size % 256 == 0 else 128
    count = hidden_size // step

    nm = nm_ref[...]
    cot = cot_ref[...]

    def units(c, carry):
        cols = pl.ds(pl.multiple_of(c * step, step), step)
        pre = mm(nm, fc1_ref[:, cols]) + b1_ref[:, cols]
        phi = 0.5 * (1.0 + lax.erf(pre * (0.5 ** 0.5)))
        hid_ref[:, cols] = (pre * phi).astype(BF)
        slope = phi + pre * (jnp.exp(-0.5 * pre * pre) * 0.3989422804014327)
        gpre_ref[:, cols] = (mm(cot, fc2_ref[cols, :], LAST_LAST) * slope).astype(BF)
        return carry

    lax.fori_loop(0, count, units, 0)

    def tile(c, carry):
        cols = pl.ds(pl.multiple_of(c * 256, 256), 256)
        gmid_ref[:, cols] = mm(gpre_ref[...], fc1_ref[cols, :], LAST_LAST).astype(BF)
        out_ref[:, cols] = mm(hid_ref[...], fc2_ref[:, cols]).astype(BF)
        return carry

    lax.fori_loop(0, features // 256, tile, 0)

def mlp_weights_kernel(count, split, me_ref, *refs):
    inputs, refs = refs[: 4 * count], refs[4 * count :]
    n_out = 5 if split else 3
    gb1_ref, *outs = refs[:n_out]
    held = refs[n_out : n_out + 4 * count]
    nts = refs[n_out + 4 * count : n_out + 5 * count]
    g1_ref, g2_ref, in_sems, out_sems = refs[n_out + 5 * count :]
    order = [4 * b + k for k in (0, 2, 1, 3) for b in range(count)]
    copies = dict(zip(order, begin(in_sems, *[(inputs[i], held[i]) for i in order])))
    blocks = [held[4 * b : 4 * b + 4] for b in range(count)]
    hidden_size = g1_ref.shape[1]
    features = g1_ref.shape[0]
    step = 384 if hidden_size % 384 == 0 else 128
    wide = features if hidden_size % features == 0 else step
    finish_all([copies[4 * b] for b in range(count)])
    for block, nt in zip(blocks, nts):
        nt[...] = block[0][...].T
    finish_all([copies[4 * b + k] for k in (2, 1) for b in range(count)])

    def second(j, carry):
        cols = ds(j * step, step)
        g2_ref[cols, :] = sum(mm(hid_ref[:, cols], cot_ref[...], ROWS_ROWS) for _, cot_ref, hid_ref, _ in blocks).astype(BF)
        return carry

    def first(j, carry):
        cols = ds(j * wide, wide)
        g1_ref[:, cols] = sum(mm(nt[...], block[3][:, cols]) for nt, block in zip(nts, blocks)).astype(BF)
        return carry

    lax.fori_loop(0, hidden_size // step, second, 0)
    me = me_ref[0]
    sent = []

    def send(k, source, target):
        sent.append(pltpu.make_async_copy(source, target, out_sems.at[k]))
        sent[-1].start()

    if split:
        for i, (target, y_rel, z_rel, c, y, z) in enumerate(each_block(me, outs[2], outs[3])):
            send(i, g2_ref.at[ds(c * 768 + y * 384 + z * 96, 96), :], target.at[y_rel, z_rel])
    else:
        send(0, g2_ref, outs[1])
    finish_all([copies[4 * b + 3] for b in range(count)])
    gb1_ref[...] = sum(jnp.sum(block[3][...].astype(F32), axis=0, keepdims=True) for block in blocks)
    lax.fori_loop(0, hidden_size // wide, first, 0)
    if split:
        for i, (target, y_rel, z_rel, c, y, z) in enumerate(each_block(me, outs[0], outs[1])):
            send(16 + i, g1_ref.at[ds(y * 384 + z * 96, 96), ds(c * 768, 768)], target.at[y_rel, z_rel])
    else:
        send(1, g1_ref, outs[0])
    finish_all(sent)


def middle_back_kernel(own_ref, peer_ref, middle_ref, cot_ref, gain_ref, gmiddle_ref, branch_ref, sums_ref):
    upstream = cot_ref[...].astype(F32)
    xhat, inv = norm_parts(middle_ref[...])
    gmid = own_ref[...].astype(F32) + peer_ref[...].astype(F32)
    sums_ref[0:1, :] = jnp.sum(gmid * xhat, axis=0, keepdims=True)
    sums_ref[1:2, :] = jnp.sum(gmid, axis=0, keepdims=True)
    gmiddle = upstream + norm_back(xhat, inv, line(gain_ref), gmid)
    gmiddle_ref[...] = gmiddle
    branch_ref[...] = gmiddle.astype(BF)
    sums_ref[2:3, :] = jnp.sum(gmiddle, axis=0, keepdims=True)
    sums_ref[3:4, :] = jnp.sum(upstream, axis=0, keepdims=True)


def attn_backward_kernel(windows, branch_ref, x_ref, prob_ref, q_ref, k_ref, v_ref, w_ref, proj_ref,
                         grads_ref, gqv_ref, gpos_ref, part_ref, sums_ref, gm_s, gq_s, gk_s, gv_s):
    rows = branch_ref.shape[0]
    groups = gm_s.shape[0]
    gpos_ref[...] = jnp.zeros(gpos_ref.shape, F32)
    masks = head_masks()
    masks_f = [m.astype(F32) for m in masks]
    ones = block_ones()
    fill(gm_s, mm(branch_ref[...], proj_ref[...], LAST_LAST).astype(BF).astype(F32))

    def window(w, carry):
        for g in range(groups):
            cols = slice(g * LANES, (g + 1) * LANES)
            places = pl.ds(w, SLOT, stride=windows)
            gm = gm_s[g, places, :].astype(BF)
            q = q_ref[w, :, cols]
            k = k_ref[w, :, cols]
            v = v_ref[w, :, cols]
            prob = prob_ref[w, g]
            prob_f = prob.astype(F32)
            gprob = mm(gm, spread(v, masks), LAST_LAST)
            both = prob_f * gprob
            delta = mm(both.astype(BF), ones)
            gs = (both - prob_f * delta).astype(BF)
            gpos_ref[g] += gs.astype(F32)
            gq_s[g, places, :] = mm(gs, spread(k, masks)) * SCALING
            gk_s[g, places, :] = collect(mm(gs, q, ROWS_ROWS), masks_f) * SCALING
            gv_s[g, places, :] = collect(mm(prob, gm, ROWS_ROWS), masks_f)
        return carry

    lax.fori_loop(0, windows, window, 0, unroll=2)
    back = None
    for part, scratch in enumerate((gq_s, gk_s, gv_s)):
        grad = empty(scratch, rows)
        grads_ref[part] = grad
        if part != 1:
            width = grad.shape[1]
            lanes = slice(part // 2 * width, (part // 2 + 1) * width)
            gqv_ref[:, lanes] = jnp.sum(grad.astype(F32), axis=0, keepdims=True)
        term = mm(grad, w_ref[part], LAST_LAST)
        back = term if back is None else back + term
    part_ref[...] = back.astype(BF)
    xhat, _ = norm_parts(x_ref[...].astype(F32))
    sums_ref[0:1, :] = jnp.sum(back * xhat, axis=0, keepdims=True)
    sums_ref[1:2, :] = jnp.sum(back, axis=0, keepdims=True)


def place_offset(i):
    return i // WSIDE * (2 * WSIDE - 1) + i % WSIDE


def offset_picks():
    row = lax.broadcasted_iota(jnp.int32, (2 * LANES, 2 * SLOT), 0)
    col = lax.broadcasted_iota(jnp.int32, (2 * LANES, 2 * SLOT), 1)
    j = col & (SLOT - 1)
    line = (j * 37) >> 8
    offset = place_offset(WIN - 1) - line * (2 * WSIDE - 1) - (j - line * WSIDE)
    hit = ((row & (LANES - 1)) == offset) & ((row >> 7) == (col >> 6)) & (j < WIN)
    return jnp.where(hit, 1.0, 0.0).astype(BF)


def position_kernel(table_ref, pos_ref, table_s, rows_s):
    heads = table_ref.shape[0]
    table_s[...] = jnp.zeros(table_s.shape, F32)
    table_s[0:heads, 0:REL] = table_ref[...]
    table = table_s[...]
    lines = table.shape[0]
    rows_s[WIN * lines :, :] = jnp.zeros((rows_s.shape[0] - WIN * lines, LANES), F32)
    for i in range(WIN):
        turned = pltpu.roll(table, (2 * LANES - place_offset(i)) % (2 * LANES), 1)
        rows_s[i * lines : (i + 1) * lines, :] = turned[:, :LANES]
    picks = offset_picks()
    for pair in range(pos_ref.shape[0] * 2):
        pieces = [rows_s[pl.ds(2 * pair + k, SLOT, stride=lines), :] for k in range(2)]
        rest = jnp.concatenate(pieces, axis=1)
        total = jnp.zeros((SLOT, 2 * SLOT), F32)
        for _ in range(3):
            top = rest.astype(BF)
            total = total + mm(top, picks)
            rest = rest - top.astype(F32)
        pos_ref[pair // 2, :, pair % 2 * LANES : (pair % 2 + 1) * LANES] = total


def attn_weights_kernel(count, split, me_ref, sums2_ref, gb1_ref, *refs):
    blocks, refs = [refs[7 * b : 7 * b + 7] for b in range(count)], refs[7 * count :]
    *outs, small_ref = refs[:3]
    gw_ref, gproj_ref, rows_s, out_sems = refs[3:]
    gproj, gqv, gpos, sums = 0.0, 0.0, 0.0, 0.0
    for _, mixed_ref, branch_ref, _, gqv_ref, gpos_ref, sums_ref in blocks:
        gproj = gproj + mm(mixed_ref[...], branch_ref[...], ROWS_ROWS)
        gqv, gpos, sums = gqv + gqv_ref[...], gpos + gpos_ref[...], sums + sums_ref[...]
    width, features = gproj.shape
    gproj_ref[...] = gproj.astype(BF)
    hidden = gb1_ref.shape[1]
    lines = [sums[k : k + 1] for k in range(2)] + [sums2_ref[k : k + 1, :] for k in range(4)]
    lines.append(gqv)
    lines += [gb1_ref[:, k : min(k + features, hidden)] for k in range(0, hidden, features)]
    small = jnp.concatenate(
        [jnp.concatenate([line, jnp.zeros((1, features - line.shape[1]), F32)], axis=1) if line.shape[1] < features else line
         for line in lines] + [jnp.zeros((12 - len(lines), features), F32)], axis=0)
    picks = offset_picks()
    for pair in range(gpos.shape[0] * 2):
        rest = gpos[pair // 2][:, pair % 2 * LANES : (pair % 2 + 1) * LANES]
        total = jnp.zeros((SLOT, 2 * LANES), F32)
        for _ in range(2):
            top = rest.astype(BF)
            total = total + mm(top, picks, LAST_LAST)
            rest = rest - top.astype(F32)
        for k in range(2):
            rows_s[pl.ds(2 * pair + k, SLOT, stride=16), :] = total[:, k * LANES : (k + 1) * LANES]
    for h in range(gpos.shape[0] * 4, 16):
        rows_s[pl.ds(h, SLOT, stride=16), :] = jnp.zeros((SLOT, LANES), F32)
    table = jnp.zeros((16, 2 * LANES), F32)
    for i in range(WIN):
        row = jnp.concatenate([rows_s[i * 16 : (i + 1) * 16, :], jnp.zeros((16, LANES), F32)], axis=1)
        table = table + (pltpu.roll(row, place_offset(i), 1) if i else row)
    packed = [jnp.concatenate([table[3 * r + k : 3 * r + k + 1] for k in range(3)], axis=1) for r in range(4)]
    small_ref[...] = jnp.concatenate([small] + packed, axis=0).astype(BF)
    sent = []

    def send(k, source, target):
        sent.append(pltpu.make_async_copy(source, target, out_sems.at[k]))
        sent[-1].start()

    if split:
        for i, (target, y_rel, z_rel, c, y, z) in enumerate(each_block(me_ref[0], *outs)):
            send(i, gproj_ref.at[ds((c * 4 + y * 2 + (z >> 1)) * 48, 48), ds((z & 1) * 384, 384)],
                 target.at[y_rel, z_rel, 48:96, 384:768])
    else:
        send(0, gproj_ref, outs[1])
    for part in range(3):
        gw = 0.0
        for normed_t_ref, _, _, grads_ref, _, _, _ in blocks:
            gw = gw + mm(normed_t_ref[...], grads_ref[part])
        gw_ref[part] = gw.astype(BF)
        if split:
            for i, (target, y_rel, z_rel, c, y, z) in enumerate(each_block(me_ref[0], *outs)):
                send(16 * (part + 1) + i, gw_ref.at[part, ds(c * 384 + y * 192 + z * 48, 48), :],
                     target.at[y_rel, z_rel, part // 2 * 48 : part // 2 * 48 + 48, part % 2 * 384 : part % 2 * 384 + 384])
        else:
            send(1 + part, gw_ref.at[part], outs[0].at[part])
    finish_all(sent)


def input_back_kernel(own_ref, peer_ref, x_ref, gain_ref, gmiddle_ref, gpatch_ref):
    gnorm = own_ref[...].astype(F32) + peer_ref[...].astype(F32)
    xhat, inv = norm_parts(x_ref[...].astype(F32))
    gpatch_ref[...] = (gmiddle_ref[...] + norm_back(xhat, inv, line(gain_ref), gnorm)).astype(BF)


def finish_kernel(me_ref, *refs):
    sources, outs, held, wide, (in_sems, out_sems) = refs[:4], refs[4:6], refs[6:10], refs[10:12], refs[12:]
    copies = begin(in_sems, *zip(sources, held))
    sent = []

    def put(value, k, where):
        wide[k][where] = value.astype(F32)
        sent.append(pltpu.make_async_copy(wide[k].at[where], outs[k].at[where], out_sems.at[len(sent)]))
        sent[-1].start()

    for source, y_rel, z_rel, c, y, z in each_block(me_ref[0], (0, 1), (2, 3)):
        source = source[y_rel]
        if z_rel == 0:
            copies[source].wait()
        piece = held[source].at[z_rel]
        lines = ds(c * 384 + y * 192 + z * 48, 48)
        put(piece[0:48, 0:384], 0, (0, lines, slice(None)))
        put(piece[0:48, 384:768], 0, (1, lines, slice(None)))
        put(piece[48:96, 0:384], 0, (2, lines, slice(None)))
        put(piece[48:96, 384:768], 1, (ds((c * 4 + y * 2 + (z >> 1)) * 48, 48), ds((z & 1) * 384, 384)))
    finish_all(sent)


def finish_mlp_kernel(me_ref, *refs):
    sources, (g1_out, g2_out, small_ref), held, (g1_ref, g2_ref, small_s, in_sems, out_sems) = (
        refs[:4], refs[4:7], refs[7:11], refs[11:])
    copies = begin(in_sems, *zip(sources, held))
    sent = []

    def put(value, k, wide, out, where):
        wide[where] = value.astype(F32)
        sent.append(pltpu.make_async_copy(wide.at[where], out.at[where], out_sems.at[k, len(sent) // 2]))
        sent[-1].start()

    for source, y_rel, z_rel, c, y, z in each_block(me_ref[0], (0, 1), (2, 3)):
        source = source[y_rel]
        if z_rel == 0:
            copies[source].wait()
        piece = held[source].at[z_rel]
        put(piece[0:BLOCK, :], 0, g1_ref, g1_out, (ds(y * 384 + z * 96, 96), ds(c * 768, 768)))
        put(piece[BLOCK : 2 * BLOCK, :], 1, g2_ref, g2_out, (ds(c * 768 + y * 384 + z * 96, 96), slice(None)))
        small_s[z * 4 + y * 2 + c] = piece[2 * BLOCK :, :].astype(F32)
    total = small_s[0]
    for d in range(1, 16):
        total = total + small_s[d]
    small_ref[...] = total
    finish_all(sent)


def shape_of(*dims, dtype=F32):
    return jax.ShapeDtypeStruct(dims, dtype)


def call(kernel, outs, scratch, name, flops, smem, *args, far=(), far_outs=(), limit=VMEM_LIMIT):
    space = lambda is_far: pl.BlockSpec(memory_space=pltpu.HBM if is_far else pltpu.VMEM)
    in_specs = [pl.BlockSpec(memory_space=pltpu.SMEM)] * len(smem) + [space(i in far) for i in range(len(args))]
    return pl.pallas_call(
        kernel,
        out_shape=outs,
        in_specs=in_specs,
        out_specs=[space(i in far_outs) for i in range(len(outs))],
        scratch_shapes=scratch,
        compiler_params=pltpu.CompilerParams(vmem_limit_bytes=limit),
        cost_estimate=pl.CostEstimate(flops=flops, bytes_accessed=flops // 256, transcendentals=0),
        name=name,
    )(*smem, *args)


def like(*arrays):
    return [pltpu.VMEM(a.shape, a.dtype) for a in arrays]


def dma(*counts):
    return [pltpu.SemaphoreType.DMA(c if isinstance(c, tuple) else (c,)) for c in counts]


SMALL = 1000000


def position(table):
    heads = table.shape[0]
    groups = -(-heads // GROUP)
    return call(position_kernel, [shape_of(groups, SLOT, GROUP * SLOT)],
                [pltpu.VMEM((16, 2 * LANES), F32), pltpu.VMEM((16 * SLOT, LANES), F32)], "position", SMALL, (), table)[0]


def attn_forward(windows, x, ln1, qkv, qv_bias, pos, mask):
    rows, features = x.shape
    width = qkv.shape[2]
    groups = width // LANES
    tile = shape_of(windows, SLOT, width, dtype=BF)
    outs = [shape_of(windows, groups, SLOT, GROUP * SLOT, dtype=BF), tile, tile, tile, shape_of(rows, width, dtype=BF),
            shape_of(features, rows, dtype=BF)]
    scratch = [pltpu.VMEM((windows, GROUP * SLOT), F32)] + [pltpu.VMEM((groups, SLOT * windows, LANES), F32)] * 4
    scratch += like(x, qkv) + dma(4)
    return call(functools.partial(attn_forward_kernel, windows), outs, scratch, "attn_forward", SMALL, (),
                x, *ln1, qkv, qv_bias, pos, mask, far=(0, 3), limit=ALL_VMEM)


def middle_norm(x, own, peer, bias, ln2):
    rows, features = x.shape
    return call(middle_kernel, [shape_of(rows, features), shape_of(rows, features, dtype=BF)], [], "middle", SMALL, (),
                x, own, peer, bias, *ln2, limit=ALL_VMEM)


def mlp(nm, cot, fc1, fc1_bias, fc2):
    rows, features = nm.shape
    hidden = fc2.shape[0]
    outs = [shape_of(rows, hidden, dtype=BF)] * 2 + [shape_of(rows, features, dtype=BF)] * 2
    return call(mlp_kernel, outs, [], "mlp", SMALL, (), nm, cot, fc1, fc1_bias, fc2)


def mlp_weights(split, me, blocks):
    rows, features = blocks[0][0].shape
    hidden = blocks[0][2].shape[1]
    grads = [shape_of(features, hidden, dtype=BF), shape_of(hidden, features, dtype=BF)]
    outs = [shape_of(1, hidden)] + ([shape_of(2, 4, BLOCK, features, dtype=BF)] * 4 if split else grads)
    flat = [a for b in blocks for a in b]
    scratch = like(*flat) + [pltpu.VMEM((features, rows), BF)] * len(blocks) + like(*grads) + dma(len(flat), 32)
    return call(functools.partial(mlp_weights_kernel, len(blocks), split), outs, scratch, "mlp_weights", SMALL,
                (me,), *flat, far=range(len(flat)), far_outs=range(1, len(outs)), limit=ALL_VMEM)


def middle_back(own, peer, middle, cot, gain):
    rows, features = middle.shape
    return call(
        middle_back_kernel, [shape_of(rows, features), shape_of(rows, features, dtype=BF), shape_of(4, features)], [],
        "middle_back", 20000 * SMALL, (), own, peer, middle, cot, gain)


def attn_backward(windows, branch, x, kept, qkv, proj):
    rows, features = branch.shape
    width = proj.shape[0]
    groups = width // LANES
    outs = [shape_of(3, rows, width, dtype=BF), shape_of(1, 2 * width), shape_of(groups, SLOT, GROUP * SLOT),
            shape_of(rows, features, dtype=BF), shape_of(2, features)]
    scratch = [pltpu.VMEM((groups, SLOT * windows, LANES), F32)] * 4
    return call(functools.partial(attn_backward_kernel, windows), outs, scratch, "attn_backward", SMALL, (),
                branch, x, *kept, qkv, proj)


def attn_weights(split, me, sums2, gb1, blocks):
    features = blocks[0][0].shape[0]
    width = blocks[0][1].shape[1]
    grads = [shape_of(3, features, width, dtype=BF), shape_of(width, features, dtype=BF)]
    outs = ([shape_of(2, 4, BLOCK, features, dtype=BF)] * 2 if split else grads) + [shape_of(16, features, dtype=BF)]
    scratch = like(*grads) + [pltpu.VMEM((16 * SLOT, LANES), F32)]
    flat = [a for b in blocks for a in b]
    return call(functools.partial(attn_weights_kernel, len(blocks), split), outs, scratch + dma(64),
                "attn_weights", SMALL, (me,), sums2, gb1, *flat, far_outs=(0, 1))


def input_back(own, peer, x, gain, gmiddle):
    rows, features = x.shape
    return call(input_back_kernel, [shape_of(rows, features, dtype=BF)], [], "input_back", SMALL, (),
                own, peer, x, gain, gmiddle)[0]


def finish(me, sources, *outs):
    scratch = like(*sources, *outs) + dma(4, 16 * 4)
    return call(finish_kernel, list(outs), scratch, "finish", SMALL, (me,), *sources, far=range(4), far_outs=range(len(outs)))


def finish_mlp(me, sources):
    features = sources[0].shape[2]
    outs = [shape_of(features, 2 * features), shape_of(2 * features, features), shape_of(16, features)]
    scratch = like(*sources, *outs[:2]) + [pltpu.VMEM((16, 16, features), F32)] + dma(4, (2, 16))
    return call(finish_mlp_kernel, outs, scratch, "finish_mlp", SMALL, (me,), *sources, far=range(4), far_outs=(0, 1))


def across(v):
    return lax.ppermute(v, "mp", [(0, 1), (1, 0)])


def flip(v, bits):
    return lax.ppermute(v, "dp", [(i, i ^ bits) for i in range(16)])


def after(v, *others):
    return lax.optimization_barrier((v, *others))[0]


def total_of(terms):
    total = terms[0].astype(F32)
    for t in terms[1:]:
        total = total + t.astype(F32)
    return total.astype(BF)


def side_send(keep, got):
    return total_of([keep[1], got[1]])


def line_sends(keep, got, side):
    return [total_of([keep[0, k], got[0, k], side[k]]) for k in (1, 2, 3)]


def own_piece(keep, got, side, line):
    return total_of([keep[0, 0], got[0, 0], side[0], *line])


def flip_line(pieces):
    return [flip(p, LINE * k) for k, p in zip((1, 2, 3), pieces)]


def shards(
    dp_size,
    mp_size,
    patches,
    token_valid,
    ln1_gain,
    ln1_shift,
    qkv_weight,
    qv_bias,
    bias_table,
    proj_weight,
    proj_bias,
    ln2_gain,
    ln2_shift,
    fc1_weight,
    fc1_bias,
    fc2_weight,
    fc2_bias,
    cotangent,
):
    windows, _, features = patches.shape
    rows = windows * WIN
    width = proj_weight.shape[0]
    heads = width // HEAD
    fast = mp_size == 2 and dp_size == 16 and features == 768
    x = patches.transpose(1, 0, 2).reshape(rows, features)
    cot = cotangent.transpose(1, 0, 2).reshape(rows, features)
    row = lambda a: a.reshape(1, -1)
    extra = -width % LANES
    qkv = jnp.pad(qkv_weight.transpose(1, 0, 2), ((0, 0), (0, 0), (0, extra)))
    proj = jnp.pad(proj_weight, ((0, extra), (0, 0)))
    pos = position(bias_table.T)
    bias = jnp.pad(qv_bias, ((0, 0), (0, extra)))
    valid = token_valid.astype(F32)
    ln1, ln2 = (ln1_gain, ln1_shift), (ln2_gain, ln2_shift)

    def blocks_of(v):
        return [v, across(v)] if fast else list(lax.all_gather(v, "mp"))

    def own_sums(parts):
        if fast:
            return parts[0], across(parts[1])
        own = lax.psum_scatter(jnp.concatenate(parts), "mp", scatter_dimension=0, tiled=True)
        return own, jnp.zeros_like(own)

    index = lax.axis_index("dp").astype(jnp.int32)
    me = index.reshape(1)
    valids = blocks_of(valid)
    kept, xs = [], []
    for x_b, valid_b in zip(blocks_of(x), valids):
        if kept:
            x_b = after(x_b, kept[0][4])
            if fast:
                core = index & 1
                half = across(lax.dynamic_slice_in_dim(proj, core * (width // 2), width // 2, 0))
        xs.append(x_b)
        kept.append(attn_forward(windows, x_b, ln1, qkv, bias, pos, valid_b))
    project = lambda mixed, weight: jnp.dot(mixed, weight, preferred_element_type=F32).astype(BF)
    if fast:
        cots = [cot, across(after(cot, kept[0][4], valids[1], half))]
        mixed = across(after(kept[1][4], cots[1]))
        half = after(half, kept[1][4])
        rest = flip(half, CORE)
        other = jnp.where(core == 0, jnp.concatenate([half, rest]), jnp.concatenate([rest, half]))
        parts = project(kept[0][4], proj), project(mixed, other)
    else:
        parts = own_sums([project(k[4], proj) for k in kept])
        cots = blocks_of(cot)
    middle, nm = middle_norm(x, *parts, proj_bias, ln2)

    blocks, outs, gmids = [], [], []
    for nm_b, cot_b in zip(blocks_of(nm), cots):
        if blocks:
            nm_b = after(nm_b, gmids[-1])
        hid, gpre, out_b, gmid_b = mlp(nm_b, cot_b, fc1_weight, row(fc1_bias), fc2_weight)
        blocks.append((nm_b, cot_b, hid, gpre))
        outs.append(out_b)
        gmids.append(gmid_b)
    gmid_own, gmid_peer = own_sums(gmids)
    gb1, *g_mlp = mlp_weights(fast, me, blocks)
    outs = own_sums(outs)
    gmid_peer = after(gmid_peer, gb1)
    gmiddle, branch, sums2 = middle_back(gmid_own, gmid_peer, middle, cot, ln2[0])
    branches = blocks_of(branch)
    if fast:
        keep1, send1, keep2, send2 = g_mlp
        got1, got2 = after(flip(send1, CORE), branch), after(flip(send2, CORE), branch)
        side1, side2 = side_send(keep1, got1), side_send(keep2, got2)
        branches[0] = after(branches[0], side1, side2)
    backs, gparts = [], []
    for b, kept_b in enumerate(kept):
        if b == 1 and fast:
            side1 = after(flip(side1, SIDE), gparts[0])
            line1 = line_sends(keep1, got1, side1)
            branches[1] = after(branches[1], *line1, gparts[0])
        *back, gpart, gsum = attn_backward(windows, branches[b], xs[b], kept_b[:4], qkv, proj)
        backs.append((*back, gsum))
        gparts.append(gpart)
    if fast:
        side2 = after(flip(side2, SIDE), gparts[1])
        line2 = line_sends(keep2, got2, side2)
        line1 = [after(r, gparts[1]) for r in flip_line(line1)]
        piece1 = own_piece(keep1, got1, side1, line1)
        branches[0] = after(branches[0], piece1, *line2, outs[1])
    *g_attn, small = attn_weights(
        fast, me, sums2, gb1, [(k[5], k[4], br, *back) for k, br, back in zip(kept, branches, backs)])
    gnorms = own_sums(gparts)
    gpatch = input_back(*gnorms, x, ln1[0], gmiddle)
    output = (middle + outs[0].astype(F32) + outs[1].astype(F32) + row(fc2_bias)).astype(BF)

    if fast:
        line2 = [after(r, small) for r in flip_line(line2)]
        piece2 = own_piece(keep2, got2, side2, line2)
        keep, send = g_attn
        got = flip(after(send, piece2), CORE)
        side = flip(side_send(keep, got), SIDE)
        fc = jnp.concatenate([piece1, piece2, small], axis=0)
        fc_quad = jnp.stack([fc] + flip_line([fc] * 3))
        side = after(side, fc_quad, output)
        line = [after(r, gpatch) for r in flip_line(line_sends(keep, got, side))]
        piece = own_piece(keep, got, side, line)
        quad = jnp.stack([piece] + flip_line([piece] * 3))
        fc_pair = after(flip(fc_quad, SIDE), quad)
        g_fc1, g_fc2, small = finish_mlp(me, (fc_quad, fc_pair, after(flip(fc_quad, CORE), quad), after(flip(fc_pair, CORE), quad)))
        pair = flip(quad, SIDE)
        gw, gproj = finish(me, (quad, pair, flip(quad, CORE), after(flip(pair, CORE), small)),
                           shape_of(3, features, width), shape_of(width, features))
        totals = small[0:6] + across(small[0:6])
    else:
        g_fc1, g_fc2, gw, gproj = [g.astype(F32) for g in lax.psum((*g_mlp, *g_attn), "dp")]
        gw, gproj = gw[:, :, :width], gproj[:width]
        small = lax.psum(small, "dp").astype(F32)
        totals = lax.psum(small[0:6], "mp")
    padded = width + extra
    gqv = jnp.stack([small[6, :width], small[6, padded : padded + width]])
    gb1 = small[7:12].reshape(-1)[: gb1.size]
    gt = small[12:].reshape(12, 2 * LANES)[:heads, :REL].T

    unrow = lambda a: a.reshape(WIN, windows, features).transpose(1, 0, 2)
    return (
        unrow(output),
        unrow(gpatch),
        totals[0],
        totals[1],
        gw.transpose(1, 0, 2),
        gqv,
        gt,
        gproj,
        totals[4],
        totals[2],
        totals[3],
        g_fc1,
        gb1,
        g_fc2,
        totals[5],
    )


def solution(mesh):
    placed = (
        P(("dp", "mp"), None, None),
        P(("dp", "mp"), None),
        P(),
        P(),
        P(None, None, "mp"),
        P(None, "mp"),
        P(None, "mp"),
        P("mp", None),
        P(),
        P(),
        P(),
        P(None, "mp"),
        P("mp"),
        P("mp", None),
        P(),
        P(("dp", "mp"), None, None),
    )
    return jax.shard_map(
        functools.partial(shards, mesh.shape["dp"], mesh.shape["mp"]),
        mesh=mesh,
        in_specs=placed,
        out_specs=(
            P(("dp", "mp"), None, None),
            P(("dp", "mp"), None, None),
            P(),
            P(),
            P(None, None, "mp"),
            P(None, "mp"),
            P(None, "mp"),
            P("mp", None),
            P(),
            P(),
            P(),
            P(None, "mp"),
            P("mp"),
            P("mp", None),
            P(),
        ),
        check_vma=False,
    )
```

time: 511 us -> 230 us (0.45); the launches traced: 504 us -> 230 us
  blocking collectives: 107 us -> 0 us
  Pallas kernels: 0 us -> 90.9 us
  matrix products: 86.4 us -> 4.08 us
  local copies, waits for them, and re-layouts: 91.4 us -> 12.9 us
  waiting for transfers between devices: 146 us -> 69.3 us
  other arithmetic: 56.4 us -> 3.95 us
  starting transfers between devices: 1.03 us -> 47.4 us
  between operations: 15.3 us -> 1.29 us
    psum x2 -> x0, blocking collectives: 102 us -> none  [the longest x1 64 us: shards(): lax.psum(sharded[1].astype(jnp.bfloat16), 'dp').astype(jnp.float32)]
    pallas_call x0 -> x14, Pallas kernels: none -> 90.9 us  [call(): pl.pallas_call(kernel, out_shape=outs, in_specs=in_specs, out_specs=[spac...]
    dot_general x23 -> x2, matrix products: 86.4 us -> 4.08 us  [shards(): jnp.dot(mixed, weight, preferred_element_type=F32).astype(BF)]
    ppermute x0 -> x39, waiting for transfers between devices: none -> 69.3 us  [the longest x28 55.6 us: flip(): return lax.ppermute(v, 'dp', [(i, i ^ bits) for i in range(16)])]
    all_gather x5 -> x0, waiting for transfers between devices: 64.5 us -> none  [the longest x1 20.1 us: shards(): normed_mid_all = lax.all_gather(normed_mid, 'mp', axis=0, tiled=True)]
    ppermute x0 -> x39, starting transfers between devices: none -> 47.4 us  [the longest x28 35 us: flip(): return lax.ppermute(v, 'dp', [(i, i ^ bits) for i in range(16)])]
    psum x1 -> x0, waiting for transfers between devices: 41.4 us -> none  [shards(): lax.psum(sharded[0].astype(jnp.bfloat16), 'dp').astype(jnp.float32)]
    reduce_scatter x4 -> x0, waiting for transfers between devices: 39.4 us -> none  [the longest x1 21.2 us: shards(): lax.psum_scatter(jnp.dot(hidden, fc2_weight, preferred_element_type=jnp.f...]
  transfers between devices with their start and end apart: 10 -> 39, of which waited for: 7 -> 15; matrix products, arithmetic and copies ran while one was open for 22% -> 3% of each run, Pallas kernels for 0% -> 35%
where the time goes in v1:
time: 230 us
  Pallas kernels  90.9 us (40%)
  waiting for transfers between devices  69.3 us (30%)
  starting transfers between devices  47.4 us (21%)
  local copies, waits for them, and re-layouts  12.9 us (6%)
  matrix products  4.08 us (2%)
  other arithmetic  3.95 us (2%)
    pallas_call x14, Pallas kernels, call(): pl.pallas_call(kernel, out_shape=outs, in_specs=in_specs, out_specs=[spac...  90.9 us
    ppermute x28, waiting for transfers between devices, flip(): return lax.ppermute(v, 'dp', [(i, i ^ bits) for i in range(16)])  55.6 us
    ppermute x28, starting transfers between devices, flip(): return lax.ppermute(v, 'dp', [(i, i ^ bits) for i in range(16)])  35 us
    ppermute x11, waiting for transfers between devices, across(): return lax.ppermute(v, 'mp', [(0, 1), (1, 0)])  13.7 us
    ppermute x11, starting transfers between devices, across(): return lax.ppermute(v, 'mp', [(0, 1), (1, 0)])  12.4 us
    unnamed x94, local copies, waits for them, and re-layouts  10 us
  transfers between devices with their start and end apart: 39, of which 15 were waited for; matrix products, arithmetic and copies ran while one was open for 3% of the time, Pallas kernels for 35%

profile of v1, /device:TPU:0, one launch (start us, length us, event | category | flops | bytes accessed | tf_op | source)
XLA Modules:
  0.0 229.9 jit_solution(795269890259237728)
XLA Ops:
  0.6 1.0 constant_dynamic-slice_fusion
  1.6 3.0 %collective-permute-start.2 = (bf16[192,768]{1,0:T(8,128)(2,1)S(1)}, bf16[192,768]{1,0:T(8,128)(2,1)S(1)}, u32[]{:S(2)}, u32[]{:S(2)}) collective-permute-start(bf16[192,768]{1,0:T(8,128)(2,1)S(1)} %constant_dynamic-slice_fusion), channel_id=1, source_target_pairs={{0,1},{1,0},{2,3},{3,2},{4,5},{5,4},{6,7},{7,6},{8,9},{9,8},{10,11... | collective-permute-start | bytes 884744 | tf_op jit(solution)/shard_map/ppermute | solution.py:589
  4.6 0.7 convert_element_type.291.valid_ref
  5.4 2.0 collective-permute-start
  7.4 0.7 copy-done.35
  9.3 12.1 %attn_forward.2 = (bf16[8,3,64,256]{3,2,1,0:T(8,128)(2,1)}, bf16[8,64,384]{2,1,0:T(8,128)(2,1)}, bf16[8,64,384]{2,1,0:T(8,128)(2,1)}, bf16[8,64,384]{2,1,0:T(8,1...) custom-call(bf16[392,768]{1,0:T(8,128)(2,1)} %bitcast.101, f32[768]{0:T(1024)} %gain_ref.9, f32[768]{0:T(1024)} %shift_ref.4, ...), custom_call_target="tpu_custom_call" | custom-call | flops 1000000 | bytes 3906 | tf_op jit(solution)/shard_map/attn_forward/pallas_call | solution.py:474
  21.5 3.9 %collective-permute-done.x_in.x_ref = bf16[392,768]{1,0:T(8,128)(2,1)S(1)} collective-permute-done((bf16[392,768]{1,0:T(8,128)(2,1)}, bf16[392,768]{1,0:T(8,128)(2,1)S(1)}, u32[]{:S(2)}, u32[]{:S(2)}) %collective-permute-start) | collective-permute-done | bytes 602144 | tf_op jit(solution)/shard_map/ppermute | solution.py:589
  25.5 0.8 copy-done.11
  26.3 11.9 %attn_forward.3 = (bf16[8,3,64,256]{3,2,1,0:T(8,128)(2,1)}, bf16[8,64,384]{2,1,0:T(8,128)(2,1)}, bf16[8,64,384]{2,1,0:T(8,128)(2,1)}, bf16[8,64,384]{2,1,0:T(8,1...) custom-call(bf16[392,768]{1,0:T(8,128)(2,1)} %copy-done.11, f32[768]{0:T(1024)} %gain_ref.9, f32[768]{0:T(1024)} %shift_ref.4, ...), custom_call_target="tpu_custom_call" | custom-call | flops 1000000 | bytes 3906 | tf_op jit(solution)/shard_map/attn_forward/pallas_call | solution.py:474
  38.3 0.8 copy-done.7
  39.1 2.1 collective-permute-start.4
  41.2 1.3 convolution_convert_fusion.1.own_ref
  42.9 4.1 %collective-permute-done.4 = bf16[392,384]{1,0:T(8,128)(2,1)} collective-permute-done((bf16[392,384]{1,0:T(8,128)(2,1)}, bf16[392,384]{1,0:T(8,128)(2,1)}, u32[]{:S(2)}, u32[]{:S(2)}) %collective-permute-start.4) | collective-permute-done | bytes 301088 | tf_op jit(solution)/shard_map/ppermute | solution.py:589
  47.0 2.8 %convolution_convert_fusion.peer_ref = bf16[392,768]{1,0:T(8,128)(2,1)} fusion(bf16[392,384]{1,0:T(8,128)(2,1)} %collective-permute-done.4, bf16[192,768]{1,0:T(8,128)(2,1)} %collective-permute-done.5, bf16[192,768]{1,0:T(8,128)(2,1)} %copy-done.46, pred[]{:T(512)S(6)} %eq.3), kind=kOutput, calls=%fused_computation | convolution fusion | flops 234166272 | bytes 1492993 | tf_op jit(solution)/shard_map/dot_general | solution.py:680
  49.8 3.0 %middle.1 = (f32[392,768]{1,0:T(8,128)}, bf16[392,768]{1,0:T(8,128)(2,1)}) custom-call(bf16[392,768]{1,0:T(8,128)(2,1)} %bitcast.102, bf16[392,768]{1,0:T(8,128)(2,1)} %convolution_convert_fusion.1.own_ref, bf16[392,768]{1,0:T(8,128)(2,1)} %convolution_convert_fusion.peer_ref, f32[768]{0:T(1024)} %bias_ref.5, f32[768]{0:T(1024)} %gain_ref.8, f32[768]{0:T(1024)} %shift_ref.5), custom_call_target="tpu_custom_call" | custom-call | flops 1000000 | bytes 3906 | tf_op jit(solution)/shard_map/middle/pallas_call | solution.py:474
  52.8 1.4 collective-permute-start.6
  54.2 1.1 copy-done.9
  55.3 6.1 %mlp.2 = (bf16[392,1536]{1,0:T(8,128)(2,1)S(1)}, bf16[392,1536]{1,0:T(8,128)(2,1)S(1)}, bf16[392,768]{1,0:T(8,128)(2,1)S(1)}, bf16[392,768]{1,0:T(8,128)(2,1)S(1)}) custom-call(bf16[392,768]{1,0:T(8,128)(2,1)S(1)} %copy-done.9, bf16[392,768]{1,0:T(8,128)(2,1)S(1)} %bitcast.107, bf16[768,1536]{1,0:T(8,128)(2,1)S(1)} %copy-done.2, ...), custom_call_target="tpu_custom_call" | custom-call | flops 1000000 | bytes 3906 | tf_op jit(solution)/shard_map/mlp/pallas_call | solution.py:474
  61.4 1.0 copy-done.14
  62.4 1.0 copy-done.15
  63.4 0.8 copy-done.25
  64.3 0.8 copy-done.38
  65.1 1.0 collective-permute-done.6.nm_ref.refs_4_
  66.1 6.9 %mlp.3 = (bf16[392,1536]{1,0:T(8,128)(2,1)S(1)}, bf16[392,1536]{1,0:T(8,128)(2,1)S(1)}, bf16[392,768]{1,0:T(8,128)(2,1)S(1)}, bf16[392,768]{1,0:T(8,128)(2,1)}) custom-call(bf16[392,768]{1,0:T(8,128)(2,1)S(1)} %collective-permute-done.6.nm_ref.refs_4_, bf16[392,768]{1,0:T(8,128)(2,1)S(1)} %copy-done.8, bf16[768,1536]{1,0:T(8,128)(2,1)S(1)} %copy-done.2, ...), custom_call_target="tpu_custom_call" | custom-call | flops 1000000 | bytes 3906 | tf_op jit(solution)/shard_map/mlp/pallas_call | solution.py:474
  73.0 1.0 copy-done.16
  74.0 1.1 copy-done.17
  75.1 0.8 collective-permute-start.8
  75.9 12.0 %mlp_weights.1 = (f32[1,1536]{1,0:T(1,128)}, bf16[2,4,96,768]{3,2,1,0:T(8,128)(2,1)}, bf16[2,4,96,768]{3,2,1,0:T(8,128)(2,1)}, bf16[2,4,96,768]{3,2,1,0:T(8,128)(2,1)}, bf16[2,4,96,768]{3,2,1,0:T(8,128)(2,1)}) custom-call(s32[1]{0:T(128)} %bitcast.10.me_ref, bf16[392,768]{1,0:T(8,128)(2,1)} %get-tuple-element.98.nm_ref.refs_0_, bf16[392,768]{1,0:T(8,128)(2,1)} %bitcast.105, ...), custom_call_target="tpu_custom_call" | custom-call | flops 1000000 | bytes 3906 | tf_op jit(solution)/shard_map/mlp_weights/pallas_call | solution.py:474
  88.5 1.1 middle_back.1
  89.7 1.3 collective-permute-start.11
  91.2 1.6 collective-permute-start.12
  92.9 1.5 collective-permute-start.17
  95.0 10.6 %attn_backward.2 = (bf16[3,392,384]{2,1,0:T(8,128)(2,1)S(1)}, f32[1,768]{1,0:T(1,128)S(1)}, f32[3,64,256]{2,1,0:T(8,128)S(1)}, bf16[392,768]{1,0:T(8,128)(2,1)S(1)}, f32[2,768]{1,0:T(2,128)S(1)}) custom-call(bf16[392,768]{1,0:T(8,128)(2,1)S(1)} %get-tuple-element.137.branch_ref.refs_2_, bf16[392,768]{1,0:T(8,128)(2,1)S(1)} %bitcast.103, ...), custom_call_target="tpu_custom_call" | custom-call | flops 1000000 | bytes 3906 | tf_op jit(solution)/shard_map/attn_backward/pallas_call | solution.py:474
  105.7 1.7 collective-permute-done.12
  107.6 3.7 %collective-permute-start.16 = (bf16[96,768]{1,0:T(8,128)(2,1)S(1)}, bf16[96,768]{1,0:T(8,128)(2,1)S(1)}, u32[]{:S(2)}, u32[]{:S(2)}) collective-permute-start(bf16[96,768]{1,0:T(8,128)(2,1)S(1)} %get-tuple-element.179), channel_id=1, source_target_pairs={{0,24},{2,26},{4,28},{6,30},{8,16},{10,18},{12,20},{14,22},{16,8},... | collective-permute-start | bytes 442376 | tf_op jit(solution)/shard_map/ppermute | solution.py:593
  111.3 0.8 collective-permute-start.14
  112.1 10.7 %attn_backward.3 = (bf16[3,392,384]{2,1,0:T(8,128)(2,1)S(1)}, f32[1,768]{1,0:T(1,128)S(1)}, f32[3,64,256]{2,1,0:T(8,128)S(1)}, bf16[392,768]{1,0:T(8,128)(2,1)S(1)}, f32[2,768]{1,0:T(2,128)S(1)}) custom-call(bf16[392,768]{1,0:T(8,128)(2,1)S(1)} %collective-permute-done.11.branch_ref.refs_9_, bf16[392,768]{1,0:T(8,128)(2,1)S(1)} %copy-done.12, ...), custom_call_target="tpu_custom_call" | custom-call | flops 1000000 | bytes 3906 | tf_op jit(solution)/shard_map/attn_backward/pallas_call | solution.py:474
  123.0 3.7 %collective-permute-start.20 = (bf16[96,768]{1,0:T(8,128)(2,1)S(1)}, bf16[96,768]{1,0:T(8,128)(2,1)S(1)}, u32[]{:S(2)}, u32[]{:S(2)}) collective-permute-start(bf16[96,768]{1,0:T(8,128)(2,1)S(1)} %get-tuple-element.176), channel_id=1, source_target_pairs={{0,24},{2,26},{4,28},{6,30},{8,16},{10,18},{12,20},{14,22},{16,8},... | collective-permute-start | bytes 442376 | tf_op jit(solution)/shard_map/ppermute | solution.py:593
  126.7 0.8 collective-permute-start.18
  127.7 5.8 %attn_weights.1 = (bf16[2,4,96,768]{3,2,1,0:T(8,128)(2,1)S(1)}, bf16[2,4,96,768]{3,2,1,0:T(8,128)(2,1)S(1)}, bf16[16,768]{1,0:T(8,128)(2,1)S(1)}) custom-call(s32[1]{0:T(128)} %bitcast.10.me_ref, f32[4,768]{1,0:T(4,128)S(1)} %get-tuple-element.135.sums2_ref, f32[1,1536]{1,0:T(1,128)S(1)} %copy-done.36, bf16[768,392]{1,0:T(8,128)(2,1)S(1)} %copy-done.21, ...), custom_call_target="tpu_custom_call" | custom-call | flops 1000000 | bytes 3906 | tf_op jit(solution)/shard_map/attn_weights/pallas_call | solution.py:474
  133.4 3.5 %collective-permute-done.19 = bf16[96,768]{1,0:T(8,128)(2,1)S(1)} collective-permute-done((bf16[96,768]{1,0:T(8,128)(2,1)S(1)}, bf16[96,768]{1,0:T(8,128)(2,1)S(1)}, u32[]{:S(2)}, u32[]{:S(2)}) %collective-permute-start.19) | collective-permute-done | bytes 147488 | tf_op jit(solution)/shard_map/ppermute | solution.py:593
  137.3 2.9 %collective-permute-start.21 = (bf16[208,768]{1,0:T(8,128)(2,1)S(1)}, bf16[208,768]{1,0:T(8,128)(2,1)S(1)}, u32[]{:S(2)}, u32[]{:S(2)}) collective-permute-start(bf16[208,768]{1,0:T(8,128)(2,1)S(1)} %get-tuple-element.183), channel_id=1, source_target_pairs={{0,8},{2,10},{4,12},{6,14},{8,0},{10,2},{12,4},{14,6},{16,24},{18,... | collective-permute-start | bytes 958472 | tf_op jit(solution)/shard_map/ppermute | solution.py:593
  140.2 1.4 collective-permute-start.23
  141.8 1.6 collective-permute-start.26
  143.4 11.6 %collective-permute-done.22 = bf16[208,768]{1,0:T(8,128)(2,1)S(1)} collective-permute-done((bf16[208,768]{1,0:T(8,128)(2,1)S(1)}, bf16[208,768]{1,0:T(8,128)(2,1)S(1)}, u32[]{:S(2)}, u32[]{:S(2)}) %collective-permute-start.22) | collective-permute-done | bytes 319520 | tf_op jit(solution)/shard_map/ppermute | solution.py:593
  155.0 6.8 %collective-permute-done.21 = bf16[208,768]{1,0:T(8,128)(2,1)S(1)} collective-permute-done((bf16[208,768]{1,0:T(8,128)(2,1)S(1)}, bf16[208,768]{1,0:T(8,128)(2,1)S(1)}, u32[]{:S(2)}, u32[]{:S(2)}) %collective-permute-start.21) | collective-permute-done | bytes 319520 | tf_op jit(solution)/shard_map/ppermute | solution.py:593
  162.0 1.6 collective-permute-start.24
  163.9 1.1 add_convert_fusion
  165.1 7.2 %collective-permute-start.27 = (bf16[96,768]{1,0:T(8,128)(2,1)S(1)}, bf16[96,768]{1,0:T(8,128)(2,1)S(1)}, u32[]{:S(2)}, u32[]{:S(2)}) collective-permute-start(bf16[96,768]{1,0:T(8,128)(2,1)S(1)} %get-tuple-element.173), channel_id=1, source_target_pairs={{0,8},{2,10},{4,12},{6,14},{8,0},{10,2},{12,4},{14,6},{16,24},{18,... | collective-permute-start | bytes 442376 | tf_op jit(solution)/shard_map/ppermute | solution.py:593
  172.3 1.4 collective-permute-start.29
  173.9 4.6 %collective-permute-done.13.peer_ref = bf16[392,768]{1,0:T(8,128)(2,1)S(1)} collective-permute-done((bf16[392,768]{1,0:T(8,128)(2,1)S(1)}, bf16[392,768]{1,0:T(8,128)(2,1)S(1)}, u32[]{:S(2)}, u32[]{:S(2)}) %collective-permute-start.13) | collective-permute-done | bytes 602144 | tf_op jit(solution)/shard_map/ppermute | solution.py:589
  178.5 1.7 input_back.1
  180.2 1.1 collective-permute-done.29
  181.3 5.3 %collective-permute-done.28 = bf16[96,768]{1,0:T(8,128)(2,1)S(1)} collective-permute-done((bf16[96,768]{1,0:T(8,128)(2,1)S(1)}, bf16[96,768]{1,0:T(8,128)(2,1)S(1)}, u32[]{:S(2)}, u32[]{:S(2)}) %collective-permute-start.28) | collective-permute-done | bytes 147488 | tf_op jit(solution)/shard_map/ppermute | solution.py:593
  186.7 1.5 collective-permute-start.32
  188.2 1.1 collective-permute-start.31
  189.3 1.8 collective-permute-start.30
  191.2 4.2 %collective-permute-done.32 = bf16[96,768]{1,0:T(8,128)(2,1)S(1)} collective-permute-done((bf16[96,768]{1,0:T(8,128)(2,1)S(1)}, bf16[96,768]{1,0:T(8,128)(2,1)S(1)}, u32[]{:S(2)}, u32[]{:S(2)}) %collective-permute-start.32) | collective-permute-done | bytes 147488 | tf_op jit(solution)/shard_map/ppermute | solution.py:593
  195.4 6.1 %collective-permute-done.31 = bf16[96,768]{1,0:T(8,128)(2,1)S(1)} collective-permute-done((bf16[96,768]{1,0:T(8,128)(2,1)S(1)}, bf16[96,768]{1,0:T(8,128)(2,1)S(1)}, u32[]{:S(2)}, u32[]{:S(2)}) %collective-permute-start.31) | collective-permute-done | bytes 147488 | tf_op jit(solution)/shard_map/ppermute | solution.py:593
  201.6 1.0 collective-permute-start.36
  202.6 14.8 %collective-permute-done.36.refs_1_ = bf16[4,96,768]{2,1,0:T(8,128)(2,1)S(1)} collective-permute-done((bf16[4,96,768]{2,1,0:T(8,128)(2,1)S(1)}, bf16[4,96,768]{2,1,0:T(8,128)(2,1)S(1)}, u32[]{:S(2)}, u32[]{:S(2)}) %collective-permute-start.36) | collective-permute-done | bytes 589856 | tf_op jit(solution)/shard_map/ppermute | solution.py:593
  217.9 5.4 %finish_mlp.1 = (f32[768,1536]{1,0:T(8,128)}, f32[1536,768]{1,0:T(8,128)}, f32[16,768]{1,0:T(8,128)S(1)}) custom-call(s32[1]{0:T(128)} %bitcast.10.me_ref, bf16[4,208,768]{2,1,0:T(8,128)(2,1)S(1)} %pad_maximum_fusion.refs_0_, bf16[4,208,768]{2,1,0:T(8,128)(2,1)S(1)} %collective-permute-done.24.refs_1_, ...), custom_call_target="tpu_custom_call" | custom-call | flops 1000000 | bytes 3906 | tf_op jit(solution)/shard_map/finish_mlp/pallas_call | solution.py:474
  223.3 0.9 collective-permute-start.35
  226.0 3.2 %finish.1 = (f32[3,768,384]{2,1,0:T(8,128)}, f32[384,768]{1,0:T(8,128)}) custom-call(s32[1]{0:T(128)} %bitcast.10.me_ref, bf16[4,96,768]{2,1,0:T(8,128)(2,1)S(1)} %pad_maximum_fusion.1.refs_0_, bf16[4,96,768]{2,1,0:T(8,128)(2,1)S(1)} %collective-permute-done.36.refs_1_, bf16[4,96,768]{2,1,0:T(8,128)(2,1)S(1)} %collective-permute-done.37.refs_2_, ...), custom_call_target="tpu_custom_call" | custom-call | flops 1000000 | bytes 3906 | tf_op jit(solution)/shard_map/finish/pallas_call | solution.py:474
  (150 shorter events, 8.4 us)
Async XLA Ops:
  1.6 19.7 %collective-permute-start.2 = (bf16[192,768]{1,0:T(8,128)(2,1)S(1)}, bf16[192,768]{1,0:T(8,128)(2,1)S(1)}, u32[]{:S(2)}, u32[]{:S(2)}) collective-permute-start(bf16[192,768]{1,0:T(8,128)(2,1)S(1)} %constant_dynamic-slice_fusion), channel_id=1, source_target_pairs={{0,1},{1,0},{2,3},{3,2},{4,5},{5,4},{6,7},{7,6},{8,9},{9,8},{10,11... | collective-permute-start | bytes 884744 | tf_op jit(solution)/shard_map/ppermute | solution.py:589
  5.3 16.0 %collective-permute-start.1 = (f32[8,49]{1,0:T(8,128)S(1)}, f32[8,49]{1,0:T(8,128)S(1)}, u32[]{:S(2)}, u32[]{:S(2)}) collective-permute-start(f32[8,49]{1,0:T(8,128)S(1)} %convert_element_type.291.valid_ref), channel_id=1, source_target_pairs={{0,1},{1,0},{2,3},{3,2},{4,5},{5,4},{6,7},{7,6},{8,9},{9,8},{10,11... | collective-permute-start | bytes 4712 | tf_op jit(solution)/shard_map/ppermute | solution.py:589
  5.4 20.1 %collective-permute-start = (bf16[392,768]{1,0:T(8,128)(2,1)}, bf16[392,768]{1,0:T(8,128)(2,1)S(1)}, u32[]{:S(2)}, u32[]{:S(2)}) collective-permute-start(bf16[392,768]{1,0:T(8,128)(2,1)} %bitcast.100), channel_id=1, source_target_pairs={{0,1},{1,0},{2,3},{3,2},{4,5},{5,4},{6,7},{7,6},{8,9},{9,8},{10,11... | collective-permute-start | bytes 1806344 | tf_op jit(solution)/shard_map/ppermute | solution.py:589
  9.3 12.1 %copy-start.5 = (bf16[8,49,768]{2,0,1:T(8,128)(2,1)S(1)}, bf16[8,49,768]{2,0,1:T(8,128)(2,1)}, u32[]{:S(2)}) copy-start(bf16[8,49,768]{2,0,1:T(8,128)(2,1)} %param.31) | copy-start | bytes 1806340
  21.4 21.5 %copy-start.46 = (bf16[192,768]{1,0:T(8,128)(2,1)}, bf16[192,768]{1,0:T(8,128)(2,1)S(1)}, u32[]{:S(2)}) copy-start(bf16[192,768]{1,0:T(8,128)(2,1)S(1)} %collective-permute-done.2) | copy-start | bytes 884740
  21.4 19.7 %copy-start.4 = (bf16[384,768]{1,0:T(8,128)(2,1)S(1)}, bf16[384,768]{1,0:T(8,128)(2,1)}, u32[]{:S(2)}) copy-start(bf16[384,768]{1,0:T(8,128)(2,1)} %proj_ref.3) | copy-start | bytes 1769476
  21.4 19.7 %copy-start.18 = (bf16[392,384]{1,0:T(8,128)(2,1)S(1)}, bf16[392,384]{1,0:T(8,128)(2,1)}, u32[]{:S(2)}) copy-start(bf16[392,384]{1,0:T(8,128)(2,1)} %get-tuple-element.91.refs_1_) | copy-start | bytes 903172
  21.4 16.8 %collective-permute-start.3 = (bf16[392,768]{1,0:T(8,128)(2,1)S(1)}, bf16[392,768]{1,0:T(8,128)(2,1)S(1)}, u32[]{:S(2)}, u32[]{:S(2)}) collective-permute-start(bf16[392,768]{1,0:T(8,128)(2,1)S(1)} %bitcast.106), channel_id=1, source_target_pairs={{0,1},{1,0},{2,3},{3,2},{4,5},{5,4},{6,7},{7,6},{8,9},{9,8},{10,11... | collective-permute-start | bytes 1806344 | tf_op jit(solution)/shard_map/ppermute | solution.py:589
  39.1 7.9 %collective-permute-start.4 = (bf16[392,384]{1,0:T(8,128)(2,1)}, bf16[392,384]{1,0:T(8,128)(2,1)}, u32[]{:S(2)}, u32[]{:S(2)}) collective-permute-start(bf16[392,384]{1,0:T(8,128)(2,1)} %get-tuple-element.95.refs_8_), channel_id=1, source_target_pairs={{0,1},{1,0},{2,3},{3,2},{4,5},{5,4},{6,7},{7,6},{8,9},{9,8},{10,11... | collective-permute-start | bytes 903176 | tf_op jit(solution)/shard_map/ppermute | solution.py:589
  41.1 1.7 collective-permute-start.5
  47.0 7.2 %copy-start.2 = (bf16[768,1536]{1,0:T(8,128)(2,1)S(1)}, bf16[768,1536]{1,0:T(8,128)(2,1)}, u32[]{:S(2)}) copy-start(bf16[768,1536]{1,0:T(8,128)(2,1)} %fc1_ref.3) | copy-start | bytes 7077892
  47.0 7.2 %copy-start.3 = (bf16[1536,768]{1,0:T(8,128)(2,1)S(1)}, bf16[1536,768]{1,0:T(8,128)(2,1)}, u32[]{:S(2)}) copy-start(bf16[1536,768]{1,0:T(8,128)(2,1)} %fc2_ref.3) | copy-start | bytes 7077892
  52.8 13.3 %collective-permute-start.6 = (bf16[392,768]{1,0:T(8,128)(2,1)}, bf16[392,768]{1,0:T(8,128)(2,1)S(1)}, u32[]{:S(2)}, u32[]{:S(2)}) collective-permute-start(bf16[392,768]{1,0:T(8,128)(2,1)} %get-tuple-element.98.nm_ref.refs_0_), channel_id=1, source_target_pairs={{0,1},{1,0},{2,3},{3,2},{4,5},{5,4},{6,7},{7,6},{8,9},{9,8},{10,11... | collective-permute-start | bytes 1806344 | tf_op jit(solution)/shard_map/ppermute | solution.py:589
  55.3 10.8 %copy-start.8 = (bf16[392,768]{1,0:T(8,128)(2,1)S(1)}, bf16[392,768]{1,0:T(8,128)(2,1)}, u32[]{:S(2)}) copy-start(bf16[392,768]{1,0:T(8,128)(2,1)} %copy-done.7) | copy-start | bytes 1806340
  66.1 6.9 %copy-start.10 = (bf16[392,768]{1,0:T(8,128)(2,1)}, bf16[392,768]{1,0:T(8,128)(2,1)S(1)}, u32[]{:S(2)}) copy-start(bf16[392,768]{1,0:T(8,128)(2,1)S(1)} %collective-permute-done.6.nm_ref.refs_4_) | copy-start | bytes 1806340
  75.1 13.4 %collective-permute-start.8 = (bf16[392,768]{1,0:T(8,128)(2,1)}, bf16[392,768]{1,0:T(8,128)(2,1)S(1)}, u32[]{:S(2)}, u32[]{:S(2)}) collective-permute-start(bf16[392,768]{1,0:T(8,128)(2,1)} %get-tuple-element.103), channel_id=1, source_target_pairs={{0,1},{1,0},{2,3},{3,2},{4,5},{5,4},{6,7},{7,6},{8,9},{9,8},{10,11... | collective-permute-start | bytes 1806344 | tf_op jit(solution)/shard_map/ppermute | solution.py:589
  75.9 12.6 %copy-start.6 = (bf16[8,49,768]{2,0,1:T(8,128)(2,1)S(1)}, bf16[8,49,768]{2,0,1:T(8,128)(2,1)}, u32[]{:S(2)}) copy-start(bf16[8,49,768]{2,0,1:T(8,128)(2,1)} %param.31) | copy-start | bytes 1806340
  75.9 12.6 %copy-start.20 = (f32[392,768]{1,0:T(8,128)S(1)}, f32[392,768]{1,0:T(8,128)}, u32[]{:S(2)}) copy-start(f32[392,768]{1,0:T(8,128)} %get-tuple-element.97.middle_ref) | copy-start | bytes 3612676
  75.9 12.6 %copy-start.37 = (f32[768]{0:T(1024)S(1)}, f32[768]{0:T(1024)}, u32[]{:S(2)}) copy-start(f32[768]{0:T(1024)} %gain_ref.8) | copy-start | bytes 9220
  75.9 12.6 %copy-start.39 = (bf16[392,768]{1,0:T(8,128)(2,1)S(1)}, bf16[392,768]{1,0:T(8,128)(2,1)}, u32[]{:S(2)}) copy-start(bf16[392,768]{1,0:T(8,128)(2,1)} %copy-done.38) | copy-start | bytes 1806340
  87.9 3.1 %collective-permute-start.9 = (bf16[2,4,96,768]{3,2,1,0:T(8,128)(2,1)}, bf16[2,4,96,768]{3,2,1,0:T(8,128)(2,1)S(1)}, u32[]{:S(2)}, u32[]{:S(2)}) collective-permute-start(bf16[2,4,96,768]{3,2,1,0:T(8,128)(2,1)} %get-tuple-element.112), channel_id=1, source_target_pairs={{0,2},{2,0},{4,6},{6,4},{8,10},{10,8},{12,14},{14,12},{16,18},{18,... | collective-permute-start | bytes 3538952 | tf_op jit(solution)/shard_map/ppermute | solution.py:593
  88.0 4.8 %collective-permute-start.10 = (bf16[2,4,96,768]{3,2,1,0:T(8,128)(2,1)}, bf16[2,4,96,768]{3,2,1,0:T(8,128)(2,1)S(1)}, u32[]{:S(2)}, u32[]{:S(2)}) collective-permute-start(bf16[2,4,96,768]{3,2,1,0:T(8,128)(2,1)} %get-tuple-element.115), channel_id=1, source_target_pairs={{0,2},{2,0},{4,6},{6,4},{8,10},{10,8},{12,14},{14,12},{16,18},{18,... | collective-permute-start | bytes 3538952 | tf_op jit(solution)/shard_map/ppermute | solution.py:593
  88.5 6.5 %copy-start.31 = (bf16[8,64,384]{2,1,0:T(8,128)(2,1)S(1)}, bf16[8,64,384]{2,1,0:T(8,128)(2,1)}, u32[]{:S(2)}) copy-start(bf16[8,64,384]{2,1,0:T(8,128)(2,1)} %get-tuple-element.120.k_ref) | copy-start | bytes 1179652
  88.5 6.5 %copy-start.32 = (bf16[8,64,384]{2,1,0:T(8,128)(2,1)S(1)}, bf16[8,64,384]{2,1,0:T(8,128)(2,1)}, u32[]{:S(2)}) copy-start(bf16[8,64,384]{2,1,0:T(8,128)(2,1)} %get-tuple-element.121.v_ref) | copy-start | bytes 1179652
  89.7 21.6 %collective-permute-start.11 = (bf16[392,768]{1,0:T(8,128)(2,1)S(1)}, bf16[392,768]{1,0:T(8,128)(2,1)S(1)}, u32[]{:S(2)}, u32[]{:S(2)}) collective-permute-start(bf16[392,768]{1,0:T(8,128)(2,1)S(1)} %get-tuple-element.137.branch_ref.refs_2_), channel_id=1, source_target_pairs={{0,1},{1,0},{2,3},{3,2},{4,5},{5,4},{6,7},{7,6},{8,9},{9,8},{10,11... | collective-permute-start | bytes 1806344 | tf_op jit(solution)/shard_map/ppermute | solution.py:589
  91.2 16.2 %collective-permute-start.12 = (bf16[4,96,768]{2,1,0:T(8,128)(2,1)S(1)}, bf16[4,96,768]{2,1,0:T(8,128)(2,1)S(1)}, u32[]{:S(2)}, u32[]{:S(2)}) collective-permute-start(bf16[4,96,768]{2,1,0:T(8,128)(2,1)S(1)} %fusion), channel_id=1, source_target_pairs={{0,4},{2,6},{4,0},{6,2},{8,12},{10,14},{12,8},{14,10},{16,20},{18,... | collective-permute-start | bytes 1769480 | tf_op jit(solution)/shard_map/ppermute | solution.py:593
  92.9 29.8 %collective-permute-start.17 = (bf16[4,96,768]{2,1,0:T(8,128)(2,1)S(1)}, bf16[4,96,768]{2,1,0:T(8,128)(2,1)S(1)}, u32[]{:S(2)}, u32[]{:S(2)}) collective-permute-start(bf16[4,96,768]{2,1,0:T(8,128)(2,1)S(1)} %fusion.1), channel_id=1, source_target_pairs={{0,4},{2,6},{4,0},{6,2},{8,12},{10,14},{12,8},{14,10},{16,20},{18,... | collective-permute-start | bytes 1769480 | tf_op jit(solution)/shard_map/ppermute | solution.py:593
  94.4 33.2 %collective-permute-start.7 = (bf16[392,768]{1,0:T(8,128)(2,1)S(1)}, bf16[392,768]{1,0:T(8,128)(2,1)S(1)}, u32[]{:S(2)}, u32[]{:S(2)}) collective-permute-start(bf16[392,768]{1,0:T(8,128)(2,1)S(1)} %get-tuple-element.102), channel_id=1, source_target_pairs={{0,1},{1,0},{2,3},{3,2},{4,5},{5,4},{6,7},{7,6},{8,9},{9,8},{10,11... | collective-permute-start | bytes 1806344 | tf_op jit(solution)/shard_map/ppermute | solution.py:589
  95.0 17.0 %copy-start.28 = (bf16[8,64,384]{2,1,0:T(8,128)(2,1)S(1)}, bf16[8,64,384]{2,1,0:T(8,128)(2,1)}, u32[]{:S(2)}) copy-start(bf16[8,64,384]{2,1,0:T(8,128)(2,1)} %get-tuple-element.127.k_ref) | copy-start | bytes 1179652
  95.0 17.0 %copy-start.29 = (bf16[8,64,384]{2,1,0:T(8,128)(2,1)S(1)}, bf16[8,64,384]{2,1,0:T(8,128)(2,1)}, u32[]{:S(2)}) copy-start(bf16[8,64,384]{2,1,0:T(8,128)(2,1)} %get-tuple-element.128.v_ref) | copy-start | bytes 1179652
  105.7 6.4 %copy-start.12 = (bf16[392,768]{1,0:T(8,128)(2,1)S(1)}, bf16[392,768]{1,0:T(8,128)(2,1)}, u32[]{:S(2)}) copy-start(bf16[392,768]{1,0:T(8,128)(2,1)} %copy-done.11) | copy-start | bytes 1806340
  105.7 6.4 %copy-start.23 = (bf16[8,3,64,256]{3,2,1,0:T(8,128)(2,1)S(1)}, bf16[8,3,64,256]{3,2,1,0:T(8,128)(2,1)}, u32[]{:S(2)}) copy-start(bf16[8,3,64,256]{3,2,1,0:T(8,128)(2,1)} %get-tuple-element.125.prob_ref) | copy-start | bytes 2359300
  105.7 6.4 %copy-start.27 = (bf16[8,64,384]{2,1,0:T(8,128)(2,1)S(1)}, bf16[8,64,384]{2,1,0:T(8,128)(2,1)}, u32[]{:S(2)}) copy-start(bf16[8,64,384]{2,1,0:T(8,128)(2,1)} %get-tuple-element.126.q_ref) | copy-start | bytes 1179652
  107.6 19.1 %collective-permute-start.16 = (bf16[96,768]{1,0:T(8,128)(2,1)S(1)}, bf16[96,768]{1,0:T(8,128)(2,1)S(1)}, u32[]{:S(2)}, u32[]{:S(2)}) collective-permute-start(bf16[96,768]{1,0:T(8,128)(2,1)S(1)} %get-tuple-element.179), channel_id=1, source_target_pairs={{0,24},{2,26},{4,28},{6,30},{8,16},{10,18},{12,20},{14,22},{16,8},... | collective-permute-start | bytes 442376 | tf_op jit(solution)/shard_map/ppermute | solution.py:593
  111.3 15.4 %collective-permute-start.15 = (bf16[96,768]{1,0:T(8,128)(2,1)S(1)}, bf16[96,768]{1,0:T(8,128)(2,1)S(1)}, u32[]{:S(2)}, u32[]{:S(2)}) collective-permute-start(bf16[96,768]{1,0:T(8,128)(2,1)S(1)} %get-tuple-element.180), channel_id=1, source_target_pairs={{0,16},{2,18},{4,20},{6,22},{8,24},{10,26},{12,28},{14,30},{16,0},... | collective-permute-start | bytes 442376 | tf_op jit(solution)/shard_map/ppermute | solution.py:593
  111.3 16.2 %collective-permute-start.14 = (bf16[96,768]{1,0:T(8,128)(2,1)S(1)}, bf16[96,768]{1,0:T(8,128)(2,1)S(1)}, u32[]{:S(2)}, u32[]{:S(2)}) collective-permute-start(bf16[96,768]{1,0:T(8,128)(2,1)S(1)} %get-tuple-element.181), channel_id=1, source_target_pairs={{0,8},{2,10},{4,12},{6,14},{8,0},{10,2},{12,4},{14,6},{16,24},{18,... | collective-permute-start | bytes 442376 | tf_op jit(solution)/shard_map/ppermute | solution.py:593
  122.8 4.8 %copy-start.19 = (bf16[392,384]{1,0:T(8,128)(2,1)S(1)}, bf16[392,384]{1,0:T(8,128)(2,1)}, u32[]{:S(2)}) copy-start(bf16[392,384]{1,0:T(8,128)(2,1)} %get-tuple-element.91.refs_1_) | copy-start | bytes 903172
  122.8 4.8 %copy-start.21 = (bf16[768,392]{1,0:T(8,128)(2,1)S(1)}, bf16[768,392]{1,0:T(8,128)(2,1)}, u32[]{:S(2)}) copy-start(bf16[768,392]{1,0:T(8,128)(2,1)} %get-tuple-element.136.refs_0_) | copy-start | bytes 1806340
  122.8 4.8 %copy-start.22 = (bf16[768,392]{1,0:T(8,128)(2,1)S(1)}, bf16[768,392]{1,0:T(8,128)(2,1)}, u32[]{:S(2)}) copy-start(bf16[768,392]{1,0:T(8,128)(2,1)} %get-tuple-element.142.refs_7_) | copy-start | bytes 1806340
  122.8 4.8 %copy-start.33 = (bf16[392,384]{1,0:T(8,128)(2,1)S(1)}, bf16[392,384]{1,0:T(8,128)(2,1)}, u32[]{:S(2)}) copy-start(bf16[392,384]{1,0:T(8,128)(2,1)} %get-tuple-element.95.refs_8_) | copy-start | bytes 903172
  122.8 4.8 %copy-start.36 = (f32[1,1536]{1,0:T(1,128)S(1)}, f32[1,1536]{1,0:T(1,128)}, u32[]{:S(2)}) copy-start(f32[1,1536]{1,0:T(1,128)} %get-tuple-element.108.gb1_ref) | copy-start | bytes 18436
  123.0 10.4 %collective-permute-start.20 = (bf16[96,768]{1,0:T(8,128)(2,1)S(1)}, bf16[96,768]{1,0:T(8,128)(2,1)S(1)}, u32[]{:S(2)}, u32[]{:S(2)}) collective-permute-start(bf16[96,768]{1,0:T(8,128)(2,1)S(1)} %get-tuple-element.176), channel_id=1, source_target_pairs={{0,24},{2,26},{4,28},{6,30},{8,16},{10,18},{12,20},{14,22},{16,8},... | collective-permute-start | bytes 442376 | tf_op jit(solution)/shard_map/ppermute | solution.py:593
  126.7 10.2 %collective-permute-start.19 = (bf16[96,768]{1,0:T(8,128)(2,1)S(1)}, bf16[96,768]{1,0:T(8,128)(2,1)S(1)}, u32[]{:S(2)}, u32[]{:S(2)}) collective-permute-start(bf16[96,768]{1,0:T(8,128)(2,1)S(1)} %get-tuple-element.177), channel_id=1, source_target_pairs={{0,16},{2,18},{4,20},{6,22},{8,24},{10,26},{12,28},{14,30},{16,0},... | collective-permute-start | bytes 442376 | tf_op jit(solution)/shard_map/ppermute | solution.py:593
  126.7 10.2 %collective-permute-start.18 = (bf16[96,768]{1,0:T(8,128)(2,1)S(1)}, bf16[96,768]{1,0:T(8,128)(2,1)S(1)}, u32[]{:S(2)}, u32[]{:S(2)}) collective-permute-start(bf16[96,768]{1,0:T(8,128)(2,1)S(1)} %get-tuple-element.178), channel_id=1, source_target_pairs={{0,8},{2,10},{4,12},{6,14},{8,0},{10,2},{12,4},{14,6},{16,24},{18,... | collective-permute-start | bytes 442376 | tf_op jit(solution)/shard_map/ppermute | solution.py:593
  137.0 4.6 %collective-permute-start.25 = (bf16[2,4,96,768]{3,2,1,0:T(8,128)(2,1)S(1)}, bf16[2,4,96,768]{3,2,1,0:T(8,128)(2,1)S(1)}, u32[]{:S(2)}, u32[]{:S(2)}) collective-permute-start(bf16[2,4,96,768]{3,2,1,0:T(8,128)(2,1)S(1)} %get-tuple-element.153), channel_id=1, source_target_pairs={{0,2},{2,0},{4,6},{6,4},{8,10},{10,8},{12,14},{14,12},{16,18},{18,... | collective-permute-start | bytes 3538952 | tf_op jit(solution)/shard_map/ppermute | solution.py:593
  137.2 17.8 %collective-permute-start.22 = (bf16[208,768]{1,0:T(8,128)(2,1)S(1)}, bf16[208,768]{1,0:T(8,128)(2,1)S(1)}, u32[]{:S(2)}, u32[]{:S(2)}) collective-permute-start(bf16[208,768]{1,0:T(8,128)(2,1)S(1)} %get-tuple-element.183), channel_id=1, source_target_pairs={{0,16},{2,18},{4,20},{6,22},{8,24},{10,26},{12,28},{14,30},{16,0},... | collective-permute-start | bytes 958472 | tf_op jit(solution)/shard_map/ppermute | solution.py:593
  137.3 24.5 %collective-permute-start.21 = (bf16[208,768]{1,0:T(8,128)(2,1)S(1)}, bf16[208,768]{1,0:T(8,128)(2,1)S(1)}, u32[]{:S(2)}, u32[]{:S(2)}) collective-permute-start(bf16[208,768]{1,0:T(8,128)(2,1)S(1)} %get-tuple-element.183), channel_id=1, source_target_pairs={{0,8},{2,10},{4,12},{6,14},{8,0},{10,2},{12,4},{14,6},{16,24},{18,... | collective-permute-start | bytes 958472 | tf_op jit(solution)/shard_map/ppermute | solution.py:593
  140.2 21.6 %collective-permute-start.23 = (bf16[208,768]{1,0:T(8,128)(2,1)S(1)}, bf16[208,768]{1,0:T(8,128)(2,1)S(1)}, u32[]{:S(2)}, u32[]{:S(2)}) collective-permute-start(bf16[208,768]{1,0:T(8,128)(2,1)S(1)} %get-tuple-element.183), channel_id=1, source_target_pairs={{0,24},{2,26},{4,28},{6,30},{8,16},{10,18},{12,20},{14,22},{16,8},... | collective-permute-start | bytes 958472 | tf_op jit(solution)/shard_map/ppermute | solution.py:593
  141.8 23.2 %collective-permute-start.26 = (bf16[4,96,768]{2,1,0:T(8,128)(2,1)S(1)}, bf16[4,96,768]{2,1,0:T(8,128)(2,1)S(1)}, u32[]{:S(2)}, u32[]{:S(2)}) collective-permute-start(bf16[4,96,768]{2,1,0:T(8,128)(2,1)S(1)} %fusion.2), channel_id=1, source_target_pairs={{0,4},{2,6},{4,0},{6,2},{8,12},{10,14},{12,8},{14,10},{16,20},{18,... | collective-permute-start | bytes 1769480 | tf_op jit(solution)/shard_map/ppermute | solution.py:593
  162.0 39.6 %collective-permute-start.24 = (bf16[4,208,768]{2,1,0:T(8,128)(2,1)S(1)}, bf16[4,208,768]{2,1,0:T(8,128)(2,1)S(1)}, u32[]{:S(2)}, u32[]{:S(2)}) collective-permute-start(bf16[4,208,768]{2,1,0:T(8,128)(2,1)S(1)} %pad_maximum_fusion.refs_0_), channel_id=1, source_target_pairs={{0,4},{2,6},{4,0},{6,2},{8,12},{10,14},{12,8},{14,10},{16,20},{18,... | collective-permute-start | bytes 3833864 | tf_op jit(solution)/shard_map/ppermute | solution.py:593
  163.5 14.9 %collective-permute-start.13 = (bf16[392,768]{1,0:T(8,128)(2,1)S(1)}, bf16[392,768]{1,0:T(8,128)(2,1)S(1)}, u32[]{:S(2)}, u32[]{:S(2)}) collective-permute-start(bf16[392,768]{1,0:T(8,128)(2,1)S(1)} %get-tuple-element.129), channel_id=1, source_target_pairs={{0,1},{1,0},{2,3},{3,2},{4,5},{5,4},{6,7},{7,6},{8,9},{9,8},{10,11... | collective-permute-start | bytes 1806344 | tf_op jit(solution)/shard_map/ppermute | solution.py:589
  164.9 13.5 %copy-start.34 = (f32[768]{0:T(1024)S(1)}, f32[768]{0:T(1024)}, u32[]{:S(2)}) copy-start(f32[768]{0:T(1024)} %gain_ref.9) | copy-start | bytes 9220
  165.1 15.0 %collective-permute-start.27 = (bf16[96,768]{1,0:T(8,128)(2,1)S(1)}, bf16[96,768]{1,0:T(8,128)(2,1)S(1)}, u32[]{:S(2)}, u32[]{:S(2)}) collective-permute-start(bf16[96,768]{1,0:T(8,128)(2,1)S(1)} %get-tuple-element.173), channel_id=1, source_target_pairs={{0,8},{2,10},{4,12},{6,14},{8,0},{10,2},{12,4},{14,6},{16,24},{18,... | collective-permute-start | bytes 442376 | tf_op jit(solution)/shard_map/ppermute | solution.py:593
  172.3 8.9 %collective-permute-start.29 = (bf16[96,768]{1,0:T(8,128)(2,1)S(1)}, bf16[96,768]{1,0:T(8,128)(2,1)S(1)}, u32[]{:S(2)}, u32[]{:S(2)}) collective-permute-start(bf16[96,768]{1,0:T(8,128)(2,1)S(1)} %get-tuple-element.174), channel_id=1, source_target_pairs={{0,24},{2,26},{4,28},{6,30},{8,16},{10,18},{12,20},{14,22},{16,8},... | collective-permute-start | bytes 442376 | tf_op jit(solution)/shard_map/ppermute | solution.py:593
  173.8 12.8 %collective-permute-start.28 = (bf16[96,768]{1,0:T(8,128)(2,1)S(1)}, bf16[96,768]{1,0:T(8,128)(2,1)S(1)}, u32[]{:S(2)}, u32[]{:S(2)}) collective-permute-start(bf16[96,768]{1,0:T(8,128)(2,1)S(1)} %get-tuple-element.175), channel_id=1, source_target_pairs={{0,16},{2,18},{4,20},{6,22},{8,24},{10,26},{12,28},{14,30},{16,0},... | collective-permute-start | bytes 442376 | tf_op jit(solution)/shard_map/ppermute | solution.py:593
  186.7 8.6 %collective-permute-start.32 = (bf16[96,768]{1,0:T(8,128)(2,1)S(1)}, bf16[96,768]{1,0:T(8,128)(2,1)S(1)}, u32[]{:S(2)}, u32[]{:S(2)}) collective-permute-start(bf16[96,768]{1,0:T(8,128)(2,1)S(1)} %fusion.15), channel_id=1, source_target_pairs={{0,24},{2,26},{4,28},{6,30},{8,16},{10,18},{12,20},{14,22},{16,8},... | collective-permute-start | bytes 442376 | tf_op jit(solution)/shard_map/ppermute | solution.py:593
  188.2 13.2 %collective-permute-start.31 = (bf16[96,768]{1,0:T(8,128)(2,1)S(1)}, bf16[96,768]{1,0:T(8,128)(2,1)S(1)}, u32[]{:S(2)}, u32[]{:S(2)}) collective-permute-start(bf16[96,768]{1,0:T(8,128)(2,1)S(1)} %fusion.15), channel_id=1, source_target_pairs={{0,16},{2,18},{4,20},{6,22},{8,24},{10,26},{12,28},{14,30},{16,0},... | collective-permute-start | bytes 442376 | tf_op jit(solution)/shard_map/ppermute | solution.py:593
  189.3 12.1 %collective-permute-start.30 = (bf16[96,768]{1,0:T(8,128)(2,1)S(1)}, bf16[96,768]{1,0:T(8,128)(2,1)S(1)}, u32[]{:S(2)}, u32[]{:S(2)}) collective-permute-start(bf16[96,768]{1,0:T(8,128)(2,1)S(1)} %fusion.15), channel_id=1, source_target_pairs={{0,8},{2,10},{4,12},{6,14},{8,0},{10,2},{12,4},{14,6},{16,24},{18,... | collective-permute-start | bytes 442376 | tf_op jit(solution)/shard_map/ppermute | solution.py:593
  191.2 26.7 %collective-permute-start.33 = (bf16[4,208,768]{2,1,0:T(8,128)(2,1)S(1)}, bf16[4,208,768]{2,1,0:T(8,128)(2,1)S(1)}, u32[]{:S(2)}, u32[]{:S(2)}) collective-permute-start(bf16[4,208,768]{2,1,0:T(8,128)(2,1)S(1)} %pad_maximum_fusion.refs_0_), channel_id=1, source_target_pairs={{0,2},{2,0},{4,6},{6,4},{8,10},{10,8},{12,14},{14,12},{16,18},{18,... | collective-permute-start | bytes 3833864 | tf_op jit(solution)/shard_map/ppermute | solution.py:593
  201.6 16.3 %collective-permute-start.34 = (bf16[4,208,768]{2,1,0:T(8,128)(2,1)S(1)}, bf16[4,208,768]{2,1,0:T(8,128)(2,1)S(1)}, u32[]{:S(2)}, u32[]{:S(2)}) collective-permute-start(bf16[4,208,768]{2,1,0:T(8,128)(2,1)S(1)} %collective-permute-done.24.refs_1_), channel_id=1, source_target_pairs={{0,2},{2,0},{4,6},{6,4},{8,10},{10,8},{12,14},{14,12},{16,18},{18,... | collective-permute-start | bytes 3833864 | tf_op jit(solution)/shard_map/ppermute | solution.py:593
  201.6 15.7 %collective-permute-start.36 = (bf16[4,96,768]{2,1,0:T(8,128)(2,1)S(1)}, bf16[4,96,768]{2,1,0:T(8,128)(2,1)S(1)}, u32[]{:S(2)}, u32[]{:S(2)}) collective-permute-start(bf16[4,96,768]{2,1,0:T(8,128)(2,1)S(1)} %pad_maximum_fusion.1.refs_0_), channel_id=1, source_target_pairs={{0,4},{2,6},{4,0},{6,2},{8,12},{10,14},{12,8},{14,10},{16,20},{18,... | collective-permute-start | bytes 1769480 | tf_op jit(solution)/shard_map/ppermute | solution.py:593
  217.4 8.0 %collective-permute-start.38 = (bf16[4,96,768]{2,1,0:T(8,128)(2,1)S(1)}, bf16[4,96,768]{2,1,0:T(8,128)(2,1)S(1)}, u32[]{:S(2)}, u32[]{:S(2)}) collective-permute-start(bf16[4,96,768]{2,1,0:T(8,128)(2,1)S(1)} %collective-permute-done.36.refs_1_), channel_id=1, source_target_pairs={{0,2},{2,0},{4,6},{6,4},{8,10},{10,8},{12,14},{14,12},{16,18},{18,... | collective-permute-start | bytes 1769480 | tf_op jit(solution)/shard_map/ppermute | solution.py:593
  217.4 8.6 %collective-permute-start.37 = (bf16[4,96,768]{2,1,0:T(8,128)(2,1)S(1)}, bf16[4,96,768]{2,1,0:T(8,128)(2,1)S(1)}, u32[]{:S(2)}, u32[]{:S(2)}) collective-permute-start(bf16[4,96,768]{2,1,0:T(8,128)(2,1)S(1)} %pad_maximum_fusion.1.refs_0_), channel_id=1, source_target_pairs={{0,2},{2,0},{4,6},{6,4},{8,10},{10,8},{12,14},{14,12},{16,18},{18,... | collective-permute-start | bytes 1769480 | tf_op jit(solution)/shard_map/ppermute | solution.py:593
  223.3 5.9 %collective-permute-start.35 = (f32[6,768]{1,0:T(8,128)S(1)}, f32[6,768]{1,0:T(8,128)S(1)}, u32[]{:S(2)}, u32[]{:S(2)}) collective-permute-start(f32[6,768]{1,0:T(8,128)S(1)} %slice.210), channel_id=1, source_target_pairs={{0,1},{1,0},{2,3},{3,2},{4,5},{5,4},{6,7},{7,6},{8,9},{9,8},{10,11... | collective-permute-start | bytes 55304 | tf_op jit(solution)/shard_map/ppermute | solution.py:589
  (22 other events, 49.0 us)

commit v2 on v1

--- a/solution.py
+++ b/solution.py
@@ -70,15 +70,22 @@
     return total
 
 
-def fill(scratch, rows):
-    count = rows.shape[0]
+def fill(scratch, rows, windows):
+    pitch = windows + 1
     for g in range(scratch.shape[0]):
-        scratch[g, 0:count, :] = rows[:, g * LANES : (g + 1) * LANES]
-        scratch[g, count:, :] = jnp.zeros((scratch.shape[1] - count, LANES), rows.dtype)
-
-
-def empty(scratch, count):
-    return jnp.concatenate([scratch[g, 0:count, :] for g in range(scratch.shape[0])], axis=1).astype(BF)
+        for place in range(WIN):
+            scratch[g, place * pitch : place * pitch + windows, :] = rows[
+                place * windows : (place + 1) * windows, g * LANES : (g + 1) * LANES]
+        scratch[g, WIN * pitch :, :] = jnp.zeros((scratch.shape[1] - WIN * pitch, LANES), rows.dtype)
+
+
+def empty(scratch, windows):
+    pitch = windows + 1
+    planes = [
+        jnp.concatenate([scratch[g, place * pitch : place * pitch + windows, :] for place in range(WIN)], axis=0)
+        for g in range(scratch.shape[0])
+    ]
+    return jnp.concatenate(planes, axis=1).astype(BF)
 
 
 def row_max(tile, low_half):
@@ -137,13 +144,13 @@
         got = mm(normed, w_ref[part])
         if part != 1:
             got = got + bias_ref[part // 2 : part // 2 + 1, :]
-        fill(scratch, got.astype(BF).astype(F32))
+        fill(scratch, got.astype(BF).astype(F32), windows)
 
     def window(w, carry):
         allowed = jnp.broadcast_to(mask_s[pl.ds(w, 1), :], (SLOT, GROUP * SLOT)) > 0.5
         for g in range(groups):
             cols = slice(g * LANES, (g + 1) * LANES)
-            places = pl.ds(w, SLOT, stride=windows)
+            places = pl.ds(w, SLOT, stride=windows + 1)
             q = q_s[g, places, :].astype(BF)
             k = k_s[g, places, :].astype(BF)
             v = v_s[g, places, :].astype(BF)
@@ -161,11 +168,25 @@
         return carry
 
     lax.fori_loop(0, windows, window, 0, unroll=2)
-    mixed_ref[...] = empty(mixed_s, rows)
-
-
-def middle_kernel(x_ref, own_ref, peer_ref, bias_ref, gain_ref, shift_ref, middle_ref, nm_ref):
-    middle = x_ref[...].astype(F32) + (own_ref[...].astype(F32) + peer_ref[...].astype(F32)) + line(bias_ref)
+    mixed_ref[...] = empty(mixed_s, windows)
+
+
+def middle_kernel(heads, me_ref, x_in, own_in, peer_in, bias_ref, gain_ref, shift_ref, *refs):
+    if heads:
+        half_in, rest_in, middle_ref, nm_ref, x_ref, own_ref, peer_ref, proj_ref, sems = refs
+        lines = half_in.shape[0]
+        core = me_ref[0] & 1
+        place = lambda c: proj_ref.at[pl.ds(pl.multiple_of(c * lines, lines), lines), :]
+        copies = begin(sems, (peer_in, peer_ref), (half_in, place(core)), (rest_in, place(1 - core)), (x_in, x_ref),
+                       (own_in, own_ref))
+        finish_all(copies[:3])
+        peer = mm(peer_ref[...], proj_ref[...])
+        finish_all(copies[3:])
+    else:
+        middle_ref, nm_ref, x_ref, own_ref, peer_ref, sems = refs
+        finish_all(begin(sems, (x_in, x_ref), (own_in, own_ref), (peer_in, peer_ref)))
+        peer = peer_ref[...].astype(F32)
+    middle = x_ref[...].astype(F32) + (own_ref[...].astype(F32) + peer) + line(bias_ref)
     middle_ref[...] = middle
     xhat, _ = norm_parts(middle)
     nm_ref[...] = (xhat * line(gain_ref) + line(shift_ref)).astype(BF)
@@ -273,12 +294,12 @@
     masks = head_masks()
     masks_f = [m.astype(F32) for m in masks]
     ones = block_ones()
-    fill(gm_s, mm(branch_ref[...], proj_ref[...], LAST_LAST).astype(BF).astype(F32))
+    fill(gm_s, mm(branch_ref[...], proj_ref[...], LAST_LAST).astype(BF).astype(F32), windows)
 
     def window(w, carry):
         for g in range(groups):
             cols = slice(g * LANES, (g + 1) * LANES)
-            places = pl.ds(w, SLOT, stride=windows)
+            places = pl.ds(w, SLOT, stride=windows + 1)
             gm = gm_s[g, places, :].astype(BF)
             q = q_ref[w, :, cols]
             k = k_ref[w, :, cols]
@@ -298,7 +319,7 @@
     lax.fori_loop(0, windows, window, 0, unroll=2)
     back = None
     for part, scratch in enumerate((gq_s, gk_s, gv_s)):
-        grad = empty(scratch, rows)
+        grad = empty(scratch, windows)
         grads_ref[part] = grad
         if part != 1:
             width = grad.shape[1]
@@ -508,16 +529,20 @@
     tile = shape_of(windows, SLOT, width, dtype=BF)
     outs = [shape_of(windows, groups, SLOT, GROUP * SLOT, dtype=BF), tile, tile, tile, shape_of(rows, width, dtype=BF),
             shape_of(features, rows, dtype=BF)]
-    scratch = [pltpu.VMEM((windows, GROUP * SLOT), F32)] + [pltpu.VMEM((groups, SLOT * windows, LANES), F32)] * 4
+    scratch = [pltpu.VMEM((windows, GROUP * SLOT), F32)] + [pltpu.VMEM((groups, SLOT * (windows + 1), LANES), F32)] * 4
     scratch += like(x, qkv) + dma(4)
     return call(functools.partial(attn_forward_kernel, windows), outs, scratch, "attn_forward", SMALL, (),
                 x, *ln1, qkv, qv_bias, pos, mask, far=(0, 3), limit=ALL_VMEM)
 
 
-def middle_norm(x, own, peer, bias, ln2):
+def middle_norm(me, x, own, peer, bias, ln2, halves):
     rows, features = x.shape
-    return call(middle_kernel, [shape_of(rows, features), shape_of(rows, features, dtype=BF)], [], "middle", SMALL, (),
-                x, own, peer, bias, *ln2, limit=ALL_VMEM)
+    scratch = like(x, own, peer)
+    if halves:
+        scratch += [pltpu.VMEM((2 * halves[0].shape[0], features), BF)]
+    return call(functools.partial(middle_kernel, bool(halves)), [shape_of(rows, features), shape_of(rows, features, dtype=BF)],
+                scratch + dma(5), "middle", SMALL, (me,), x, own, peer, bias, *ln2, *halves, far=(0, 1, 2, 6, 7),
+                limit=ALL_VMEM)
 
 
 def mlp(nm, cot, fc1, fc1_bias, fc2):
@@ -551,7 +576,7 @@
     groups = width // LANES
     outs = [shape_of(3, rows, width, dtype=BF), shape_of(1, 2 * width), shape_of(groups, SLOT, GROUP * SLOT),
             shape_of(rows, features, dtype=BF), shape_of(2, features)]
-    scratch = [pltpu.VMEM((groups, SLOT * windows, LANES), F32)] * 4
+    scratch = [pltpu.VMEM((groups, SLOT * (windows + 1), LANES), F32)] * 4
     return call(functools.partial(attn_backward_kernel, windows), outs, scratch, "attn_backward", SMALL, (),
                 branch, x, *kept, qkv, proj)
 
@@ -683,12 +708,11 @@
         mixed = across(after(kept[1][4], cots[1]))
         half = after(half, kept[1][4])
         rest = flip(half, CORE)
-        other = jnp.where(core == 0, jnp.concatenate([half, rest]), jnp.concatenate([rest, half]))
-        parts = project(kept[0][4], proj), project(mixed, other)
+        parts, halves = (project(kept[0][4], proj), mixed), (half, rest)
     else:
-        parts = own_sums([project(k[4], proj) for k in kept])
+        parts, halves = own_sums([project(k[4], proj) for k in kept]), ()
         cots = blocks_of(cot)
-    middle, nm = middle_norm(x, *parts, proj_bias, ln2)
+    middle, nm = middle_norm(me, x, *parts, proj_bias, ln2, halves)
 
     blocks, outs, gmids = [], [], []
     for nm_b, cot_b in zip(blocks_of(nm), cots):
@@ -744,8 +768,8 @@
         quad = jnp.stack([piece] + flip_line([piece] * 3))
         fc_pair = after(flip(fc_quad, SIDE), quad)
         g_fc1, g_fc2, small = finish_mlp(me, (fc_quad, fc_pair, after(flip(fc_quad, CORE), quad), after(flip(fc_pair, CORE), quad)))
-        pair = flip(quad, SIDE)
-        gw, gproj = finish(me, (quad, pair, flip(quad, CORE), after(flip(pair, CORE), small)),
+        pair = after(flip(quad, SIDE), small)
+        gw, gproj = finish(me, (quad, pair, flip(quad, CORE), flip(pair, CORE)),
                            shape_of(3, features, width), shape_of(width, features))
         totals = small[0:6] + across(small[0:6])
     else:

time: 230 us -> 225 us (0.978)
  waiting for transfers between devices: 69.3 us -> 65.6 us
  matrix products: 4.08 us -> 1.29 us
    ppermute x28, waiting for transfers between devices: 55.6 us -> 50.5 us  [flip(): return lax.ppermute(v, 'dp', [(i, i ^ bits) for i in range(16)])]
    dot_general x2 -> x1, matrix products: 4.08 us -> 1.29 us  [shards(): jnp.dot(mixed, weight, preferred_element_type=F32).astype(BF)]
  transfers between devices with their start and end apart: 39 -> 39, of which waited for: 15 -> 17; matrix products, arithmetic and copies ran while one was open for 3% -> 3% of each run, Pallas kernels for 35% -> 35%
where the time goes in v2:
time: 225 us
  Pallas kernels  92 us (41%)
  waiting for transfers between devices  65.6 us (29%)
  starting transfers between devices  46.9 us (21%)
  local copies, waits for them, and re-layouts  13.8 us (6%)
  other arithmetic  3.94 us (2%)
    pallas_call x14, Pallas kernels, call(): pl.pallas_call(kernel, out_shape=outs, in_specs=in_specs, out_specs=[spac...  92 us
    ppermute x28, waiting for transfers between devices, flip(): return lax.ppermute(v, 'dp', [(i, i ^ bits) for i in range(16)])  50.5 us
    ppermute x28, starting transfers between devices, flip(): return lax.ppermute(v, 'dp', [(i, i ^ bits) for i in range(16)])  34.6 us
    ppermute x11, waiting for transfers between devices, across(): return lax.ppermute(v, 'mp', [(0, 1), (1, 0)])  15.1 us
    ppermute x11, starting transfers between devices, across(): return lax.ppermute(v, 'mp', [(0, 1), (1, 0)])  12.3 us
    unnamed x94, local copies, waits for them, and re-layouts  10.9 us
  transfers between devices with their start and end apart: 39, of which 17 were waited for; matrix products, arithmetic and copies ran while one was open for 3% of the time, Pallas kernels for 35%

profile of v2, /device:TPU:0, one launch (start us, length us, event | category | flops | bytes accessed | tf_op | source)
XLA Modules:
  0.0 224.9 jit_solution(5362490312959374520)
XLA Ops:
  0.7 1.0 constant_dynamic-slice_fusion
  1.6 3.0 %collective-permute-start.2 = (bf16[192,768]{1,0:T(8,128)(2,1)S(1)}, bf16[192,768]{1,0:T(8,128)(2,1)}, u32[]{:S(2)}, u32[]{:S(2)}) collective-permute-start(bf16[192,768]{1,0:T(8,128)(2,1)S(1)} %constant_dynamic-slice_fusion), channel_id=1, source_target_pairs={{0,1},{1,0},{2,3},{3,2},{4,5},{5,4},{6,7},{7,6},{8,9},{9,8},{10,11... | collective-permute-start | bytes 884744 | tf_op jit(solution)/shard_map/ppermute | solution.py:614
  5.4 2.0 collective-permute-start
  9.3 12.0 %attn_forward.2 = (bf16[8,3,64,256]{3,2,1,0:T(8,128)(2,1)}, bf16[8,64,384]{2,1,0:T(8,128)(2,1)}, bf16[8,64,384]{2,1,0:T(8,128)(2,1)}, bf16[8,64,384]{2,1,0:T(8,1...) custom-call(bf16[392,768]{1,0:T(8,128)(2,1)} %bitcast.100, f32[768]{0:T(1024)} %gain_ref.9, f32[768]{0:T(1024)} %shift_ref.4, ...), custom_call_target="tpu_custom_call" | custom-call | flops 1000000 | bytes 3906 | tf_op jit(solution)/shard_map/attn_forward/pallas_call | solution.py:495
  21.5 4.0 %collective-permute-done.x_in.x_ref = bf16[392,768]{1,0:T(8,128)(2,1)S(1)} collective-permute-done((bf16[392,768]{1,0:T(8,128)(2,1)}, bf16[392,768]{1,0:T(8,128)(2,1)S(1)}, u32[]{:S(2)}, u32[]{:S(2)}) %collective-permute-start) | collective-permute-done | bytes 602144 | tf_op jit(solution)/shard_map/ppermute | solution.py:614
  25.5 0.8 copy-done.11
  26.3 12.1 %attn_forward.3 = (bf16[8,3,64,256]{3,2,1,0:T(8,128)(2,1)}, bf16[8,64,384]{2,1,0:T(8,128)(2,1)}, bf16[8,64,384]{2,1,0:T(8,128)(2,1)}, bf16[8,64,384]{2,1,0:T(8,1...) custom-call(bf16[392,768]{1,0:T(8,128)(2,1)} %copy-done.11, f32[768]{0:T(1024)} %gain_ref.9, f32[768]{0:T(1024)} %shift_ref.4, ...), custom_call_target="tpu_custom_call" | custom-call | flops 1000000 | bytes 3906 | tf_op jit(solution)/shard_map/attn_forward/pallas_call | solution.py:495
  38.4 0.8 copy-done.7
  39.2 2.1 collective-permute-start.4
  41.3 1.3 convolution_convert_fusion.own_in
  43.2 3.8 %collective-permute-done.4.peer_in = bf16[392,384]{1,0:T(8,128)(2,1)} collective-permute-done((bf16[392,384]{1,0:T(8,128)(2,1)}, bf16[392,384]{1,0:T(8,128)(2,1)}, u32[]{:S(2)}, u32[]{:S(2)}) %collective-permute-start.4) | collective-permute-done | bytes 301088 | tf_op jit(solution)/shard_map/ppermute | solution.py:614
  47.0 3.8 %middle.1 = (f32[392,768]{1,0:T(8,128)}, bf16[392,768]{1,0:T(8,128)(2,1)}) custom-call(s32[1]{0:T(128)} %bitcast.me_ref, bf16[392,768]{1,0:T(8,128)(2,1)} %bitcast.101, bf16[392,768]{1,0:T(8,128)(2,1)} %convolution_convert_fusion.own_in, bf16[392,384]{1,0:T(8,128)(2,1)} %collective-permute-done.4.peer_in, f32[768]{0:T(1024)} %bias_ref.5, f32[768]{0:T(1024)} %gain_ref.8, ...), custom_call_target="tpu_custom_call" | custom-call | flops 1000000 | bytes 3906 | tf_op jit(solution)/shard_map/middle/pallas_call | solution.py:495
  50.9 1.5 collective-permute-start.6
  52.4 1.1 copy-done.9
  53.5 6.1 %mlp.2 = (bf16[392,1536]{1,0:T(8,128)(2,1)S(1)}, bf16[392,1536]{1,0:T(8,128)(2,1)S(1)}, bf16[392,768]{1,0:T(8,128)(2,1)S(1)}, bf16[392,768]{1,0:T(8,128)(2,1)S(1)}) custom-call(bf16[392,768]{1,0:T(8,128)(2,1)S(1)} %copy-done.9, bf16[392,768]{1,0:T(8,128)(2,1)S(1)} %bitcast.106, bf16[768,1536]{1,0:T(8,128)(2,1)S(1)} %copy-done.2, ...), custom_call_target="tpu_custom_call" | custom-call | flops 1000000 | bytes 3906 | tf_op jit(solution)/shard_map/mlp/pallas_call | solution.py:495
  59.6 1.0 copy-done.14
  60.6 1.0 copy-done.15
  61.6 0.8 copy-done.24
  62.5 0.9 copy-done.39
  63.3 0.8 collective-permute-done.6.nm_ref.refs_4_
  64.2 6.9 %mlp.3 = (bf16[392,1536]{1,0:T(8,128)(2,1)S(1)}, bf16[392,1536]{1,0:T(8,128)(2,1)S(1)}, bf16[392,768]{1,0:T(8,128)(2,1)S(1)}, bf16[392,768]{1,0:T(8,128)(2,1)}) custom-call(bf16[392,768]{1,0:T(8,128)(2,1)S(1)} %collective-permute-done.6.nm_ref.refs_4_, bf16[392,768]{1,0:T(8,128)(2,1)S(1)} %copy-done.8, bf16[768,1536]{1,0:T(8,128)(2,1)S(1)} %copy-done.2, ...), custom_call_target="tpu_custom_call" | custom-call | flops 1000000 | bytes 3906 | tf_op jit(solution)/shard_map/mlp/pallas_call | solution.py:495
  71.1 1.0 copy-done.16
  72.1 1.1 copy-done.17
  73.1 0.8 copy-done.37
  74.0 0.8 collective-permute-start.8
  74.8 12.0 %mlp_weights.1 = (f32[1,1536]{1,0:T(1,128)}, bf16[2,4,96,768]{3,2,1,0:T(8,128)(2,1)}, bf16[2,4,96,768]{3,2,1,0:T(8,128)(2,1)}, bf16[2,4,96,768]{3,2,1,0:T(8,128)(2,1)}, bf16[2,4,96,768]{3,2,1,0:T(8,128)(2,1)}) custom-call(s32[1]{0:T(128)} %bitcast.me_ref, bf16[392,768]{1,0:T(8,128)(2,1)} %get-tuple-element.98.nm_ref.refs_0_, bf16[392,768]{1,0:T(8,128)(2,1)} %bitcast.104, ...), custom_call_target="tpu_custom_call" | custom-call | flops 1000000 | bytes 3906 | tf_op jit(solution)/shard_map/mlp_weights/pallas_call | solution.py:495
  87.5 1.1 middle_back.1
  88.6 1.3 collective-permute-start.11
  90.2 1.6 collective-permute-start.12
  91.9 1.5 collective-permute-start.17
  93.9 10.6 %attn_backward.2 = (bf16[3,392,384]{2,1,0:T(8,128)(2,1)S(1)}, f32[1,768]{1,0:T(1,128)S(1)}, f32[3,64,256]{2,1,0:T(8,128)S(1)}, bf16[392,768]{1,0:T(8,128)(2,1)S(1)}, f32[2,768]{1,0:T(2,128)S(1)}) custom-call(bf16[392,768]{1,0:T(8,128)(2,1)S(1)} %get-tuple-element.137.branch_ref.refs_2_, bf16[392,768]{1,0:T(8,128)(2,1)S(1)} %bitcast.102, ...), custom_call_target="tpu_custom_call" | custom-call | flops 1000000 | bytes 3906 | tf_op jit(solution)/shard_map/attn_backward/pallas_call | solution.py:495
  104.5 1.9 collective-permute-done.12
  106.6 3.7 %collective-permute-start.16 = (bf16[96,768]{1,0:T(8,128)(2,1)S(1)}, bf16[96,768]{1,0:T(8,128)(2,1)S(1)}, u32[]{:S(2)}, u32[]{:S(2)}) collective-permute-start(bf16[96,768]{1,0:T(8,128)(2,1)S(1)} %get-tuple-element.179), channel_id=1, source_target_pairs={{0,24},{2,26},{4,28},{6,30},{8,16},{10,18},{12,20},{14,22},{16,8},... | collective-permute-start | bytes 442376 | tf_op jit(solution)/shard_map/ppermute | solution.py:618
  110.3 0.8 collective-permute-start.14
  111.1 10.7 %attn_backward.3 = (bf16[3,392,384]{2,1,0:T(8,128)(2,1)S(1)}, f32[1,768]{1,0:T(1,128)S(1)}, f32[3,64,256]{2,1,0:T(8,128)S(1)}, bf16[392,768]{1,0:T(8,128)(2,1)S(1)}, f32[2,768]{1,0:T(2,128)S(1)}) custom-call(bf16[392,768]{1,0:T(8,128)(2,1)S(1)} %collective-permute-done.11.branch_ref.refs_9_, bf16[392,768]{1,0:T(8,128)(2,1)S(1)} %copy-done.12, ...), custom_call_target="tpu_custom_call" | custom-call | flops 1000000 | bytes 3906 | tf_op jit(solution)/shard_map/attn_backward/pallas_call | solution.py:495
  121.9 3.7 %collective-permute-start.20 = (bf16[96,768]{1,0:T(8,128)(2,1)S(1)}, bf16[96,768]{1,0:T(8,128)(2,1)S(1)}, u32[]{:S(2)}, u32[]{:S(2)}) collective-permute-start(bf16[96,768]{1,0:T(8,128)(2,1)S(1)} %get-tuple-element.176), channel_id=1, source_target_pairs={{0,24},{2,26},{4,28},{6,30},{8,16},{10,18},{12,20},{14,22},{16,8},... | collective-permute-start | bytes 442376 | tf_op jit(solution)/shard_map/ppermute | solution.py:618
  125.6 0.8 collective-permute-start.18
  126.6 5.7 %attn_weights.1 = (bf16[2,4,96,768]{3,2,1,0:T(8,128)(2,1)S(1)}, bf16[2,4,96,768]{3,2,1,0:T(8,128)(2,1)S(1)}, bf16[16,768]{1,0:T(8,128)(2,1)S(1)}) custom-call(s32[1]{0:T(128)} %bitcast.me_ref, f32[4,768]{1,0:T(4,128)S(1)} %get-tuple-element.135.sums2_ref, f32[1,1536]{1,0:T(1,128)S(1)} %copy-done.35, bf16[768,392]{1,0:T(8,128)(2,1)S(1)} %copy-done.20, ...), custom_call_target="tpu_custom_call" | custom-call | flops 1000000 | bytes 3906 | tf_op jit(solution)/shard_map/attn_weights/pallas_call | solution.py:495
  132.4 3.5 %collective-permute-done.19 = bf16[96,768]{1,0:T(8,128)(2,1)S(1)} collective-permute-done((bf16[96,768]{1,0:T(8,128)(2,1)S(1)}, bf16[96,768]{1,0:T(8,128)(2,1)S(1)}, u32[]{:S(2)}, u32[]{:S(2)}) %collective-permute-start.19) | collective-permute-done | bytes 147488 | tf_op jit(solution)/shard_map/ppermute | solution.py:618
  136.2 2.9 %collective-permute-start.21 = (bf16[208,768]{1,0:T(8,128)(2,1)S(1)}, bf16[208,768]{1,0:T(8,128)(2,1)S(1)}, u32[]{:S(2)}, u32[]{:S(2)}) collective-permute-start(bf16[208,768]{1,0:T(8,128)(2,1)S(1)} %get-tuple-element.183), channel_id=1, source_target_pairs={{0,8},{2,10},{4,12},{6,14},{8,0},{10,2},{12,4},{14,6},{16,24},{18,... | collective-permute-start | bytes 958472 | tf_op jit(solution)/shard_map/ppermute | solution.py:618
  139.1 1.4 collective-permute-start.23
  140.7 1.6 collective-permute-start.26
  142.3 11.6 %collective-permute-done.22 = bf16[208,768]{1,0:T(8,128)(2,1)S(1)} collective-permute-done((bf16[208,768]{1,0:T(8,128)(2,1)S(1)}, bf16[208,768]{1,0:T(8,128)(2,1)S(1)}, u32[]{:S(2)}, u32[]{:S(2)}) %collective-permute-start.22) | collective-permute-done | bytes 319520 | tf_op jit(solution)/shard_map/ppermute | solution.py:618
  153.9 6.8 %collective-permute-done.21 = bf16[208,768]{1,0:T(8,128)(2,1)S(1)} collective-permute-done((bf16[208,768]{1,0:T(8,128)(2,1)S(1)}, bf16[208,768]{1,0:T(8,128)(2,1)S(1)}, u32[]{:S(2)}, u32[]{:S(2)}) %collective-permute-start.21) | collective-permute-done | bytes 319520 | tf_op jit(solution)/shard_map/ppermute | solution.py:618
  160.9 1.6 collective-permute-start.24
  162.8 1.1 add_convert_fusion
  164.1 7.2 %collective-permute-start.27 = (bf16[96,768]{1,0:T(8,128)(2,1)S(1)}, bf16[96,768]{1,0:T(8,128)(2,1)S(1)}, u32[]{:S(2)}, u32[]{:S(2)}) collective-permute-start(bf16[96,768]{1,0:T(8,128)(2,1)S(1)} %get-tuple-element.173), channel_id=1, source_target_pairs={{0,8},{2,10},{4,12},{6,14},{8,0},{10,2},{12,4},{14,6},{16,24},{18,... | collective-permute-start | bytes 442376 | tf_op jit(solution)/shard_map/ppermute | solution.py:618
  171.3 1.4 collective-permute-start.29
  172.8 4.6 %collective-permute-done.13.peer_ref = bf16[392,768]{1,0:T(8,128)(2,1)S(1)} collective-permute-done((bf16[392,768]{1,0:T(8,128)(2,1)S(1)}, bf16[392,768]{1,0:T(8,128)(2,1)S(1)}, u32[]{:S(2)}, u32[]{:S(2)}) %collective-permute-start.13) | collective-permute-done | bytes 602144 | tf_op jit(solution)/shard_map/ppermute | solution.py:614
  177.4 1.7 input_back.1
  179.2 1.1 collective-permute-done.29
  180.2 5.3 %collective-permute-done.28 = bf16[96,768]{1,0:T(8,128)(2,1)S(1)} collective-permute-done((bf16[96,768]{1,0:T(8,128)(2,1)S(1)}, bf16[96,768]{1,0:T(8,128)(2,1)S(1)}, u32[]{:S(2)}, u32[]{:S(2)}) %collective-permute-start.28) | collective-permute-done | bytes 147488 | tf_op jit(solution)/shard_map/ppermute | solution.py:618
  185.7 1.5 collective-permute-start.32
  187.2 1.2 collective-permute-start.31
  188.4 1.8 collective-permute-start.30
  190.1 4.2 %collective-permute-done.32 = bf16[96,768]{1,0:T(8,128)(2,1)S(1)} collective-permute-done((bf16[96,768]{1,0:T(8,128)(2,1)S(1)}, bf16[96,768]{1,0:T(8,128)(2,1)S(1)}, u32[]{:S(2)}, u32[]{:S(2)}) %collective-permute-start.32) | collective-permute-done | bytes 147488 | tf_op jit(solution)/shard_map/ppermute | solution.py:618
  194.3 6.1 %collective-permute-done.31 = bf16[96,768]{1,0:T(8,128)(2,1)S(1)} collective-permute-done((bf16[96,768]{1,0:T(8,128)(2,1)S(1)}, bf16[96,768]{1,0:T(8,128)(2,1)S(1)}, u32[]{:S(2)}, u32[]{:S(2)}) %collective-permute-start.31) | collective-permute-done | bytes 147488 | tf_op jit(solution)/shard_map/ppermute | solution.py:618
  200.6 0.9 collective-permute-start.36
  201.7 1.9 collective-permute-done.34.refs_3_
  203.6 5.4 %finish_mlp.1 = (f32[768,1536]{1,0:T(8,128)}, f32[1536,768]{1,0:T(8,128)}, f32[16,768]{1,0:T(8,128)S(1)}) custom-call(s32[1]{0:T(128)} %bitcast.me_ref, bf16[4,208,768]{2,1,0:T(8,128)(2,1)S(1)} %pad_maximum_fusion.refs_0_, bf16[4,208,768]{2,1,0:T(8,128)(2,1)S(1)} %collective-permute-done.24.refs_1_, ...), custom_call_target="tpu_custom_call" | custom-call | flops 1000000 | bytes 3906 | tf_op jit(solution)/shard_map/finish_mlp/pallas_call | solution.py:495
  209.0 7.3 %collective-permute-done.36.refs_1_ = bf16[4,96,768]{2,1,0:T(8,128)(2,1)S(1)} collective-permute-done((bf16[4,96,768]{2,1,0:T(8,128)(2,1)S(1)}, bf16[4,96,768]{2,1,0:T(8,128)(2,1)S(1)}, u32[]{:S(2)}, u32[]{:S(2)}) %collective-permute-start.36) | collective-permute-done | bytes 589856 | tf_op jit(solution)/shard_map/ppermute | solution.py:618
  217.0 0.8 collective-permute-start.35
  219.0 1.8 collective-permute-done.35
  221.5 3.2 %finish.1 = (f32[3,768,384]{2,1,0:T(8,128)}, f32[384,768]{1,0:T(8,128)}) custom-call(s32[1]{0:T(128)} %bitcast.me_ref, bf16[4,96,768]{2,1,0:T(8,128)(2,1)S(1)} %pad_maximum_fusion.1.refs_0_, bf16[4,96,768]{2,1,0:T(8,128)(2,1)S(1)} %collective-permute-done.36.refs_1_, bf16[4,96,768]{2,1,0:T(8,128)(2,1)S(1)} %collective-permute-done.37.refs_2_, ...), custom_call_target="tpu_custom_call" | custom-call | flops 1000000 | bytes 3906 | tf_op jit(solution)/shard_map/finish/pallas_call | solution.py:495
  (149 shorter events, 9.5 us)
Async XLA Ops:
  1.6 19.7 %collective-permute-start.2 = (bf16[192,768]{1,0:T(8,128)(2,1)S(1)}, bf16[192,768]{1,0:T(8,128)(2,1)}, u32[]{:S(2)}, u32[]{:S(2)}) collective-permute-start(bf16[192,768]{1,0:T(8,128)(2,1)S(1)} %constant_dynamic-slice_fusion), channel_id=1, source_target_pairs={{0,1},{1,0},{2,3},{3,2},{4,5},{5,4},{6,7},{7,6},{8,9},{9,8},{10,11... | collective-permute-start | bytes 884744 | tf_op jit(solution)/shard_map/ppermute | solution.py:614
  5.3 16.0 %collective-permute-start.1 = (f32[8,49]{1,0:T(8,128)S(1)}, f32[8,49]{1,0:T(8,128)S(1)}, u32[]{:S(2)}, u32[]{:S(2)}) collective-permute-start(f32[8,49]{1,0:T(8,128)S(1)} %convert_element_type.288.valid_ref), channel_id=1, source_target_pairs={{0,1},{1,0},{2,3},{3,2},{4,5},{5,4},{6,7},{7,6},{8,9},{9,8},{10,11... | collective-permute-start | bytes 4712 | tf_op jit(solution)/shard_map/ppermute | solution.py:614
  5.4 20.1 %collective-permute-start = (bf16[392,768]{1,0:T(8,128)(2,1)}, bf16[392,768]{1,0:T(8,128)(2,1)S(1)}, u32[]{:S(2)}, u32[]{:S(2)}) collective-permute-start(bf16[392,768]{1,0:T(8,128)(2,1)} %bitcast.99), channel_id=1, source_target_pairs={{0,1},{1,0},{2,3},{3,2},{4,5},{5,4},{6,7},{7,6},{8,9},{9,8},{10,11... | collective-permute-start | bytes 1806344 | tf_op jit(solution)/shard_map/ppermute | solution.py:614
  9.3 12.1 %copy-start.5 = (bf16[8,49,768]{2,0,1:T(8,128)(2,1)S(1)}, bf16[8,49,768]{2,0,1:T(8,128)(2,1)}, u32[]{:S(2)}) copy-start(bf16[8,49,768]{2,0,1:T(8,128)(2,1)} %param.31) | copy-start | bytes 1806340
  21.4 19.9 %copy-start.4 = (bf16[384,768]{1,0:T(8,128)(2,1)S(1)}, bf16[384,768]{1,0:T(8,128)(2,1)}, u32[]{:S(2)}) copy-start(bf16[384,768]{1,0:T(8,128)(2,1)} %proj_ref.3) | copy-start | bytes 1769476
  21.4 19.9 %copy-start.18 = (bf16[392,384]{1,0:T(8,128)(2,1)S(1)}, bf16[392,384]{1,0:T(8,128)(2,1)}, u32[]{:S(2)}) copy-start(bf16[392,384]{1,0:T(8,128)(2,1)} %get-tuple-element.91.refs_1_) | copy-start | bytes 903172
  21.4 17.0 %collective-permute-start.3 = (bf16[392,768]{1,0:T(8,128)(2,1)S(1)}, bf16[392,768]{1,0:T(8,128)(2,1)S(1)}, u32[]{:S(2)}, u32[]{:S(2)}) collective-permute-start(bf16[392,768]{1,0:T(8,128)(2,1)S(1)} %bitcast.105), channel_id=1, source_target_pairs={{0,1},{1,0},{2,3},{3,2},{4,5},{5,4},{6,7},{7,6},{8,9},{9,8},{10,11... | collective-permute-start | bytes 1806344 | tf_op jit(solution)/shard_map/ppermute | solution.py:614
  26.3 26.1 %copy-start.3 = (bf16[1536,768]{1,0:T(8,128)(2,1)S(1)}, bf16[1536,768]{1,0:T(8,128)(2,1)}, u32[]{:S(2)}) copy-start(bf16[1536,768]{1,0:T(8,128)(2,1)} %fc2_ref.3) | copy-start | bytes 7077892
  39.2 7.8 %collective-permute-start.4 = (bf16[392,384]{1,0:T(8,128)(2,1)}, bf16[392,384]{1,0:T(8,128)(2,1)}, u32[]{:S(2)}, u32[]{:S(2)}) collective-permute-start(bf16[392,384]{1,0:T(8,128)(2,1)} %get-tuple-element.95.refs_8_), channel_id=1, source_target_pairs={{0,1},{1,0},{2,3},{3,2},{4,5},{5,4},{6,7},{7,6},{8,9},{9,8},{10,11... | collective-permute-start | bytes 903176 | tf_op jit(solution)/shard_map/ppermute | solution.py:614
  41.3 1.9 collective-permute-start.5
  41.3 11.1 %copy-start.2 = (bf16[768,1536]{1,0:T(8,128)(2,1)S(1)}, bf16[768,1536]{1,0:T(8,128)(2,1)}, u32[]{:S(2)}) copy-start(bf16[768,1536]{1,0:T(8,128)(2,1)} %fc1_ref.3) | copy-start | bytes 7077892
  42.6 9.8 %copy-start.44 = (f32[1536]{0:T(1024)S(1)}, f32[1536]{0:T(1024)}, u32[]{:S(2)}) copy-start(f32[1536]{0:T(1024)} %param.28) | copy-start | bytes 18436
  50.9 13.3 %collective-permute-start.6 = (bf16[392,768]{1,0:T(8,128)(2,1)}, bf16[392,768]{1,0:T(8,128)(2,1)S(1)}, u32[]{:S(2)}, u32[]{:S(2)}) collective-permute-start(bf16[392,768]{1,0:T(8,128)(2,1)} %get-tuple-element.98.nm_ref.refs_0_), channel_id=1, source_target_pairs={{0,1},{1,0},{2,3},{3,2},{4,5},{5,4},{6,7},{7,6},{8,9},{9,8},{10,11... | collective-permute-start | bytes 1806344 | tf_op jit(solution)/shard_map/ppermute | solution.py:614
  53.5 10.7 %copy-start.8 = (bf16[392,768]{1,0:T(8,128)(2,1)S(1)}, bf16[392,768]{1,0:T(8,128)(2,1)}, u32[]{:S(2)}) copy-start(bf16[392,768]{1,0:T(8,128)(2,1)} %copy-done.7) | copy-start | bytes 1806340
  64.1 6.9 %copy-start.10 = (bf16[392,768]{1,0:T(8,128)(2,1)}, bf16[392,768]{1,0:T(8,128)(2,1)S(1)}, u32[]{:S(2)}) copy-start(bf16[392,768]{1,0:T(8,128)(2,1)S(1)} %collective-permute-done.6.nm_ref.refs_4_) | copy-start | bytes 1806340
  74.0 13.5 %collective-permute-start.8 = (bf16[392,768]{1,0:T(8,128)(2,1)}, bf16[392,768]{1,0:T(8,128)(2,1)S(1)}, u32[]{:S(2)}, u32[]{:S(2)}) collective-permute-start(bf16[392,768]{1,0:T(8,128)(2,1)} %get-tuple-element.103), channel_id=1, source_target_pairs={{0,1},{1,0},{2,3},{3,2},{4,5},{5,4},{6,7},{7,6},{8,9},{9,8},{10,11... | collective-permute-start | bytes 1806344 | tf_op jit(solution)/shard_map/ppermute | solution.py:614
  74.8 12.6 %copy-start.6 = (bf16[8,49,768]{2,0,1:T(8,128)(2,1)S(1)}, bf16[8,49,768]{2,0,1:T(8,128)(2,1)}, u32[]{:S(2)}) copy-start(bf16[8,49,768]{2,0,1:T(8,128)(2,1)} %param.31) | copy-start | bytes 1806340
  74.8 12.6 %copy-start.19 = (f32[392,768]{1,0:T(8,128)S(1)}, f32[392,768]{1,0:T(8,128)}, u32[]{:S(2)}) copy-start(f32[392,768]{1,0:T(8,128)} %get-tuple-element.97.middle_ref) | copy-start | bytes 3612676
  74.8 12.6 %copy-start.36 = (f32[768]{0:T(1024)S(1)}, f32[768]{0:T(1024)}, u32[]{:S(2)}) copy-start(f32[768]{0:T(1024)} %gain_ref.8) | copy-start | bytes 9220
  74.8 12.7 %copy-start.40 = (bf16[392,768]{1,0:T(8,128)(2,1)S(1)}, bf16[392,768]{1,0:T(8,128)(2,1)}, u32[]{:S(2)}) copy-start(bf16[392,768]{1,0:T(8,128)(2,1)} %copy-done.39) | copy-start | bytes 1806340
  86.9 3.1 %collective-permute-start.9 = (bf16[2,4,96,768]{3,2,1,0:T(8,128)(2,1)}, bf16[2,4,96,768]{3,2,1,0:T(8,128)(2,1)S(1)}, u32[]{:S(2)}, u32[]{:S(2)}) collective-permute-start(bf16[2,4,96,768]{3,2,1,0:T(8,128)(2,1)} %get-tuple-element.112), channel_id=1, source_target_pairs={{0,2},{2,0},{4,6},{6,4},{8,10},{10,8},{12,14},{14,12},{16,18},{18,... | collective-permute-start | bytes 3538952 | tf_op jit(solution)/shard_map/ppermute | solution.py:618
  86.9 4.8 %collective-permute-start.10 = (bf16[2,4,96,768]{3,2,1,0:T(8,128)(2,1)}, bf16[2,4,96,768]{3,2,1,0:T(8,128)(2,1)S(1)}, u32[]{:S(2)}, u32[]{:S(2)}) collective-permute-start(bf16[2,4,96,768]{3,2,1,0:T(8,128)(2,1)} %get-tuple-element.115), channel_id=1, source_target_pairs={{0,2},{2,0},{4,6},{6,4},{8,10},{10,8},{12,14},{14,12},{16,18},{18,... | collective-permute-start | bytes 3538952 | tf_op jit(solution)/shard_map/ppermute | solution.py:618
  87.5 5.9 %copy-start.38 = (bf16[392,768]{1,0:T(8,128)(2,1)S(1)}, bf16[392,768]{1,0:T(8,128)(2,1)}, u32[]{:S(2)}) copy-start(bf16[392,768]{1,0:T(8,128)(2,1)} %copy-done.37) | copy-start | bytes 1806340
  87.5 6.3 %copy-start.30 = (bf16[8,64,384]{2,1,0:T(8,128)(2,1)S(1)}, bf16[8,64,384]{2,1,0:T(8,128)(2,1)}, u32[]{:S(2)}) copy-start(bf16[8,64,384]{2,1,0:T(8,128)(2,1)} %get-tuple-element.120.k_ref) | copy-start | bytes 1179652
  87.5 6.3 %copy-start.31 = (bf16[8,64,384]{2,1,0:T(8,128)(2,1)S(1)}, bf16[8,64,384]{2,1,0:T(8,128)(2,1)}, u32[]{:S(2)}) copy-start(bf16[8,64,384]{2,1,0:T(8,128)(2,1)} %get-tuple-element.121.v_ref) | copy-start | bytes 1179652
  88.6 21.6 %collective-permute-start.11 = (bf16[392,768]{1,0:T(8,128)(2,1)S(1)}, bf16[392,768]{1,0:T(8,128)(2,1)S(1)}, u32[]{:S(2)}, u32[]{:S(2)}) collective-permute-start(bf16[392,768]{1,0:T(8,128)(2,1)S(1)} %get-tuple-element.137.branch_ref.refs_2_), channel_id=1, source_target_pairs={{0,1},{1,0},{2,3},{3,2},{4,5},{5,4},{6,7},{7,6},{8,9},{9,8},{10,11... | collective-permute-start | bytes 1806344 | tf_op jit(solution)/shard_map/ppermute | solution.py:614
  90.2 16.2 %collective-permute-start.12 = (bf16[4,96,768]{2,1,0:T(8,128)(2,1)S(1)}, bf16[4,96,768]{2,1,0:T(8,128)(2,1)S(1)}, u32[]{:S(2)}, u32[]{:S(2)}) collective-permute-start(bf16[4,96,768]{2,1,0:T(8,128)(2,1)S(1)} %fusion), channel_id=1, source_target_pairs={{0,4},{2,6},{4,0},{6,2},{8,12},{10,14},{12,8},{14,10},{16,20},{18,... | collective-permute-start | bytes 1769480 | tf_op jit(solution)/shard_map/ppermute | solution.py:618
  91.9 29.8 %collective-permute-start.17 = (bf16[4,96,768]{2,1,0:T(8,128)(2,1)S(1)}, bf16[4,96,768]{2,1,0:T(8,128)(2,1)S(1)}, u32[]{:S(2)}, u32[]{:S(2)}) collective-permute-start(bf16[4,96,768]{2,1,0:T(8,128)(2,1)S(1)} %fusion.1), channel_id=1, source_target_pairs={{0,4},{2,6},{4,0},{6,2},{8,12},{10,14},{12,8},{14,10},{16,20},{18,... | collective-permute-start | bytes 1769480 | tf_op jit(solution)/shard_map/ppermute | solution.py:618
  93.4 33.1 %collective-permute-start.7 = (bf16[392,768]{1,0:T(8,128)(2,1)S(1)}, bf16[392,768]{1,0:T(8,128)(2,1)S(1)}, u32[]{:S(2)}, u32[]{:S(2)}) collective-permute-start(bf16[392,768]{1,0:T(8,128)(2,1)S(1)} %copy-done.38), channel_id=1, source_target_pairs={{0,1},{1,0},{2,3},{3,2},{4,5},{5,4},{6,7},{7,6},{8,9},{9,8},{10,11... | collective-permute-start | bytes 1806344 | tf_op jit(solution)/shard_map/ppermute | solution.py:614
  93.8 17.2 %copy-start.27 = (bf16[8,64,384]{2,1,0:T(8,128)(2,1)S(1)}, bf16[8,64,384]{2,1,0:T(8,128)(2,1)}, u32[]{:S(2)}) copy-start(bf16[8,64,384]{2,1,0:T(8,128)(2,1)} %get-tuple-element.127.k_ref) | copy-start | bytes 1179652
  93.8 17.2 %copy-start.28 = (bf16[8,64,384]{2,1,0:T(8,128)(2,1)S(1)}, bf16[8,64,384]{2,1,0:T(8,128)(2,1)}, u32[]{:S(2)}) copy-start(bf16[8,64,384]{2,1,0:T(8,128)(2,1)} %get-tuple-element.128.v_ref) | copy-start | bytes 1179652
  104.5 6.5 %copy-start.12 = (bf16[392,768]{1,0:T(8,128)(2,1)S(1)}, bf16[392,768]{1,0:T(8,128)(2,1)}, u32[]{:S(2)}) copy-start(bf16[392,768]{1,0:T(8,128)(2,1)} %copy-done.11) | copy-start | bytes 1806340
  104.5 6.5 %copy-start.22 = (bf16[8,3,64,256]{3,2,1,0:T(8,128)(2,1)S(1)}, bf16[8,3,64,256]{3,2,1,0:T(8,128)(2,1)}, u32[]{:S(2)}) copy-start(bf16[8,3,64,256]{3,2,1,0:T(8,128)(2,1)} %get-tuple-element.125.prob_ref) | copy-start | bytes 2359300
  104.5 6.5 %copy-start.26 = (bf16[8,64,384]{2,1,0:T(8,128)(2,1)S(1)}, bf16[8,64,384]{2,1,0:T(8,128)(2,1)}, u32[]{:S(2)}) copy-start(bf16[8,64,384]{2,1,0:T(8,128)(2,1)} %get-tuple-element.126.q_ref) | copy-start | bytes 1179652
  106.6 19.0 %collective-permute-start.16 = (bf16[96,768]{1,0:T(8,128)(2,1)S(1)}, bf16[96,768]{1,0:T(8,128)(2,1)S(1)}, u32[]{:S(2)}, u32[]{:S(2)}) collective-permute-start(bf16[96,768]{1,0:T(8,128)(2,1)S(1)} %get-tuple-element.179), channel_id=1, source_target_pairs={{0,24},{2,26},{4,28},{6,30},{8,16},{10,18},{12,20},{14,22},{16,8},... | collective-permute-start | bytes 442376 | tf_op jit(solution)/shard_map/ppermute | solution.py:618
  110.2 15.4 %collective-permute-start.15 = (bf16[96,768]{1,0:T(8,128)(2,1)S(1)}, bf16[96,768]{1,0:T(8,128)(2,1)S(1)}, u32[]{:S(2)}, u32[]{:S(2)}) collective-permute-start(bf16[96,768]{1,0:T(8,128)(2,1)S(1)} %get-tuple-element.180), channel_id=1, source_target_pairs={{0,16},{2,18},{4,20},{6,22},{8,24},{10,26},{12,28},{14,30},{16,0},... | collective-permute-start | bytes 442376 | tf_op jit(solution)/shard_map/ppermute | solution.py:618
  110.3 16.2 %collective-permute-start.14 = (bf16[96,768]{1,0:T(8,128)(2,1)S(1)}, bf16[96,768]{1,0:T(8,128)(2,1)S(1)}, u32[]{:S(2)}, u32[]{:S(2)}) collective-permute-start(bf16[96,768]{1,0:T(8,128)(2,1)S(1)} %get-tuple-element.181), channel_id=1, source_target_pairs={{0,8},{2,10},{4,12},{6,14},{8,0},{10,2},{12,4},{14,6},{16,24},{18,... | collective-permute-start | bytes 442376 | tf_op jit(solution)/shard_map/ppermute | solution.py:618
  121.7 4.8 %copy-start.20 = (bf16[768,392]{1,0:T(8,128)(2,1)S(1)}, bf16[768,392]{1,0:T(8,128)(2,1)}, u32[]{:S(2)}) copy-start(bf16[768,392]{1,0:T(8,128)(2,1)} %get-tuple-element.136.refs_0_) | copy-start | bytes 1806340
  121.7 4.8 %copy-start.21 = (bf16[768,392]{1,0:T(8,128)(2,1)S(1)}, bf16[768,392]{1,0:T(8,128)(2,1)}, u32[]{:S(2)}) copy-start(bf16[768,392]{1,0:T(8,128)(2,1)} %get-tuple-element.142.refs_7_) | copy-start | bytes 1806340
  121.7 4.8 %copy-start.32 = (bf16[392,384]{1,0:T(8,128)(2,1)S(1)}, bf16[392,384]{1,0:T(8,128)(2,1)}, u32[]{:S(2)}) copy-start(bf16[392,384]{1,0:T(8,128)(2,1)} %get-tuple-element.95.refs_8_) | copy-start | bytes 903172
  121.8 4.8 %copy-start.35 = (f32[1,1536]{1,0:T(1,128)S(1)}, f32[1,1536]{1,0:T(1,128)}, u32[]{:S(2)}) copy-start(f32[1,1536]{1,0:T(1,128)} %get-tuple-element.108.gb1_ref) | copy-start | bytes 18436
  121.9 10.4 %collective-permute-start.20 = (bf16[96,768]{1,0:T(8,128)(2,1)S(1)}, bf16[96,768]{1,0:T(8,128)(2,1)S(1)}, u32[]{:S(2)}, u32[]{:S(2)}) collective-permute-start(bf16[96,768]{1,0:T(8,128)(2,1)S(1)} %get-tuple-element.176), channel_id=1, source_target_pairs={{0,24},{2,26},{4,28},{6,30},{8,16},{10,18},{12,20},{14,22},{16,8},... | collective-permute-start | bytes 442376 | tf_op jit(solution)/shard_map/ppermute | solution.py:618
  125.6 10.2 %collective-permute-start.19 = (bf16[96,768]{1,0:T(8,128)(2,1)S(1)}, bf16[96,768]{1,0:T(8,128)(2,1)S(1)}, u32[]{:S(2)}, u32[]{:S(2)}) collective-permute-start(bf16[96,768]{1,0:T(8,128)(2,1)S(1)} %get-tuple-element.177), channel_id=1, source_target_pairs={{0,16},{2,18},{4,20},{6,22},{8,24},{10,26},{12,28},{14,30},{16,0},... | collective-permute-start | bytes 442376 | tf_op jit(solution)/shard_map/ppermute | solution.py:618
  125.6 10.2 %collective-permute-start.18 = (bf16[96,768]{1,0:T(8,128)(2,1)S(1)}, bf16[96,768]{1,0:T(8,128)(2,1)S(1)}, u32[]{:S(2)}, u32[]{:S(2)}) collective-permute-start(bf16[96,768]{1,0:T(8,128)(2,1)S(1)} %get-tuple-element.178), channel_id=1, source_target_pairs={{0,8},{2,10},{4,12},{6,14},{8,0},{10,2},{12,4},{14,6},{16,24},{18,... | collective-permute-start | bytes 442376 | tf_op jit(solution)/shard_map/ppermute | solution.py:618
  136.0 4.6 %collective-permute-start.25 = (bf16[2,4,96,768]{3,2,1,0:T(8,128)(2,1)S(1)}, bf16[2,4,96,768]{3,2,1,0:T(8,128)(2,1)S(1)}, u32[]{:S(2)}, u32[]{:S(2)}) collective-permute-start(bf16[2,4,96,768]{3,2,1,0:T(8,128)(2,1)S(1)} %get-tuple-element.153), channel_id=1, source_target_pairs={{0,2},{2,0},{4,6},{6,4},{8,10},{10,8},{12,14},{14,12},{16,18},{18,... | collective-permute-start | bytes 3538952 | tf_op jit(solution)/shard_map/ppermute | solution.py:618
  136.1 17.8 %collective-permute-start.22 = (bf16[208,768]{1,0:T(8,128)(2,1)S(1)}, bf16[208,768]{1,0:T(8,128)(2,1)S(1)}, u32[]{:S(2)}, u32[]{:S(2)}) collective-permute-start(bf16[208,768]{1,0:T(8,128)(2,1)S(1)} %get-tuple-element.183), channel_id=1, source_target_pairs={{0,16},{2,18},{4,20},{6,22},{8,24},{10,26},{12,28},{14,30},{16,0},... | collective-permute-start | bytes 958472 | tf_op jit(solution)/shard_map/ppermute | solution.py:618
  136.2 24.5 %collective-permute-start.21 = (bf16[208,768]{1,0:T(8,128)(2,1)S(1)}, bf16[208,768]{1,0:T(8,128)(2,1)S(1)}, u32[]{:S(2)}, u32[]{:S(2)}) collective-permute-start(bf16[208,768]{1,0:T(8,128)(2,1)S(1)} %get-tuple-element.183), channel_id=1, source_target_pairs={{0,8},{2,10},{4,12},{6,14},{8,0},{10,2},{12,4},{14,6},{16,24},{18,... | collective-permute-start | bytes 958472 | tf_op jit(solution)/shard_map/ppermute | solution.py:618
  139.1 21.6 %collective-permute-start.23 = (bf16[208,768]{1,0:T(8,128)(2,1)S(1)}, bf16[208,768]{1,0:T(8,128)(2,1)S(1)}, u32[]{:S(2)}, u32[]{:S(2)}) collective-permute-start(bf16[208,768]{1,0:T(8,128)(2,1)S(1)} %get-tuple-element.183), channel_id=1, source_target_pairs={{0,24},{2,26},{4,28},{6,30},{8,16},{10,18},{12,20},{14,22},{16,8},... | collective-permute-start | bytes 958472 | tf_op jit(solution)/shard_map/ppermute | solution.py:618
  140.7 23.2 %collective-permute-start.26 = (bf16[4,96,768]{2,1,0:T(8,128)(2,1)S(1)}, bf16[4,96,768]{2,1,0:T(8,128)(2,1)S(1)}, u32[]{:S(2)}, u32[]{:S(2)}) collective-permute-start(bf16[4,96,768]{2,1,0:T(8,128)(2,1)S(1)} %fusion.2), channel_id=1, source_target_pairs={{0,4},{2,6},{4,0},{6,2},{8,12},{10,14},{12,8},{14,10},{16,20},{18,... | collective-permute-start | bytes 1769480 | tf_op jit(solution)/shard_map/ppermute | solution.py:618
  160.9 39.6 %collective-permute-start.24 = (bf16[4,208,768]{2,1,0:T(8,128)(2,1)S(1)}, bf16[4,208,768]{2,1,0:T(8,128)(2,1)S(1)}, u32[]{:S(2)}, u32[]{:S(2)}) collective-permute-start(bf16[4,208,768]{2,1,0:T(8,128)(2,1)S(1)} %pad_maximum_fusion.refs_0_), channel_id=1, source_target_pairs={{0,4},{2,6},{4,0},{6,2},{8,12},{10,14},{12,8},{14,10},{16,20},{18,... | collective-permute-start | bytes 3833864 | tf_op jit(solution)/shard_map/ppermute | solution.py:618
  162.5 14.9 %collective-permute-start.13 = (bf16[392,768]{1,0:T(8,128)(2,1)S(1)}, bf16[392,768]{1,0:T(8,128)(2,1)S(1)}, u32[]{:S(2)}, u32[]{:S(2)}) collective-permute-start(bf16[392,768]{1,0:T(8,128)(2,1)S(1)} %get-tuple-element.129), channel_id=1, source_target_pairs={{0,1},{1,0},{2,3},{3,2},{4,5},{5,4},{6,7},{7,6},{8,9},{9,8},{10,11... | collective-permute-start | bytes 1806344 | tf_op jit(solution)/shard_map/ppermute | solution.py:614
  163.9 13.5 %copy-start.33 = (f32[768]{0:T(1024)S(1)}, f32[768]{0:T(1024)}, u32[]{:S(2)}) copy-start(f32[768]{0:T(1024)} %gain_ref.9) | copy-start | bytes 9220
  164.1 15.1 %collective-permute-start.27 = (bf16[96,768]{1,0:T(8,128)(2,1)S(1)}, bf16[96,768]{1,0:T(8,128)(2,1)S(1)}, u32[]{:S(2)}, u32[]{:S(2)}) collective-permute-start(bf16[96,768]{1,0:T(8,128)(2,1)S(1)} %get-tuple-element.173), channel_id=1, source_target_pairs={{0,8},{2,10},{4,12},{6,14},{8,0},{10,2},{12,4},{14,6},{16,24},{18,... | collective-permute-start | bytes 442376 | tf_op jit(solution)/shard_map/ppermute | solution.py:618
  171.3 8.9 %collective-permute-start.29 = (bf16[96,768]{1,0:T(8,128)(2,1)S(1)}, bf16[96,768]{1,0:T(8,128)(2,1)S(1)}, u32[]{:S(2)}, u32[]{:S(2)}) collective-permute-start(bf16[96,768]{1,0:T(8,128)(2,1)S(1)} %get-tuple-element.174), channel_id=1, source_target_pairs={{0,24},{2,26},{4,28},{6,30},{8,16},{10,18},{12,20},{14,22},{16,8},... | collective-permute-start | bytes 442376 | tf_op jit(solution)/shard_map/ppermute | solution.py:618
  172.7 12.8 %collective-permute-start.28 = (bf16[96,768]{1,0:T(8,128)(2,1)S(1)}, bf16[96,768]{1,0:T(8,128)(2,1)S(1)}, u32[]{:S(2)}, u32[]{:S(2)}) collective-permute-start(bf16[96,768]{1,0:T(8,128)(2,1)S(1)} %get-tuple-element.175), channel_id=1, source_target_pairs={{0,16},{2,18},{4,20},{6,22},{8,24},{10,26},{12,28},{14,30},{16,0},... | collective-permute-start | bytes 442376 | tf_op jit(solution)/shard_map/ppermute | solution.py:618
  185.7 8.7 %collective-permute-start.32 = (bf16[96,768]{1,0:T(8,128)(2,1)S(1)}, bf16[96,768]{1,0:T(8,128)(2,1)S(1)}, u32[]{:S(2)}, u32[]{:S(2)}) collective-permute-start(bf16[96,768]{1,0:T(8,128)(2,1)S(1)} %fusion.9), channel_id=1, source_target_pairs={{0,24},{2,26},{4,28},{6,30},{8,16},{10,18},{12,20},{14,22},{16,8},... | collective-permute-start | bytes 442376 | tf_op jit(solution)/shard_map/ppermute | solution.py:618
  187.2 13.3 %collective-permute-start.31 = (bf16[96,768]{1,0:T(8,128)(2,1)S(1)}, bf16[96,768]{1,0:T(8,128)(2,1)S(1)}, u32[]{:S(2)}, u32[]{:S(2)}) collective-permute-start(bf16[96,768]{1,0:T(8,128)(2,1)S(1)} %fusion.9), channel_id=1, source_target_pairs={{0,16},{2,18},{4,20},{6,22},{8,24},{10,26},{12,28},{14,30},{16,0},... | collective-permute-start | bytes 442376 | tf_op jit(solution)/shard_map/ppermute | solution.py:618
  188.4 12.1 %collective-permute-start.30 = (bf16[96,768]{1,0:T(8,128)(2,1)S(1)}, bf16[96,768]{1,0:T(8,128)(2,1)S(1)}, u32[]{:S(2)}, u32[]{:S(2)}) collective-permute-start(bf16[96,768]{1,0:T(8,128)(2,1)S(1)} %fusion.9), channel_id=1, source_target_pairs={{0,8},{2,10},{4,12},{6,14},{8,0},{10,2},{12,4},{14,6},{16,24},{18,... | collective-permute-start | bytes 442376 | tf_op jit(solution)/shard_map/ppermute | solution.py:618
  190.1 11.6 %collective-permute-start.33 = (bf16[4,208,768]{2,1,0:T(8,128)(2,1)S(1)}, bf16[4,208,768]{2,1,0:T(8,128)(2,1)S(1)}, u32[]{:S(2)}, u32[]{:S(2)}) collective-permute-start(bf16[4,208,768]{2,1,0:T(8,128)(2,1)S(1)} %pad_maximum_fusion.refs_0_), channel_id=1, source_target_pairs={{0,2},{2,0},{4,6},{6,4},{8,10},{10,8},{12,14},{14,12},{16,18},{18,... | collective-permute-start | bytes 3833864 | tf_op jit(solution)/shard_map/ppermute | solution.py:618
  200.6 3.1 %collective-permute-start.34 = (bf16[4,208,768]{2,1,0:T(8,128)(2,1)S(1)}, bf16[4,208,768]{2,1,0:T(8,128)(2,1)S(1)}, u32[]{:S(2)}, u32[]{:S(2)}) collective-permute-start(bf16[4,208,768]{2,1,0:T(8,128)(2,1)S(1)} %collective-permute-done.24.refs_1_), channel_id=1, source_target_pairs={{0,2},{2,0},{4,6},{6,4},{8,10},{10,8},{12,14},{14,12},{16,18},{18,... | collective-permute-start | bytes 3833864 | tf_op jit(solution)/shard_map/ppermute | solution.py:618
  200.6 15.7 %collective-permute-start.36 = (bf16[4,96,768]{2,1,0:T(8,128)(2,1)S(1)}, bf16[4,96,768]{2,1,0:T(8,128)(2,1)S(1)}, u32[]{:S(2)}, u32[]{:S(2)}) collective-permute-start(bf16[4,96,768]{2,1,0:T(8,128)(2,1)S(1)} %pad_maximum_fusion.1.refs_0_), channel_id=1, source_target_pairs={{0,4},{2,6},{4,0},{6,2},{8,12},{10,14},{12,8},{14,10},{16,20},{18,... | collective-permute-start | bytes 1769480 | tf_op jit(solution)/shard_map/ppermute | solution.py:618
  201.5 19.9 %collective-permute-start.37 = (bf16[4,96,768]{2,1,0:T(8,128)(2,1)S(1)}, bf16[4,96,768]{2,1,0:T(8,128)(2,1)S(1)}, u32[]{:S(2)}, u32[]{:S(2)}) collective-permute-start(bf16[4,96,768]{2,1,0:T(8,128)(2,1)S(1)} %pad_maximum_fusion.1.refs_0_), channel_id=1, source_target_pairs={{0,2},{2,0},{4,6},{6,4},{8,10},{10,8},{12,14},{14,12},{16,18},{18,... | collective-permute-start | bytes 1769480 | tf_op jit(solution)/shard_map/ppermute | solution.py:618
  217.0 3.8 %collective-permute-start.35 = (f32[6,768]{1,0:T(8,128)S(1)}, f32[6,768]{1,0:T(8,128)S(1)}, u32[]{:S(2)}, u32[]{:S(2)}) collective-permute-start(f32[6,768]{1,0:T(8,128)S(1)} %slice.210), channel_id=1, source_target_pairs={{0,1},{1,0},{2,3},{3,2},{4,5},{5,4},{6,7},{7,6},{8,9},{9,8},{10,11... | collective-permute-start | bytes 55304 | tf_op jit(solution)/shard_map/ppermute | solution.py:614
  217.8 3.7 %collective-permute-start.38 = (bf16[4,96,768]{2,1,0:T(8,128)(2,1)S(1)}, bf16[4,96,768]{2,1,0:T(8,128)(2,1)S(1)}, u32[]{:S(2)}, u32[]{:S(2)}) collective-permute-start(bf16[4,96,768]{2,1,0:T(8,128)(2,1)S(1)} %collective-permute-done.36.refs_1_), channel_id=1, source_target_pairs={{0,2},{2,0},{4,6},{6,4},{8,10},{10,8},{12,14},{14,12},{16,18},{18,... | collective-permute-start | bytes 1769480 | tf_op jit(solution)/shard_map/ppermute | solution.py:618
  (22 other events, 45.0 us)

commit v3 on v2

--- a/solution.py
+++ b/solution.py
@@ -91,6 +91,12 @@
 def row_max(tile, low_half):
     low = jnp.max(jnp.where(low_half, tile, -3e38), axis=-1, keepdims=True)
     high = jnp.max(jnp.where(low_half, -3e38, tile), axis=-1, keepdims=True)
+    return jnp.where(low_half, low, high)
+
+
+def row_sum(tile, low_half):
+    low = jnp.sum(jnp.where(low_half, tile, 0.0), axis=-1, keepdims=True)
+    high = jnp.sum(jnp.where(low_half, 0.0, tile), axis=-1, keepdims=True)
     return jnp.where(low_half, low, high)
 
 
@@ -162,7 +168,8 @@
             top = jnp.concatenate([row_max(scores[:, :LANES], low_half), row_max(scores[:, LANES:], low_half)], axis=1)
             e = jnp.exp(scores - top)
             total = mm(e.astype(BF), ones)
-            prob = (e / total).astype(BF)
+            inv = pl.reciprocal(total, approx=True)
+            prob = (e * (inv * (2.0 - total * inv))).astype(BF)
             prob_ref[w, g] = prob
             mixed_s[g, places, :] = mm(prob, spread(v, masks))
         return carry
@@ -226,20 +233,33 @@
     gb1_ref, *outs = refs[:n_out]
     held = refs[n_out : n_out + 4 * count]
     nts = refs[n_out + 4 * count : n_out + 5 * count]
-    g1_ref, g2_ref, in_sems, out_sems = refs[n_out + 5 * count :]
-    order = [4 * b + k for k in (0, 2, 1, 3) for b in range(count)]
-    copies = dict(zip(order, begin(in_sems, *[(inputs[i], held[i]) for i in order])))
+    g1_ref, g2_ref, in_sems, unit_sems, out_sems = refs[n_out + 5 * count :]
     blocks = [held[4 * b : 4 * b + 4] for b in range(count)]
     hidden_size = g1_ref.shape[1]
     features = g1_ref.shape[0]
     step = 384 if hidden_size % 384 == 0 else 128
     wide = features if hidden_size % features == 0 else step
+
+    def units_in(j):
+        cols = ds(j * step, step)
+        return [pltpu.make_async_copy(inputs[4 * b + 2].at[:, cols], held[4 * b + 2].at[:, cols], unit_sems.at[b, j])
+                for b in range(count)]
+
+    order = [4 * b + k for k in (0, 1) for b in range(count)]
+    copies = dict(zip(order, begin(in_sems, *[(inputs[i], held[i]) for i in order])))
+    for j in range(hidden_size // step):
+        for copy in units_in(j):
+            copy.start()
+    last = [pltpu.make_async_copy(inputs[4 * b + 3], held[4 * b + 3], in_sems.at[2 * count + b]) for b in range(count)]
+    for copy in last:
+        copy.start()
     finish_all([copies[4 * b] for b in range(count)])
     for block, nt in zip(blocks, nts):
         nt[...] = block[0][...].T
-    finish_all([copies[4 * b + k] for k in (2, 1) for b in range(count)])
+    finish_all([copies[4 * b + 1] for b in range(count)])
 
     def second(j, carry):
+        finish_all(units_in(j))
         cols = ds(j * step, step)
         g2_ref[cols, :] = sum(mm(hid_ref[:, cols], cot_ref[...], ROWS_ROWS) for _, cot_ref, hid_ref, _ in blocks).astype(BF)
         return carry
@@ -262,7 +282,7 @@
             send(i, g2_ref.at[ds(c * 768 + y * 384 + z * 96, 96), :], target.at[y_rel, z_rel])
     else:
         send(0, g2_ref, outs[1])
-    finish_all([copies[4 * b + 3] for b in range(count)])
+    finish_all(last)
     gb1_ref[...] = sum(jnp.sum(block[3][...].astype(F32), axis=0, keepdims=True) for block in blocks)
     lax.fori_loop(0, hidden_size // wide, first, 0)
     if split:
@@ -293,7 +313,7 @@
     gpos_ref[...] = jnp.zeros(gpos_ref.shape, F32)
     masks = head_masks()
     masks_f = [m.astype(F32) for m in masks]
-    ones = block_ones()
+    low_half = lax.broadcasted_iota(jnp.int32, (SLOT, LANES), 1) < SLOT
     fill(gm_s, mm(branch_ref[...], proj_ref[...], LAST_LAST).astype(BF).astype(F32), windows)
 
     def window(w, carry):
@@ -308,7 +328,7 @@
             prob_f = prob.astype(F32)
             gprob = mm(gm, spread(v, masks), LAST_LAST)
             both = prob_f * gprob
-            delta = mm(both.astype(BF), ones)
+            delta = jnp.concatenate([row_sum(both[:, :LANES], low_half), row_sum(both[:, LANES:], low_half)], axis=1)
             gs = (both - prob_f * delta).astype(BF)
             gpos_ref[g] += gs.astype(F32)
             gq_s[g, places, :] = mm(gs, spread(k, masks)) * SCALING
@@ -558,7 +578,7 @@
     grads = [shape_of(features, hidden, dtype=BF), shape_of(hidden, features, dtype=BF)]
     outs = [shape_of(1, hidden)] + ([shape_of(2, 4, BLOCK, features, dtype=BF)] * 4 if split else grads)
     flat = [a for b in blocks for a in b]
-    scratch = like(*flat) + [pltpu.VMEM((features, rows), BF)] * len(blocks) + like(*grads) + dma(len(flat), 32)
+    scratch = like(*flat) + [pltpu.VMEM((features, rows), BF)] * len(blocks) + like(*grads) + dma(3 * len(blocks), (len(blocks), hidden // 128), 32)
     return call(functools.partial(mlp_weights_kernel, len(blocks), split), outs, scratch, "mlp_weights", SMALL,
                 (me,), *flat, far=range(len(flat)), far_outs=range(1, len(outs)), limit=ALL_VMEM)
 
@@ -697,15 +717,14 @@
     for x_b, valid_b in zip(blocks_of(x), valids):
         if kept:
             x_b = after(x_b, kept[0][4])
-            if fast:
-                core = index & 1
-                half = across(lax.dynamic_slice_in_dim(proj, core * (width // 2), width // 2, 0))
         xs.append(x_b)
         kept.append(attn_forward(windows, x_b, ln1, qkv, bias, pos, valid_b))
     project = lambda mixed, weight: jnp.dot(mixed, weight, preferred_element_type=F32).astype(BF)
     if fast:
-        cots = [cot, across(after(cot, kept[0][4], valids[1], half))]
-        mixed = across(after(kept[1][4], cots[1]))
+        core = index & 1
+        half = across(lax.dynamic_slice_in_dim(after(proj, valids[1]), core * (width // 2), width // 2, 0))
+        cots = [cot, across(after(cot, valids[1]))]
+        mixed = across(after(kept[1][4], cots[1], half))
         half = after(half, kept[1][4])
         rest = flip(half, CORE)
         parts, halves = (project(kept[0][4], proj), mixed), (half, rest)
@@ -761,17 +780,17 @@
         got = flip(after(send, piece2), CORE)
         side = flip(side_send(keep, got), SIDE)
         fc = jnp.concatenate([piece1, piece2, small], axis=0)
-        fc_quad = jnp.stack([fc] + flip_line([fc] * 3))
-        side = after(side, fc_quad, output)
-        line = [after(r, gpatch) for r in flip_line(line_sends(keep, got, side))]
+        fc_quad = jnp.stack([fc] + [after(r, output, gpatch) for r in flip_line([fc] * 3)])
+        side = after(side, fc_quad, output, gpatch)
+        line = flip_line(line_sends(keep, got, side))
         piece = own_piece(keep, got, side, line)
         quad = jnp.stack([piece] + flip_line([piece] * 3))
         fc_pair = after(flip(fc_quad, SIDE), quad)
         g_fc1, g_fc2, small = finish_mlp(me, (fc_quad, fc_pair, after(flip(fc_quad, CORE), quad), after(flip(fc_pair, CORE), quad)))
-        pair = after(flip(quad, SIDE), small)
+        totals = small[0:6] + across(small[0:6])
+        pair = after(flip(quad, SIDE), totals)
         gw, gproj = finish(me, (quad, pair, flip(quad, CORE), flip(pair, CORE)),
                            shape_of(3, features, width), shape_of(width, features))
-        totals = small[0:6] + across(small[0:6])
     else:
         g_fc1, g_fc2, gw, gproj = [g.astype(F32) for g in lax.psum((*g_mlp, *g_attn), "dp")]
         gw, gproj = gw[:, :, :width], gproj[:width]

time: 225 us -> 220 us (0.978)
  waiting for transfers between devices: 65.6 us -> 62.8 us
    ppermute x28, waiting for transfers between devices: 50.5 us -> 40.7 us  [flip(): return lax.ppermute(v, 'dp', [(i, i ^ bits) for i in range(16)])]
    ppermute x11, waiting for transfers between devices: 15.1 us -> 22.2 us  [across(): return lax.ppermute(v, 'mp', [(0, 1), (1, 0)])]
    unnamed x94 -> x98, local copies, waits for them, and re-layouts: 10.9 us -> 11.6 us
  transfers between devices with their start and end apart: 39 -> 39, of which waited for: 17 -> 18; matrix products, arithmetic and copies ran while one was open for 3% -> 4% of each run, Pallas kernels for 35% -> 35%
where the time goes in v3:
time: 220 us
  Pallas kernels  89.9 us (41%)
  waiting for transfers between devices  62.8 us (29%)
  starting transfers between devices  44.8 us (20%)
  local copies, waits for them, and re-layouts  14.5 us (7%)
  other arithmetic  4 us (2%)
  matrix products  2.41 us (1%)
    pallas_call x14, Pallas kernels, call(): pl.pallas_call(kernel, out_shape=outs, in_specs=in_specs, out_specs=[spac...  89.9 us
    ppermute x28, waiting for transfers between devices, flip(): return lax.ppermute(v, 'dp', [(i, i ^ bits) for i in range(16)])  40.7 us
    ppermute x28, starting transfers between devices, flip(): return lax.ppermute(v, 'dp', [(i, i ^ bits) for i in range(16)])  33.2 us
    ppermute x11, waiting for transfers between devices, across(): return lax.ppermute(v, 'mp', [(0, 1), (1, 0)])  22.2 us
    unnamed x98, local copies, waits for them, and re-layouts  11.6 us
    ppermute x11, starting transfers between devices, across(): return lax.ppermute(v, 'mp', [(0, 1), (1, 0)])  11.6 us
  transfers between devices with their start and end apart: 39, of which 18 were waited for; matrix products, arithmetic and copies ran while one was open for 4% of the time, Pallas kernels for 35%

profile of v3, /device:TPU:0, one launch (start us, length us, event | category | flops | bytes accessed | tf_op | source)
XLA Modules:
  0.0 219.9 jit_solution(14384811258192906428)
XLA Ops:
  1.3 2.9 %collective-permute-start.1 = (f32[8,49]{1,0:T(8,128)S(1)}, f32[8,49]{1,0:T(8,128)S(1)}, u32[]{:S(2)}, u32[]{:S(2)}) collective-permute-start(f32[8,49]{1,0:T(8,128)S(1)} %convert_element_type.288.valid_ref), channel_id=1, source_target_pairs={{0,1},{1,0},{2,3},{3,2},{4,5},{5,4},{6,7},{7,6},{8,9},{9,8},{10,11... | collective-permute-start | bytes 4712 | tf_op jit(solution)/shard_map/ppermute | solution.py:634
  4.3 1.6 collective-permute-done.1.valid_ref
  5.9 2.0 collective-permute-start.2
  7.9 1.0 constant_dynamic-slice_fusion
  10.9 12.1 %attn_forward.2 = (bf16[8,3,64,256]{3,2,1,0:T(8,128)(2,1)}, bf16[8,64,384]{2,1,0:T(8,128)(2,1)}, bf16[8,64,384]{2,1,0:T(8,128)(2,1)}, bf16[8,64,384]{2,1,0:T(8,1...) custom-call(bf16[392,768]{1,0:T(8,128)(2,1)} %bitcast.100, f32[768]{0:T(1024)} %gain_ref.9, f32[768]{0:T(1024)} %shift_ref.4, ...), custom_call_target="tpu_custom_call" | custom-call | flops 1000000 | bytes 3906 | tf_op jit(solution)/shard_map/attn_forward/pallas_call | solution.py:515
  23.0 0.8 copy-done.11
  23.8 12.1 %attn_forward.3 = (bf16[8,3,64,256]{3,2,1,0:T(8,128)(2,1)}, bf16[8,64,384]{2,1,0:T(8,128)(2,1)}, bf16[8,64,384]{2,1,0:T(8,128)(2,1)}, bf16[8,64,384]{2,1,0:T(8,1...) custom-call(bf16[392,768]{1,0:T(8,128)(2,1)} %copy-done.11, f32[768]{0:T(1024)} %gain_ref.9, f32[768]{0:T(1024)} %shift_ref.4, ...), custom_call_target="tpu_custom_call" | custom-call | flops 1000000 | bytes 3906 | tf_op jit(solution)/shard_map/attn_forward/pallas_call | solution.py:515
  35.9 2.9 %collective-permute-done.3.refs_0_ = bf16[192,768]{1,0:T(8,128)(2,1)} collective-permute-done((bf16[192,768]{1,0:T(8,128)(2,1)S(1)}, bf16[192,768]{1,0:T(8,128)(2,1)}, u32[]{:S(2)}, u32[]{:S(2)}) %collective-permute-start.3) | collective-permute-done | bytes 294944 | tf_op jit(solution)/shard_map/ppermute | solution.py:634
  38.9 0.8 copy-done.7
  40.1 2.4 %convolution_convert_fusion.own_in = bf16[392,768]{1,0:T(8,128)(2,1)} fusion(bf16[392,384]{1,0:T(8,128)(2,1)} %get-tuple-element.92.refs_1_, bf16[384,768]{1,0:T(8,128)(2,1)S(1)} %copy-done.4), kind=kOutput, calls=%fused_computation | convolution fusion | flops 231512064 | bytes 1492992 | tf_op jit(solution)/shard_map/dot_general | solution.py:722
  42.5 5.1 %collective-permute-done.4.peer_in = bf16[392,384]{1,0:T(8,128)(2,1)S(1)} collective-permute-done((bf16[392,384]{1,0:T(8,128)(2,1)}, bf16[392,384]{1,0:T(8,128)(2,1)S(1)}, u32[]{:S(2)}, u32[]{:S(2)}) %collective-permute-start.4) | collective-permute-done | bytes 301088 | tf_op jit(solution)/shard_map/ppermute | solution.py:634
  47.6 0.7 copy-done.43
  48.3 3.8 %middle.1 = (f32[392,768]{1,0:T(8,128)}, bf16[392,768]{1,0:T(8,128)(2,1)}) custom-call(s32[1]{0:T(128)} %bitcast.me_ref, bf16[392,768]{1,0:T(8,128)(2,1)} %bitcast.101, bf16[392,768]{1,0:T(8,128)(2,1)} %convolution_convert_fusion.own_in, bf16[392,384]{1,0:T(8,128)(2,1)} %copy-done.43, f32[768]{0:T(1024)} %bias_ref.5, f32[768]{0:T(1024)} %gain_ref.8, ...), custom_call_target="tpu_custom_call" | custom-call | flops 1000000 | bytes 3906 | tf_op jit(solution)/shard_map/middle/pallas_call | solution.py:515
  52.2 0.8 collective-permute-start.6
  53.0 1.1 copy-done.9
  54.1 6.1 %mlp.2 = (bf16[392,1536]{1,0:T(8,128)(2,1)S(1)}, bf16[392,1536]{1,0:T(8,128)(2,1)S(1)}, bf16[392,768]{1,0:T(8,128)(2,1)S(1)}, bf16[392,768]{1,0:T(8,128)(2,1)S(1)}) custom-call(bf16[392,768]{1,0:T(8,128)(2,1)S(1)} %copy-done.9, bf16[392,768]{1,0:T(8,128)(2,1)S(1)} %bitcast.106, bf16[768,1536]{1,0:T(8,128)(2,1)S(1)} %copy-done.2, ...), custom_call_target="tpu_custom_call" | custom-call | flops 1000000 | bytes 3906 | tf_op jit(solution)/shard_map/mlp/pallas_call | solution.py:515
  60.2 1.0 copy-done.14
  61.2 0.8 copy-done.24
  62.0 0.8 copy-done.37
  62.9 2.8 %collective-permute-done.6.nm_ref.refs_4_ = bf16[392,768]{1,0:T(8,128)(2,1)S(1)} collective-permute-done((bf16[392,768]{1,0:T(8,128)(2,1)}, bf16[392,768]{1,0:T(8,128)(2,1)S(1)}, u32[]{:S(2)}, u32[]{:S(2)}) %collective-permute-start.6) | collective-permute-done | bytes 602144 | tf_op jit(solution)/shard_map/ppermute | solution.py:634
  65.7 6.9 %mlp.3 = (bf16[392,1536]{1,0:T(8,128)(2,1)S(1)}, bf16[392,1536]{1,0:T(8,128)(2,1)S(1)}, bf16[392,768]{1,0:T(8,128)(2,1)S(1)}, bf16[392,768]{1,0:T(8,128)(2,1)}) custom-call(bf16[392,768]{1,0:T(8,128)(2,1)S(1)} %collective-permute-done.6.nm_ref.refs_4_, bf16[392,768]{1,0:T(8,128)(2,1)S(1)} %copy-done.8, bf16[768,1536]{1,0:T(8,128)(2,1)S(1)} %copy-done.2, ...), custom_call_target="tpu_custom_call" | custom-call | flops 1000000 | bytes 3906 | tf_op jit(solution)/shard_map/mlp/pallas_call | solution.py:515
  72.6 1.0 copy-done.16
  73.6 1.1 copy-done.17
  74.7 1.1 collective-permute-start.8
  75.7 11.7 %mlp_weights.1 = (f32[1,1536]{1,0:T(1,128)}, bf16[2,4,96,768]{3,2,1,0:T(8,128)(2,1)}, bf16[2,4,96,768]{3,2,1,0:T(8,128)(2,1)}, bf16[2,4,96,768]{3,2,1,0:T(8,128)(2,1)}, bf16[2,4,96,768]{3,2,1,0:T(8,128)(2,1)}) custom-call(s32[1]{0:T(128)} %bitcast.me_ref, bf16[392,768]{1,0:T(8,128)(2,1)} %get-tuple-element.100.nm_ref.refs_0_, bf16[392,768]{1,0:T(8,128)(2,1)} %bitcast.105, ...), custom_call_target="tpu_custom_call" | custom-call | flops 1000000 | bytes 3906 | tf_op jit(solution)/shard_map/mlp_weights/pallas_call | solution.py:515
  88.1 0.8 copy-done.39
  88.9 1.1 copy-done.40
  90.0 1.1 middle_back.1
  91.1 1.0 collective-permute-start.11
  92.3 1.6 collective-permute-start.12
  94.6 1.1 collective-permute-start.7
  95.7 9.7 %attn_backward.2 = (bf16[3,392,384]{2,1,0:T(8,128)(2,1)S(1)}, f32[1,768]{1,0:T(1,128)S(1)}, f32[3,64,256]{2,1,0:T(8,128)S(1)}, bf16[392,768]{1,0:T(8,128)(2,1)S(1)}, f32[2,768]{1,0:T(2,128)S(1)}) custom-call(bf16[392,768]{1,0:T(8,128)(2,1)S(1)} %get-tuple-element.139.branch_ref.refs_2_, bf16[392,768]{1,0:T(8,128)(2,1)S(1)} %bitcast.102, ...), custom_call_target="tpu_custom_call" | custom-call | flops 1000000 | bytes 3906 | tf_op jit(solution)/shard_map/attn_backward/pallas_call | solution.py:515
  105.5 3.1 %collective-permute-done.12 = bf16[4,96,768]{2,1,0:T(8,128)(2,1)S(1)} collective-permute-done((bf16[4,96,768]{2,1,0:T(8,128)(2,1)S(1)}, bf16[4,96,768]{2,1,0:T(8,128)(2,1)S(1)}, u32[]{:S(2)}, u32[]{:S(2)}) %collective-permute-start.12) | collective-permute-done | bytes 589856 | tf_op jit(solution)/shard_map/ppermute | solution.py:638
  108.7 3.7 %collective-permute-start.16 = (bf16[96,768]{1,0:T(8,128)(2,1)S(1)}, bf16[96,768]{1,0:T(8,128)(2,1)S(1)}, u32[]{:S(2)}, u32[]{:S(2)}) collective-permute-start(bf16[96,768]{1,0:T(8,128)(2,1)S(1)} %get-tuple-element.181), channel_id=1, source_target_pairs={{0,24},{2,26},{4,28},{6,30},{8,16},{10,18},{12,20},{14,22},{16,8},... | collective-permute-start | bytes 442376 | tf_op jit(solution)/shard_map/ppermute | solution.py:638
  112.4 0.8 collective-permute-start.14
  113.2 9.7 %attn_backward.3 = (bf16[3,392,384]{2,1,0:T(8,128)(2,1)S(1)}, f32[1,768]{1,0:T(1,128)S(1)}, f32[3,64,256]{2,1,0:T(8,128)S(1)}, bf16[392,768]{1,0:T(8,128)(2,1)S(1)}, f32[2,768]{1,0:T(2,128)S(1)}) custom-call(bf16[392,768]{1,0:T(8,128)(2,1)S(1)} %collective-permute-done.11.branch_ref.refs_9_, bf16[392,768]{1,0:T(8,128)(2,1)S(1)} %copy-done.12, ...), custom_call_target="tpu_custom_call" | custom-call | flops 1000000 | bytes 3906 | tf_op jit(solution)/shard_map/attn_backward/pallas_call | solution.py:515
  123.2 3.7 %collective-permute-start.20 = (bf16[96,768]{1,0:T(8,128)(2,1)S(1)}, bf16[96,768]{1,0:T(8,128)(2,1)S(1)}, u32[]{:S(2)}, u32[]{:S(2)}) collective-permute-start(bf16[96,768]{1,0:T(8,128)(2,1)S(1)} %get-tuple-element.178), channel_id=1, source_target_pairs={{0,24},{2,26},{4,28},{6,30},{8,16},{10,18},{12,20},{14,22},{16,8},... | collective-permute-start | bytes 442376 | tf_op jit(solution)/shard_map/ppermute | solution.py:638
  126.9 0.8 collective-permute-start.18
  127.9 5.8 %attn_weights.1 = (bf16[2,4,96,768]{3,2,1,0:T(8,128)(2,1)S(1)}, bf16[2,4,96,768]{3,2,1,0:T(8,128)(2,1)S(1)}, bf16[16,768]{1,0:T(8,128)(2,1)S(1)}) custom-call(s32[1]{0:T(128)} %bitcast.me_ref, f32[4,768]{1,0:T(4,128)S(1)} %get-tuple-element.137.sums2_ref, f32[1,1536]{1,0:T(1,128)S(1)} %copy-done.35, bf16[768,392]{1,0:T(8,128)(2,1)S(1)} %copy-done.20, ...), custom_call_target="tpu_custom_call" | custom-call | flops 1000000 | bytes 3906 | tf_op jit(solution)/shard_map/attn_weights/pallas_call | solution.py:515
  133.6 2.7 %collective-permute-done.19 = bf16[96,768]{1,0:T(8,128)(2,1)S(1)} collective-permute-done((bf16[96,768]{1,0:T(8,128)(2,1)S(1)}, bf16[96,768]{1,0:T(8,128)(2,1)S(1)}, u32[]{:S(2)}, u32[]{:S(2)}) %collective-permute-start.19) | collective-permute-done | bytes 147488 | tf_op jit(solution)/shard_map/ppermute | solution.py:638
  136.6 0.7 collective-permute-start.13
  137.5 2.9 %collective-permute-start.21 = (bf16[208,768]{1,0:T(8,128)(2,1)S(1)}, bf16[208,768]{1,0:T(8,128)(2,1)S(1)}, u32[]{:S(2)}, u32[]{:S(2)}) collective-permute-start(bf16[208,768]{1,0:T(8,128)(2,1)S(1)} %get-tuple-element.185), channel_id=1, source_target_pairs={{0,8},{2,10},{4,12},{6,14},{8,0},{10,2},{12,4},{14,6},{16,24},{18,... | collective-permute-start | bytes 958472 | tf_op jit(solution)/shard_map/ppermute | solution.py:638
  140.4 1.4 collective-permute-start.23
  142.0 1.6 collective-permute-start.26
  143.6 1.1 add_convert_fusion
  144.7 7.9 %collective-permute-done.13.peer_ref = bf16[392,768]{1,0:T(8,128)(2,1)S(1)} collective-permute-done((bf16[392,768]{1,0:T(8,128)(2,1)S(1)}, bf16[392,768]{1,0:T(8,128)(2,1)S(1)}, u32[]{:S(2)}, u32[]{:S(2)}) %collective-permute-start.13) | collective-permute-done | bytes 602144 | tf_op jit(solution)/shard_map/ppermute | solution.py:634
  152.6 1.7 input_back.1
  154.3 7.3 %collective-permute-done.23 = bf16[208,768]{1,0:T(8,128)(2,1)S(1)} collective-permute-done((bf16[208,768]{1,0:T(8,128)(2,1)S(1)}, bf16[208,768]{1,0:T(8,128)(2,1)S(1)}, u32[]{:S(2)}, u32[]{:S(2)}) %collective-permute-start.23) | collective-permute-done | bytes 319520 | tf_op jit(solution)/shard_map/ppermute | solution.py:638
  161.8 1.6 collective-permute-start.24
  163.6 7.2 %collective-permute-start.27 = (bf16[96,768]{1,0:T(8,128)(2,1)S(1)}, bf16[96,768]{1,0:T(8,128)(2,1)S(1)}, u32[]{:S(2)}, u32[]{:S(2)}) collective-permute-start(bf16[96,768]{1,0:T(8,128)(2,1)S(1)} %get-tuple-element.175), channel_id=1, source_target_pairs={{0,8},{2,10},{4,12},{6,14},{8,0},{10,2},{12,4},{14,6},{16,24},{18,... | collective-permute-start | bytes 442376 | tf_op jit(solution)/shard_map/ppermute | solution.py:638
  170.8 1.4 collective-permute-start.29
  172.4 2.7 %collective-permute-done.27 = bf16[96,768]{1,0:T(8,128)(2,1)S(1)} collective-permute-done((bf16[96,768]{1,0:T(8,128)(2,1)S(1)}, bf16[96,768]{1,0:T(8,128)(2,1)S(1)}, u32[]{:S(2)}, u32[]{:S(2)}) %collective-permute-start.27) | collective-permute-done | bytes 147488 | tf_op jit(solution)/shard_map/ppermute | solution.py:638
  175.1 4.9 %collective-permute-done.29 = bf16[96,768]{1,0:T(8,128)(2,1)S(1)} collective-permute-done((bf16[96,768]{1,0:T(8,128)(2,1)S(1)}, bf16[96,768]{1,0:T(8,128)(2,1)S(1)}, u32[]{:S(2)}, u32[]{:S(2)}) %collective-permute-start.29) | collective-permute-done | bytes 147488 | tf_op jit(solution)/shard_map/ppermute | solution.py:638
  180.0 5.3 %collective-permute-done.28 = bf16[96,768]{1,0:T(8,128)(2,1)S(1)} collective-permute-done((bf16[96,768]{1,0:T(8,128)(2,1)S(1)}, bf16[96,768]{1,0:T(8,128)(2,1)S(1)}, u32[]{:S(2)}, u32[]{:S(2)}) %collective-permute-start.28) | collective-permute-done | bytes 147488 | tf_op jit(solution)/shard_map/ppermute | solution.py:638
  185.5 1.5 collective-permute-start.32
  187.0 2.9 %collective-permute-start.30 = (bf16[96,768]{1,0:T(8,128)(2,1)S(1)}, bf16[96,768]{1,0:T(8,128)(2,1)S(1)}, u32[]{:S(2)}, u32[]{:S(2)}) collective-permute-start(bf16[96,768]{1,0:T(8,128)(2,1)S(1)} %fusion.9), channel_id=1, source_target_pairs={{0,8},{2,10},{4,12},{6,14},{8,0},{10,2},{12,4},{14,6},{16,24},{18,... | collective-permute-start | bytes 442376 | tf_op jit(solution)/shard_map/ppermute | solution.py:638
  189.9 4.3 %collective-permute-done.32 = bf16[96,768]{1,0:T(8,128)(2,1)S(1)} collective-permute-done((bf16[96,768]{1,0:T(8,128)(2,1)S(1)}, bf16[96,768]{1,0:T(8,128)(2,1)S(1)}, u32[]{:S(2)}, u32[]{:S(2)}) %collective-permute-start.32) | collective-permute-done | bytes 147488 | tf_op jit(solution)/shard_map/ppermute | solution.py:638
  194.2 4.3 %collective-permute-done.31 = bf16[96,768]{1,0:T(8,128)(2,1)S(1)} collective-permute-done((bf16[96,768]{1,0:T(8,128)(2,1)S(1)}, bf16[96,768]{1,0:T(8,128)(2,1)S(1)}, u32[]{:S(2)}, u32[]{:S(2)}) %collective-permute-start.31) | collective-permute-done | bytes 147488 | tf_op jit(solution)/shard_map/ppermute | solution.py:638
  199.3 2.4 %collective-permute-done.34.refs_3_ = bf16[4,208,768]{2,1,0:T(8,128)(2,1)S(1)} collective-permute-done((bf16[4,208,768]{2,1,0:T(8,128)(2,1)S(1)}, bf16[4,208,768]{2,1,0:T(8,128)(2,1)S(1)}, u32[]{:S(2)}, u32[]{:S(2)}) %collective-permute-start.34) | collective-permute-done | bytes 1277984 | tf_op jit(solution)/shard_map/ppermute | solution.py:638
  201.7 5.4 %finish_mlp.1 = (f32[768,1536]{1,0:T(8,128)}, f32[1536,768]{1,0:T(8,128)}, f32[16,768]{1,0:T(8,128)S(1)}) custom-call(s32[1]{0:T(128)} %bitcast.me_ref, bf16[4,208,768]{2,1,0:T(8,128)(2,1)S(1)} %pad_maximum_fusion.refs_0_, bf16[4,208,768]{2,1,0:T(8,128)(2,1)S(1)} %collective-permute-done.24.refs_1_, ...), custom_call_target="tpu_custom_call" | custom-call | flops 1000000 | bytes 3906 | tf_op jit(solution)/shard_map/finish_mlp/pallas_call | solution.py:515
  207.1 1.4 collective-permute-start.35
  209.1 1.8 collective-permute-done.35
  211.0 3.5 %collective-permute-done.36.refs_1_ = bf16[4,96,768]{2,1,0:T(8,128)(2,1)S(1)} collective-permute-done((bf16[4,96,768]{2,1,0:T(8,128)(2,1)S(1)}, bf16[4,96,768]{2,1,0:T(8,128)(2,1)S(1)}, u32[]{:S(2)}, u32[]{:S(2)}) %collective-permute-start.36) | collective-permute-done | bytes 589856 | tf_op jit(solution)/shard_map/ppermute | solution.py:638
  216.4 3.2 %finish.1 = (f32[3,768,384]{2,1,0:T(8,128)}, f32[384,768]{1,0:T(8,128)}) custom-call(s32[1]{0:T(128)} %bitcast.me_ref, bf16[4,96,768]{2,1,0:T(8,128)(2,1)S(1)} %pad_maximum_fusion.1.refs_0_, bf16[4,96,768]{2,1,0:T(8,128)(2,1)S(1)} %collective-permute-done.36.refs_1_, bf16[4,96,768]{2,1,0:T(8,128)(2,1)S(1)} %collective-permute-done.37.refs_2_, ...), custom_call_target="tpu_custom_call" | custom-call | flops 1000000 | bytes 3906 | tf_op jit(solution)/shard_map/finish/pallas_call | solution.py:515
  (153 shorter events, 9.7 us)
Async XLA Ops:
  1.3 9.6 %copy-start.45 = (f32[8,49]{1,0:T(8,128)}, f32[8,49]{1,0:T(8,128)S(1)}, u32[]{:S(2)}) copy-start(f32[8,49]{1,0:T(8,128)S(1)} %convert_element_type.288.valid_ref) | copy-start | bytes 4708
  1.3 4.5 %collective-permute-start.1 = (f32[8,49]{1,0:T(8,128)S(1)}, f32[8,49]{1,0:T(8,128)S(1)}, u32[]{:S(2)}, u32[]{:S(2)}) collective-permute-start(f32[8,49]{1,0:T(8,128)S(1)} %convert_element_type.288.valid_ref), channel_id=1, source_target_pairs={{0,1},{1,0},{2,3},{3,2},{4,5},{5,4},{6,7},{7,6},{8,9},{9,8},{10,11... | collective-permute-start | bytes 4712 | tf_op jit(solution)/shard_map/ppermute | solution.py:634
  4.3 18.7 %collective-permute-start = (bf16[392,768]{1,0:T(8,128)(2,1)}, bf16[392,768]{1,0:T(8,128)(2,1)S(1)}, u32[]{:S(2)}, u32[]{:S(2)}) collective-permute-start(bf16[392,768]{1,0:T(8,128)(2,1)} %bitcast.99), channel_id=1, source_target_pairs={{0,1},{1,0},{2,3},{3,2},{4,5},{5,4},{6,7},{7,6},{8,9},{9,8},{10,11... | collective-permute-start | bytes 1806344 | tf_op jit(solution)/shard_map/ppermute | solution.py:634
  5.9 17.1 %copy-start.48 = (f32[8,49]{1,0:T(8,128)}, f32[8,49]{1,0:T(8,128)S(1)}, u32[]{:S(2)}) copy-start(f32[8,49]{1,0:T(8,128)S(1)} %collective-permute-done.1.valid_ref) | copy-start | bytes 4708
  5.9 33.0 %collective-permute-start.2 = (bf16[392,768]{1,0:T(8,128)(2,1)}, bf16[392,768]{1,0:T(8,128)(2,1)S(1)}, u32[]{:S(2)}, u32[]{:S(2)}) collective-permute-start(bf16[392,768]{1,0:T(8,128)(2,1)} %bitcast.104), channel_id=1, source_target_pairs={{0,1},{1,0},{2,3},{3,2},{4,5},{5,4},{6,7},{7,6},{8,9},{9,8},{10,11... | collective-permute-start | bytes 1806344 | tf_op jit(solution)/shard_map/ppermute | solution.py:634
  8.9 30.0 %collective-permute-start.3 = (bf16[192,768]{1,0:T(8,128)(2,1)S(1)}, bf16[192,768]{1,0:T(8,128)(2,1)}, u32[]{:S(2)}, u32[]{:S(2)}) collective-permute-start(bf16[192,768]{1,0:T(8,128)(2,1)S(1)} %constant_dynamic-slice_fusion), channel_id=1, source_target_pairs={{0,1},{1,0},{2,3},{3,2},{4,5},{5,4},{6,7},{7,6},{8,9},{9,8},{10,11... | collective-permute-start | bytes 884744 | tf_op jit(solution)/shard_map/ppermute | solution.py:634
  10.9 29.2 %copy-start.4 = (bf16[384,768]{1,0:T(8,128)(2,1)S(1)}, bf16[384,768]{1,0:T(8,128)(2,1)}, u32[]{:S(2)}) copy-start(bf16[384,768]{1,0:T(8,128)(2,1)} %proj_ref.3) | copy-start | bytes 1769476
  23.8 29.1 %copy-start.3 = (bf16[1536,768]{1,0:T(8,128)(2,1)S(1)}, bf16[1536,768]{1,0:T(8,128)(2,1)}, u32[]{:S(2)}) copy-start(bf16[1536,768]{1,0:T(8,128)(2,1)} %fc2_ref.3) | copy-start | bytes 7077892
  39.7 7.9 %collective-permute-start.4 = (bf16[392,384]{1,0:T(8,128)(2,1)}, bf16[392,384]{1,0:T(8,128)(2,1)S(1)}, u32[]{:S(2)}, u32[]{:S(2)}) collective-permute-start(bf16[392,384]{1,0:T(8,128)(2,1)} %get-tuple-element.97.refs_8_), channel_id=1, source_target_pairs={{0,1},{1,0},{2,3},{3,2},{4,5},{5,4},{6,7},{7,6},{8,9},{9,8},{10,11... | collective-permute-start | bytes 903176 | tf_op jit(solution)/shard_map/ppermute | solution.py:634
  40.1 2.4 %collective-permute-start.5 = (bf16[192,768]{1,0:T(8,128)(2,1)}, bf16[192,768]{1,0:T(8,128)(2,1)S(1)}, u32[]{:S(2)}, u32[]{:S(2)}) collective-permute-start(bf16[192,768]{1,0:T(8,128)(2,1)} %collective-permute-done.3.refs_0_), channel_id=1, source_target_pairs={{0,2},{2,0},{4,6},{6,4},{8,10},{10,8},{12,14},{14,12},{16,18},{18,... | collective-permute-start | bytes 884744 | tf_op jit(solution)/shard_map/ppermute | solution.py:638
  40.1 12.9 %copy-start.2 = (bf16[768,1536]{1,0:T(8,128)(2,1)S(1)}, bf16[768,1536]{1,0:T(8,128)(2,1)}, u32[]{:S(2)}) copy-start(bf16[768,1536]{1,0:T(8,128)(2,1)} %fc1_ref.3) | copy-start | bytes 7077892
  42.5 10.5 %copy-start.46 = (f32[1536]{0:T(1024)S(1)}, f32[1536]{0:T(1024)}, u32[]{:S(2)}) copy-start(f32[1536]{0:T(1024)} %param.28) | copy-start | bytes 18436
  42.5 10.5 %copy-start.5 = (bf16[8,49,768]{2,0,1:T(8,128)(2,1)S(1)}, bf16[8,49,768]{2,0,1:T(8,128)(2,1)}, u32[]{:S(2)}) copy-start(bf16[8,49,768]{2,0,1:T(8,128)(2,1)} %param.31) | copy-start | bytes 1806340
  42.5 5.1 %copy-start.44 = (bf16[192,768]{1,0:T(8,128)(2,1)}, bf16[192,768]{1,0:T(8,128)(2,1)S(1)}, u32[]{:S(2)}) copy-start(bf16[192,768]{1,0:T(8,128)(2,1)S(1)} %collective-permute-done.5.refs_1_) | copy-start | bytes 884740
  52.2 13.5 %collective-permute-start.6 = (bf16[392,768]{1,0:T(8,128)(2,1)}, bf16[392,768]{1,0:T(8,128)(2,1)S(1)}, u32[]{:S(2)}, u32[]{:S(2)}) collective-permute-start(bf16[392,768]{1,0:T(8,128)(2,1)} %get-tuple-element.100.nm_ref.refs_0_), channel_id=1, source_target_pairs={{0,1},{1,0},{2,3},{3,2},{4,5},{5,4},{6,7},{7,6},{8,9},{9,8},{10,11... | collective-permute-start | bytes 1806344 | tf_op jit(solution)/shard_map/ppermute | solution.py:634
  54.1 11.6 %copy-start.8 = (bf16[392,768]{1,0:T(8,128)(2,1)S(1)}, bf16[392,768]{1,0:T(8,128)(2,1)}, u32[]{:S(2)}) copy-start(bf16[392,768]{1,0:T(8,128)(2,1)} %copy-done.7) | copy-start | bytes 1806340
  62.9 9.7 %copy-start.15 = (bf16[392,1536]{1,0:T(8,128)(2,1)}, bf16[392,1536]{1,0:T(8,128)(2,1)S(1)}, u32[]{:S(2)}) copy-start(bf16[392,1536]{1,0:T(8,128)(2,1)S(1)} %get-tuple-element.107.refs_3_) | copy-start | bytes 3612676
  65.7 6.9 %copy-start.10 = (bf16[392,768]{1,0:T(8,128)(2,1)}, bf16[392,768]{1,0:T(8,128)(2,1)S(1)}, u32[]{:S(2)}) copy-start(bf16[392,768]{1,0:T(8,128)(2,1)S(1)} %collective-permute-done.6.nm_ref.refs_4_) | copy-start | bytes 1806340
  74.7 13.4 %collective-permute-start.8 = (bf16[392,768]{1,0:T(8,128)(2,1)}, bf16[392,768]{1,0:T(8,128)(2,1)S(1)}, u32[]{:S(2)}, u32[]{:S(2)}) collective-permute-start(bf16[392,768]{1,0:T(8,128)(2,1)} %get-tuple-element.105), channel_id=1, source_target_pairs={{0,1},{1,0},{2,3},{3,2},{4,5},{5,4},{6,7},{7,6},{8,9},{9,8},{10,11... | collective-permute-start | bytes 1806344 | tf_op jit(solution)/shard_map/ppermute | solution.py:634
  75.7 13.1 %copy-start.6 = (bf16[8,49,768]{2,0,1:T(8,128)(2,1)S(1)}, bf16[8,49,768]{2,0,1:T(8,128)(2,1)}, u32[]{:S(2)}) copy-start(bf16[8,49,768]{2,0,1:T(8,128)(2,1)} %param.31) | copy-start | bytes 1806340
  75.7 13.1 %copy-start.19 = (f32[392,768]{1,0:T(8,128)S(1)}, f32[392,768]{1,0:T(8,128)}, u32[]{:S(2)}) copy-start(f32[392,768]{1,0:T(8,128)} %get-tuple-element.99.middle_ref) | copy-start | bytes 3612676
  75.7 13.1 %copy-start.36 = (f32[768]{0:T(1024)S(1)}, f32[768]{0:T(1024)}, u32[]{:S(2)}) copy-start(f32[768]{0:T(1024)} %gain_ref.8) | copy-start | bytes 9220
  75.7 13.1 %copy-start.38 = (bf16[392,768]{1,0:T(8,128)(2,1)S(1)}, bf16[392,768]{1,0:T(8,128)(2,1)}, u32[]{:S(2)}) copy-start(bf16[392,768]{1,0:T(8,128)(2,1)} %copy-done.37) | copy-start | bytes 1806340
  87.5 4.6 %collective-permute-start.9 = (bf16[2,4,96,768]{3,2,1,0:T(8,128)(2,1)}, bf16[2,4,96,768]{3,2,1,0:T(8,128)(2,1)S(1)}, u32[]{:S(2)}, u32[]{:S(2)}) collective-permute-start(bf16[2,4,96,768]{3,2,1,0:T(8,128)(2,1)} %get-tuple-element.114), channel_id=1, source_target_pairs={{0,2},{2,0},{4,6},{6,4},{8,10},{10,8},{12,14},{14,12},{16,18},{18,... | collective-permute-start | bytes 3538952 | tf_op jit(solution)/shard_map/ppermute | solution.py:638
  87.5 6.3 %collective-permute-start.10 = (bf16[2,4,96,768]{3,2,1,0:T(8,128)(2,1)}, bf16[2,4,96,768]{3,2,1,0:T(8,128)(2,1)S(1)}, u32[]{:S(2)}, u32[]{:S(2)}) collective-permute-start(bf16[2,4,96,768]{3,2,1,0:T(8,128)(2,1)} %get-tuple-element.117), channel_id=1, source_target_pairs={{0,2},{2,0},{4,6},{6,4},{8,10},{10,8},{12,14},{14,12},{16,18},{18,... | collective-permute-start | bytes 3538952 | tf_op jit(solution)/shard_map/ppermute | solution.py:638
  90.0 5.7 %copy-start.30 = (bf16[8,64,384]{2,1,0:T(8,128)(2,1)S(1)}, bf16[8,64,384]{2,1,0:T(8,128)(2,1)}, u32[]{:S(2)}) copy-start(bf16[8,64,384]{2,1,0:T(8,128)(2,1)} %get-tuple-element.122.k_ref) | copy-start | bytes 1179652
  90.0 5.7 %copy-start.31 = (bf16[8,64,384]{2,1,0:T(8,128)(2,1)S(1)}, bf16[8,64,384]{2,1,0:T(8,128)(2,1)}, u32[]{:S(2)}) copy-start(bf16[8,64,384]{2,1,0:T(8,128)(2,1)} %get-tuple-element.123.v_ref) | copy-start | bytes 1179652
  91.1 21.3 %collective-permute-start.11 = (bf16[392,768]{1,0:T(8,128)(2,1)S(1)}, bf16[392,768]{1,0:T(8,128)(2,1)S(1)}, u32[]{:S(2)}, u32[]{:S(2)}) collective-permute-start(bf16[392,768]{1,0:T(8,128)(2,1)S(1)} %get-tuple-element.139.branch_ref.refs_2_), channel_id=1, source_target_pairs={{0,1},{1,0},{2,3},{3,2},{4,5},{5,4},{6,7},{7,6},{8,9},{9,8},{10,11... | collective-permute-start | bytes 1806344 | tf_op jit(solution)/shard_map/ppermute | solution.py:634
  92.3 16.3 %collective-permute-start.12 = (bf16[4,96,768]{2,1,0:T(8,128)(2,1)S(1)}, bf16[4,96,768]{2,1,0:T(8,128)(2,1)S(1)}, u32[]{:S(2)}, u32[]{:S(2)}) collective-permute-start(bf16[4,96,768]{2,1,0:T(8,128)(2,1)S(1)} %fusion), channel_id=1, source_target_pairs={{0,4},{2,6},{4,0},{6,2},{8,12},{10,14},{12,8},{14,10},{16,20},{18,... | collective-permute-start | bytes 1769480 | tf_op jit(solution)/shard_map/ppermute | solution.py:638
  94.0 28.9 %collective-permute-start.17 = (bf16[4,96,768]{2,1,0:T(8,128)(2,1)S(1)}, bf16[4,96,768]{2,1,0:T(8,128)(2,1)S(1)}, u32[]{:S(2)}, u32[]{:S(2)}) collective-permute-start(bf16[4,96,768]{2,1,0:T(8,128)(2,1)S(1)} %fusion.1), channel_id=1, source_target_pairs={{0,4},{2,6},{4,0},{6,2},{8,12},{10,14},{12,8},{14,10},{16,20},{18,... | collective-permute-start | bytes 1769480 | tf_op jit(solution)/shard_map/ppermute | solution.py:638
  94.6 33.2 %collective-permute-start.7 = (bf16[392,768]{1,0:T(8,128)(2,1)S(1)}, bf16[392,768]{1,0:T(8,128)(2,1)S(1)}, u32[]{:S(2)}, u32[]{:S(2)}) collective-permute-start(bf16[392,768]{1,0:T(8,128)(2,1)S(1)} %get-tuple-element.104), channel_id=1, source_target_pairs={{0,1},{1,0},{2,3},{3,2},{4,5},{5,4},{6,7},{7,6},{8,9},{9,8},{10,11... | collective-permute-start | bytes 1806344 | tf_op jit(solution)/shard_map/ppermute | solution.py:634
  95.7 17.5 %copy-start.27 = (bf16[8,64,384]{2,1,0:T(8,128)(2,1)S(1)}, bf16[8,64,384]{2,1,0:T(8,128)(2,1)}, u32[]{:S(2)}) copy-start(bf16[8,64,384]{2,1,0:T(8,128)(2,1)} %get-tuple-element.129.k_ref) | copy-start | bytes 1179652
  95.7 17.5 %copy-start.28 = (bf16[8,64,384]{2,1,0:T(8,128)(2,1)S(1)}, bf16[8,64,384]{2,1,0:T(8,128)(2,1)}, u32[]{:S(2)}) copy-start(bf16[8,64,384]{2,1,0:T(8,128)(2,1)} %get-tuple-element.130.v_ref) | copy-start | bytes 1179652
  105.5 7.7 %copy-start.12 = (bf16[392,768]{1,0:T(8,128)(2,1)S(1)}, bf16[392,768]{1,0:T(8,128)(2,1)}, u32[]{:S(2)}) copy-start(bf16[392,768]{1,0:T(8,128)(2,1)} %copy-done.11) | copy-start | bytes 1806340
  105.5 7.7 %copy-start.22 = (bf16[8,3,64,256]{3,2,1,0:T(8,128)(2,1)S(1)}, bf16[8,3,64,256]{3,2,1,0:T(8,128)(2,1)}, u32[]{:S(2)}) copy-start(bf16[8,3,64,256]{3,2,1,0:T(8,128)(2,1)} %get-tuple-element.127.prob_ref) | copy-start | bytes 2359300
  105.5 7.7 %copy-start.26 = (bf16[8,64,384]{2,1,0:T(8,128)(2,1)S(1)}, bf16[8,64,384]{2,1,0:T(8,128)(2,1)}, u32[]{:S(2)}) copy-start(bf16[8,64,384]{2,1,0:T(8,128)(2,1)} %get-tuple-element.128.q_ref) | copy-start | bytes 1179652
  108.7 18.1 %collective-permute-start.16 = (bf16[96,768]{1,0:T(8,128)(2,1)S(1)}, bf16[96,768]{1,0:T(8,128)(2,1)S(1)}, u32[]{:S(2)}, u32[]{:S(2)}) collective-permute-start(bf16[96,768]{1,0:T(8,128)(2,1)S(1)} %get-tuple-element.181), channel_id=1, source_target_pairs={{0,24},{2,26},{4,28},{6,30},{8,16},{10,18},{12,20},{14,22},{16,8},... | collective-permute-start | bytes 442376 | tf_op jit(solution)/shard_map/ppermute | solution.py:638
  112.4 14.5 %collective-permute-start.15 = (bf16[96,768]{1,0:T(8,128)(2,1)S(1)}, bf16[96,768]{1,0:T(8,128)(2,1)S(1)}, u32[]{:S(2)}, u32[]{:S(2)}) collective-permute-start(bf16[96,768]{1,0:T(8,128)(2,1)S(1)} %get-tuple-element.182), channel_id=1, source_target_pairs={{0,16},{2,18},{4,20},{6,22},{8,24},{10,26},{12,28},{14,30},{16,0},... | collective-permute-start | bytes 442376 | tf_op jit(solution)/shard_map/ppermute | solution.py:638
  112.4 15.3 %collective-permute-start.14 = (bf16[96,768]{1,0:T(8,128)(2,1)S(1)}, bf16[96,768]{1,0:T(8,128)(2,1)S(1)}, u32[]{:S(2)}, u32[]{:S(2)}) collective-permute-start(bf16[96,768]{1,0:T(8,128)(2,1)S(1)} %get-tuple-element.183), channel_id=1, source_target_pairs={{0,8},{2,10},{4,12},{6,14},{8,0},{10,2},{12,4},{14,6},{16,24},{18,... | collective-permute-start | bytes 442376 | tf_op jit(solution)/shard_map/ppermute | solution.py:638
  123.2 10.4 %collective-permute-start.20 = (bf16[96,768]{1,0:T(8,128)(2,1)S(1)}, bf16[96,768]{1,0:T(8,128)(2,1)S(1)}, u32[]{:S(2)}, u32[]{:S(2)}) collective-permute-start(bf16[96,768]{1,0:T(8,128)(2,1)S(1)} %get-tuple-element.178), channel_id=1, source_target_pairs={{0,24},{2,26},{4,28},{6,30},{8,16},{10,18},{12,20},{14,22},{16,8},... | collective-permute-start | bytes 442376 | tf_op jit(solution)/shard_map/ppermute | solution.py:638
  126.9 9.5 %collective-permute-start.19 = (bf16[96,768]{1,0:T(8,128)(2,1)S(1)}, bf16[96,768]{1,0:T(8,128)(2,1)S(1)}, u32[]{:S(2)}, u32[]{:S(2)}) collective-permute-start(bf16[96,768]{1,0:T(8,128)(2,1)S(1)} %get-tuple-element.179), channel_id=1, source_target_pairs={{0,16},{2,18},{4,20},{6,22},{8,24},{10,26},{12,28},{14,30},{16,0},... | collective-permute-start | bytes 442376 | tf_op jit(solution)/shard_map/ppermute | solution.py:638
  126.9 9.5 %collective-permute-start.18 = (bf16[96,768]{1,0:T(8,128)(2,1)S(1)}, bf16[96,768]{1,0:T(8,128)(2,1)S(1)}, u32[]{:S(2)}, u32[]{:S(2)}) collective-permute-start(bf16[96,768]{1,0:T(8,128)(2,1)S(1)} %get-tuple-element.180), channel_id=1, source_target_pairs={{0,8},{2,10},{4,12},{6,14},{8,0},{10,2},{12,4},{14,6},{16,24},{18,... | collective-permute-start | bytes 442376 | tf_op jit(solution)/shard_map/ppermute | solution.py:638
  136.5 7.1 %copy-start.25 = (bf16[392,768]{1,0:T(8,128)(2,1)S(1)}, bf16[392,768]{1,0:T(8,128)(2,1)}, u32[]{:S(2)}) copy-start(bf16[392,768]{1,0:T(8,128)(2,1)} %copy-done.24) | copy-start | bytes 1806340
  136.5 7.1 %copy-start.47 = (f32[768]{0:T(1024)S(1)}, f32[768]{0:T(1024)}, u32[]{:S(2)}) copy-start(f32[768]{0:T(1024)} %param.30) | copy-start | bytes 9220
  136.5 5.3 %collective-permute-start.25 = (bf16[2,4,96,768]{3,2,1,0:T(8,128)(2,1)S(1)}, bf16[2,4,96,768]{3,2,1,0:T(8,128)(2,1)S(1)}, u32[]{:S(2)}, u32[]{:S(2)}) collective-permute-start(bf16[2,4,96,768]{3,2,1,0:T(8,128)(2,1)S(1)} %get-tuple-element.158), channel_id=1, source_target_pairs={{0,2},{2,0},{4,6},{6,4},{8,10},{10,8},{12,14},{14,12},{16,18},{18,... | collective-permute-start | bytes 3538952 | tf_op jit(solution)/shard_map/ppermute | solution.py:638
  136.6 16.0 %collective-permute-start.13 = (bf16[392,768]{1,0:T(8,128)(2,1)S(1)}, bf16[392,768]{1,0:T(8,128)(2,1)S(1)}, u32[]{:S(2)}, u32[]{:S(2)}) collective-permute-start(bf16[392,768]{1,0:T(8,128)(2,1)S(1)} %get-tuple-element.131), channel_id=1, source_target_pairs={{0,1},{1,0},{2,3},{3,2},{4,5},{5,4},{6,7},{7,6},{8,9},{9,8},{10,11... | collective-permute-start | bytes 1806344 | tf_op jit(solution)/shard_map/ppermute | solution.py:634
  137.4 24.2 %collective-permute-start.22 = (bf16[208,768]{1,0:T(8,128)(2,1)S(1)}, bf16[208,768]{1,0:T(8,128)(2,1)S(1)}, u32[]{:S(2)}, u32[]{:S(2)}) collective-permute-start(bf16[208,768]{1,0:T(8,128)(2,1)S(1)} %get-tuple-element.185), channel_id=1, source_target_pairs={{0,16},{2,18},{4,20},{6,22},{8,24},{10,26},{12,28},{14,30},{16,0},... | collective-permute-start | bytes 958472 | tf_op jit(solution)/shard_map/ppermute | solution.py:638
  137.5 24.2 %collective-permute-start.21 = (bf16[208,768]{1,0:T(8,128)(2,1)S(1)}, bf16[208,768]{1,0:T(8,128)(2,1)S(1)}, u32[]{:S(2)}, u32[]{:S(2)}) collective-permute-start(bf16[208,768]{1,0:T(8,128)(2,1)S(1)} %get-tuple-element.185), channel_id=1, source_target_pairs={{0,8},{2,10},{4,12},{6,14},{8,0},{10,2},{12,4},{14,6},{16,24},{18,... | collective-permute-start | bytes 958472 | tf_op jit(solution)/shard_map/ppermute | solution.py:638
  140.4 21.2 %collective-permute-start.23 = (bf16[208,768]{1,0:T(8,128)(2,1)S(1)}, bf16[208,768]{1,0:T(8,128)(2,1)S(1)}, u32[]{:S(2)}, u32[]{:S(2)}) collective-permute-start(bf16[208,768]{1,0:T(8,128)(2,1)S(1)} %get-tuple-element.185), channel_id=1, source_target_pairs={{0,24},{2,26},{4,28},{6,30},{8,16},{10,18},{12,20},{14,22},{16,8},... | collective-permute-start | bytes 958472 | tf_op jit(solution)/shard_map/ppermute | solution.py:638
  142.0 21.4 %collective-permute-start.26 = (bf16[4,96,768]{2,1,0:T(8,128)(2,1)S(1)}, bf16[4,96,768]{2,1,0:T(8,128)(2,1)S(1)}, u32[]{:S(2)}, u32[]{:S(2)}) collective-permute-start(bf16[4,96,768]{2,1,0:T(8,128)(2,1)S(1)} %fusion.2), channel_id=1, source_target_pairs={{0,4},{2,6},{4,0},{6,2},{8,12},{10,14},{12,8},{14,10},{16,20},{18,... | collective-permute-start | bytes 1769480 | tf_op jit(solution)/shard_map/ppermute | solution.py:638
  143.6 9.0 %copy-start.33 = (f32[768]{0:T(1024)S(1)}, f32[768]{0:T(1024)}, u32[]{:S(2)}) copy-start(f32[768]{0:T(1024)} %gain_ref.9) | copy-start | bytes 9220
  161.8 36.8 %collective-permute-start.24 = (bf16[4,208,768]{2,1,0:T(8,128)(2,1)S(1)}, bf16[4,208,768]{2,1,0:T(8,128)(2,1)S(1)}, u32[]{:S(2)}, u32[]{:S(2)}) collective-permute-start(bf16[4,208,768]{2,1,0:T(8,128)(2,1)S(1)} %pad_maximum_fusion.refs_0_), channel_id=1, source_target_pairs={{0,4},{2,6},{4,0},{6,2},{8,12},{10,14},{12,8},{14,10},{16,20},{18,... | collective-permute-start | bytes 3833864 | tf_op jit(solution)/shard_map/ppermute | solution.py:638
  163.6 11.5 %collective-permute-start.27 = (bf16[96,768]{1,0:T(8,128)(2,1)S(1)}, bf16[96,768]{1,0:T(8,128)(2,1)S(1)}, u32[]{:S(2)}, u32[]{:S(2)}) collective-permute-start(bf16[96,768]{1,0:T(8,128)(2,1)S(1)} %get-tuple-element.175), channel_id=1, source_target_pairs={{0,8},{2,10},{4,12},{6,14},{8,0},{10,2},{12,4},{14,6},{16,24},{18,... | collective-permute-start | bytes 442376 | tf_op jit(solution)/shard_map/ppermute | solution.py:638
  170.8 9.2 %collective-permute-start.29 = (bf16[96,768]{1,0:T(8,128)(2,1)S(1)}, bf16[96,768]{1,0:T(8,128)(2,1)S(1)}, u32[]{:S(2)}, u32[]{:S(2)}) collective-permute-start(bf16[96,768]{1,0:T(8,128)(2,1)S(1)} %get-tuple-element.176), channel_id=1, source_target_pairs={{0,24},{2,26},{4,28},{6,30},{8,16},{10,18},{12,20},{14,22},{16,8},... | collective-permute-start | bytes 442376 | tf_op jit(solution)/shard_map/ppermute | solution.py:638
  172.3 13.1 %collective-permute-start.28 = (bf16[96,768]{1,0:T(8,128)(2,1)S(1)}, bf16[96,768]{1,0:T(8,128)(2,1)S(1)}, u32[]{:S(2)}, u32[]{:S(2)}) collective-permute-start(bf16[96,768]{1,0:T(8,128)(2,1)S(1)} %get-tuple-element.177), channel_id=1, source_target_pairs={{0,16},{2,18},{4,20},{6,22},{8,24},{10,26},{12,28},{14,30},{16,0},... | collective-permute-start | bytes 442376 | tf_op jit(solution)/shard_map/ppermute | solution.py:638
  185.5 8.7 %collective-permute-start.32 = (bf16[96,768]{1,0:T(8,128)(2,1)S(1)}, bf16[96,768]{1,0:T(8,128)(2,1)S(1)}, u32[]{:S(2)}, u32[]{:S(2)}) collective-permute-start(bf16[96,768]{1,0:T(8,128)(2,1)S(1)} %fusion.9), channel_id=1, source_target_pairs={{0,24},{2,26},{4,28},{6,30},{8,16},{10,18},{12,20},{14,22},{16,8},... | collective-permute-start | bytes 442376 | tf_op jit(solution)/shard_map/ppermute | solution.py:638
  187.0 11.5 %collective-permute-start.31 = (bf16[96,768]{1,0:T(8,128)(2,1)S(1)}, bf16[96,768]{1,0:T(8,128)(2,1)S(1)}, u32[]{:S(2)}, u32[]{:S(2)}) collective-permute-start(bf16[96,768]{1,0:T(8,128)(2,1)S(1)} %fusion.9), channel_id=1, source_target_pairs={{0,16},{2,18},{4,20},{6,22},{8,24},{10,26},{12,28},{14,30},{16,0},... | collective-permute-start | bytes 442376 | tf_op jit(solution)/shard_map/ppermute | solution.py:638
  187.0 11.5 %collective-permute-start.30 = (bf16[96,768]{1,0:T(8,128)(2,1)S(1)}, bf16[96,768]{1,0:T(8,128)(2,1)S(1)}, u32[]{:S(2)}, u32[]{:S(2)}) collective-permute-start(bf16[96,768]{1,0:T(8,128)(2,1)S(1)} %fusion.9), channel_id=1, source_target_pairs={{0,8},{2,10},{4,12},{6,14},{8,0},{10,2},{12,4},{14,6},{16,24},{18,... | collective-permute-start | bytes 442376 | tf_op jit(solution)/shard_map/ppermute | solution.py:638
  189.9 9.3 %collective-permute-start.33 = (bf16[4,208,768]{2,1,0:T(8,128)(2,1)S(1)}, bf16[4,208,768]{2,1,0:T(8,128)(2,1)S(1)}, u32[]{:S(2)}, u32[]{:S(2)}) collective-permute-start(bf16[4,208,768]{2,1,0:T(8,128)(2,1)S(1)} %pad_maximum_fusion.refs_0_), channel_id=1, source_target_pairs={{0,2},{2,0},{4,6},{6,4},{8,10},{10,8},{12,14},{14,12},{16,18},{18,... | collective-permute-start | bytes 3833864 | tf_op jit(solution)/shard_map/ppermute | solution.py:638
  198.6 3.1 %collective-permute-start.34 = (bf16[4,208,768]{2,1,0:T(8,128)(2,1)S(1)}, bf16[4,208,768]{2,1,0:T(8,128)(2,1)S(1)}, u32[]{:S(2)}, u32[]{:S(2)}) collective-permute-start(bf16[4,208,768]{2,1,0:T(8,128)(2,1)S(1)} %collective-permute-done.24.refs_1_), channel_id=1, source_target_pairs={{0,2},{2,0},{4,6},{6,4},{8,10},{10,8},{12,14},{14,12},{16,18},{18,... | collective-permute-start | bytes 3833864 | tf_op jit(solution)/shard_map/ppermute | solution.py:638
  198.7 15.7 %collective-permute-start.36 = (bf16[4,96,768]{2,1,0:T(8,128)(2,1)S(1)}, bf16[4,96,768]{2,1,0:T(8,128)(2,1)S(1)}, u32[]{:S(2)}, u32[]{:S(2)}) collective-permute-start(bf16[4,96,768]{2,1,0:T(8,128)(2,1)S(1)} %pad_maximum_fusion.1.refs_0_), channel_id=1, source_target_pairs={{0,4},{2,6},{4,0},{6,2},{8,12},{10,14},{12,8},{14,10},{16,20},{18,... | collective-permute-start | bytes 1769480 | tf_op jit(solution)/shard_map/ppermute | solution.py:638
  207.1 3.9 %collective-permute-start.35 = (f32[6,768]{1,0:T(8,128)S(1)}, f32[6,768]{1,0:T(8,128)S(1)}, u32[]{:S(2)}, u32[]{:S(2)}) collective-permute-start(f32[6,768]{1,0:T(8,128)S(1)} %slice.210), channel_id=1, source_target_pairs={{0,1},{1,0},{2,3},{3,2},{4,5},{5,4},{6,7},{7,6},{8,9},{9,8},{10,11... | collective-permute-start | bytes 55304 | tf_op jit(solution)/shard_map/ppermute | solution.py:634
  208.5 7.8 %collective-permute-start.37 = (bf16[4,96,768]{2,1,0:T(8,128)(2,1)S(1)}, bf16[4,96,768]{2,1,0:T(8,128)(2,1)S(1)}, u32[]{:S(2)}, u32[]{:S(2)}) collective-permute-start(bf16[4,96,768]{2,1,0:T(8,128)(2,1)S(1)} %pad_maximum_fusion.1.refs_0_), channel_id=1, source_target_pairs={{0,2},{2,0},{4,6},{6,4},{8,10},{10,8},{12,14},{14,12},{16,18},{18,... | collective-permute-start | bytes 1769480 | tf_op jit(solution)/shard_map/ppermute | solution.py:638
  214.4 2.0 collective-permute-start.38
  (24 other events, 56.0 us)

commit v4 on v3

--- a/solution.py
+++ b/solution.py
@@ -663,6 +663,16 @@
 
 def flip_line(pieces):
     return [flip(p, LINE * k) for k, p in zip((1, 2, 3), pieces)]
+
+
+def sum_line(sends):
+    near, far, both = sends
+    return [flip(near, LINE), flip(total_of([far, flip(both, LINE)]), 2 * LINE)]
+
+
+def gather_line(piece):
+    far = flip(piece, 2 * LINE)
+    return [flip(piece, LINE), far, flip(far, LINE)]
 
 
 def shards(
@@ -780,11 +790,11 @@
         got = flip(after(send, piece2), CORE)
         side = flip(side_send(keep, got), SIDE)
         fc = jnp.concatenate([piece1, piece2, small], axis=0)
-        fc_quad = jnp.stack([fc] + [after(r, output, gpatch) for r in flip_line([fc] * 3)])
+        fc_quad = jnp.stack([fc] + [after(r, output, gpatch) for r in gather_line(fc)])
         side = after(side, fc_quad, output, gpatch)
-        line = flip_line(line_sends(keep, got, side))
+        line = sum_line(line_sends(keep, got, side))
         piece = own_piece(keep, got, side, line)
-        quad = jnp.stack([piece] + flip_line([piece] * 3))
+        quad = jnp.stack([piece] + gather_line(piece))
         fc_pair = after(flip(fc_quad, SIDE), quad)
         g_fc1, g_fc2, small = finish_mlp(me, (fc_quad, fc_pair, after(flip(fc_quad, CORE), quad), after(flip(fc_pair, CORE), quad)))
         totals = small[0:6] + across(small[0:6])

time: 220 us -> 216 us (0.982)
  starting transfers between devices: 44.8 us -> 32.8 us
  waiting for transfers between devices: 62.8 us -> 70.9 us
    ppermute x28, waiting for transfers between devices: 40.7 us -> 56.7 us  [flip(): return lax.ppermute(v, 'dp', [(i, i ^ bits) for i in range(16)])]
    ppermute x28, starting transfers between devices: 33.2 us -> 21.2 us  [flip(): return lax.ppermute(v, 'dp', [(i, i ^ bits) for i in range(16)])]
    ppermute x11, waiting for transfers between devices: 22.2 us -> 14.2 us  [across(): return lax.ppermute(v, 'mp', [(0, 1), (1, 0)])]
  transfers between devices with their start and end apart: 39 -> 39, of which waited for: 18 -> 19; matrix products, arithmetic and copies ran while one was open for 4% -> 4% of each run, Pallas kernels for 35% -> 35%
where the time goes in v4:
time: 216 us
  Pallas kernels  89.9 us (42%)
  waiting for transfers between devices  70.9 us (33%)
  starting transfers between devices  32.8 us (15%)
  local copies, waits for them, and re-layouts  14.5 us (7%)
  other arithmetic  4.01 us (2%)
  matrix products  2.41 us (1%)
    pallas_call x14, Pallas kernels, call(): pl.pallas_call(kernel, out_shape=outs, in_specs=in_specs, out_specs=[spac...  89.9 us
    ppermute x28, waiting for transfers between devices, flip(): return lax.ppermute(v, 'dp', [(i, i ^ bits) for i in range(16)])  56.7 us
    ppermute x28, starting transfers between devices, flip(): return lax.ppermute(v, 'dp', [(i, i ^ bits) for i in range(16)])  21.2 us
    ppermute x11, waiting for transfers between devices, across(): return lax.ppermute(v, 'mp', [(0, 1), (1, 0)])  14.2 us
    unnamed x98, local copies, waits for them, and re-layouts  11.6 us
    ppermute x11, starting transfers between devices, across(): return lax.ppermute(v, 'mp', [(0, 1), (1, 0)])  11.6 us
  transfers between devices with their start and end apart: 39, of which 19 were waited for; matrix products, arithmetic and copies ran while one was open for 4% of the time, Pallas kernels for 35%

profile of v4, /device:TPU:0, one launch (start us, length us, event | category | flops | bytes accessed | tf_op | source)
XLA Modules:
  0.0 215.9 jit_solution(8704989266110969071)
XLA Ops:
  1.3 2.9 %collective-permute-start.1 = (f32[8,49]{1,0:T(8,128)S(1)}, f32[8,49]{1,0:T(8,128)S(1)}, u32[]{:S(2)}, u32[]{:S(2)}) collective-permute-start(f32[8,49]{1,0:T(8,128)S(1)} %convert_element_type.294.valid_ref), channel_id=1, source_target_pairs={{0,1},{1,0},{2,3},{3,2},{4,5},{5,4},{6,7},{7,6},{8,9},{9,8},{10,11... | collective-permute-start | bytes 4712 | tf_op jit(solution)/shard_map/ppermute | solution.py:634
  4.3 1.6 collective-permute-done.1.valid_ref
  5.9 2.0 collective-permute-start.2
  7.9 1.0 constant_dynamic-slice_fusion
  10.9 12.1 %attn_forward.2 = (bf16[8,3,64,256]{3,2,1,0:T(8,128)(2,1)}, bf16[8,64,384]{2,1,0:T(8,128)(2,1)}, bf16[8,64,384]{2,1,0:T(8,128)(2,1)}, bf16[8,64,384]{2,1,0:T(8,1...) custom-call(bf16[392,768]{1,0:T(8,128)(2,1)} %bitcast.102, f32[768]{0:T(1024)} %gain_ref.9, f32[768]{0:T(1024)} %shift_ref.4, ...), custom_call_target="tpu_custom_call" | custom-call | flops 1000000 | bytes 3906 | tf_op jit(solution)/shard_map/attn_forward/pallas_call | solution.py:515
  23.0 0.8 copy-done.11
  23.8 12.1 %attn_forward.3 = (bf16[8,3,64,256]{3,2,1,0:T(8,128)(2,1)}, bf16[8,64,384]{2,1,0:T(8,128)(2,1)}, bf16[8,64,384]{2,1,0:T(8,128)(2,1)}, bf16[8,64,384]{2,1,0:T(8,1...) custom-call(bf16[392,768]{1,0:T(8,128)(2,1)} %copy-done.11, f32[768]{0:T(1024)} %gain_ref.9, f32[768]{0:T(1024)} %shift_ref.4, ...), custom_call_target="tpu_custom_call" | custom-call | flops 1000000 | bytes 3906 | tf_op jit(solution)/shard_map/attn_forward/pallas_call | solution.py:515
  35.9 2.9 %collective-permute-done.3.refs_0_ = bf16[192,768]{1,0:T(8,128)(2,1)} collective-permute-done((bf16[192,768]{1,0:T(8,128)(2,1)S(1)}, bf16[192,768]{1,0:T(8,128)(2,1)}, u32[]{:S(2)}, u32[]{:S(2)}) %collective-permute-start.3) | collective-permute-done | bytes 294944 | tf_op jit(solution)/shard_map/ppermute | solution.py:634
  38.9 0.8 copy-done.7
  40.1 2.4 %convolution_convert_fusion.own_in = bf16[392,768]{1,0:T(8,128)(2,1)} fusion(bf16[392,384]{1,0:T(8,128)(2,1)} %get-tuple-element.92.refs_1_, bf16[384,768]{1,0:T(8,128)(2,1)S(1)} %copy-done.4), kind=kOutput, calls=%fused_computation | convolution fusion | flops 231512064 | bytes 1492992 | tf_op jit(solution)/shard_map/dot_general | solution.py:732
  42.5 5.1 %collective-permute-done.4.peer_in = bf16[392,384]{1,0:T(8,128)(2,1)S(1)} collective-permute-done((bf16[392,384]{1,0:T(8,128)(2,1)}, bf16[392,384]{1,0:T(8,128)(2,1)S(1)}, u32[]{:S(2)}, u32[]{:S(2)}) %collective-permute-start.4) | collective-permute-done | bytes 301088 | tf_op jit(solution)/shard_map/ppermute | solution.py:634
  47.6 0.7 copy-done.43
  48.3 3.8 %middle.1 = (f32[392,768]{1,0:T(8,128)}, bf16[392,768]{1,0:T(8,128)(2,1)}) custom-call(s32[1]{0:T(128)} %bitcast.me_ref, bf16[392,768]{1,0:T(8,128)(2,1)} %bitcast.103, bf16[392,768]{1,0:T(8,128)(2,1)} %convolution_convert_fusion.own_in, bf16[392,384]{1,0:T(8,128)(2,1)} %copy-done.43, f32[768]{0:T(1024)} %bias_ref.5, f32[768]{0:T(1024)} %gain_ref.8, ...), custom_call_target="tpu_custom_call" | custom-call | flops 1000000 | bytes 3906 | tf_op jit(solution)/shard_map/middle/pallas_call | solution.py:515
  52.2 0.8 collective-permute-start.6
  53.0 1.1 copy-done.9
  54.1 6.1 %mlp.2 = (bf16[392,1536]{1,0:T(8,128)(2,1)S(1)}, bf16[392,1536]{1,0:T(8,128)(2,1)S(1)}, bf16[392,768]{1,0:T(8,128)(2,1)S(1)}, bf16[392,768]{1,0:T(8,128)(2,1)S(1)}) custom-call(bf16[392,768]{1,0:T(8,128)(2,1)S(1)} %copy-done.9, bf16[392,768]{1,0:T(8,128)(2,1)S(1)} %bitcast.108, bf16[768,1536]{1,0:T(8,128)(2,1)S(1)} %copy-done.2, ...), custom_call_target="tpu_custom_call" | custom-call | flops 1000000 | bytes 3906 | tf_op jit(solution)/shard_map/mlp/pallas_call | solution.py:515
  60.2 1.0 copy-done.14
  61.2 0.8 copy-done.24
  62.0 0.8 copy-done.37
  62.9 2.8 %collective-permute-done.6.nm_ref.refs_4_ = bf16[392,768]{1,0:T(8,128)(2,1)S(1)} collective-permute-done((bf16[392,768]{1,0:T(8,128)(2,1)}, bf16[392,768]{1,0:T(8,128)(2,1)S(1)}, u32[]{:S(2)}, u32[]{:S(2)}) %collective-permute-start.6) | collective-permute-done | bytes 602144 | tf_op jit(solution)/shard_map/ppermute | solution.py:634
  65.7 6.9 %mlp.3 = (bf16[392,1536]{1,0:T(8,128)(2,1)S(1)}, bf16[392,1536]{1,0:T(8,128)(2,1)S(1)}, bf16[392,768]{1,0:T(8,128)(2,1)S(1)}, bf16[392,768]{1,0:T(8,128)(2,1)}) custom-call(bf16[392,768]{1,0:T(8,128)(2,1)S(1)} %collective-permute-done.6.nm_ref.refs_4_, bf16[392,768]{1,0:T(8,128)(2,1)S(1)} %copy-done.8, bf16[768,1536]{1,0:T(8,128)(2,1)S(1)} %copy-done.2, ...), custom_call_target="tpu_custom_call" | custom-call | flops 1000000 | bytes 3906 | tf_op jit(solution)/shard_map/mlp/pallas_call | solution.py:515
  72.6 1.0 copy-done.16
  73.6 1.1 copy-done.17
  74.7 1.1 collective-permute-start.8
  75.7 11.7 %mlp_weights.1 = (f32[1,1536]{1,0:T(1,128)}, bf16[2,4,96,768]{3,2,1,0:T(8,128)(2,1)}, bf16[2,4,96,768]{3,2,1,0:T(8,128)(2,1)}, bf16[2,4,96,768]{3,2,1,0:T(8,128)(2,1)}, bf16[2,4,96,768]{3,2,1,0:T(8,128)(2,1)}) custom-call(s32[1]{0:T(128)} %bitcast.me_ref, bf16[392,768]{1,0:T(8,128)(2,1)} %get-tuple-element.100.nm_ref.refs_0_, bf16[392,768]{1,0:T(8,128)(2,1)} %bitcast.107, ...), custom_call_target="tpu_custom_call" | custom-call | flops 1000000 | bytes 3906 | tf_op jit(solution)/shard_map/mlp_weights/pallas_call | solution.py:515
  88.1 0.8 copy-done.39
  88.9 1.1 copy-done.40
  90.0 1.1 middle_back.1
  91.1 1.0 collective-permute-start.11
  92.3 1.6 collective-permute-start.12
  94.6 1.1 collective-permute-start.7
  95.7 9.7 %attn_backward.2 = (bf16[3,392,384]{2,1,0:T(8,128)(2,1)S(1)}, f32[1,768]{1,0:T(1,128)S(1)}, f32[3,64,256]{2,1,0:T(8,128)S(1)}, bf16[392,768]{1,0:T(8,128)(2,1)S(1)}, f32[2,768]{1,0:T(2,128)S(1)}) custom-call(bf16[392,768]{1,0:T(8,128)(2,1)S(1)} %get-tuple-element.139.branch_ref.refs_2_, bf16[392,768]{1,0:T(8,128)(2,1)S(1)} %bitcast.104, ...), custom_call_target="tpu_custom_call" | custom-call | flops 1000000 | bytes 3906 | tf_op jit(solution)/shard_map/attn_backward/pallas_call | solution.py:515
  105.5 3.1 %collective-permute-done.12 = bf16[4,96,768]{2,1,0:T(8,128)(2,1)S(1)} collective-permute-done((bf16[4,96,768]{2,1,0:T(8,128)(2,1)S(1)}, bf16[4,96,768]{2,1,0:T(8,128)(2,1)S(1)}, u32[]{:S(2)}, u32[]{:S(2)}) %collective-permute-start.12) | collective-permute-done | bytes 589856 | tf_op jit(solution)/shard_map/ppermute | solution.py:638
  108.7 3.7 %collective-permute-start.16 = (bf16[96,768]{1,0:T(8,128)(2,1)S(1)}, bf16[96,768]{1,0:T(8,128)(2,1)S(1)}, u32[]{:S(2)}, u32[]{:S(2)}) collective-permute-start(bf16[96,768]{1,0:T(8,128)(2,1)S(1)} %get-tuple-element.180), channel_id=1, source_target_pairs={{0,24},{2,26},{4,28},{6,30},{8,16},{10,18},{12,20},{14,22},{16,8},... | collective-permute-start | bytes 442376 | tf_op jit(solution)/shard_map/ppermute | solution.py:638
  112.4 0.8 collective-permute-start.14
  113.2 9.7 %attn_backward.3 = (bf16[3,392,384]{2,1,0:T(8,128)(2,1)S(1)}, f32[1,768]{1,0:T(1,128)S(1)}, f32[3,64,256]{2,1,0:T(8,128)S(1)}, bf16[392,768]{1,0:T(8,128)(2,1)S(1)}, f32[2,768]{1,0:T(2,128)S(1)}) custom-call(bf16[392,768]{1,0:T(8,128)(2,1)S(1)} %collective-permute-done.11.branch_ref.refs_9_, bf16[392,768]{1,0:T(8,128)(2,1)S(1)} %copy-done.12, ...), custom_call_target="tpu_custom_call" | custom-call | flops 1000000 | bytes 3906 | tf_op jit(solution)/shard_map/attn_backward/pallas_call | solution.py:515
  123.2 3.7 %collective-permute-start.20 = (bf16[96,768]{1,0:T(8,128)(2,1)S(1)}, bf16[96,768]{1,0:T(8,128)(2,1)S(1)}, u32[]{:S(2)}, u32[]{:S(2)}) collective-permute-start(bf16[96,768]{1,0:T(8,128)(2,1)S(1)} %get-tuple-element.177), channel_id=1, source_target_pairs={{0,24},{2,26},{4,28},{6,30},{8,16},{10,18},{12,20},{14,22},{16,8},... | collective-permute-start | bytes 442376 | tf_op jit(solution)/shard_map/ppermute | solution.py:638
  126.9 0.8 collective-permute-start.18
  127.9 5.8 %attn_weights.1 = (bf16[2,4,96,768]{3,2,1,0:T(8,128)(2,1)S(1)}, bf16[2,4,96,768]{3,2,1,0:T(8,128)(2,1)S(1)}, bf16[16,768]{1,0:T(8,128)(2,1)S(1)}) custom-call(s32[1]{0:T(128)} %bitcast.me_ref, f32[4,768]{1,0:T(4,128)S(1)} %get-tuple-element.137.sums2_ref, f32[1,1536]{1,0:T(1,128)S(1)} %copy-done.35, bf16[768,392]{1,0:T(8,128)(2,1)S(1)} %copy-done.20, ...), custom_call_target="tpu_custom_call" | custom-call | flops 1000000 | bytes 3906 | tf_op jit(solution)/shard_map/attn_weights/pallas_call | solution.py:515
  133.6 2.7 %collective-permute-done.19 = bf16[96,768]{1,0:T(8,128)(2,1)S(1)} collective-permute-done((bf16[96,768]{1,0:T(8,128)(2,1)S(1)}, bf16[96,768]{1,0:T(8,128)(2,1)S(1)}, u32[]{:S(2)}, u32[]{:S(2)}) %collective-permute-start.19) | collective-permute-done | bytes 147488 | tf_op jit(solution)/shard_map/ppermute | solution.py:638
  136.6 0.7 collective-permute-start.13
  137.5 2.0 collective-permute-done.25
  139.6 1.6 collective-permute-start.26
  141.2 1.0 collective-permute-start.21
  142.1 12.5 %collective-permute-done.22 = bf16[208,768]{1,0:T(8,128)(2,1)S(1)} collective-permute-done((bf16[208,768]{1,0:T(8,128)(2,1)S(1)}, bf16[208,768]{1,0:T(8,128)(2,1)S(1)}, u32[]{:S(2)}, u32[]{:S(2)}) %collective-permute-start.22) | collective-permute-done | bytes 319520 | tf_op jit(solution)/shard_map/ppermute | solution.py:638
  154.7 1.1 add_convert_fusion
  155.8 1.7 input_back.1
  157.5 6.6 %collective-permute-done.23 = bf16[208,768]{1,0:T(8,128)(2,1)S(1)} collective-permute-done((bf16[208,768]{1,0:T(8,128)(2,1)S(1)}, bf16[208,768]{1,0:T(8,128)(2,1)S(1)}, u32[]{:S(2)}, u32[]{:S(2)}) %collective-permute-start.23) | collective-permute-done | bytes 319520 | tf_op jit(solution)/shard_map/ppermute | solution.py:638
  164.2 1.6 collective-permute-start.24
  166.3 1.7 collective-permute-start.27
  168.0 4.2 %collective-permute-done.28 = bf16[96,768]{1,0:T(8,128)(2,1)S(1)} collective-permute-done((bf16[96,768]{1,0:T(8,128)(2,1)S(1)}, bf16[96,768]{1,0:T(8,128)(2,1)S(1)}, u32[]{:S(2)}, u32[]{:S(2)}) %collective-permute-start.28) | collective-permute-done | bytes 147488 | tf_op jit(solution)/shard_map/ppermute | solution.py:638
  172.9 1.9 collective-permute-done.27
  174.9 7.6 %collective-permute-done.29 = bf16[96,768]{1,0:T(8,128)(2,1)S(1)} collective-permute-done((bf16[96,768]{1,0:T(8,128)(2,1)S(1)}, bf16[96,768]{1,0:T(8,128)(2,1)S(1)}, u32[]{:S(2)}, u32[]{:S(2)}) %collective-permute-start.29) | collective-permute-done | bytes 147488 | tf_op jit(solution)/shard_map/ppermute | solution.py:638
  182.7 1.6 collective-permute-start.30
  184.3 5.2 %collective-permute-done.31 = bf16[96,768]{1,0:T(8,128)(2,1)S(1)} collective-permute-done((bf16[96,768]{1,0:T(8,128)(2,1)S(1)}, bf16[96,768]{1,0:T(8,128)(2,1)S(1)}, u32[]{:S(2)}, u32[]{:S(2)}) %collective-permute-start.31) | collective-permute-done | bytes 147488 | tf_op jit(solution)/shard_map/ppermute | solution.py:638
  189.4 0.8 collective-permute-done.30
  190.3 4.3 %collective-permute-done.32 = bf16[96,768]{1,0:T(8,128)(2,1)S(1)} collective-permute-done((bf16[96,768]{1,0:T(8,128)(2,1)S(1)}, bf16[96,768]{1,0:T(8,128)(2,1)S(1)}, u32[]{:S(2)}, u32[]{:S(2)}) %collective-permute-start.32) | collective-permute-done | bytes 147488 | tf_op jit(solution)/shard_map/ppermute | solution.py:638
  194.8 0.8 collective-permute-start.36
  195.6 2.2 collective-permute-done.34.refs_3_
  197.7 5.4 %finish_mlp.1 = (f32[768,1536]{1,0:T(8,128)}, f32[1536,768]{1,0:T(8,128)}, f32[16,768]{1,0:T(8,128)S(1)}) custom-call(s32[1]{0:T(128)} %bitcast.me_ref, bf16[4,208,768]{2,1,0:T(8,128)(2,1)S(1)} %pad_maximum_fusion.refs_0_, bf16[4,208,768]{2,1,0:T(8,128)(2,1)S(1)} %collective-permute-done.24.refs_1_, ...), custom_call_target="tpu_custom_call" | custom-call | flops 1000000 | bytes 3906 | tf_op jit(solution)/shard_map/finish_mlp/pallas_call | solution.py:515
  203.1 1.4 collective-permute-start.35
  205.2 1.8 collective-permute-done.35
  207.0 3.5 %collective-permute-done.36.refs_1_ = bf16[4,96,768]{2,1,0:T(8,128)(2,1)S(1)} collective-permute-done((bf16[4,96,768]{2,1,0:T(8,128)(2,1)S(1)}, bf16[4,96,768]{2,1,0:T(8,128)(2,1)S(1)}, u32[]{:S(2)}, u32[]{:S(2)}) %collective-permute-start.36) | collective-permute-done | bytes 589856 | tf_op jit(solution)/shard_map/ppermute | solution.py:638
  212.5 3.2 %finish.1 = (f32[3,768,384]{2,1,0:T(8,128)}, f32[384,768]{1,0:T(8,128)}) custom-call(s32[1]{0:T(128)} %bitcast.me_ref, bf16[4,96,768]{2,1,0:T(8,128)(2,1)S(1)} %pad_maximum_fusion.1.refs_0_, bf16[4,96,768]{2,1,0:T(8,128)(2,1)S(1)} %collective-permute-done.36.refs_1_, bf16[4,96,768]{2,1,0:T(8,128)(2,1)S(1)} %collective-permute-done.37.refs_2_, ...), custom_call_target="tpu_custom_call" | custom-call | flops 1000000 | bytes 3906 | tf_op jit(solution)/shard_map/finish/pallas_call | solution.py:515
  (154 shorter events, 10.0 us)
Async XLA Ops:
  1.3 9.6 %copy-start.45 = (f32[8,49]{1,0:T(8,128)}, f32[8,49]{1,0:T(8,128)S(1)}, u32[]{:S(2)}) copy-start(f32[8,49]{1,0:T(8,128)S(1)} %convert_element_type.294.valid_ref) | copy-start | bytes 4708
  1.3 4.5 %collective-permute-start.1 = (f32[8,49]{1,0:T(8,128)S(1)}, f32[8,49]{1,0:T(8,128)S(1)}, u32[]{:S(2)}, u32[]{:S(2)}) collective-permute-start(f32[8,49]{1,0:T(8,128)S(1)} %convert_element_type.294.valid_ref), channel_id=1, source_target_pairs={{0,1},{1,0},{2,3},{3,2},{4,5},{5,4},{6,7},{7,6},{8,9},{9,8},{10,11... | collective-permute-start | bytes 4712 | tf_op jit(solution)/shard_map/ppermute | solution.py:634
  4.3 18.7 %collective-permute-start = (bf16[392,768]{1,0:T(8,128)(2,1)}, bf16[392,768]{1,0:T(8,128)(2,1)S(1)}, u32[]{:S(2)}, u32[]{:S(2)}) collective-permute-start(bf16[392,768]{1,0:T(8,128)(2,1)} %bitcast.101), channel_id=1, source_target_pairs={{0,1},{1,0},{2,3},{3,2},{4,5},{5,4},{6,7},{7,6},{8,9},{9,8},{10,11... | collective-permute-start | bytes 1806344 | tf_op jit(solution)/shard_map/ppermute | solution.py:634
  5.9 17.1 %copy-start.48 = (f32[8,49]{1,0:T(8,128)}, f32[8,49]{1,0:T(8,128)S(1)}, u32[]{:S(2)}) copy-start(f32[8,49]{1,0:T(8,128)S(1)} %collective-permute-done.1.valid_ref) | copy-start | bytes 4708
  5.9 33.0 %collective-permute-start.2 = (bf16[392,768]{1,0:T(8,128)(2,1)}, bf16[392,768]{1,0:T(8,128)(2,1)S(1)}, u32[]{:S(2)}, u32[]{:S(2)}) collective-permute-start(bf16[392,768]{1,0:T(8,128)(2,1)} %bitcast.106), channel_id=1, source_target_pairs={{0,1},{1,0},{2,3},{3,2},{4,5},{5,4},{6,7},{7,6},{8,9},{9,8},{10,11... | collective-permute-start | bytes 1806344 | tf_op jit(solution)/shard_map/ppermute | solution.py:634
  8.9 30.0 %collective-permute-start.3 = (bf16[192,768]{1,0:T(8,128)(2,1)S(1)}, bf16[192,768]{1,0:T(8,128)(2,1)}, u32[]{:S(2)}, u32[]{:S(2)}) collective-permute-start(bf16[192,768]{1,0:T(8,128)(2,1)S(1)} %constant_dynamic-slice_fusion), channel_id=1, source_target_pairs={{0,1},{1,0},{2,3},{3,2},{4,5},{5,4},{6,7},{7,6},{8,9},{9,8},{10,11... | collective-permute-start | bytes 884744 | tf_op jit(solution)/shard_map/ppermute | solution.py:634
  10.9 29.2 %copy-start.4 = (bf16[384,768]{1,0:T(8,128)(2,1)S(1)}, bf16[384,768]{1,0:T(8,128)(2,1)}, u32[]{:S(2)}) copy-start(bf16[384,768]{1,0:T(8,128)(2,1)} %proj_ref.3) | copy-start | bytes 1769476
  23.8 29.1 %copy-start.3 = (bf16[1536,768]{1,0:T(8,128)(2,1)S(1)}, bf16[1536,768]{1,0:T(8,128)(2,1)}, u32[]{:S(2)}) copy-start(bf16[1536,768]{1,0:T(8,128)(2,1)} %fc2_ref.3) | copy-start | bytes 7077892
  39.7 7.9 %collective-permute-start.4 = (bf16[392,384]{1,0:T(8,128)(2,1)}, bf16[392,384]{1,0:T(8,128)(2,1)S(1)}, u32[]{:S(2)}, u32[]{:S(2)}) collective-permute-start(bf16[392,384]{1,0:T(8,128)(2,1)} %get-tuple-element.97.refs_8_), channel_id=1, source_target_pairs={{0,1},{1,0},{2,3},{3,2},{4,5},{5,4},{6,7},{7,6},{8,9},{9,8},{10,11... | collective-permute-start | bytes 903176 | tf_op jit(solution)/shard_map/ppermute | solution.py:634
  40.1 2.4 %collective-permute-start.5 = (bf16[192,768]{1,0:T(8,128)(2,1)}, bf16[192,768]{1,0:T(8,128)(2,1)S(1)}, u32[]{:S(2)}, u32[]{:S(2)}) collective-permute-start(bf16[192,768]{1,0:T(8,128)(2,1)} %collective-permute-done.3.refs_0_), channel_id=1, source_target_pairs={{0,2},{2,0},{4,6},{6,4},{8,10},{10,8},{12,14},{14,12},{16,18},{18,... | collective-permute-start | bytes 884744 | tf_op jit(solution)/shard_map/ppermute | solution.py:638
  40.1 12.9 %copy-start.2 = (bf16[768,1536]{1,0:T(8,128)(2,1)S(1)}, bf16[768,1536]{1,0:T(8,128)(2,1)}, u32[]{:S(2)}) copy-start(bf16[768,1536]{1,0:T(8,128)(2,1)} %fc1_ref.3) | copy-start | bytes 7077892
  42.5 10.5 %copy-start.46 = (f32[1536]{0:T(1024)S(1)}, f32[1536]{0:T(1024)}, u32[]{:S(2)}) copy-start(f32[1536]{0:T(1024)} %param.28) | copy-start | bytes 18436
  42.5 10.5 %copy-start.5 = (bf16[8,49,768]{2,0,1:T(8,128)(2,1)S(1)}, bf16[8,49,768]{2,0,1:T(8,128)(2,1)}, u32[]{:S(2)}) copy-start(bf16[8,49,768]{2,0,1:T(8,128)(2,1)} %param.31) | copy-start | bytes 1806340
  42.5 5.1 %copy-start.44 = (bf16[192,768]{1,0:T(8,128)(2,1)}, bf16[192,768]{1,0:T(8,128)(2,1)S(1)}, u32[]{:S(2)}) copy-start(bf16[192,768]{1,0:T(8,128)(2,1)S(1)} %collective-permute-done.5.refs_1_) | copy-start | bytes 884740
  52.2 13.5 %collective-permute-start.6 = (bf16[392,768]{1,0:T(8,128)(2,1)}, bf16[392,768]{1,0:T(8,128)(2,1)S(1)}, u32[]{:S(2)}, u32[]{:S(2)}) collective-permute-start(bf16[392,768]{1,0:T(8,128)(2,1)} %get-tuple-element.100.nm_ref.refs_0_), channel_id=1, source_target_pairs={{0,1},{1,0},{2,3},{3,2},{4,5},{5,4},{6,7},{7,6},{8,9},{9,8},{10,11... | collective-permute-start | bytes 1806344 | tf_op jit(solution)/shard_map/ppermute | solution.py:634
  54.1 11.6 %copy-start.8 = (bf16[392,768]{1,0:T(8,128)(2,1)S(1)}, bf16[392,768]{1,0:T(8,128)(2,1)}, u32[]{:S(2)}) copy-start(bf16[392,768]{1,0:T(8,128)(2,1)} %copy-done.7) | copy-start | bytes 1806340
  62.9 9.7 %copy-start.15 = (bf16[392,1536]{1,0:T(8,128)(2,1)}, bf16[392,1536]{1,0:T(8,128)(2,1)S(1)}, u32[]{:S(2)}) copy-start(bf16[392,1536]{1,0:T(8,128)(2,1)S(1)} %get-tuple-element.107.refs_3_) | copy-start | bytes 3612676
  65.7 6.9 %copy-start.10 = (bf16[392,768]{1,0:T(8,128)(2,1)}, bf16[392,768]{1,0:T(8,128)(2,1)S(1)}, u32[]{:S(2)}) copy-start(bf16[392,768]{1,0:T(8,128)(2,1)S(1)} %collective-permute-done.6.nm_ref.refs_4_) | copy-start | bytes 1806340
  74.7 13.4 %collective-permute-start.8 = (bf16[392,768]{1,0:T(8,128)(2,1)}, bf16[392,768]{1,0:T(8,128)(2,1)S(1)}, u32[]{:S(2)}, u32[]{:S(2)}) collective-permute-start(bf16[392,768]{1,0:T(8,128)(2,1)} %get-tuple-element.105), channel_id=1, source_target_pairs={{0,1},{1,0},{2,3},{3,2},{4,5},{5,4},{6,7},{7,6},{8,9},{9,8},{10,11... | collective-permute-start | bytes 1806344 | tf_op jit(solution)/shard_map/ppermute | solution.py:634
  75.7 13.1 %copy-start.6 = (bf16[8,49,768]{2,0,1:T(8,128)(2,1)S(1)}, bf16[8,49,768]{2,0,1:T(8,128)(2,1)}, u32[]{:S(2)}) copy-start(bf16[8,49,768]{2,0,1:T(8,128)(2,1)} %param.31) | copy-start | bytes 1806340
  75.7 13.1 %copy-start.19 = (f32[392,768]{1,0:T(8,128)S(1)}, f32[392,768]{1,0:T(8,128)}, u32[]{:S(2)}) copy-start(f32[392,768]{1,0:T(8,128)} %get-tuple-element.99.middle_ref) | copy-start | bytes 3612676
  75.7 13.1 %copy-start.36 = (f32[768]{0:T(1024)S(1)}, f32[768]{0:T(1024)}, u32[]{:S(2)}) copy-start(f32[768]{0:T(1024)} %gain_ref.8) | copy-start | bytes 9220
  75.7 13.1 %copy-start.38 = (bf16[392,768]{1,0:T(8,128)(2,1)S(1)}, bf16[392,768]{1,0:T(8,128)(2,1)}, u32[]{:S(2)}) copy-start(bf16[392,768]{1,0:T(8,128)(2,1)} %copy-done.37) | copy-start | bytes 1806340
  87.5 4.6 %collective-permute-start.9 = (bf16[2,4,96,768]{3,2,1,0:T(8,128)(2,1)}, bf16[2,4,96,768]{3,2,1,0:T(8,128)(2,1)S(1)}, u32[]{:S(2)}, u32[]{:S(2)}) collective-permute-start(bf16[2,4,96,768]{3,2,1,0:T(8,128)(2,1)} %get-tuple-element.114), channel_id=1, source_target_pairs={{0,2},{2,0},{4,6},{6,4},{8,10},{10,8},{12,14},{14,12},{16,18},{18,... | collective-permute-start | bytes 3538952 | tf_op jit(solution)/shard_map/ppermute | solution.py:638
  87.5 6.3 %collective-permute-start.10 = (bf16[2,4,96,768]{3,2,1,0:T(8,128)(2,1)}, bf16[2,4,96,768]{3,2,1,0:T(8,128)(2,1)S(1)}, u32[]{:S(2)}, u32[]{:S(2)}) collective-permute-start(bf16[2,4,96,768]{3,2,1,0:T(8,128)(2,1)} %get-tuple-element.117), channel_id=1, source_target_pairs={{0,2},{2,0},{4,6},{6,4},{8,10},{10,8},{12,14},{14,12},{16,18},{18,... | collective-permute-start | bytes 3538952 | tf_op jit(solution)/shard_map/ppermute | solution.py:638
  90.0 5.7 %copy-start.30 = (bf16[8,64,384]{2,1,0:T(8,128)(2,1)S(1)}, bf16[8,64,384]{2,1,0:T(8,128)(2,1)}, u32[]{:S(2)}) copy-start(bf16[8,64,384]{2,1,0:T(8,128)(2,1)} %get-tuple-element.122.k_ref) | copy-start | bytes 1179652
  90.0 5.7 %copy-start.31 = (bf16[8,64,384]{2,1,0:T(8,128)(2,1)S(1)}, bf16[8,64,384]{2,1,0:T(8,128)(2,1)}, u32[]{:S(2)}) copy-start(bf16[8,64,384]{2,1,0:T(8,128)(2,1)} %get-tuple-element.123.v_ref) | copy-start | bytes 1179652
  91.1 21.3 %collective-permute-start.11 = (bf16[392,768]{1,0:T(8,128)(2,1)S(1)}, bf16[392,768]{1,0:T(8,128)(2,1)S(1)}, u32[]{:S(2)}, u32[]{:S(2)}) collective-permute-start(bf16[392,768]{1,0:T(8,128)(2,1)S(1)} %get-tuple-element.139.branch_ref.refs_2_), channel_id=1, source_target_pairs={{0,1},{1,0},{2,3},{3,2},{4,5},{5,4},{6,7},{7,6},{8,9},{9,8},{10,11... | collective-permute-start | bytes 1806344 | tf_op jit(solution)/shard_map/ppermute | solution.py:634
  92.3 16.3 %collective-permute-start.12 = (bf16[4,96,768]{2,1,0:T(8,128)(2,1)S(1)}, bf16[4,96,768]{2,1,0:T(8,128)(2,1)S(1)}, u32[]{:S(2)}, u32[]{:S(2)}) collective-permute-start(bf16[4,96,768]{2,1,0:T(8,128)(2,1)S(1)} %fusion), channel_id=1, source_target_pairs={{0,4},{2,6},{4,0},{6,2},{8,12},{10,14},{12,8},{14,10},{16,20},{18,... | collective-permute-start | bytes 1769480 | tf_op jit(solution)/shard_map/ppermute | solution.py:638
  94.0 28.9 %collective-permute-start.17 = (bf16[4,96,768]{2,1,0:T(8,128)(2,1)S(1)}, bf16[4,96,768]{2,1,0:T(8,128)(2,1)S(1)}, u32[]{:S(2)}, u32[]{:S(2)}) collective-permute-start(bf16[4,96,768]{2,1,0:T(8,128)(2,1)S(1)} %fusion.1), channel_id=1, source_target_pairs={{0,4},{2,6},{4,0},{6,2},{8,12},{10,14},{12,8},{14,10},{16,20},{18,... | collective-permute-start | bytes 1769480 | tf_op jit(solution)/shard_map/ppermute | solution.py:638
  94.6 33.2 %collective-permute-start.7 = (bf16[392,768]{1,0:T(8,128)(2,1)S(1)}, bf16[392,768]{1,0:T(8,128)(2,1)S(1)}, u32[]{:S(2)}, u32[]{:S(2)}) collective-permute-start(bf16[392,768]{1,0:T(8,128)(2,1)S(1)} %get-tuple-element.104), channel_id=1, source_target_pairs={{0,1},{1,0},{2,3},{3,2},{4,5},{5,4},{6,7},{7,6},{8,9},{9,8},{10,11... | collective-permute-start | bytes 1806344 | tf_op jit(solution)/shard_map/ppermute | solution.py:634
  95.7 17.5 %copy-start.27 = (bf16[8,64,384]{2,1,0:T(8,128)(2,1)S(1)}, bf16[8,64,384]{2,1,0:T(8,128)(2,1)}, u32[]{:S(2)}) copy-start(bf16[8,64,384]{2,1,0:T(8,128)(2,1)} %get-tuple-element.129.k_ref) | copy-start | bytes 1179652
  95.7 17.5 %copy-start.28 = (bf16[8,64,384]{2,1,0:T(8,128)(2,1)S(1)}, bf16[8,64,384]{2,1,0:T(8,128)(2,1)}, u32[]{:S(2)}) copy-start(bf16[8,64,384]{2,1,0:T(8,128)(2,1)} %get-tuple-element.130.v_ref) | copy-start | bytes 1179652
  105.5 7.7 %copy-start.12 = (bf16[392,768]{1,0:T(8,128)(2,1)S(1)}, bf16[392,768]{1,0:T(8,128)(2,1)}, u32[]{:S(2)}) copy-start(bf16[392,768]{1,0:T(8,128)(2,1)} %copy-done.11) | copy-start | bytes 1806340
  105.5 7.7 %copy-start.22 = (bf16[8,3,64,256]{3,2,1,0:T(8,128)(2,1)S(1)}, bf16[8,3,64,256]{3,2,1,0:T(8,128)(2,1)}, u32[]{:S(2)}) copy-start(bf16[8,3,64,256]{3,2,1,0:T(8,128)(2,1)} %get-tuple-element.127.prob_ref) | copy-start | bytes 2359300
  105.5 7.7 %copy-start.26 = (bf16[8,64,384]{2,1,0:T(8,128)(2,1)S(1)}, bf16[8,64,384]{2,1,0:T(8,128)(2,1)}, u32[]{:S(2)}) copy-start(bf16[8,64,384]{2,1,0:T(8,128)(2,1)} %get-tuple-element.128.q_ref) | copy-start | bytes 1179652
  108.7 18.1 %collective-permute-start.16 = (bf16[96,768]{1,0:T(8,128)(2,1)S(1)}, bf16[96,768]{1,0:T(8,128)(2,1)S(1)}, u32[]{:S(2)}, u32[]{:S(2)}) collective-permute-start(bf16[96,768]{1,0:T(8,128)(2,1)S(1)} %get-tuple-element.180), channel_id=1, source_target_pairs={{0,24},{2,26},{4,28},{6,30},{8,16},{10,18},{12,20},{14,22},{16,8},... | collective-permute-start | bytes 442376 | tf_op jit(solution)/shard_map/ppermute | solution.py:638
  112.4 14.5 %collective-permute-start.15 = (bf16[96,768]{1,0:T(8,128)(2,1)S(1)}, bf16[96,768]{1,0:T(8,128)(2,1)S(1)}, u32[]{:S(2)}, u32[]{:S(2)}) collective-permute-start(bf16[96,768]{1,0:T(8,128)(2,1)S(1)} %get-tuple-element.181), channel_id=1, source_target_pairs={{0,16},{2,18},{4,20},{6,22},{8,24},{10,26},{12,28},{14,30},{16,0},... | collective-permute-start | bytes 442376 | tf_op jit(solution)/shard_map/ppermute | solution.py:638
  112.4 15.3 %collective-permute-start.14 = (bf16[96,768]{1,0:T(8,128)(2,1)S(1)}, bf16[96,768]{1,0:T(8,128)(2,1)S(1)}, u32[]{:S(2)}, u32[]{:S(2)}) collective-permute-start(bf16[96,768]{1,0:T(8,128)(2,1)S(1)} %get-tuple-element.182), channel_id=1, source_target_pairs={{0,8},{2,10},{4,12},{6,14},{8,0},{10,2},{12,4},{14,6},{16,24},{18,... | collective-permute-start | bytes 442376 | tf_op jit(solution)/shard_map/ppermute | solution.py:638
  123.0 4.8 %copy-start.18 = (bf16[392,384]{1,0:T(8,128)(2,1)S(1)}, bf16[392,384]{1,0:T(8,128)(2,1)}, u32[]{:S(2)}) copy-start(bf16[392,384]{1,0:T(8,128)(2,1)} %get-tuple-element.92.refs_1_) | copy-start | bytes 903172
  123.2 10.4 %collective-permute-start.20 = (bf16[96,768]{1,0:T(8,128)(2,1)S(1)}, bf16[96,768]{1,0:T(8,128)(2,1)S(1)}, u32[]{:S(2)}, u32[]{:S(2)}) collective-permute-start(bf16[96,768]{1,0:T(8,128)(2,1)S(1)} %get-tuple-element.177), channel_id=1, source_target_pairs={{0,24},{2,26},{4,28},{6,30},{8,16},{10,18},{12,20},{14,22},{16,8},... | collective-permute-start | bytes 442376 | tf_op jit(solution)/shard_map/ppermute | solution.py:638
  126.9 9.5 %collective-permute-start.19 = (bf16[96,768]{1,0:T(8,128)(2,1)S(1)}, bf16[96,768]{1,0:T(8,128)(2,1)S(1)}, u32[]{:S(2)}, u32[]{:S(2)}) collective-permute-start(bf16[96,768]{1,0:T(8,128)(2,1)S(1)} %get-tuple-element.178), channel_id=1, source_target_pairs={{0,16},{2,18},{4,20},{6,22},{8,24},{10,26},{12,28},{14,30},{16,0},... | collective-permute-start | bytes 442376 | tf_op jit(solution)/shard_map/ppermute | solution.py:638
  126.9 9.5 %collective-permute-start.18 = (bf16[96,768]{1,0:T(8,128)(2,1)S(1)}, bf16[96,768]{1,0:T(8,128)(2,1)S(1)}, u32[]{:S(2)}, u32[]{:S(2)}) collective-permute-start(bf16[96,768]{1,0:T(8,128)(2,1)S(1)} %get-tuple-element.179), channel_id=1, source_target_pairs={{0,8},{2,10},{4,12},{6,14},{8,0},{10,2},{12,4},{14,6},{16,24},{18,... | collective-permute-start | bytes 442376 | tf_op jit(solution)/shard_map/ppermute | solution.py:638
  136.5 18.2 %copy-start.25 = (bf16[392,768]{1,0:T(8,128)(2,1)S(1)}, bf16[392,768]{1,0:T(8,128)(2,1)}, u32[]{:S(2)}) copy-start(bf16[392,768]{1,0:T(8,128)(2,1)} %copy-done.24) | copy-start | bytes 1806340
  136.5 18.1 %copy-start.47 = (f32[768]{0:T(1024)S(1)}, f32[768]{0:T(1024)}, u32[]{:S(2)}) copy-start(f32[768]{0:T(1024)} %param.30) | copy-start | bytes 9220
  136.5 2.9 %collective-permute-start.25 = (bf16[2,4,96,768]{3,2,1,0:T(8,128)(2,1)S(1)}, bf16[2,4,96,768]{3,2,1,0:T(8,128)(2,1)S(1)}, u32[]{:S(2)}, u32[]{:S(2)}) collective-permute-start(bf16[2,4,96,768]{3,2,1,0:T(8,128)(2,1)S(1)} %get-tuple-element.158), channel_id=1, source_target_pairs={{0,2},{2,0},{4,6},{6,4},{8,10},{10,8},{12,14},{14,12},{16,18},{18,... | collective-permute-start | bytes 3538952 | tf_op jit(solution)/shard_map/ppermute | solution.py:638
  136.6 19.2 %collective-permute-start.13 = (bf16[392,768]{1,0:T(8,128)(2,1)S(1)}, bf16[392,768]{1,0:T(8,128)(2,1)S(1)}, u32[]{:S(2)}, u32[]{:S(2)}) collective-permute-start(bf16[392,768]{1,0:T(8,128)(2,1)S(1)} %get-tuple-element.131), channel_id=1, source_target_pairs={{0,1},{1,0},{2,3},{3,2},{4,5},{5,4},{6,7},{7,6},{8,9},{9,8},{10,11... | collective-permute-start | bytes 1806344 | tf_op jit(solution)/shard_map/ppermute | solution.py:634
  137.4 17.3 %collective-permute-start.22 = (bf16[208,768]{1,0:T(8,128)(2,1)S(1)}, bf16[208,768]{1,0:T(8,128)(2,1)S(1)}, u32[]{:S(2)}, u32[]{:S(2)}) collective-permute-start(bf16[208,768]{1,0:T(8,128)(2,1)S(1)} %get-tuple-element.184), channel_id=1, source_target_pairs={{0,16},{2,18},{4,20},{6,22},{8,24},{10,26},{12,28},{14,30},{16,0},... | collective-permute-start | bytes 958472 | tf_op jit(solution)/shard_map/ppermute | solution.py:638
  139.6 26.2 %collective-permute-start.26 = (bf16[4,96,768]{2,1,0:T(8,128)(2,1)S(1)}, bf16[4,96,768]{2,1,0:T(8,128)(2,1)S(1)}, u32[]{:S(2)}, u32[]{:S(2)}) collective-permute-start(bf16[4,96,768]{2,1,0:T(8,128)(2,1)S(1)} %fusion.2), channel_id=1, source_target_pairs={{0,4},{2,6},{4,0},{6,2},{8,12},{10,14},{12,8},{14,10},{16,20},{18,... | collective-permute-start | bytes 1769480 | tf_op jit(solution)/shard_map/ppermute | solution.py:638
  141.2 16.3 %collective-permute-start.21 = (bf16[208,768]{1,0:T(8,128)(2,1)S(1)}, bf16[208,768]{1,0:T(8,128)(2,1)S(1)}, u32[]{:S(2)}, u32[]{:S(2)}) collective-permute-start(bf16[208,768]{1,0:T(8,128)(2,1)S(1)} %get-tuple-element.184), channel_id=1, source_target_pairs={{0,8},{2,10},{4,12},{6,14},{8,0},{10,2},{12,4},{14,6},{16,24},{18,... | collective-permute-start | bytes 958472 | tf_op jit(solution)/shard_map/ppermute | solution.py:638
  154.6 9.4 %collective-permute-start.23 = (bf16[208,768]{1,0:T(8,128)(2,1)S(1)}, bf16[208,768]{1,0:T(8,128)(2,1)S(1)}, u32[]{:S(2)}, u32[]{:S(2)}) collective-permute-start(bf16[208,768]{1,0:T(8,128)(2,1)S(1)} %collective-permute-done.22), channel_id=1, source_target_pairs={{0,8},{2,10},{4,12},{6,14},{8,0},{10,2},{12,4},{14,6},{16,24},{18,... | collective-permute-start | bytes 958472 | tf_op jit(solution)/shard_map/ppermute | solution.py:638
  164.2 30.4 %collective-permute-start.24 = (bf16[4,208,768]{2,1,0:T(8,128)(2,1)S(1)}, bf16[4,208,768]{2,1,0:T(8,128)(2,1)S(1)}, u32[]{:S(2)}, u32[]{:S(2)}) collective-permute-start(bf16[4,208,768]{2,1,0:T(8,128)(2,1)S(1)} %pad_maximum_fusion.refs_0_), channel_id=1, source_target_pairs={{0,4},{2,6},{4,0},{6,2},{8,12},{10,14},{12,8},{14,10},{16,20},{18,... | collective-permute-start | bytes 3833864 | tf_op jit(solution)/shard_map/ppermute | solution.py:638
  165.9 6.2 %collective-permute-start.28 = (bf16[96,768]{1,0:T(8,128)(2,1)S(1)}, bf16[96,768]{1,0:T(8,128)(2,1)S(1)}, u32[]{:S(2)}, u32[]{:S(2)}) collective-permute-start(bf16[96,768]{1,0:T(8,128)(2,1)S(1)} %get-tuple-element.176), channel_id=1, source_target_pairs={{0,8},{2,10},{4,12},{6,14},{8,0},{10,2},{12,4},{14,6},{16,24},{18,... | collective-permute-start | bytes 442376 | tf_op jit(solution)/shard_map/ppermute | solution.py:638
  166.3 8.6 %collective-permute-start.27 = (bf16[96,768]{1,0:T(8,128)(2,1)S(1)}, bf16[96,768]{1,0:T(8,128)(2,1)S(1)}, u32[]{:S(2)}, u32[]{:S(2)}) collective-permute-start(bf16[96,768]{1,0:T(8,128)(2,1)S(1)} %get-tuple-element.175), channel_id=1, source_target_pairs={{0,8},{2,10},{4,12},{6,14},{8,0},{10,2},{12,4},{14,6},{16,24},{18,... | collective-permute-start | bytes 442376 | tf_op jit(solution)/shard_map/ppermute | solution.py:638
  172.3 10.2 %collective-permute-start.29 = (bf16[96,768]{1,0:T(8,128)(2,1)S(1)}, bf16[96,768]{1,0:T(8,128)(2,1)S(1)}, u32[]{:S(2)}, u32[]{:S(2)}) collective-permute-start(bf16[96,768]{1,0:T(8,128)(2,1)S(1)} %add_convert_fusion.4), channel_id=1, source_target_pairs={{0,16},{2,18},{4,20},{6,22},{8,24},{10,26},{12,28},{14,30},{16,0},... | collective-permute-start | bytes 442376 | tf_op jit(solution)/shard_map/ppermute | solution.py:638
  182.6 6.8 %collective-permute-start.31 = (bf16[96,768]{1,0:T(8,128)(2,1)S(1)}, bf16[96,768]{1,0:T(8,128)(2,1)S(1)}, u32[]{:S(2)}, u32[]{:S(2)}) collective-permute-start(bf16[96,768]{1,0:T(8,128)(2,1)S(1)} %fusion.8), channel_id=1, source_target_pairs={{0,16},{2,18},{4,20},{6,22},{8,24},{10,26},{12,28},{14,30},{16,0},... | collective-permute-start | bytes 442376 | tf_op jit(solution)/shard_map/ppermute | solution.py:638
  182.7 7.6 %collective-permute-start.30 = (bf16[96,768]{1,0:T(8,128)(2,1)S(1)}, bf16[96,768]{1,0:T(8,128)(2,1)S(1)}, u32[]{:S(2)}, u32[]{:S(2)}) collective-permute-start(bf16[96,768]{1,0:T(8,128)(2,1)S(1)} %fusion.8), channel_id=1, source_target_pairs={{0,8},{2,10},{4,12},{6,14},{8,0},{10,2},{12,4},{14,6},{16,24},{18,... | collective-permute-start | bytes 442376 | tf_op jit(solution)/shard_map/ppermute | solution.py:638
  189.4 5.1 %collective-permute-start.32 = (bf16[96,768]{1,0:T(8,128)(2,1)S(1)}, bf16[96,768]{1,0:T(8,128)(2,1)S(1)}, u32[]{:S(2)}, u32[]{:S(2)}) collective-permute-start(bf16[96,768]{1,0:T(8,128)(2,1)S(1)} %collective-permute-done.31), channel_id=1, source_target_pairs={{0,8},{2,10},{4,12},{6,14},{8,0},{10,2},{12,4},{14,6},{16,24},{18,... | collective-permute-start | bytes 442376 | tf_op jit(solution)/shard_map/ppermute | solution.py:638
  189.4 6.1 %collective-permute-start.33 = (bf16[4,208,768]{2,1,0:T(8,128)(2,1)S(1)}, bf16[4,208,768]{2,1,0:T(8,128)(2,1)S(1)}, u32[]{:S(2)}, u32[]{:S(2)}) collective-permute-start(bf16[4,208,768]{2,1,0:T(8,128)(2,1)S(1)} %pad_maximum_fusion.refs_0_), channel_id=1, source_target_pairs={{0,2},{2,0},{4,6},{6,4},{8,10},{10,8},{12,14},{14,12},{16,18},{18,... | collective-permute-start | bytes 3833864 | tf_op jit(solution)/shard_map/ppermute | solution.py:638
  194.7 3.1 %collective-permute-start.34 = (bf16[4,208,768]{2,1,0:T(8,128)(2,1)S(1)}, bf16[4,208,768]{2,1,0:T(8,128)(2,1)S(1)}, u32[]{:S(2)}, u32[]{:S(2)}) collective-permute-start(bf16[4,208,768]{2,1,0:T(8,128)(2,1)S(1)} %collective-permute-done.24.refs_1_), channel_id=1, source_target_pairs={{0,2},{2,0},{4,6},{6,4},{8,10},{10,8},{12,14},{14,12},{16,18},{18,... | collective-permute-start | bytes 3833864 | tf_op jit(solution)/shard_map/ppermute | solution.py:638
  194.8 15.7 %collective-permute-start.36 = (bf16[4,96,768]{2,1,0:T(8,128)(2,1)S(1)}, bf16[4,96,768]{2,1,0:T(8,128)(2,1)S(1)}, u32[]{:S(2)}, u32[]{:S(2)}) collective-permute-start(bf16[4,96,768]{2,1,0:T(8,128)(2,1)S(1)} %pad_maximum_fusion.1.refs_0_), channel_id=1, source_target_pairs={{0,4},{2,6},{4,0},{6,2},{8,12},{10,14},{12,8},{14,10},{16,20},{18,... | collective-permute-start | bytes 1769480 | tf_op jit(solution)/shard_map/ppermute | solution.py:638
  203.1 3.9 %collective-permute-start.35 = (f32[6,768]{1,0:T(8,128)S(1)}, f32[6,768]{1,0:T(8,128)S(1)}, u32[]{:S(2)}, u32[]{:S(2)}) collective-permute-start(f32[6,768]{1,0:T(8,128)S(1)} %slice.210), channel_id=1, source_target_pairs={{0,1},{1,0},{2,3},{3,2},{4,5},{5,4},{6,7},{7,6},{8,9},{9,8},{10,11... | collective-permute-start | bytes 55304 | tf_op jit(solution)/shard_map/ppermute | solution.py:634
  204.6 7.8 %collective-permute-start.37 = (bf16[4,96,768]{2,1,0:T(8,128)(2,1)S(1)}, bf16[4,96,768]{2,1,0:T(8,128)(2,1)S(1)}, u32[]{:S(2)}, u32[]{:S(2)}) collective-permute-start(bf16[4,96,768]{2,1,0:T(8,128)(2,1)S(1)} %pad_maximum_fusion.1.refs_0_), channel_id=1, source_target_pairs={{0,2},{2,0},{4,6},{6,4},{8,10},{10,8},{12,14},{14,12},{16,18},{18,... | collective-permute-start | bytes 1769480 | tf_op jit(solution)/shard_map/ppermute | solution.py:638
  210.5 2.0 collective-permute-start.38
  (24 other events, 52.3 us)

commit v5 on v4

--- a/solution.py
+++ b/solution.py
@@ -227,70 +227,76 @@
 
     lax.fori_loop(0, features // 256, tile, 0)
 
-def mlp_weights_kernel(count, split, me_ref, *refs):
-    inputs, refs = refs[: 4 * count], refs[4 * count :]
-    n_out = 5 if split else 3
-    gb1_ref, *outs = refs[:n_out]
-    held = refs[n_out : n_out + 4 * count]
-    nts = refs[n_out + 4 * count : n_out + 5 * count]
-    g1_ref, g2_ref, in_sems, unit_sems, out_sems = refs[n_out + 5 * count :]
-    blocks = [held[4 * b : 4 * b + 4] for b in range(count)]
-    hidden_size = g1_ref.shape[1]
-    features = g1_ref.shape[0]
+def fc2_weights_kernel(count, split, me_ref, *refs):
+    inputs, refs = refs[: 2 * count], refs[2 * count :]
+    n_out = 2 if split else 1
+    outs, held, (g_ref, in_sems, unit_sems, out_sems) = refs[:n_out], refs[n_out : n_out + 2 * count], refs[n_out + 2 * count :]
+    hidden_size = g_ref.shape[0]
     step = 384 if hidden_size % 384 == 0 else 128
-    wide = features if hidden_size % features == 0 else step
 
     def units_in(j):
         cols = ds(j * step, step)
-        return [pltpu.make_async_copy(inputs[4 * b + 2].at[:, cols], held[4 * b + 2].at[:, cols], unit_sems.at[b, j])
+        return [pltpu.make_async_copy(inputs[2 * b + 1].at[:, cols], held[2 * b + 1].at[:, cols], unit_sems.at[b, j])
                 for b in range(count)]
 
-    order = [4 * b + k for k in (0, 1) for b in range(count)]
-    copies = dict(zip(order, begin(in_sems, *[(inputs[i], held[i]) for i in order])))
+    copies = begin(in_sems, *[(inputs[2 * b], held[2 * b]) for b in range(count)])
     for j in range(hidden_size // step):
         for copy in units_in(j):
             copy.start()
-    last = [pltpu.make_async_copy(inputs[4 * b + 3], held[4 * b + 3], in_sems.at[2 * count + b]) for b in range(count)]
-    for copy in last:
-        copy.start()
-    finish_all([copies[4 * b] for b in range(count)])
-    for block, nt in zip(blocks, nts):
-        nt[...] = block[0][...].T
-    finish_all([copies[4 * b + 1] for b in range(count)])
-
-    def second(j, carry):
+    finish_all(copies)
+
+    def units(j, carry):
         finish_all(units_in(j))
         cols = ds(j * step, step)
-        g2_ref[cols, :] = sum(mm(hid_ref[:, cols], cot_ref[...], ROWS_ROWS) for _, cot_ref, hid_ref, _ in blocks).astype(BF)
+        g_ref[cols, :] = sum(
+            mm(held[2 * b + 1][:, cols], held[2 * b][...], ROWS_ROWS) for b in range(count)).astype(BF)
         return carry
 
-    def first(j, carry):
+    lax.fori_loop(0, hidden_size // step, units, 0)
+    if split:
+        finish_all(begin(out_sems, *[
+            (g_ref.at[ds(c * 768 + y * 384 + z * 96, 96), :], target.at[y_rel, z_rel])
+            for target, y_rel, z_rel, c, y, z in each_block(me_ref[0], *outs)]))
+    else:
+        finish_all(begin(out_sems, (g_ref, outs[0])))
+
+
+def fc1_weights_kernel(count, split, me_ref, *refs):
+    inputs, refs = refs[: 2 * count], refs[2 * count :]
+    n_out = 3 if split else 2
+    (gb1_ref, *outs), held = refs[:n_out], refs[n_out : n_out + 2 * count]
+    nts = refs[n_out + 2 * count : n_out + 3 * count]
+    g_ref, in_sems, out_sems = refs[n_out + 3 * count :]
+    features, hidden_size = g_ref.shape
+    wide = features if hidden_size % features == 0 else 128
+    copies = begin(in_sems, *[(inputs[2 * b + k], held[2 * b + k]) for k in range(2) for b in range(count)])
+    finish_all(copies[:count])
+    for b in range(count):
+        nts[b][...] = held[2 * b][...].T
+    finish_all(copies[count:])
+    gb1_ref[...] = sum(jnp.sum(held[2 * b + 1][...].astype(F32), axis=0, keepdims=True) for b in range(count))
+    sent = []
+    if split:
+        moves = [(c_rel, pltpu.make_async_copy(
+            g_ref.at[ds(y * 384 + z * 96, 96), ds(c * 768, 768)], target.at[y_rel, z_rel], out_sems.at[i]))
+            for i, ((c_rel, target), y_rel, z_rel, c, y, z) in enumerate(each_block(me_ref[0], *enumerate(outs)))]
+
+    def units(j, carry):
         cols = ds(j * wide, wide)
-        g1_ref[:, cols] = sum(mm(nt[...], block[3][:, cols]) for nt, block in zip(nts, blocks)).astype(BF)
+        g_ref[:, cols] = sum(mm(nts[b][...], held[2 * b + 1][:, cols]) for b in range(count)).astype(BF)
         return carry
 
-    lax.fori_loop(0, hidden_size // step, second, 0)
-    me = me_ref[0]
-    sent = []
-
-    def send(k, source, target):
-        sent.append(pltpu.make_async_copy(source, target, out_sems.at[k]))
-        sent[-1].start()
-
     if split:
-        for i, (target, y_rel, z_rel, c, y, z) in enumerate(each_block(me, outs[2], outs[3])):
-            send(i, g2_ref.at[ds(c * 768 + y * 384 + z * 96, 96), :], target.at[y_rel, z_rel])
+        core = me_ref[0] & 1
+        for c_rel in (1, 0):
+            units(core ^ c_rel, 0)
+            for which, move in moves:
+                if which == c_rel:
+                    move.start()
+        finish_all([move for _, move in moves])
     else:
-        send(0, g2_ref, outs[1])
-    finish_all(last)
-    gb1_ref[...] = sum(jnp.sum(block[3][...].astype(F32), axis=0, keepdims=True) for block in blocks)
-    lax.fori_loop(0, hidden_size // wide, first, 0)
-    if split:
-        for i, (target, y_rel, z_rel, c, y, z) in enumerate(each_block(me, outs[0], outs[1])):
-            send(16 + i, g1_ref.at[ds(y * 384 + z * 96, 96), ds(c * 768, 768)], target.at[y_rel, z_rel])
-    else:
-        send(1, g1_ref, outs[0])
-    finish_all(sent)
+        lax.fori_loop(0, hidden_size // wide, units, 0)
+        finish_all(begin(out_sems, (g_ref, outs[0])))
 
 
 def middle_back_kernel(own_ref, peer_ref, middle_ref, cot_ref, gain_ref, gmiddle_ref, branch_ref, sums_ref):
@@ -456,8 +462,11 @@
     gpatch_ref[...] = (gmiddle_ref[...] + norm_back(xhat, inv, line(gain_ref), gnorm)).astype(BF)
 
 
-def finish_kernel(me_ref, *refs):
-    sources, outs, held, wide, (in_sems, out_sems) = refs[:4], refs[4:6], refs[6:10], refs[10:12], refs[12:]
+def finish_kernel(y_rels, me_ref, *refs):
+    sources, refs = refs[:2], refs[2:]
+    if y_rels[0] == 1:
+        refs = refs[2:]
+    outs, held, wide, (in_sems, out_sems) = refs[:2], refs[2:4], refs[4:6], refs[6:]
     copies = begin(in_sems, *zip(sources, held))
     sent = []
 
@@ -466,8 +475,9 @@
         sent.append(pltpu.make_async_copy(wide[k].at[where], outs[k].at[where], out_sems.at[len(sent)]))
         sent[-1].start()
 
-    for source, y_rel, z_rel, c, y, z in each_block(me_ref[0], (0, 1), (2, 3)):
-        source = source[y_rel]
+    for source, y_rel, z_rel, c, y, z in each_block(me_ref[0], 0, 1):
+        if y_rel not in y_rels:
+            continue
         if z_rel == 0:
             copies[source].wait()
         piece = held[source].at[z_rel]
@@ -509,7 +519,7 @@
     return jax.ShapeDtypeStruct(dims, dtype)
 
 
-def call(kernel, outs, scratch, name, flops, smem, *args, far=(), far_outs=(), limit=VMEM_LIMIT):
+def call(kernel, outs, scratch, name, flops, smem, *args, far=(), far_outs=(), limit=VMEM_LIMIT, aliases=None):
     space = lambda is_far: pl.BlockSpec(memory_space=pltpu.HBM if is_far else pltpu.VMEM)
     in_specs = [pl.BlockSpec(memory_space=pltpu.SMEM)] * len(smem) + [space(i in far) for i in range(len(args))]
     return pl.pallas_call(
@@ -520,6 +530,7 @@
         scratch_shapes=scratch,
         compiler_params=pltpu.CompilerParams(vmem_limit_bytes=limit),
         cost_estimate=pl.CostEstimate(flops=flops, bytes_accessed=flops // 256, transcendentals=0),
+        input_output_aliases=aliases or {},
         name=name,
     )(*smem, *args)
 
@@ -572,14 +583,25 @@
     return call(mlp_kernel, outs, [], "mlp", SMALL, (), nm, cot, fc1, fc1_bias, fc2)
 
 
-def mlp_weights(split, me, blocks):
+def fc2_weights(split, me, blocks):
     rows, features = blocks[0][0].shape
-    hidden = blocks[0][2].shape[1]
-    grads = [shape_of(features, hidden, dtype=BF), shape_of(hidden, features, dtype=BF)]
-    outs = [shape_of(1, hidden)] + ([shape_of(2, 4, BLOCK, features, dtype=BF)] * 4 if split else grads)
+    hidden = blocks[0][1].shape[1]
+    grad = shape_of(hidden, features, dtype=BF)
+    outs = [shape_of(2, 4, BLOCK, features, dtype=BF)] * 2 if split else [grad]
     flat = [a for b in blocks for a in b]
-    scratch = like(*flat) + [pltpu.VMEM((features, rows), BF)] * len(blocks) + like(*grads) + dma(3 * len(blocks), (len(blocks), hidden // 128), 32)
-    return call(functools.partial(mlp_weights_kernel, len(blocks), split), outs, scratch, "mlp_weights", SMALL,
+    scratch = like(*flat, grad) + dma(len(blocks), (len(blocks), hidden // 128), 16)
+    return call(functools.partial(fc2_weights_kernel, len(blocks), split), outs, scratch, "fc2_weights", SMALL,
+                (me,), *flat, far=range(len(flat)), far_outs=range(len(outs)), limit=ALL_VMEM)
+
+
+def fc1_weights(split, me, blocks):
+    rows, features = blocks[0][0].shape
+    hidden = blocks[0][1].shape[1]
+    grad = shape_of(features, hidden, dtype=BF)
+    outs = [shape_of(1, hidden)] + ([shape_of(2, 4, BLOCK, features, dtype=BF)] * 2 if split else [grad])
+    flat = [a for b in blocks for a in b]
+    scratch = like(*flat) + [pltpu.VMEM((features, rows), BF)] * len(blocks) + like(grad) + dma(len(flat), 16)
+    return call(functools.partial(fc1_weights_kernel, len(blocks), split), outs, scratch, "fc1_weights", SMALL,
                 (me,), *flat, far=range(len(flat)), far_outs=range(1, len(outs)), limit=ALL_VMEM)
 
 
@@ -587,17 +609,17 @@
     rows, features = middle.shape
     return call(
         middle_back_kernel, [shape_of(rows, features), shape_of(rows, features, dtype=BF), shape_of(4, features)], [],
-        "middle_back", 20000 * SMALL, (), own, peer, middle, cot, gain)
-
-
-def attn_backward(windows, branch, x, kept, qkv, proj):
+        "middle_back", 10000 * SMALL, (), own, peer, middle, cot, gain)
+
+
+def attn_backward(windows, cost, branch, x, kept, qkv, proj):
     rows, features = branch.shape
     width = proj.shape[0]
     groups = width // LANES
     outs = [shape_of(3, rows, width, dtype=BF), shape_of(1, 2 * width), shape_of(groups, SLOT, GROUP * SLOT),
             shape_of(rows, features, dtype=BF), shape_of(2, features)]
     scratch = [pltpu.VMEM((groups, SLOT * (windows + 1), LANES), F32)] * 4
-    return call(functools.partial(attn_backward_kernel, windows), outs, scratch, "attn_backward", SMALL, (),
+    return call(functools.partial(attn_backward_kernel, windows), outs, scratch, "attn_backward", cost, (),
                 branch, x, *kept, qkv, proj)
 
 
@@ -618,9 +640,10 @@
                 own, peer, x, gain, gmiddle)[0]
 
 
-def finish(me, sources, *outs):
-    scratch = like(*sources, *outs) + dma(4, 16 * 4)
-    return call(finish_kernel, list(outs), scratch, "finish", SMALL, (me,), *sources, far=range(4), far_outs=range(len(outs)))
+def finish(me, y_rel, sources, outs, before=()):
+    scratch = like(*sources, *outs) + dma(2, 8 * 4)
+    return call(functools.partial(finish_kernel, (y_rel,)), list(outs), scratch, "finish", SMALL, (me,), *sources, *before,
+                far=range(2 + len(before)), far_outs=range(len(outs)), aliases={3: 0, 4: 1} if before else {})
 
 
 def finish_mlp(me, sources):
@@ -752,23 +775,26 @@
         outs.append(out_b)
         gmids.append(gmid_b)
     gmid_own, gmid_peer = own_sums(gmids)
-    gb1, *g_mlp = mlp_weights(fast, me, blocks)
+    g_fc2 = fc2_weights(fast, me, [(cot_b, hid) for _, cot_b, hid, _ in blocks])
+    gb1, *g_fc1 = fc1_weights(fast, me, [(after(nm_b, g_fc2[0]), gpre) for nm_b, _, _, gpre in blocks])
     outs = own_sums(outs)
     gmid_peer = after(gmid_peer, gb1)
     gmiddle, branch, sums2 = middle_back(gmid_own, gmid_peer, middle, cot, ln2[0])
     branches = blocks_of(branch)
     if fast:
-        keep1, send1, keep2, send2 = g_mlp
-        got1, got2 = after(flip(send1, CORE), branch), after(flip(send2, CORE), branch)
-        side1, side2 = side_send(keep1, got1), side_send(keep2, got2)
-        branches[0] = after(branches[0], side1, side2)
+        (keep2, send2), (keep1, send1) = g_fc1, g_fc2
+        got1 = after(flip(send1, CORE), branch)
+        side1 = side_send(keep1, got1)
+        branches[0] = after(branches[0], side1)
     backs, gparts = [], []
     for b, kept_b in enumerate(kept):
         if b == 1 and fast:
+            got2 = after(flip(send2, CORE), gparts[0])
+            side2 = side_send(keep2, got2)
             side1 = after(flip(side1, SIDE), gparts[0])
             line1 = line_sends(keep1, got1, side1)
-            branches[1] = after(branches[1], *line1, gparts[0])
-        *back, gpart, gsum = attn_backward(windows, branches[b], xs[b], kept_b[:4], qkv, proj)
+            branches[1] = after(branches[1], *line1, side2, gparts[0])
+        *back, gpart, gsum = attn_backward(windows, SMALL if b else 20000 * SMALL, branches[b], xs[b], kept_b[:4], qkv, proj)
         backs.append((*back, gsum))
         gparts.append(gpart)
     if fast:
@@ -789,7 +815,7 @@
         keep, send = g_attn
         got = flip(after(send, piece2), CORE)
         side = flip(side_send(keep, got), SIDE)
-        fc = jnp.concatenate([piece1, piece2, small], axis=0)
+        fc = jnp.concatenate([piece2, piece1, small], axis=0)
         fc_quad = jnp.stack([fc] + [after(r, output, gpatch) for r in gather_line(fc)])
         side = after(side, fc_quad, output, gpatch)
         line = sum_line(line_sends(keep, got, side))
@@ -799,10 +825,12 @@
         g_fc1, g_fc2, small = finish_mlp(me, (fc_quad, fc_pair, after(flip(fc_quad, CORE), quad), after(flip(fc_pair, CORE), quad)))
         totals = small[0:6] + across(small[0:6])
         pair = after(flip(quad, SIDE), totals)
-        gw, gproj = finish(me, (quad, pair, flip(quad, CORE), flip(pair, CORE)),
-                           shape_of(3, features, width), shape_of(width, features))
+        shapes = shape_of(3, features, width), shape_of(width, features)
+        half_done = finish(me, 0, (quad, flip(quad, CORE)), shapes)
+        pair = after(pair, half_done[0])
+        gw, gproj = finish(me, 1, (pair, flip(pair, CORE)), shapes, half_done)
     else:
-        g_fc1, g_fc2, gw, gproj = [g.astype(F32) for g in lax.psum((*g_mlp, *g_attn), "dp")]
+        g_fc1, g_fc2, gw, gproj = [g.astype(F32) for g in lax.psum((*g_fc1, *g_fc2, *g_attn), "dp")]
         gw, gproj = gw[:, :, :width], gproj[:width]
         small = lax.psum(small, "dp").astype(F32)
         totals = lax.psum(small[0:6], "mp")

time: 216 us -> 222 us (1.028)
  Pallas kernels: 89.9 us -> 94.2 us
  other arithmetic: 4.01 us -> 7.13 us
  waiting for transfers between devices: 70.9 us -> 68.3 us
    pallas_call x14 -> x16, Pallas kernels: 89.9 us -> 94.2 us  [call(): pl.pallas_call(kernel, out_shape=outs, in_specs=in_specs, out_specs=[spac...]
    convert_element_type x10 -> x9, other arithmetic: 1.35 us -> 4.5 us  [total_of(): return total.astype(BF)]
    ppermute x11, waiting for transfers between devices: 14.2 us -> 11.4 us  [across(): return lax.ppermute(v, 'mp', [(0, 1), (1, 0)])]
    unnamed x98 -> x94, local copies, waits for them, and re-layouts: 11.6 us -> 11.8 us
  transfers between devices with their start and end apart: 39 -> 39, of which waited for: 19 -> 19; matrix products, arithmetic and copies ran while one was open for 4% -> 5% of each run, Pallas kernels for 35% -> 36%
where the time goes in v5:
time: 222 us; the launch traced here: 221 us
  Pallas kernels  94.2 us (42%)
  waiting for transfers between devices  68.3 us (31%)
  starting transfers between devices  33.2 us (15%)
  local copies, waits for them, and re-layouts  14.7 us (7%)
  other arithmetic  7.13 us (3%)
  matrix products  2.4 us (1%)
    pallas_call x16, Pallas kernels, call(): pl.pallas_call(kernel, out_shape=outs, in_specs=in_specs, out_specs=[spac...  94.2 us
    ppermute x28, waiting for transfers between devices, flip(): return lax.ppermute(v, 'dp', [(i, i ^ bits) for i in range(16)])  56.9 us
    ppermute x28, starting transfers between devices, flip(): return lax.ppermute(v, 'dp', [(i, i ^ bits) for i in range(16)])  21.9 us
    unnamed x94, local copies, waits for them, and re-layouts  11.8 us
    ppermute x11, waiting for transfers between devices, across(): return lax.ppermute(v, 'mp', [(0, 1), (1, 0)])  11.4 us
    ppermute x11, starting transfers between devices, across(): return lax.ppermute(v, 'mp', [(0, 1), (1, 0)])  11.3 us
    convert_element_type x9, other arithmetic, total_of(): return total.astype(BF)  4.5 us
  transfers between devices with their start and end apart: 39, of which 19 were waited for; matrix products, arithmetic and copies ran while one was open for 5% of the time, Pallas kernels for 36%

profile of v5, /device:TPU:0, one launch (start us, length us, event | category | flops | bytes accessed | tf_op | source)
XLA Modules:
  0.0 221.4 jit_solution(17479666451129150256)
XLA Ops:
  1.3 2.9 %collective-permute-start.1 = (f32[8,49]{1,0:T(8,128)S(1)}, f32[8,49]{1,0:T(8,128)S(1)}, u32[]{:S(2)}, u32[]{:S(2)}) collective-permute-start(f32[8,49]{1,0:T(8,128)S(1)} %convert_element_type.294.valid_ref), channel_id=1, source_target_pairs={{0,1},{1,0},{2,3},{3,2},{4,5},{5,4},{6,7},{7,6},{8,9},{9,8},{10,11... | collective-permute-start | bytes 4712 | tf_op jit(solution)/shard_map/ppermute | solution.py:657
  4.3 1.6 collective-permute-done.1.valid_ref
  5.9 2.0 collective-permute-start.2
  7.9 1.0 constant_dynamic-slice_fusion
  10.9 12.1 %attn_forward.2 = (bf16[8,3,64,256]{3,2,1,0:T(8,128)(2,1)}, bf16[8,64,384]{2,1,0:T(8,128)(2,1)}, bf16[8,64,384]{2,1,0:T(8,128)(2,1)}, bf16[8,64,384]{2,1,0:T(8,1...) custom-call(bf16[392,768]{1,0:T(8,128)(2,1)} %bitcast.102, f32[768]{0:T(1024)} %gain_ref.9, f32[768]{0:T(1024)} %shift_ref.4, ...), custom_call_target="tpu_custom_call" | custom-call | flops 1000000 | bytes 3906 | tf_op jit(solution)/shard_map/attn_forward/pallas_call | solution.py:525
  23.0 0.8 copy-done.5
  23.8 12.2 %attn_forward.3 = (bf16[8,3,64,256]{3,2,1,0:T(8,128)(2,1)}, bf16[8,64,384]{2,1,0:T(8,128)(2,1)}, bf16[8,64,384]{2,1,0:T(8,128)(2,1)}, bf16[8,64,384]{2,1,0:T(8,1...) custom-call(bf16[392,768]{1,0:T(8,128)(2,1)} %copy-done.5, f32[768]{0:T(1024)} %gain_ref.9, f32[768]{0:T(1024)} %shift_ref.4, ...), custom_call_target="tpu_custom_call" | custom-call | flops 1000000 | bytes 3906 | tf_op jit(solution)/shard_map/attn_forward/pallas_call | solution.py:525
  36.0 2.9 %collective-permute-done.3.refs_0_ = bf16[192,768]{1,0:T(8,128)(2,1)} collective-permute-done((bf16[192,768]{1,0:T(8,128)(2,1)S(1)}, bf16[192,768]{1,0:T(8,128)(2,1)}, u32[]{:S(2)}, u32[]{:S(2)}) %collective-permute-start.3) | collective-permute-done | bytes 294944 | tf_op jit(solution)/shard_map/ppermute | solution.py:657
  39.2 2.4 %convolution_convert_fusion.own_in = bf16[392,768]{1,0:T(8,128)(2,1)} fusion(bf16[392,384]{1,0:T(8,128)(2,1)} %get-tuple-element.97.refs_1_, bf16[384,768]{1,0:T(8,128)(2,1)S(1)} %copy-done.4), kind=kOutput, calls=%fused_computation | convolution fusion | flops 231512064 | bytes 1492992 | tf_op jit(solution)/shard_map/dot_general | solution.py:755
  41.7 5.1 %collective-permute-done.4.peer_in = bf16[392,384]{1,0:T(8,128)(2,1)S(1)} collective-permute-done((bf16[392,384]{1,0:T(8,128)(2,1)}, bf16[392,384]{1,0:T(8,128)(2,1)S(1)}, u32[]{:S(2)}, u32[]{:S(2)}) %collective-permute-start.4) | collective-permute-done | bytes 301088 | tf_op jit(solution)/shard_map/ppermute | solution.py:657
  47.5 3.8 %middle.1 = (f32[392,768]{1,0:T(8,128)}, bf16[392,768]{1,0:T(8,128)(2,1)}) custom-call(s32[1]{0:T(128)} %bitcast.me_ref, bf16[392,768]{1,0:T(8,128)(2,1)} %bitcast.103, bf16[392,768]{1,0:T(8,128)(2,1)} %convolution_convert_fusion.own_in, bf16[392,384]{1,0:T(8,128)(2,1)} %copy-done.41, f32[768]{0:T(1024)} %bias_ref.5, f32[768]{0:T(1024)} %gain_ref.8, ...), custom_call_target="tpu_custom_call" | custom-call | flops 1000000 | bytes 3906 | tf_op jit(solution)/shard_map/middle/pallas_call | solution.py:525
  51.3 0.8 collective-permute-start.6
  52.2 1.1 copy-done.9
  53.3 6.1 %mlp.2 = (bf16[392,1536]{1,0:T(8,128)(2,1)S(1)}, bf16[392,1536]{1,0:T(8,128)(2,1)S(1)}, bf16[392,768]{1,0:T(8,128)(2,1)S(1)}, bf16[392,768]{1,0:T(8,128)(2,1)S(1)}) custom-call(bf16[392,768]{1,0:T(8,128)(2,1)S(1)} %copy-done.9, bf16[392,768]{1,0:T(8,128)(2,1)S(1)} %bitcast.108, bf16[768,1536]{1,0:T(8,128)(2,1)S(1)} %copy-done.1, ...), custom_call_target="tpu_custom_call" | custom-call | flops 1000000 | bytes 3906 | tf_op jit(solution)/shard_map/mlp/pallas_call | solution.py:525
  59.3 1.0 copy-done.14
  60.4 1.0 copy-done.16
  61.4 0.8 copy-done.21
  62.2 0.8 copy-done.32
  63.0 1.8 collective-permute-done.6.nm_ref.refs_2_
  64.8 8.2 %mlp.3 = (bf16[392,1536]{1,0:T(8,128)(2,1)S(1)}, bf16[392,1536]{1,0:T(8,128)(2,1)S(1)}, bf16[392,768]{1,0:T(8,128)(2,1)S(1)}, bf16[392,768]{1,0:T(8,128)(2,1)}) custom-call(bf16[392,768]{1,0:T(8,128)(2,1)S(1)} %collective-permute-done.6.nm_ref.refs_2_, bf16[392,768]{1,0:T(8,128)(2,1)} %collective-permute-done.2.cot_ref.refs_2_, ...), custom_call_target="tpu_custom_call" | custom-call | flops 1000000 | bytes 3906 | tf_op jit(solution)/shard_map/mlp/pallas_call | solution.py:525
  73.0 1.0 copy-done.15
  74.0 1.1 copy-done.17
  75.1 1.1 collective-permute-start.8
  76.2 7.3 %fc2_weights.1 = (bf16[2,4,96,768]{3,2,1,0:T(8,128)(2,1)}, bf16[2,4,96,768]{3,2,1,0:T(8,128)(2,1)}) custom-call(s32[1]{0:T(128)} %bitcast.me_ref, bf16[392,768]{1,0:T(8,128)(2,1)} %bitcast.107, bf16[392,1536]{1,0:T(8,128)(2,1)} %copy-done.16, bf16[392,768]{1,0:T(8,128)(2,1)} %collective-permute-done.2.cot_ref.refs_2_, bf16[392,1536]{1,0:T(8,128)(2,1)} %copy-done.17), custom_call_target="tpu_custom_call" | custom-call | flops 1000000 | bytes 3906 | tf_op jit(solution)/shard_map/fc2_weights/pallas_call | solution.py:525
  83.6 6.8 %fc1_weights.1 = (f32[1,1536]{1,0:T(1,128)}, bf16[2,4,96,768]{3,2,1,0:T(8,128)(2,1)}, bf16[2,4,96,768]{3,2,1,0:T(8,128)(2,1)}) custom-call(s32[1]{0:T(128)} %bitcast.me_ref, bf16[392,768]{1,0:T(8,128)(2,1)} %get-tuple-element.114.nm_ref.refs_0_, bf16[392,1536]{1,0:T(8,128)(2,1)} %copy-done.14, bf16[392,768]{1,0:T(8,128)(2,1)} %copy-done.10, ...), custom_call_target="tpu_custom_call" | custom-call | flops 1000000 | bytes 3906 | tf_op jit(solution)/shard_map/fc1_weights/pallas_call | solution.py:525
  90.9 0.8 copy-done.34
  91.7 1.1 copy-done.35
  92.8 1.1 middle_back.1
  93.9 1.0 collective-permute-start.10
  95.0 1.2 fusion
  96.2 1.6 collective-permute-start.11
  97.8 9.7 %attn_backward.2 = (bf16[3,392,384]{2,1,0:T(8,128)(2,1)S(1)}, f32[1,768]{1,0:T(1,128)S(1)}, f32[3,64,256]{2,1,0:T(8,128)S(1)}, bf16[392,768]{1,0:T(8,128)(2,1)S(1)}, f32[2,768]{1,0:T(2,128)S(1)}) custom-call(bf16[392,768]{1,0:T(8,128)(2,1)S(1)} %get-tuple-element.146.branch_ref.refs_2_, bf16[392,768]{1,0:T(8,128)(2,1)S(1)} %bitcast.104, ...), custom_call_target="tpu_custom_call" | custom-call | flops 20000000000 | bytes 78125000 | tf_op jit(solution)/shard_map/attn_backward/pallas_call | solution.py:525
  108.3 1.1 collective-permute-start.7
  109.4 3.1 %collective-permute-done.11 = bf16[4,96,768]{2,1,0:T(8,128)(2,1)S(1)} collective-permute-done((bf16[4,96,768]{2,1,0:T(8,128)(2,1)S(1)}, bf16[4,96,768]{2,1,0:T(8,128)(2,1)S(1)}, u32[]{:S(2)}, u32[]{:S(2)}) %collective-permute-start.11) | collective-permute-done | bytes 589856 | tf_op jit(solution)/shard_map/ppermute | solution.py:661
  112.4 1.2 fusion.20
  113.7 3.7 %collective-permute-start.18 = (bf16[96,768]{1,0:T(8,128)(2,1)S(1)}, bf16[96,768]{1,0:T(8,128)(2,1)S(1)}, u32[]{:S(2)}, u32[]{:S(2)}) collective-permute-start(bf16[96,768]{1,0:T(8,128)(2,1)S(1)} %get-tuple-element.190), channel_id=1, source_target_pairs={{0,24},{2,26},{4,28},{6,30},{8,16},{10,18},{12,20},{14,22},{16,8},... | collective-permute-start | bytes 442376 | tf_op jit(solution)/shard_map/ppermute | solution.py:661
  117.3 0.8 collective-permute-start.16
  118.2 9.7 %attn_backward.3 = (bf16[3,392,384]{2,1,0:T(8,128)(2,1)S(1)}, f32[1,768]{1,0:T(1,128)S(1)}, f32[3,64,256]{2,1,0:T(8,128)S(1)}, bf16[392,768]{1,0:T(8,128)(2,1)S(1)}, f32[2,768]{1,0:T(2,128)S(1)}) custom-call(bf16[392,768]{1,0:T(8,128)(2,1)S(1)} %collective-permute-done.10.branch_ref.refs_9_, bf16[392,768]{1,0:T(8,128)(2,1)S(1)} %copy-done.6, ...), custom_call_target="tpu_custom_call" | custom-call | flops 1000000 | bytes 3906 | tf_op jit(solution)/shard_map/attn_backward/pallas_call | solution.py:525
  128.0 1.4 fusion.9
  129.3 3.7 %collective-permute-start.20 = (bf16[96,768]{1,0:T(8,128)(2,1)S(1)}, bf16[96,768]{1,0:T(8,128)(2,1)S(1)}, u32[]{:S(2)}, u32[]{:S(2)}) collective-permute-start(bf16[96,768]{1,0:T(8,128)(2,1)S(1)} %get-tuple-element.187), channel_id=1, source_target_pairs={{0,24},{2,26},{4,28},{6,30},{8,16},{10,18},{12,20},{14,22},{16,8},... | collective-permute-start | bytes 442376 | tf_op jit(solution)/shard_map/ppermute | solution.py:661
  133.8 5.8 %attn_weights.1 = (bf16[2,4,96,768]{3,2,1,0:T(8,128)(2,1)S(1)}, bf16[2,4,96,768]{3,2,1,0:T(8,128)(2,1)S(1)}, bf16[16,768]{1,0:T(8,128)(2,1)S(1)}) custom-call(s32[1]{0:T(128)} %bitcast.me_ref, f32[4,768]{1,0:T(4,128)S(1)} %get-tuple-element.141.sums2_ref, f32[1,1536]{1,0:T(1,128)S(1)} %copy-done.29, bf16[768,392]{1,0:T(8,128)(2,1)S(1)} %copy-done.18, ...), custom_call_target="tpu_custom_call" | custom-call | flops 1000000 | bytes 3906 | tf_op jit(solution)/shard_map/attn_weights/pallas_call | solution.py:525
  139.6 3.9 %collective-permute-done.19 = bf16[96,768]{1,0:T(8,128)(2,1)S(1)} collective-permute-done((bf16[96,768]{1,0:T(8,128)(2,1)S(1)}, bf16[96,768]{1,0:T(8,128)(2,1)S(1)}, u32[]{:S(2)}, u32[]{:S(2)}) %collective-permute-start.19) | collective-permute-done | bytes 147488 | tf_op jit(solution)/shard_map/ppermute | solution.py:661
  144.5 2.1 collective-permute-done.25
  146.7 1.6 collective-permute-start.26
  148.8 12.5 %collective-permute-done.22 = bf16[208,768]{1,0:T(8,128)(2,1)S(1)} collective-permute-done((bf16[208,768]{1,0:T(8,128)(2,1)S(1)}, bf16[208,768]{1,0:T(8,128)(2,1)S(1)}, u32[]{:S(2)}, u32[]{:S(2)}) %collective-permute-start.22) | collective-permute-done | bytes 319520 | tf_op jit(solution)/shard_map/ppermute | solution.py:661
  161.4 1.1 add_convert_fusion
  162.4 1.7 input_back.1
  164.8 6.5 %collective-permute-done.23 = bf16[208,768]{1,0:T(8,128)(2,1)S(1)} collective-permute-done((bf16[208,768]{1,0:T(8,128)(2,1)S(1)}, bf16[208,768]{1,0:T(8,128)(2,1)S(1)}, u32[]{:S(2)}, u32[]{:S(2)}) %collective-permute-start.23) | collective-permute-done | bytes 319520 | tf_op jit(solution)/shard_map/ppermute | solution.py:661
  171.4 1.1 collective-permute-start.24
  173.0 1.7 collective-permute-start.27
  174.7 4.2 %collective-permute-done.28 = bf16[96,768]{1,0:T(8,128)(2,1)S(1)} collective-permute-done((bf16[96,768]{1,0:T(8,128)(2,1)S(1)}, bf16[96,768]{1,0:T(8,128)(2,1)S(1)}, u32[]{:S(2)}, u32[]{:S(2)}) %collective-permute-start.28) | collective-permute-done | bytes 147488 | tf_op jit(solution)/shard_map/ppermute | solution.py:661
  179.0 1.2 collective-permute-start.29
  180.2 1.4 collective-permute-done.27
  181.5 7.2 %collective-permute-done.29 = bf16[96,768]{1,0:T(8,128)(2,1)S(1)} collective-permute-done((bf16[96,768]{1,0:T(8,128)(2,1)S(1)}, bf16[96,768]{1,0:T(8,128)(2,1)S(1)}, u32[]{:S(2)}, u32[]{:S(2)}) %collective-permute-start.29) | collective-permute-done | bytes 147488 | tf_op jit(solution)/shard_map/ppermute | solution.py:661
  189.0 2.5 %collective-permute-start.30 = (bf16[96,768]{1,0:T(8,128)(2,1)S(1)}, bf16[96,768]{1,0:T(8,128)(2,1)S(1)}, u32[]{:S(2)}, u32[]{:S(2)}) collective-permute-start(bf16[96,768]{1,0:T(8,128)(2,1)S(1)} %fusion.8), channel_id=1, source_target_pairs={{0,8},{2,10},{4,12},{6,14},{8,0},{10,2},{12,4},{14,6},{16,24},{18,... | collective-permute-start | bytes 442376 | tf_op jit(solution)/shard_map/ppermute | solution.py:661
  191.5 4.7 %collective-permute-done.31 = bf16[96,768]{1,0:T(8,128)(2,1)S(1)} collective-permute-done((bf16[96,768]{1,0:T(8,128)(2,1)S(1)}, bf16[96,768]{1,0:T(8,128)(2,1)S(1)}, u32[]{:S(2)}, u32[]{:S(2)}) %collective-permute-start.31) | collective-permute-done | bytes 147488 | tf_op jit(solution)/shard_map/ppermute | solution.py:661
  196.2 0.8 collective-permute-done.30
  197.0 4.4 %collective-permute-done.32 = bf16[96,768]{1,0:T(8,128)(2,1)S(1)} collective-permute-done((bf16[96,768]{1,0:T(8,128)(2,1)S(1)}, bf16[96,768]{1,0:T(8,128)(2,1)S(1)}, u32[]{:S(2)}, u32[]{:S(2)}) %collective-permute-start.32) | collective-permute-done | bytes 147488 | tf_op jit(solution)/shard_map/ppermute | solution.py:661
  202.5 2.0 collective-permute-done.34.refs_3_
  204.5 5.4 %finish_mlp.1 = (f32[768,1536]{1,0:T(8,128)}, f32[1536,768]{1,0:T(8,128)}, f32[16,768]{1,0:T(8,128)S(1)}) custom-call(s32[1]{0:T(128)} %bitcast.me_ref, bf16[4,208,768]{2,1,0:T(8,128)(2,1)S(1)} %pad_maximum_fusion.refs_0_, bf16[4,208,768]{2,1,0:T(8,128)(2,1)S(1)} %collective-permute-done.24.refs_1_, ...), custom_call_target="tpu_custom_call" | custom-call | flops 1000000 | bytes 3906 | tf_op jit(solution)/shard_map/finish_mlp/pallas_call | solution.py:525
  209.9 1.3 collective-permute-start.35
  211.2 1.9 finish.2
  213.8 3.5 %collective-permute-done.36.refs_0_ = bf16[4,96,768]{2,1,0:T(8,128)(2,1)S(1)} collective-permute-done((bf16[4,96,768]{2,1,0:T(8,128)(2,1)S(1)}, bf16[4,96,768]{2,1,0:T(8,128)(2,1)S(1)}, u32[]{:S(2)}, u32[]{:S(2)}) %collective-permute-start.36) | collective-permute-done | bytes 589856 | tf_op jit(solution)/shard_map/ppermute | solution.py:661
  219.3 1.9 finish.3
  (151 shorter events, 12.9 us)
Async XLA Ops:
  1.3 9.6 %copy-start.43 = (f32[8,49]{1,0:T(8,128)}, f32[8,49]{1,0:T(8,128)S(1)}, u32[]{:S(2)}) copy-start(f32[8,49]{1,0:T(8,128)S(1)} %convert_element_type.294.valid_ref) | copy-start | bytes 4708
  1.3 4.5 %collective-permute-start.1 = (f32[8,49]{1,0:T(8,128)S(1)}, f32[8,49]{1,0:T(8,128)S(1)}, u32[]{:S(2)}, u32[]{:S(2)}) collective-permute-start(f32[8,49]{1,0:T(8,128)S(1)} %convert_element_type.294.valid_ref), channel_id=1, source_target_pairs={{0,1},{1,0},{2,3},{3,2},{4,5},{5,4},{6,7},{7,6},{8,9},{9,8},{10,11... | collective-permute-start | bytes 4712 | tf_op jit(solution)/shard_map/ppermute | solution.py:657
  4.3 18.7 %collective-permute-start = (bf16[392,768]{1,0:T(8,128)(2,1)}, bf16[392,768]{1,0:T(8,128)(2,1)S(1)}, u32[]{:S(2)}, u32[]{:S(2)}) collective-permute-start(bf16[392,768]{1,0:T(8,128)(2,1)} %bitcast.101), channel_id=1, source_target_pairs={{0,1},{1,0},{2,3},{3,2},{4,5},{5,4},{6,7},{7,6},{8,9},{9,8},{10,11... | collective-permute-start | bytes 1806344 | tf_op jit(solution)/shard_map/ppermute | solution.py:657
  5.9 17.1 %copy-start.46 = (f32[8,49]{1,0:T(8,128)}, f32[8,49]{1,0:T(8,128)S(1)}, u32[]{:S(2)}) copy-start(f32[8,49]{1,0:T(8,128)S(1)} %collective-permute-done.1.valid_ref) | copy-start | bytes 4708
  5.9 33.0 %collective-permute-start.2 = (bf16[392,768]{1,0:T(8,128)(2,1)}, bf16[392,768]{1,0:T(8,128)(2,1)}, u32[]{:S(2)}, u32[]{:S(2)}) collective-permute-start(bf16[392,768]{1,0:T(8,128)(2,1)} %bitcast.106), channel_id=1, source_target_pairs={{0,1},{1,0},{2,3},{3,2},{4,5},{5,4},{6,7},{7,6},{8,9},{9,8},{10,11... | collective-permute-start | bytes 1806344 | tf_op jit(solution)/shard_map/ppermute | solution.py:657
  8.9 30.0 %collective-permute-start.3 = (bf16[192,768]{1,0:T(8,128)(2,1)S(1)}, bf16[192,768]{1,0:T(8,128)(2,1)}, u32[]{:S(2)}, u32[]{:S(2)}) collective-permute-start(bf16[192,768]{1,0:T(8,128)(2,1)S(1)} %constant_dynamic-slice_fusion), channel_id=1, source_target_pairs={{0,1},{1,0},{2,3},{3,2},{4,5},{5,4},{6,7},{7,6},{8,9},{9,8},{10,11... | collective-permute-start | bytes 884744 | tf_op jit(solution)/shard_map/ppermute | solution.py:657
  10.9 28.3 %copy-start.4 = (bf16[384,768]{1,0:T(8,128)(2,1)S(1)}, bf16[384,768]{1,0:T(8,128)(2,1)}, u32[]{:S(2)}) copy-start(bf16[384,768]{1,0:T(8,128)(2,1)} %proj_ref.3) | copy-start | bytes 1769476
  23.8 28.3 %copy-start.2 = (bf16[1536,768]{1,0:T(8,128)(2,1)S(1)}, bf16[1536,768]{1,0:T(8,128)(2,1)}, u32[]{:S(2)}) copy-start(bf16[1536,768]{1,0:T(8,128)(2,1)} %fc2_ref.3) | copy-start | bytes 7077892
  38.9 7.9 %collective-permute-start.4 = (bf16[392,384]{1,0:T(8,128)(2,1)}, bf16[392,384]{1,0:T(8,128)(2,1)S(1)}, u32[]{:S(2)}, u32[]{:S(2)}) collective-permute-start(bf16[392,384]{1,0:T(8,128)(2,1)} %get-tuple-element.102.refs_8_), channel_id=1, source_target_pairs={{0,1},{1,0},{2,3},{3,2},{4,5},{5,4},{6,7},{7,6},{8,9},{9,8},{10,11... | collective-permute-start | bytes 903176 | tf_op jit(solution)/shard_map/ppermute | solution.py:657
  39.2 2.4 %collective-permute-start.5 = (bf16[192,768]{1,0:T(8,128)(2,1)}, bf16[192,768]{1,0:T(8,128)(2,1)S(1)}, u32[]{:S(2)}, u32[]{:S(2)}) collective-permute-start(bf16[192,768]{1,0:T(8,128)(2,1)} %collective-permute-done.3.refs_0_), channel_id=1, source_target_pairs={{0,2},{2,0},{4,6},{6,4},{8,10},{10,8},{12,14},{14,12},{16,18},{18,... | collective-permute-start | bytes 884744 | tf_op jit(solution)/shard_map/ppermute | solution.py:661
  39.2 12.9 %copy-start.1 = (bf16[768,1536]{1,0:T(8,128)(2,1)S(1)}, bf16[768,1536]{1,0:T(8,128)(2,1)}, u32[]{:S(2)}) copy-start(bf16[768,1536]{1,0:T(8,128)(2,1)} %fc1_ref.3) | copy-start | bytes 7077892
  41.6 10.5 %copy-start.44 = (f32[1536]{0:T(1024)S(1)}, f32[1536]{0:T(1024)}, u32[]{:S(2)}) copy-start(f32[1536]{0:T(1024)} %param.28) | copy-start | bytes 18436
  41.6 10.5 %copy-start.7 = (bf16[8,49,768]{2,0,1:T(8,128)(2,1)S(1)}, bf16[8,49,768]{2,0,1:T(8,128)(2,1)}, u32[]{:S(2)}) copy-start(bf16[8,49,768]{2,0,1:T(8,128)(2,1)} %param.31) | copy-start | bytes 1806340
  51.3 13.5 %collective-permute-start.6 = (bf16[392,768]{1,0:T(8,128)(2,1)}, bf16[392,768]{1,0:T(8,128)(2,1)S(1)}, u32[]{:S(2)}, u32[]{:S(2)}) collective-permute-start(bf16[392,768]{1,0:T(8,128)(2,1)} %get-tuple-element.114.nm_ref.refs_0_), channel_id=1, source_target_pairs={{0,1},{1,0},{2,3},{3,2},{4,5},{5,4},{6,7},{7,6},{8,9},{9,8},{10,11... | collective-permute-start | bytes 1806344 | tf_op jit(solution)/shard_map/ppermute | solution.py:657
  64.8 8.2 %copy-start.10 = (bf16[392,768]{1,0:T(8,128)(2,1)}, bf16[392,768]{1,0:T(8,128)(2,1)S(1)}, u32[]{:S(2)}) copy-start(bf16[392,768]{1,0:T(8,128)(2,1)S(1)} %collective-permute-done.6.nm_ref.refs_2_) | copy-start | bytes 1806340
  75.1 15.8 %collective-permute-start.8 = (bf16[392,768]{1,0:T(8,128)(2,1)}, bf16[392,768]{1,0:T(8,128)(2,1)S(1)}, u32[]{:S(2)}, u32[]{:S(2)}) collective-permute-start(bf16[392,768]{1,0:T(8,128)(2,1)} %get-tuple-element.110), channel_id=1, source_target_pairs={{0,1},{1,0},{2,3},{3,2},{4,5},{5,4},{6,7},{7,6},{8,9},{9,8},{10,11... | collective-permute-start | bytes 1806344 | tf_op jit(solution)/shard_map/ppermute | solution.py:657
  83.4 11.5 %collective-permute-start.9 = (bf16[2,4,96,768]{3,2,1,0:T(8,128)(2,1)}, bf16[2,4,96,768]{3,2,1,0:T(8,128)(2,1)}, u32[]{:S(2)}, u32[]{:S(2)}) collective-permute-start(bf16[2,4,96,768]{3,2,1,0:T(8,128)(2,1)} %get-tuple-element.121), channel_id=1, source_target_pairs={{0,2},{2,0},{4,6},{6,4},{8,10},{10,8},{12,14},{14,12},{16,18},{18,... | collective-permute-start | bytes 3538952 | tf_op jit(solution)/shard_map/ppermute | solution.py:661
  83.5 8.2 %copy-start.8 = (bf16[8,49,768]{2,0,1:T(8,128)(2,1)S(1)}, bf16[8,49,768]{2,0,1:T(8,128)(2,1)}, u32[]{:S(2)}) copy-start(bf16[8,49,768]{2,0,1:T(8,128)(2,1)} %param.31) | copy-start | bytes 1806340
  83.5 8.2 %copy-start.13 = (f32[392,768]{1,0:T(8,128)S(1)}, f32[392,768]{1,0:T(8,128)}, u32[]{:S(2)}) copy-start(f32[392,768]{1,0:T(8,128)} %get-tuple-element.104.middle_ref) | copy-start | bytes 3612676
  83.5 8.2 %copy-start.30 = (f32[768]{0:T(1024)S(1)}, f32[768]{0:T(1024)}, u32[]{:S(2)}) copy-start(f32[768]{0:T(1024)} %gain_ref.8) | copy-start | bytes 9220
  83.6 8.1 %copy-start.33 = (bf16[392,768]{1,0:T(8,128)(2,1)S(1)}, bf16[392,768]{1,0:T(8,128)(2,1)}, u32[]{:S(2)}) copy-start(bf16[392,768]{1,0:T(8,128)(2,1)} %copy-done.32) | copy-start | bytes 1806340
  90.4 17.2 %collective-permute-start.12 = (bf16[2,4,96,768]{3,2,1,0:T(8,128)(2,1)}, bf16[2,4,96,768]{3,2,1,0:T(8,128)(2,1)S(1)}, u32[]{:S(2)}, u32[]{:S(2)}) collective-permute-start(bf16[2,4,96,768]{3,2,1,0:T(8,128)(2,1)} %get-tuple-element.131), channel_id=1, source_target_pairs={{0,2},{2,0},{4,6},{6,4},{8,10},{10,8},{12,14},{14,12},{16,18},{18,... | collective-permute-start | bytes 3538952 | tf_op jit(solution)/shard_map/ppermute | solution.py:661
  93.9 23.4 %collective-permute-start.10 = (bf16[392,768]{1,0:T(8,128)(2,1)S(1)}, bf16[392,768]{1,0:T(8,128)(2,1)S(1)}, u32[]{:S(2)}, u32[]{:S(2)}) collective-permute-start(bf16[392,768]{1,0:T(8,128)(2,1)S(1)} %get-tuple-element.146.branch_ref.refs_2_), channel_id=1, source_target_pairs={{0,1},{1,0},{2,3},{3,2},{4,5},{5,4},{6,7},{7,6},{8,9},{9,8},{10,11... | collective-permute-start | bytes 1806344 | tf_op jit(solution)/shard_map/ppermute | solution.py:657
  96.2 16.3 %collective-permute-start.11 = (bf16[4,96,768]{2,1,0:T(8,128)(2,1)S(1)}, bf16[4,96,768]{2,1,0:T(8,128)(2,1)S(1)}, u32[]{:S(2)}, u32[]{:S(2)}) collective-permute-start(bf16[4,96,768]{2,1,0:T(8,128)(2,1)S(1)} %fusion), channel_id=1, source_target_pairs={{0,4},{2,6},{4,0},{6,2},{8,12},{10,14},{12,8},{14,10},{16,20},{18,... | collective-permute-start | bytes 1769480 | tf_op jit(solution)/shard_map/ppermute | solution.py:661
  97.8 9.8 %copy-start.40 = (bf16[2,4,96,768]{3,2,1,0:T(8,128)(2,1)S(1)}, bf16[2,4,96,768]{3,2,1,0:T(8,128)(2,1)}, u32[]{:S(2)}) copy-start(bf16[2,4,96,768]{3,2,1,0:T(8,128)(2,1)} %get-tuple-element.130) | copy-start | bytes 3538948
  107.6 10.6 %copy-start.24 = (bf16[8,64,384]{2,1,0:T(8,128)(2,1)S(1)}, bf16[8,64,384]{2,1,0:T(8,128)(2,1)}, u32[]{:S(2)}) copy-start(bf16[8,64,384]{2,1,0:T(8,128)(2,1)} %get-tuple-element.136.k_ref) | copy-start | bytes 1179652
  107.6 10.6 %copy-start.25 = (bf16[8,64,384]{2,1,0:T(8,128)(2,1)S(1)}, bf16[8,64,384]{2,1,0:T(8,128)(2,1)}, u32[]{:S(2)}) copy-start(bf16[8,64,384]{2,1,0:T(8,128)(2,1)} %get-tuple-element.137.v_ref) | copy-start | bytes 1179652
  107.7 10.4 %copy-start.6 = (bf16[392,768]{1,0:T(8,128)(2,1)S(1)}, bf16[392,768]{1,0:T(8,128)(2,1)}, u32[]{:S(2)}) copy-start(bf16[392,768]{1,0:T(8,128)(2,1)} %copy-done.5) | copy-start | bytes 1806340
  107.7 10.4 %copy-start.20 = (bf16[8,3,64,256]{3,2,1,0:T(8,128)(2,1)S(1)}, bf16[8,3,64,256]{3,2,1,0:T(8,128)(2,1)}, u32[]{:S(2)}) copy-start(bf16[8,3,64,256]{3,2,1,0:T(8,128)(2,1)} %get-tuple-element.134.prob_ref) | copy-start | bytes 2359300
  107.7 10.4 %copy-start.23 = (bf16[8,64,384]{2,1,0:T(8,128)(2,1)S(1)}, bf16[8,64,384]{2,1,0:T(8,128)(2,1)}, u32[]{:S(2)}) copy-start(bf16[8,64,384]{2,1,0:T(8,128)(2,1)} %get-tuple-element.135.q_ref) | copy-start | bytes 1179652
  107.8 20.1 %collective-permute-start.14 = (bf16[4,96,768]{2,1,0:T(8,128)(2,1)S(1)}, bf16[4,96,768]{2,1,0:T(8,128)(2,1)S(1)}, u32[]{:S(2)}, u32[]{:S(2)}) collective-permute-start(bf16[4,96,768]{2,1,0:T(8,128)(2,1)S(1)} %fusion.1), channel_id=1, source_target_pairs={{0,4},{2,6},{4,0},{6,2},{8,12},{10,14},{12,8},{14,10},{16,20},{18,... | collective-permute-start | bytes 1769480 | tf_op jit(solution)/shard_map/ppermute | solution.py:661
  108.3 25.5 %collective-permute-start.7 = (bf16[392,768]{1,0:T(8,128)(2,1)S(1)}, bf16[392,768]{1,0:T(8,128)(2,1)S(1)}, u32[]{:S(2)}, u32[]{:S(2)}) collective-permute-start(bf16[392,768]{1,0:T(8,128)(2,1)S(1)} %get-tuple-element.109), channel_id=1, source_target_pairs={{0,1},{1,0},{2,3},{3,2},{4,5},{5,4},{6,7},{7,6},{8,9},{9,8},{10,11... | collective-permute-start | bytes 1806344 | tf_op jit(solution)/shard_map/ppermute | solution.py:657
  113.7 14.3 %collective-permute-start.18 = (bf16[96,768]{1,0:T(8,128)(2,1)S(1)}, bf16[96,768]{1,0:T(8,128)(2,1)S(1)}, u32[]{:S(2)}, u32[]{:S(2)}) collective-permute-start(bf16[96,768]{1,0:T(8,128)(2,1)S(1)} %get-tuple-element.190), channel_id=1, source_target_pairs={{0,24},{2,26},{4,28},{6,30},{8,16},{10,18},{12,20},{14,22},{16,8},... | collective-permute-start | bytes 442376 | tf_op jit(solution)/shard_map/ppermute | solution.py:661
  117.3 10.6 %collective-permute-start.17 = (bf16[96,768]{1,0:T(8,128)(2,1)S(1)}, bf16[96,768]{1,0:T(8,128)(2,1)S(1)}, u32[]{:S(2)}, u32[]{:S(2)}) collective-permute-start(bf16[96,768]{1,0:T(8,128)(2,1)S(1)} %get-tuple-element.191), channel_id=1, source_target_pairs={{0,16},{2,18},{4,20},{6,22},{8,24},{10,26},{12,28},{14,30},{16,0},... | collective-permute-start | bytes 442376 | tf_op jit(solution)/shard_map/ppermute | solution.py:661
  117.3 10.6 %collective-permute-start.16 = (bf16[96,768]{1,0:T(8,128)(2,1)S(1)}, bf16[96,768]{1,0:T(8,128)(2,1)S(1)}, u32[]{:S(2)}, u32[]{:S(2)}) collective-permute-start(bf16[96,768]{1,0:T(8,128)(2,1)S(1)} %get-tuple-element.192), channel_id=1, source_target_pairs={{0,8},{2,10},{4,12},{6,14},{8,0},{10,2},{12,4},{14,6},{16,24},{18,... | collective-permute-start | bytes 442376 | tf_op jit(solution)/shard_map/ppermute | solution.py:661
  127.9 5.9 %copy-start.12 = (bf16[392,384]{1,0:T(8,128)(2,1)S(1)}, bf16[392,384]{1,0:T(8,128)(2,1)}, u32[]{:S(2)}) copy-start(bf16[392,384]{1,0:T(8,128)(2,1)} %get-tuple-element.97.refs_1_) | copy-start | bytes 903172
  127.9 5.9 %copy-start.18 = (bf16[768,392]{1,0:T(8,128)(2,1)S(1)}, bf16[768,392]{1,0:T(8,128)(2,1)}, u32[]{:S(2)}) copy-start(bf16[768,392]{1,0:T(8,128)(2,1)} %get-tuple-element.142.refs_0_) | copy-start | bytes 1806340
  127.9 5.9 %copy-start.19 = (bf16[768,392]{1,0:T(8,128)(2,1)S(1)}, bf16[768,392]{1,0:T(8,128)(2,1)}, u32[]{:S(2)}) copy-start(bf16[768,392]{1,0:T(8,128)(2,1)} %get-tuple-element.151.refs_7_) | copy-start | bytes 1806340
  127.9 5.9 %copy-start.26 = (bf16[392,384]{1,0:T(8,128)(2,1)S(1)}, bf16[392,384]{1,0:T(8,128)(2,1)}, u32[]{:S(2)}) copy-start(bf16[392,384]{1,0:T(8,128)(2,1)} %get-tuple-element.102.refs_8_) | copy-start | bytes 903172
  127.9 5.9 %copy-start.29 = (f32[1,1536]{1,0:T(1,128)S(1)}, f32[1,1536]{1,0:T(1,128)}, u32[]{:S(2)}) copy-start(f32[1,1536]{1,0:T(1,128)} %get-tuple-element.118.gb1_ref) | copy-start | bytes 18436
  129.3 10.3 %collective-permute-start.20 = (bf16[96,768]{1,0:T(8,128)(2,1)S(1)}, bf16[96,768]{1,0:T(8,128)(2,1)S(1)}, u32[]{:S(2)}, u32[]{:S(2)}) collective-permute-start(bf16[96,768]{1,0:T(8,128)(2,1)S(1)} %get-tuple-element.187), channel_id=1, source_target_pairs={{0,24},{2,26},{4,28},{6,30},{8,16},{10,18},{12,20},{14,22},{16,8},... | collective-permute-start | bytes 442376 | tf_op jit(solution)/shard_map/ppermute | solution.py:661
  133.0 10.5 %collective-permute-start.19 = (bf16[96,768]{1,0:T(8,128)(2,1)S(1)}, bf16[96,768]{1,0:T(8,128)(2,1)S(1)}, u32[]{:S(2)}, u32[]{:S(2)}) collective-permute-start(bf16[96,768]{1,0:T(8,128)(2,1)S(1)} %get-tuple-element.188), channel_id=1, source_target_pairs={{0,16},{2,18},{4,20},{6,22},{8,24},{10,26},{12,28},{14,30},{16,0},... | collective-permute-start | bytes 442376 | tf_op jit(solution)/shard_map/ppermute | solution.py:661
  133.0 10.5 %collective-permute-start.15 = (bf16[96,768]{1,0:T(8,128)(2,1)S(1)}, bf16[96,768]{1,0:T(8,128)(2,1)S(1)}, u32[]{:S(2)}, u32[]{:S(2)}) collective-permute-start(bf16[96,768]{1,0:T(8,128)(2,1)S(1)} %get-tuple-element.189), channel_id=1, source_target_pairs={{0,8},{2,10},{4,12},{6,14},{8,0},{10,2},{12,4},{14,6},{16,24},{18,... | collective-permute-start | bytes 442376 | tf_op jit(solution)/shard_map/ppermute | solution.py:661
  143.7 17.7 %copy-start.22 = (bf16[392,768]{1,0:T(8,128)(2,1)S(1)}, bf16[392,768]{1,0:T(8,128)(2,1)}, u32[]{:S(2)}) copy-start(bf16[392,768]{1,0:T(8,128)(2,1)} %copy-done.21) | copy-start | bytes 1806340
  143.7 17.7 %copy-start.45 = (f32[768]{0:T(1024)S(1)}, f32[768]{0:T(1024)}, u32[]{:S(2)}) copy-start(f32[768]{0:T(1024)} %param.30) | copy-start | bytes 9220
  143.7 2.9 %collective-permute-start.25 = (bf16[2,4,96,768]{3,2,1,0:T(8,128)(2,1)S(1)}, bf16[2,4,96,768]{3,2,1,0:T(8,128)(2,1)S(1)}, u32[]{:S(2)}, u32[]{:S(2)}) collective-permute-start(bf16[2,4,96,768]{3,2,1,0:T(8,128)(2,1)S(1)} %get-tuple-element.165), channel_id=1, source_target_pairs={{0,2},{2,0},{4,6},{6,4},{8,10},{10,8},{12,14},{14,12},{16,18},{18,... | collective-permute-start | bytes 3538952 | tf_op jit(solution)/shard_map/ppermute | solution.py:661
  143.8 18.7 %collective-permute-start.13 = (bf16[392,768]{1,0:T(8,128)(2,1)S(1)}, bf16[392,768]{1,0:T(8,128)(2,1)S(1)}, u32[]{:S(2)}, u32[]{:S(2)}) collective-permute-start(bf16[392,768]{1,0:T(8,128)(2,1)S(1)} %get-tuple-element.138), channel_id=1, source_target_pairs={{0,1},{1,0},{2,3},{3,2},{4,5},{5,4},{6,7},{7,6},{8,9},{9,8},{10,11... | collective-permute-start | bytes 1806344 | tf_op jit(solution)/shard_map/ppermute | solution.py:657
  144.4 17.0 %collective-permute-start.22 = (bf16[208,768]{1,0:T(8,128)(2,1)S(1)}, bf16[208,768]{1,0:T(8,128)(2,1)S(1)}, u32[]{:S(2)}, u32[]{:S(2)}) collective-permute-start(bf16[208,768]{1,0:T(8,128)(2,1)S(1)} %get-tuple-element.194), channel_id=1, source_target_pairs={{0,16},{2,18},{4,20},{6,22},{8,24},{10,26},{12,28},{14,30},{16,0},... | collective-permute-start | bytes 958472 | tf_op jit(solution)/shard_map/ppermute | solution.py:661
  146.7 25.8 %collective-permute-start.26 = (bf16[4,96,768]{2,1,0:T(8,128)(2,1)S(1)}, bf16[4,96,768]{2,1,0:T(8,128)(2,1)S(1)}, u32[]{:S(2)}, u32[]{:S(2)}) collective-permute-start(bf16[4,96,768]{2,1,0:T(8,128)(2,1)S(1)} %fusion.2), channel_id=1, source_target_pairs={{0,4},{2,6},{4,0},{6,2},{8,12},{10,14},{12,8},{14,10},{16,20},{18,... | collective-permute-start | bytes 1769480 | tf_op jit(solution)/shard_map/ppermute | solution.py:661
  148.3 16.4 %collective-permute-start.21 = (bf16[208,768]{1,0:T(8,128)(2,1)S(1)}, bf16[208,768]{1,0:T(8,128)(2,1)S(1)}, u32[]{:S(2)}, u32[]{:S(2)}) collective-permute-start(bf16[208,768]{1,0:T(8,128)(2,1)S(1)} %get-tuple-element.194), channel_id=1, source_target_pairs={{0,8},{2,10},{4,12},{6,14},{8,0},{10,2},{12,4},{14,6},{16,24},{18,... | collective-permute-start | bytes 958472 | tf_op jit(solution)/shard_map/ppermute | solution.py:661
  161.3 9.9 %collective-permute-start.23 = (bf16[208,768]{1,0:T(8,128)(2,1)S(1)}, bf16[208,768]{1,0:T(8,128)(2,1)S(1)}, u32[]{:S(2)}, u32[]{:S(2)}) collective-permute-start(bf16[208,768]{1,0:T(8,128)(2,1)S(1)} %collective-permute-done.22), channel_id=1, source_target_pairs={{0,8},{2,10},{4,12},{6,14},{8,0},{10,2},{12,4},{14,6},{16,24},{18,... | collective-permute-start | bytes 958472 | tf_op jit(solution)/shard_map/ppermute | solution.py:661
  171.4 30.0 %collective-permute-start.24 = (bf16[4,208,768]{2,1,0:T(8,128)(2,1)S(1)}, bf16[4,208,768]{2,1,0:T(8,128)(2,1)S(1)}, u32[]{:S(2)}, u32[]{:S(2)}) collective-permute-start(bf16[4,208,768]{2,1,0:T(8,128)(2,1)S(1)} %pad_maximum_fusion.refs_0_), channel_id=1, source_target_pairs={{0,4},{2,6},{4,0},{6,2},{8,12},{10,14},{12,8},{14,10},{16,20},{18,... | collective-permute-start | bytes 3833864 | tf_op jit(solution)/shard_map/ppermute | solution.py:661
  172.6 6.2 %collective-permute-start.28 = (bf16[96,768]{1,0:T(8,128)(2,1)S(1)}, bf16[96,768]{1,0:T(8,128)(2,1)S(1)}, u32[]{:S(2)}, u32[]{:S(2)}) collective-permute-start(bf16[96,768]{1,0:T(8,128)(2,1)S(1)} %get-tuple-element.186), channel_id=1, source_target_pairs={{0,8},{2,10},{4,12},{6,14},{8,0},{10,2},{12,4},{14,6},{16,24},{18,... | collective-permute-start | bytes 442376 | tf_op jit(solution)/shard_map/ppermute | solution.py:661
  173.0 8.6 %collective-permute-start.27 = (bf16[96,768]{1,0:T(8,128)(2,1)S(1)}, bf16[96,768]{1,0:T(8,128)(2,1)S(1)}, u32[]{:S(2)}, u32[]{:S(2)}) collective-permute-start(bf16[96,768]{1,0:T(8,128)(2,1)S(1)} %get-tuple-element.185), channel_id=1, source_target_pairs={{0,8},{2,10},{4,12},{6,14},{8,0},{10,2},{12,4},{14,6},{16,24},{18,... | collective-permute-start | bytes 442376 | tf_op jit(solution)/shard_map/ppermute | solution.py:661
  179.0 9.8 %collective-permute-start.29 = (bf16[96,768]{1,0:T(8,128)(2,1)S(1)}, bf16[96,768]{1,0:T(8,128)(2,1)S(1)}, u32[]{:S(2)}, u32[]{:S(2)}) collective-permute-start(bf16[96,768]{1,0:T(8,128)(2,1)S(1)} %add_convert_fusion.4), channel_id=1, source_target_pairs={{0,16},{2,18},{4,20},{6,22},{8,24},{10,26},{12,28},{14,30},{16,0},... | collective-permute-start | bytes 442376 | tf_op jit(solution)/shard_map/ppermute | solution.py:661
  188.9 7.3 %collective-permute-start.31 = (bf16[96,768]{1,0:T(8,128)(2,1)S(1)}, bf16[96,768]{1,0:T(8,128)(2,1)S(1)}, u32[]{:S(2)}, u32[]{:S(2)}) collective-permute-start(bf16[96,768]{1,0:T(8,128)(2,1)S(1)} %fusion.8), channel_id=1, source_target_pairs={{0,16},{2,18},{4,20},{6,22},{8,24},{10,26},{12,28},{14,30},{16,0},... | collective-permute-start | bytes 442376 | tf_op jit(solution)/shard_map/ppermute | solution.py:661
  189.0 8.0 %collective-permute-start.30 = (bf16[96,768]{1,0:T(8,128)(2,1)S(1)}, bf16[96,768]{1,0:T(8,128)(2,1)S(1)}, u32[]{:S(2)}, u32[]{:S(2)}) collective-permute-start(bf16[96,768]{1,0:T(8,128)(2,1)S(1)} %fusion.8), channel_id=1, source_target_pairs={{0,8},{2,10},{4,12},{6,14},{8,0},{10,2},{12,4},{14,6},{16,24},{18,... | collective-permute-start | bytes 442376 | tf_op jit(solution)/shard_map/ppermute | solution.py:661
  196.2 5.1 %collective-permute-start.32 = (bf16[96,768]{1,0:T(8,128)(2,1)S(1)}, bf16[96,768]{1,0:T(8,128)(2,1)S(1)}, u32[]{:S(2)}, u32[]{:S(2)}) collective-permute-start(bf16[96,768]{1,0:T(8,128)(2,1)S(1)} %collective-permute-done.31), channel_id=1, source_target_pairs={{0,8},{2,10},{4,12},{6,14},{8,0},{10,2},{12,4},{14,6},{16,24},{18,... | collective-permute-start | bytes 442376 | tf_op jit(solution)/shard_map/ppermute | solution.py:661
  196.2 6.3 %collective-permute-start.33 = (bf16[4,208,768]{2,1,0:T(8,128)(2,1)S(1)}, bf16[4,208,768]{2,1,0:T(8,128)(2,1)S(1)}, u32[]{:S(2)}, u32[]{:S(2)}) collective-permute-start(bf16[4,208,768]{2,1,0:T(8,128)(2,1)S(1)} %pad_maximum_fusion.refs_0_), channel_id=1, source_target_pairs={{0,2},{2,0},{4,6},{6,4},{8,10},{10,8},{12,14},{14,12},{16,18},{18,... | collective-permute-start | bytes 3833864 | tf_op jit(solution)/shard_map/ppermute | solution.py:661
  201.4 3.1 %collective-permute-start.34 = (bf16[4,208,768]{2,1,0:T(8,128)(2,1)S(1)}, bf16[4,208,768]{2,1,0:T(8,128)(2,1)S(1)}, u32[]{:S(2)}, u32[]{:S(2)}) collective-permute-start(bf16[4,208,768]{2,1,0:T(8,128)(2,1)S(1)} %collective-permute-done.24.refs_1_), channel_id=1, source_target_pairs={{0,2},{2,0},{4,6},{6,4},{8,10},{10,8},{12,14},{14,12},{16,18},{18,... | collective-permute-start | bytes 3833864 | tf_op jit(solution)/shard_map/ppermute | solution.py:661
  201.5 9.7 %collective-permute-start.37 = (bf16[4,96,768]{2,1,0:T(8,128)(2,1)S(1)}, bf16[4,96,768]{2,1,0:T(8,128)(2,1)S(1)}, u32[]{:S(2)}, u32[]{:S(2)}) collective-permute-start(bf16[4,96,768]{2,1,0:T(8,128)(2,1)S(1)} %pad_maximum_fusion.1.refs_0_), channel_id=1, source_target_pairs={{0,2},{2,0},{4,6},{6,4},{8,10},{10,8},{12,14},{14,12},{16,18},{18,... | collective-permute-start | bytes 1769480 | tf_op jit(solution)/shard_map/ppermute | solution.py:661
  202.0 15.3 %collective-permute-start.36 = (bf16[4,96,768]{2,1,0:T(8,128)(2,1)S(1)}, bf16[4,96,768]{2,1,0:T(8,128)(2,1)S(1)}, u32[]{:S(2)}, u32[]{:S(2)}) collective-permute-start(bf16[4,96,768]{2,1,0:T(8,128)(2,1)S(1)} %pad_maximum_fusion.1.refs_0_), channel_id=1, source_target_pairs={{0,4},{2,6},{4,0},{6,2},{8,12},{10,14},{12,8},{14,10},{16,20},{18,... | collective-permute-start | bytes 1769480 | tf_op jit(solution)/shard_map/ppermute | solution.py:661
  209.9 3.9 %collective-permute-start.35 = (f32[6,768]{1,0:T(8,128)S(1)}, f32[6,768]{1,0:T(8,128)S(1)}, u32[]{:S(2)}, u32[]{:S(2)}) collective-permute-start(f32[6,768]{1,0:T(8,128)S(1)} %slice.210), channel_id=1, source_target_pairs={{0,1},{1,0},{2,3},{3,2},{4,5},{5,4},{6,7},{7,6},{8,9},{9,8},{10,11... | collective-permute-start | bytes 55304 | tf_op jit(solution)/shard_map/ppermute | solution.py:657
  217.3 2.0 collective-permute-start.38
  (22 other events, 48.7 us)

commit v6 on v4

--- a/solution.py
+++ b/solution.py
@@ -456,8 +456,11 @@
     gpatch_ref[...] = (gmiddle_ref[...] + norm_back(xhat, inv, line(gain_ref), gnorm)).astype(BF)
 
 
-def finish_kernel(me_ref, *refs):
-    sources, outs, held, wide, (in_sems, out_sems) = refs[:4], refs[4:6], refs[6:10], refs[10:12], refs[12:]
+def finish_kernel(y_rels, me_ref, *refs):
+    sources, refs = refs[:2], refs[2:]
+    if y_rels[0] == 1:
+        refs = refs[2:]
+    outs, held, wide, (in_sems, out_sems) = refs[:2], refs[2:4], refs[4:6], refs[6:]
     copies = begin(in_sems, *zip(sources, held))
     sent = []
 
@@ -466,8 +469,9 @@
         sent.append(pltpu.make_async_copy(wide[k].at[where], outs[k].at[where], out_sems.at[len(sent)]))
         sent[-1].start()
 
-    for source, y_rel, z_rel, c, y, z in each_block(me_ref[0], (0, 1), (2, 3)):
-        source = source[y_rel]
+    for source, y_rel, z_rel, c, y, z in each_block(me_ref[0], 0, 1):
+        if y_rel not in y_rels:
+            continue
         if z_rel == 0:
             copies[source].wait()
         piece = held[source].at[z_rel]
@@ -509,7 +513,7 @@
     return jax.ShapeDtypeStruct(dims, dtype)
 
 
-def call(kernel, outs, scratch, name, flops, smem, *args, far=(), far_outs=(), limit=VMEM_LIMIT):
+def call(kernel, outs, scratch, name, flops, smem, *args, far=(), far_outs=(), limit=VMEM_LIMIT, aliases=None):
     space = lambda is_far: pl.BlockSpec(memory_space=pltpu.HBM if is_far else pltpu.VMEM)
     in_specs = [pl.BlockSpec(memory_space=pltpu.SMEM)] * len(smem) + [space(i in far) for i in range(len(args))]
     return pl.pallas_call(
@@ -520,6 +524,7 @@
         scratch_shapes=scratch,
         compiler_params=pltpu.CompilerParams(vmem_limit_bytes=limit),
         cost_estimate=pl.CostEstimate(flops=flops, bytes_accessed=flops // 256, transcendentals=0),
+        input_output_aliases=aliases or {},
         name=name,
     )(*smem, *args)
 
@@ -618,9 +623,10 @@
                 own, peer, x, gain, gmiddle)[0]
 
 
-def finish(me, sources, *outs):
-    scratch = like(*sources, *outs) + dma(4, 16 * 4)
-    return call(finish_kernel, list(outs), scratch, "finish", SMALL, (me,), *sources, far=range(4), far_outs=range(len(outs)))
+def finish(me, y_rel, sources, outs, before=()):
+    scratch = like(*sources, *outs) + dma(2, 8 * 4)
+    return call(functools.partial(finish_kernel, (y_rel,)), list(outs), scratch, "finish", SMALL, (me,), *sources, *before,
+                far=range(2 + len(before)), far_outs=range(len(outs)), aliases={3: 0, 4: 1} if before else {})
 
 
 def finish_mlp(me, sources):
@@ -663,11 +669,6 @@
 
 def flip_line(pieces):
     return [flip(p, LINE * k) for k, p in zip((1, 2, 3), pieces)]
-
-
-def sum_line(sends):
-    near, far, both = sends
-    return [flip(near, LINE), flip(total_of([far, flip(both, LINE)]), 2 * LINE)]
 
 
 def gather_line(piece):
@@ -788,19 +789,22 @@
         piece2 = own_piece(keep2, got2, side2, line2)
         keep, send = g_attn
         got = flip(after(send, piece2), CORE)
-        side = flip(side_send(keep, got), SIDE)
+        side = after(flip(side_send(keep, got), SIDE), gnorms[1])
         fc = jnp.concatenate([piece1, piece2, small], axis=0)
-        fc_quad = jnp.stack([fc] + [after(r, output, gpatch) for r in gather_line(fc)])
-        side = after(side, fc_quad, output, gpatch)
-        line = sum_line(line_sends(keep, got, side))
+        near, far, both = line_sends(keep, got, side)
+        both = flip(both, LINE)
+        fc_quad = jnp.stack([fc] + [after(r, both) for r in gather_line(fc)])
+        line = [after(flip(near, LINE), output, gpatch), flip(total_of([far, both]), 2 * LINE)]
         piece = own_piece(keep, got, side, line)
         quad = jnp.stack([piece] + gather_line(piece))
         fc_pair = after(flip(fc_quad, SIDE), quad)
         g_fc1, g_fc2, small = finish_mlp(me, (fc_quad, fc_pair, after(flip(fc_quad, CORE), quad), after(flip(fc_pair, CORE), quad)))
         totals = small[0:6] + across(small[0:6])
         pair = after(flip(quad, SIDE), totals)
-        gw, gproj = finish(me, (quad, pair, flip(quad, CORE), flip(pair, CORE)),
-                           shape_of(3, features, width), shape_of(width, features))
+        shapes = shape_of(3, features, width), shape_of(width, features)
+        half_done = finish(me, 0, (quad, flip(quad, CORE)), shapes)
+        pair = after(pair, half_done[0])
+        gw, gproj = finish(me, 1, (pair, flip(pair, CORE)), shapes, half_done)
     else:
         g_fc1, g_fc2, gw, gproj = [g.astype(F32) for g in lax.psum((*g_mlp, *g_attn), "dp")]
         gw, gproj = gw[:, :, :width], gproj[:width]

time: 216 us -> 220 us (1.019)
    ppermute x28, starting transfers between devices: 21.2 us -> 24 us  [flip(): return lax.ppermute(v, 'dp', [(i, i ^ bits) for i in range(16)])]
    ppermute x28, waiting for transfers between devices: 56.7 us -> 59.2 us  [flip(): return lax.ppermute(v, 'dp', [(i, i ^ bits) for i in range(16)])]
    pallas_call x14 -> x15, Pallas kernels: 89.9 us -> 90.7 us  [call(): pl.pallas_call(kernel, out_shape=outs, in_specs=in_specs, out_specs=[spac...]
  transfers between devices with their start and end apart: 39 -> 39, of which waited for: 19 -> 20; matrix products, arithmetic and copies ran while one was open for 4% -> 4% of each run, Pallas kernels for 35% -> 35%
where the time goes in v6:
time: 220 us
  Pallas kernels  90.7 us (41%)
  waiting for transfers between devices  72.2 us (33%)
  starting transfers between devices  34.9 us (16%)
  local copies, waits for them, and re-layouts  14.5 us (7%)
  other arithmetic  3.95 us (2%)
  matrix products  2.4 us (1%)
    pallas_call x15, Pallas kernels, call(): pl.pallas_call(kernel, out_shape=outs, in_specs=in_specs, out_specs=[spac...  90.7 us
    ppermute x28, waiting for transfers between devices, flip(): return lax.ppermute(v, 'dp', [(i, i ^ bits) for i in range(16)])  59.2 us
    ppermute x28, starting transfers between devices, flip(): return lax.ppermute(v, 'dp', [(i, i ^ bits) for i in range(16)])  24 us
    ppermute x11, waiting for transfers between devices, across(): return lax.ppermute(v, 'mp', [(0, 1), (1, 0)])  13 us
    unnamed x98, local copies, waits for them, and re-layouts  11.6 us
    ppermute x11, starting transfers between devices, across(): return lax.ppermute(v, 'mp', [(0, 1), (1, 0)])  10.8 us
  transfers between devices with their start and end apart: 39, of which 20 were waited for; matrix products, arithmetic and copies ran while one was open for 4% of the time, Pallas kernels for 35%

profile of v6, /device:TPU:0, one launch (start us, length us, event | category | flops | bytes accessed | tf_op | source)
XLA Modules:
  0.0 220.0 jit_solution(12367830689164193760)
XLA Ops:
  1.3 2.9 %collective-permute-start.1 = (f32[8,49]{1,0:T(8,128)S(1)}, f32[8,49]{1,0:T(8,128)S(1)}, u32[]{:S(2)}, u32[]{:S(2)}) collective-permute-start(f32[8,49]{1,0:T(8,128)S(1)} %convert_element_type.294.valid_ref), channel_id=1, source_target_pairs={{0,1},{1,0},{2,3},{3,2},{4,5},{5,4},{6,7},{7,6},{8,9},{9,8},{10,11... | collective-permute-start | bytes 4712 | tf_op jit(solution)/shard_map/ppermute | solution.py:640
  4.3 1.6 collective-permute-done.1.valid_ref
  5.9 2.0 collective-permute-start.2
  7.9 1.0 constant_dynamic-slice_fusion
  10.9 12.1 %attn_forward.2 = (bf16[8,3,64,256]{3,2,1,0:T(8,128)(2,1)}, bf16[8,64,384]{2,1,0:T(8,128)(2,1)}, bf16[8,64,384]{2,1,0:T(8,128)(2,1)}, bf16[8,64,384]{2,1,0:T(8,1...) custom-call(bf16[392,768]{1,0:T(8,128)(2,1)} %bitcast.102, f32[768]{0:T(1024)} %gain_ref.9, f32[768]{0:T(1024)} %shift_ref.4, ...), custom_call_target="tpu_custom_call" | custom-call | flops 1000000 | bytes 3906 | tf_op jit(solution)/shard_map/attn_forward/pallas_call | solution.py:519
  23.0 0.8 copy-done.11
  23.8 12.1 %attn_forward.3 = (bf16[8,3,64,256]{3,2,1,0:T(8,128)(2,1)}, bf16[8,64,384]{2,1,0:T(8,128)(2,1)}, bf16[8,64,384]{2,1,0:T(8,128)(2,1)}, bf16[8,64,384]{2,1,0:T(8,1...) custom-call(bf16[392,768]{1,0:T(8,128)(2,1)} %copy-done.11, f32[768]{0:T(1024)} %gain_ref.9, f32[768]{0:T(1024)} %shift_ref.4, ...), custom_call_target="tpu_custom_call" | custom-call | flops 1000000 | bytes 3906 | tf_op jit(solution)/shard_map/attn_forward/pallas_call | solution.py:519
  35.9 2.9 %collective-permute-done.3.refs_0_ = bf16[192,768]{1,0:T(8,128)(2,1)} collective-permute-done((bf16[192,768]{1,0:T(8,128)(2,1)S(1)}, bf16[192,768]{1,0:T(8,128)(2,1)}, u32[]{:S(2)}, u32[]{:S(2)}) %collective-permute-start.3) | collective-permute-done | bytes 294944 | tf_op jit(solution)/shard_map/ppermute | solution.py:640
  38.9 0.8 copy-done.7
  40.1 2.4 %convolution_convert_fusion.own_in = bf16[392,768]{1,0:T(8,128)(2,1)} fusion(bf16[392,384]{1,0:T(8,128)(2,1)} %get-tuple-element.96.refs_1_, bf16[384,768]{1,0:T(8,128)(2,1)S(1)} %copy-done.4), kind=kOutput, calls=%fused_computation | convolution fusion | flops 231512064 | bytes 1492992 | tf_op jit(solution)/shard_map/dot_general | solution.py:733
  42.5 5.1 %collective-permute-done.4.peer_in = bf16[392,384]{1,0:T(8,128)(2,1)S(1)} collective-permute-done((bf16[392,384]{1,0:T(8,128)(2,1)}, bf16[392,384]{1,0:T(8,128)(2,1)S(1)}, u32[]{:S(2)}, u32[]{:S(2)}) %collective-permute-start.4) | collective-permute-done | bytes 301088 | tf_op jit(solution)/shard_map/ppermute | solution.py:640
  47.6 0.7 copy-done.43
  48.3 3.8 %middle.1 = (f32[392,768]{1,0:T(8,128)}, bf16[392,768]{1,0:T(8,128)(2,1)}) custom-call(s32[1]{0:T(128)} %bitcast.me_ref, bf16[392,768]{1,0:T(8,128)(2,1)} %bitcast.103, bf16[392,768]{1,0:T(8,128)(2,1)} %convolution_convert_fusion.own_in, bf16[392,384]{1,0:T(8,128)(2,1)} %copy-done.43, f32[768]{0:T(1024)} %bias_ref.5, f32[768]{0:T(1024)} %gain_ref.8, ...), custom_call_target="tpu_custom_call" | custom-call | flops 1000000 | bytes 3906 | tf_op jit(solution)/shard_map/middle/pallas_call | solution.py:519
  52.2 0.8 collective-permute-start.6
  53.0 1.1 copy-done.9
  54.1 6.1 %mlp.2 = (bf16[392,1536]{1,0:T(8,128)(2,1)S(1)}, bf16[392,1536]{1,0:T(8,128)(2,1)S(1)}, bf16[392,768]{1,0:T(8,128)(2,1)S(1)}, bf16[392,768]{1,0:T(8,128)(2,1)S(1)}) custom-call(bf16[392,768]{1,0:T(8,128)(2,1)S(1)} %copy-done.9, bf16[392,768]{1,0:T(8,128)(2,1)S(1)} %bitcast.108, bf16[768,1536]{1,0:T(8,128)(2,1)S(1)} %copy-done.2, ...), custom_call_target="tpu_custom_call" | custom-call | flops 1000000 | bytes 3906 | tf_op jit(solution)/shard_map/mlp/pallas_call | solution.py:519
  60.2 1.0 copy-done.14
  61.2 0.8 copy-done.24
  62.0 0.8 copy-done.37
  62.9 2.8 %collective-permute-done.6.nm_ref.refs_4_ = bf16[392,768]{1,0:T(8,128)(2,1)S(1)} collective-permute-done((bf16[392,768]{1,0:T(8,128)(2,1)}, bf16[392,768]{1,0:T(8,128)(2,1)S(1)}, u32[]{:S(2)}, u32[]{:S(2)}) %collective-permute-start.6) | collective-permute-done | bytes 602144 | tf_op jit(solution)/shard_map/ppermute | solution.py:640
  65.7 6.9 %mlp.3 = (bf16[392,1536]{1,0:T(8,128)(2,1)S(1)}, bf16[392,1536]{1,0:T(8,128)(2,1)S(1)}, bf16[392,768]{1,0:T(8,128)(2,1)S(1)}, bf16[392,768]{1,0:T(8,128)(2,1)}) custom-call(bf16[392,768]{1,0:T(8,128)(2,1)S(1)} %collective-permute-done.6.nm_ref.refs_4_, bf16[392,768]{1,0:T(8,128)(2,1)S(1)} %copy-done.8, bf16[768,1536]{1,0:T(8,128)(2,1)S(1)} %copy-done.2, ...), custom_call_target="tpu_custom_call" | custom-call | flops 1000000 | bytes 3906 | tf_op jit(solution)/shard_map/mlp/pallas_call | solution.py:519
  72.6 1.0 copy-done.16
  73.6 1.0 copy-done.17
  74.6 1.1 collective-permute-start.8
  75.7 11.9 %mlp_weights.1 = (f32[1,1536]{1,0:T(1,128)}, bf16[2,4,96,768]{3,2,1,0:T(8,128)(2,1)}, bf16[2,4,96,768]{3,2,1,0:T(8,128)(2,1)}, bf16[2,4,96,768]{3,2,1,0:T(8,128)(2,1)}, bf16[2,4,96,768]{3,2,1,0:T(8,128)(2,1)}) custom-call(s32[1]{0:T(128)} %bitcast.me_ref, bf16[392,768]{1,0:T(8,128)(2,1)} %get-tuple-element.104.nm_ref.refs_0_, bf16[392,768]{1,0:T(8,128)(2,1)} %bitcast.107, ...), custom_call_target="tpu_custom_call" | custom-call | flops 1000000 | bytes 3906 | tf_op jit(solution)/shard_map/mlp_weights/pallas_call | solution.py:519
  88.2 0.8 copy-done.39
  89.0 1.1 copy-done.40
  90.1 1.1 middle_back.1
  91.2 1.0 collective-permute-start.11
  92.4 1.6 collective-permute-start.12
  94.7 1.1 collective-permute-start.7
  95.9 9.7 %attn_backward.2 = (bf16[3,392,384]{2,1,0:T(8,128)(2,1)S(1)}, f32[1,768]{1,0:T(1,128)S(1)}, f32[3,64,256]{2,1,0:T(8,128)S(1)}, bf16[392,768]{1,0:T(8,128)(2,1)S(1)}, f32[2,768]{1,0:T(2,128)S(1)}) custom-call(bf16[392,768]{1,0:T(8,128)(2,1)S(1)} %get-tuple-element.143.branch_ref.refs_2_, bf16[392,768]{1,0:T(8,128)(2,1)S(1)} %bitcast.104, ...), custom_call_target="tpu_custom_call" | custom-call | flops 1000000 | bytes 3906 | tf_op jit(solution)/shard_map/attn_backward/pallas_call | solution.py:519
  105.6 3.1 %collective-permute-done.12 = bf16[4,96,768]{2,1,0:T(8,128)(2,1)S(1)} collective-permute-done((bf16[4,96,768]{2,1,0:T(8,128)(2,1)S(1)}, bf16[4,96,768]{2,1,0:T(8,128)(2,1)S(1)}, u32[]{:S(2)}, u32[]{:S(2)}) %collective-permute-start.12) | collective-permute-done | bytes 589856 | tf_op jit(solution)/shard_map/ppermute | solution.py:644
  108.9 3.7 %collective-permute-start.16 = (bf16[96,768]{1,0:T(8,128)(2,1)S(1)}, bf16[96,768]{1,0:T(8,128)(2,1)S(1)}, u32[]{:S(2)}, u32[]{:S(2)}) collective-permute-start(bf16[96,768]{1,0:T(8,128)(2,1)S(1)} %get-tuple-element.188), channel_id=1, source_target_pairs={{0,24},{2,26},{4,28},{6,30},{8,16},{10,18},{12,20},{14,22},{16,8},... | collective-permute-start | bytes 442376 | tf_op jit(solution)/shard_map/ppermute | solution.py:644
  112.5 0.8 collective-permute-start.14
  113.3 9.7 %attn_backward.3 = (bf16[3,392,384]{2,1,0:T(8,128)(2,1)S(1)}, f32[1,768]{1,0:T(1,128)S(1)}, f32[3,64,256]{2,1,0:T(8,128)S(1)}, bf16[392,768]{1,0:T(8,128)(2,1)S(1)}, f32[2,768]{1,0:T(2,128)S(1)}) custom-call(bf16[392,768]{1,0:T(8,128)(2,1)S(1)} %collective-permute-done.11.branch_ref.refs_9_, bf16[392,768]{1,0:T(8,128)(2,1)S(1)} %copy-done.12, ...), custom_call_target="tpu_custom_call" | custom-call | flops 1000000 | bytes 3906 | tf_op jit(solution)/shard_map/attn_backward/pallas_call | solution.py:519
  123.3 3.7 %collective-permute-start.20 = (bf16[96,768]{1,0:T(8,128)(2,1)S(1)}, bf16[96,768]{1,0:T(8,128)(2,1)S(1)}, u32[]{:S(2)}, u32[]{:S(2)}) collective-permute-start(bf16[96,768]{1,0:T(8,128)(2,1)S(1)} %get-tuple-element.185), channel_id=1, source_target_pairs={{0,24},{2,26},{4,28},{6,30},{8,16},{10,18},{12,20},{14,22},{16,8},... | collective-permute-start | bytes 442376 | tf_op jit(solution)/shard_map/ppermute | solution.py:644
  127.0 0.8 collective-permute-start.18
  128.0 5.8 %attn_weights.1 = (bf16[2,4,96,768]{3,2,1,0:T(8,128)(2,1)S(1)}, bf16[2,4,96,768]{3,2,1,0:T(8,128)(2,1)S(1)}, bf16[16,768]{1,0:T(8,128)(2,1)S(1)}) custom-call(s32[1]{0:T(128)} %bitcast.me_ref, f32[4,768]{1,0:T(4,128)S(1)} %get-tuple-element.141.sums2_ref, f32[1,1536]{1,0:T(1,128)S(1)} %copy-done.35, bf16[768,392]{1,0:T(8,128)(2,1)S(1)} %copy-done.20, ...), custom_call_target="tpu_custom_call" | custom-call | flops 1000000 | bytes 3906 | tf_op jit(solution)/shard_map/attn_weights/pallas_call | solution.py:519
  133.8 2.7 %collective-permute-done.19 = bf16[96,768]{1,0:T(8,128)(2,1)S(1)} collective-permute-done((bf16[96,768]{1,0:T(8,128)(2,1)S(1)}, bf16[96,768]{1,0:T(8,128)(2,1)S(1)}, u32[]{:S(2)}, u32[]{:S(2)}) %collective-permute-start.19) | collective-permute-done | bytes 147488 | tf_op jit(solution)/shard_map/ppermute | solution.py:644
  136.7 0.7 collective-permute-start.13
  137.4 2.1 collective-permute-done.22
  139.7 1.6 collective-permute-start.23
  141.4 2.9 %collective-permute-start.21 = (bf16[208,768]{1,0:T(8,128)(2,1)S(1)}, bf16[208,768]{1,0:T(8,128)(2,1)S(1)}, u32[]{:S(2)}, u32[]{:S(2)}) collective-permute-start(bf16[208,768]{1,0:T(8,128)(2,1)S(1)} %get-tuple-element.192), channel_id=1, source_target_pairs={{0,8},{2,10},{4,12},{6,14},{8,0},{10,2},{12,4},{14,6},{16,24},{18,... | collective-permute-start | bytes 958472 | tf_op jit(solution)/shard_map/ppermute | solution.py:644
  144.3 13.9 %collective-permute-done.25 = bf16[208,768]{1,0:T(8,128)(2,1)S(1)} collective-permute-done((bf16[208,768]{1,0:T(8,128)(2,1)S(1)}, bf16[208,768]{1,0:T(8,128)(2,1)S(1)}, u32[]{:S(2)}, u32[]{:S(2)}) %collective-permute-start.25) | collective-permute-done | bytes 319520 | tf_op jit(solution)/shard_map/ppermute | solution.py:644
  158.3 2.1 collective-permute-start.24
  160.4 8.2 %collective-permute-done.26 = bf16[208,768]{1,0:T(8,128)(2,1)S(1)} collective-permute-done((bf16[208,768]{1,0:T(8,128)(2,1)S(1)}, bf16[208,768]{1,0:T(8,128)(2,1)S(1)}, u32[]{:S(2)}, u32[]{:S(2)}) %collective-permute-start.26) | collective-permute-done | bytes 319520 | tf_op jit(solution)/shard_map/ppermute | solution.py:644
  168.7 2.1 collective-permute-done.24
  172.1 1.7 collective-permute-start.29
  173.8 1.1 add_convert_fusion
  174.9 1.7 input_back.1
  176.6 2.1 collective-permute-done.28
  178.7 2.2 collective-permute-done.29
  181.2 1.8 collective-permute-start.30
  183.0 5.3 %collective-permute-done.31 = bf16[96,768]{1,0:T(8,128)(2,1)S(1)} collective-permute-done((bf16[96,768]{1,0:T(8,128)(2,1)S(1)}, bf16[96,768]{1,0:T(8,128)(2,1)S(1)}, u32[]{:S(2)}, u32[]{:S(2)}) %collective-permute-start.31) | collective-permute-done | bytes 147488 | tf_op jit(solution)/shard_map/ppermute | solution.py:644
  188.3 0.9 collective-permute-done.30
  189.2 4.2 %collective-permute-done.32 = bf16[96,768]{1,0:T(8,128)(2,1)S(1)} collective-permute-done((bf16[96,768]{1,0:T(8,128)(2,1)S(1)}, bf16[96,768]{1,0:T(8,128)(2,1)S(1)}, u32[]{:S(2)}, u32[]{:S(2)}) %collective-permute-start.32) | collective-permute-done | bytes 147488 | tf_op jit(solution)/shard_map/ppermute | solution.py:644
  193.5 6.7 %collective-permute-done.27.refs_1_ = bf16[4,208,768]{2,1,0:T(8,128)(2,1)S(1)} collective-permute-done((bf16[4,208,768]{2,1,0:T(8,128)(2,1)S(1)}, bf16[4,208,768]{2,1,0:T(8,128)(2,1)S(1)}, u32[]{:S(2)}, u32[]{:S(2)}) %collective-permute-start.27) | collective-permute-done | bytes 1277984 | tf_op jit(solution)/shard_map/ppermute | solution.py:644
  201.2 2.0 collective-permute-done.34.refs_3_
  203.1 5.4 %finish_mlp.1 = (f32[768,1536]{1,0:T(8,128)}, f32[1536,768]{1,0:T(8,128)}, f32[16,768]{1,0:T(8,128)S(1)}) custom-call(s32[1]{0:T(128)} %bitcast.me_ref, bf16[4,208,768]{2,1,0:T(8,128)(2,1)S(1)} %pad_maximum_fusion.refs_0_, bf16[4,208,768]{2,1,0:T(8,128)(2,1)S(1)} %collective-permute-done.27.refs_1_, ...), custom_call_target="tpu_custom_call" | custom-call | flops 1000000 | bytes 3906 | tf_op jit(solution)/shard_map/finish_mlp/pallas_call | solution.py:519
  208.6 0.7 collective-permute-start.35
  209.3 1.9 finish.2
  212.4 3.5 %collective-permute-done.36.refs_0_ = bf16[4,96,768]{2,1,0:T(8,128)(2,1)S(1)} collective-permute-done((bf16[4,96,768]{2,1,0:T(8,128)(2,1)S(1)}, bf16[4,96,768]{2,1,0:T(8,128)(2,1)S(1)}, u32[]{:S(2)}, u32[]{:S(2)}) %collective-permute-start.36) | collective-permute-done | bytes 589856 | tf_op jit(solution)/shard_map/ppermute | solution.py:644
  217.9 1.9 finish.3
  (155 shorter events, 11.6 us)
Async XLA Ops:
  1.3 9.6 %copy-start.45 = (f32[8,49]{1,0:T(8,128)}, f32[8,49]{1,0:T(8,128)S(1)}, u32[]{:S(2)}) copy-start(f32[8,49]{1,0:T(8,128)S(1)} %convert_element_type.294.valid_ref) | copy-start | bytes 4708
  1.3 4.5 %collective-permute-start.1 = (f32[8,49]{1,0:T(8,128)S(1)}, f32[8,49]{1,0:T(8,128)S(1)}, u32[]{:S(2)}, u32[]{:S(2)}) collective-permute-start(f32[8,49]{1,0:T(8,128)S(1)} %convert_element_type.294.valid_ref), channel_id=1, source_target_pairs={{0,1},{1,0},{2,3},{3,2},{4,5},{5,4},{6,7},{7,6},{8,9},{9,8},{10,11... | collective-permute-start | bytes 4712 | tf_op jit(solution)/shard_map/ppermute | solution.py:640
  4.3 18.7 %collective-permute-start = (bf16[392,768]{1,0:T(8,128)(2,1)}, bf16[392,768]{1,0:T(8,128)(2,1)S(1)}, u32[]{:S(2)}, u32[]{:S(2)}) collective-permute-start(bf16[392,768]{1,0:T(8,128)(2,1)} %bitcast.101), channel_id=1, source_target_pairs={{0,1},{1,0},{2,3},{3,2},{4,5},{5,4},{6,7},{7,6},{8,9},{9,8},{10,11... | collective-permute-start | bytes 1806344 | tf_op jit(solution)/shard_map/ppermute | solution.py:640
  5.9 17.1 %copy-start.48 = (f32[8,49]{1,0:T(8,128)}, f32[8,49]{1,0:T(8,128)S(1)}, u32[]{:S(2)}) copy-start(f32[8,49]{1,0:T(8,128)S(1)} %collective-permute-done.1.valid_ref) | copy-start | bytes 4708
  5.9 33.0 %collective-permute-start.2 = (bf16[392,768]{1,0:T(8,128)(2,1)}, bf16[392,768]{1,0:T(8,128)(2,1)S(1)}, u32[]{:S(2)}, u32[]{:S(2)}) collective-permute-start(bf16[392,768]{1,0:T(8,128)(2,1)} %bitcast.106), channel_id=1, source_target_pairs={{0,1},{1,0},{2,3},{3,2},{4,5},{5,4},{6,7},{7,6},{8,9},{9,8},{10,11... | collective-permute-start | bytes 1806344 | tf_op jit(solution)/shard_map/ppermute | solution.py:640
  8.9 30.0 %collective-permute-start.3 = (bf16[192,768]{1,0:T(8,128)(2,1)S(1)}, bf16[192,768]{1,0:T(8,128)(2,1)}, u32[]{:S(2)}, u32[]{:S(2)}) collective-permute-start(bf16[192,768]{1,0:T(8,128)(2,1)S(1)} %constant_dynamic-slice_fusion), channel_id=1, source_target_pairs={{0,1},{1,0},{2,3},{3,2},{4,5},{5,4},{6,7},{7,6},{8,9},{9,8},{10,11... | collective-permute-start | bytes 884744 | tf_op jit(solution)/shard_map/ppermute | solution.py:640
  10.9 29.2 %copy-start.4 = (bf16[384,768]{1,0:T(8,128)(2,1)S(1)}, bf16[384,768]{1,0:T(8,128)(2,1)}, u32[]{:S(2)}) copy-start(bf16[384,768]{1,0:T(8,128)(2,1)} %proj_ref.3) | copy-start | bytes 1769476
  23.8 29.2 %copy-start.3 = (bf16[1536,768]{1,0:T(8,128)(2,1)S(1)}, bf16[1536,768]{1,0:T(8,128)(2,1)}, u32[]{:S(2)}) copy-start(bf16[1536,768]{1,0:T(8,128)(2,1)} %fc2_ref.3) | copy-start | bytes 7077892
  39.7 7.9 %collective-permute-start.4 = (bf16[392,384]{1,0:T(8,128)(2,1)}, bf16[392,384]{1,0:T(8,128)(2,1)S(1)}, u32[]{:S(2)}, u32[]{:S(2)}) collective-permute-start(bf16[392,384]{1,0:T(8,128)(2,1)} %get-tuple-element.101.refs_8_), channel_id=1, source_target_pairs={{0,1},{1,0},{2,3},{3,2},{4,5},{5,4},{6,7},{7,6},{8,9},{9,8},{10,11... | collective-permute-start | bytes 903176 | tf_op jit(solution)/shard_map/ppermute | solution.py:640
  40.1 2.4 %collective-permute-start.5 = (bf16[192,768]{1,0:T(8,128)(2,1)}, bf16[192,768]{1,0:T(8,128)(2,1)S(1)}, u32[]{:S(2)}, u32[]{:S(2)}) collective-permute-start(bf16[192,768]{1,0:T(8,128)(2,1)} %collective-permute-done.3.refs_0_), channel_id=1, source_target_pairs={{0,2},{2,0},{4,6},{6,4},{8,10},{10,8},{12,14},{14,12},{16,18},{18,... | collective-permute-start | bytes 884744 | tf_op jit(solution)/shard_map/ppermute | solution.py:644
  40.1 12.9 %copy-start.2 = (bf16[768,1536]{1,0:T(8,128)(2,1)S(1)}, bf16[768,1536]{1,0:T(8,128)(2,1)}, u32[]{:S(2)}) copy-start(bf16[768,1536]{1,0:T(8,128)(2,1)} %fc1_ref.3) | copy-start | bytes 7077892
  42.5 10.5 %copy-start.46 = (f32[1536]{0:T(1024)S(1)}, f32[1536]{0:T(1024)}, u32[]{:S(2)}) copy-start(f32[1536]{0:T(1024)} %param.28) | copy-start | bytes 18436
  42.5 10.5 %copy-start.5 = (bf16[8,49,768]{2,0,1:T(8,128)(2,1)S(1)}, bf16[8,49,768]{2,0,1:T(8,128)(2,1)}, u32[]{:S(2)}) copy-start(bf16[8,49,768]{2,0,1:T(8,128)(2,1)} %param.31) | copy-start | bytes 1806340
  42.5 5.1 %copy-start.44 = (bf16[192,768]{1,0:T(8,128)(2,1)}, bf16[192,768]{1,0:T(8,128)(2,1)S(1)}, u32[]{:S(2)}) copy-start(bf16[192,768]{1,0:T(8,128)(2,1)S(1)} %collective-permute-done.5.refs_1_) | copy-start | bytes 884740
  52.2 13.5 %collective-permute-start.6 = (bf16[392,768]{1,0:T(8,128)(2,1)}, bf16[392,768]{1,0:T(8,128)(2,1)S(1)}, u32[]{:S(2)}, u32[]{:S(2)}) collective-permute-start(bf16[392,768]{1,0:T(8,128)(2,1)} %get-tuple-element.104.nm_ref.refs_0_), channel_id=1, source_target_pairs={{0,1},{1,0},{2,3},{3,2},{4,5},{5,4},{6,7},{7,6},{8,9},{9,8},{10,11... | collective-permute-start | bytes 1806344 | tf_op jit(solution)/shard_map/ppermute | solution.py:640
  54.1 11.6 %copy-start.8 = (bf16[392,768]{1,0:T(8,128)(2,1)S(1)}, bf16[392,768]{1,0:T(8,128)(2,1)}, u32[]{:S(2)}) copy-start(bf16[392,768]{1,0:T(8,128)(2,1)} %copy-done.7) | copy-start | bytes 1806340
  62.9 9.7 %copy-start.15 = (bf16[392,1536]{1,0:T(8,128)(2,1)}, bf16[392,1536]{1,0:T(8,128)(2,1)S(1)}, u32[]{:S(2)}) copy-start(bf16[392,1536]{1,0:T(8,128)(2,1)S(1)} %get-tuple-element.111.refs_3_) | copy-start | bytes 3612676
  65.7 6.9 %copy-start.10 = (bf16[392,768]{1,0:T(8,128)(2,1)}, bf16[392,768]{1,0:T(8,128)(2,1)S(1)}, u32[]{:S(2)}) copy-start(bf16[392,768]{1,0:T(8,128)(2,1)S(1)} %collective-permute-done.6.nm_ref.refs_4_) | copy-start | bytes 1806340
  74.6 13.6 %collective-permute-start.8 = (bf16[392,768]{1,0:T(8,128)(2,1)}, bf16[392,768]{1,0:T(8,128)(2,1)S(1)}, u32[]{:S(2)}, u32[]{:S(2)}) collective-permute-start(bf16[392,768]{1,0:T(8,128)(2,1)} %get-tuple-element.109), channel_id=1, source_target_pairs={{0,1},{1,0},{2,3},{3,2},{4,5},{5,4},{6,7},{7,6},{8,9},{9,8},{10,11... | collective-permute-start | bytes 1806344 | tf_op jit(solution)/shard_map/ppermute | solution.py:640
  75.7 13.3 %copy-start.6 = (bf16[8,49,768]{2,0,1:T(8,128)(2,1)S(1)}, bf16[8,49,768]{2,0,1:T(8,128)(2,1)}, u32[]{:S(2)}) copy-start(bf16[8,49,768]{2,0,1:T(8,128)(2,1)} %param.31) | copy-start | bytes 1806340
  75.7 13.3 %copy-start.19 = (f32[392,768]{1,0:T(8,128)S(1)}, f32[392,768]{1,0:T(8,128)}, u32[]{:S(2)}) copy-start(f32[392,768]{1,0:T(8,128)} %get-tuple-element.103.middle_ref) | copy-start | bytes 3612676
  75.7 13.3 %copy-start.36 = (f32[768]{0:T(1024)S(1)}, f32[768]{0:T(1024)}, u32[]{:S(2)}) copy-start(f32[768]{0:T(1024)} %gain_ref.8) | copy-start | bytes 9220
  75.7 13.3 %copy-start.38 = (bf16[392,768]{1,0:T(8,128)(2,1)S(1)}, bf16[392,768]{1,0:T(8,128)(2,1)}, u32[]{:S(2)}) copy-start(bf16[392,768]{1,0:T(8,128)(2,1)} %copy-done.37) | copy-start | bytes 1806340
  87.6 4.6 %collective-permute-start.9 = (bf16[2,4,96,768]{3,2,1,0:T(8,128)(2,1)}, bf16[2,4,96,768]{3,2,1,0:T(8,128)(2,1)S(1)}, u32[]{:S(2)}, u32[]{:S(2)}) collective-permute-start(bf16[2,4,96,768]{3,2,1,0:T(8,128)(2,1)} %get-tuple-element.118), channel_id=1, source_target_pairs={{0,2},{2,0},{4,6},{6,4},{8,10},{10,8},{12,14},{14,12},{16,18},{18,... | collective-permute-start | bytes 3538952 | tf_op jit(solution)/shard_map/ppermute | solution.py:644
  87.7 6.3 %collective-permute-start.10 = (bf16[2,4,96,768]{3,2,1,0:T(8,128)(2,1)}, bf16[2,4,96,768]{3,2,1,0:T(8,128)(2,1)S(1)}, u32[]{:S(2)}, u32[]{:S(2)}) collective-permute-start(bf16[2,4,96,768]{3,2,1,0:T(8,128)(2,1)} %get-tuple-element.121), channel_id=1, source_target_pairs={{0,2},{2,0},{4,6},{6,4},{8,10},{10,8},{12,14},{14,12},{16,18},{18,... | collective-permute-start | bytes 3538952 | tf_op jit(solution)/shard_map/ppermute | solution.py:644
  90.1 5.7 %copy-start.30 = (bf16[8,64,384]{2,1,0:T(8,128)(2,1)S(1)}, bf16[8,64,384]{2,1,0:T(8,128)(2,1)}, u32[]{:S(2)}) copy-start(bf16[8,64,384]{2,1,0:T(8,128)(2,1)} %get-tuple-element.126.k_ref) | copy-start | bytes 1179652
  90.1 5.7 %copy-start.31 = (bf16[8,64,384]{2,1,0:T(8,128)(2,1)S(1)}, bf16[8,64,384]{2,1,0:T(8,128)(2,1)}, u32[]{:S(2)}) copy-start(bf16[8,64,384]{2,1,0:T(8,128)(2,1)} %get-tuple-element.127.v_ref) | copy-start | bytes 1179652
  91.2 21.3 %collective-permute-start.11 = (bf16[392,768]{1,0:T(8,128)(2,1)S(1)}, bf16[392,768]{1,0:T(8,128)(2,1)S(1)}, u32[]{:S(2)}, u32[]{:S(2)}) collective-permute-start(bf16[392,768]{1,0:T(8,128)(2,1)S(1)} %get-tuple-element.143.branch_ref.refs_2_), channel_id=1, source_target_pairs={{0,1},{1,0},{2,3},{3,2},{4,5},{5,4},{6,7},{7,6},{8,9},{9,8},{10,11... | collective-permute-start | bytes 1806344 | tf_op jit(solution)/shard_map/ppermute | solution.py:640
  92.4 16.3 %collective-permute-start.12 = (bf16[4,96,768]{2,1,0:T(8,128)(2,1)S(1)}, bf16[4,96,768]{2,1,0:T(8,128)(2,1)S(1)}, u32[]{:S(2)}, u32[]{:S(2)}) collective-permute-start(bf16[4,96,768]{2,1,0:T(8,128)(2,1)S(1)} %fusion), channel_id=1, source_target_pairs={{0,4},{2,6},{4,0},{6,2},{8,12},{10,14},{12,8},{14,10},{16,20},{18,... | collective-permute-start | bytes 1769480 | tf_op jit(solution)/shard_map/ppermute | solution.py:644
  94.1 29.0 %collective-permute-start.17 = (bf16[4,96,768]{2,1,0:T(8,128)(2,1)S(1)}, bf16[4,96,768]{2,1,0:T(8,128)(2,1)S(1)}, u32[]{:S(2)}, u32[]{:S(2)}) collective-permute-start(bf16[4,96,768]{2,1,0:T(8,128)(2,1)S(1)} %fusion.1), channel_id=1, source_target_pairs={{0,4},{2,6},{4,0},{6,2},{8,12},{10,14},{12,8},{14,10},{16,20},{18,... | collective-permute-start | bytes 1769480 | tf_op jit(solution)/shard_map/ppermute | solution.py:644
  94.7 33.2 %collective-permute-start.7 = (bf16[392,768]{1,0:T(8,128)(2,1)S(1)}, bf16[392,768]{1,0:T(8,128)(2,1)S(1)}, u32[]{:S(2)}, u32[]{:S(2)}) collective-permute-start(bf16[392,768]{1,0:T(8,128)(2,1)S(1)} %get-tuple-element.108), channel_id=1, source_target_pairs={{0,1},{1,0},{2,3},{3,2},{4,5},{5,4},{6,7},{7,6},{8,9},{9,8},{10,11... | collective-permute-start | bytes 1806344 | tf_op jit(solution)/shard_map/ppermute | solution.py:640
  95.8 17.5 %copy-start.27 = (bf16[8,64,384]{2,1,0:T(8,128)(2,1)S(1)}, bf16[8,64,384]{2,1,0:T(8,128)(2,1)}, u32[]{:S(2)}) copy-start(bf16[8,64,384]{2,1,0:T(8,128)(2,1)} %get-tuple-element.133.k_ref) | copy-start | bytes 1179652
  95.9 17.5 %copy-start.28 = (bf16[8,64,384]{2,1,0:T(8,128)(2,1)S(1)}, bf16[8,64,384]{2,1,0:T(8,128)(2,1)}, u32[]{:S(2)}) copy-start(bf16[8,64,384]{2,1,0:T(8,128)(2,1)} %get-tuple-element.134.v_ref) | copy-start | bytes 1179652
  105.6 7.7 %copy-start.12 = (bf16[392,768]{1,0:T(8,128)(2,1)S(1)}, bf16[392,768]{1,0:T(8,128)(2,1)}, u32[]{:S(2)}) copy-start(bf16[392,768]{1,0:T(8,128)(2,1)} %copy-done.11) | copy-start | bytes 1806340
  105.6 7.7 %copy-start.22 = (bf16[8,3,64,256]{3,2,1,0:T(8,128)(2,1)S(1)}, bf16[8,3,64,256]{3,2,1,0:T(8,128)(2,1)}, u32[]{:S(2)}) copy-start(bf16[8,3,64,256]{3,2,1,0:T(8,128)(2,1)} %get-tuple-element.131.prob_ref) | copy-start | bytes 2359300
  105.6 7.7 %copy-start.26 = (bf16[8,64,384]{2,1,0:T(8,128)(2,1)S(1)}, bf16[8,64,384]{2,1,0:T(8,128)(2,1)}, u32[]{:S(2)}) copy-start(bf16[8,64,384]{2,1,0:T(8,128)(2,1)} %get-tuple-element.132.q_ref) | copy-start | bytes 1179652
  108.9 18.1 %collective-permute-start.16 = (bf16[96,768]{1,0:T(8,128)(2,1)S(1)}, bf16[96,768]{1,0:T(8,128)(2,1)S(1)}, u32[]{:S(2)}, u32[]{:S(2)}) collective-permute-start(bf16[96,768]{1,0:T(8,128)(2,1)S(1)} %get-tuple-element.188), channel_id=1, source_target_pairs={{0,24},{2,26},{4,28},{6,30},{8,16},{10,18},{12,20},{14,22},{16,8},... | collective-permute-start | bytes 442376 | tf_op jit(solution)/shard_map/ppermute | solution.py:644
  112.5 14.5 %collective-permute-start.15 = (bf16[96,768]{1,0:T(8,128)(2,1)S(1)}, bf16[96,768]{1,0:T(8,128)(2,1)S(1)}, u32[]{:S(2)}, u32[]{:S(2)}) collective-permute-start(bf16[96,768]{1,0:T(8,128)(2,1)S(1)} %get-tuple-element.189), channel_id=1, source_target_pairs={{0,16},{2,18},{4,20},{6,22},{8,24},{10,26},{12,28},{14,30},{16,0},... | collective-permute-start | bytes 442376 | tf_op jit(solution)/shard_map/ppermute | solution.py:644
  112.5 15.3 %collective-permute-start.14 = (bf16[96,768]{1,0:T(8,128)(2,1)S(1)}, bf16[96,768]{1,0:T(8,128)(2,1)S(1)}, u32[]{:S(2)}, u32[]{:S(2)}) collective-permute-start(bf16[96,768]{1,0:T(8,128)(2,1)S(1)} %get-tuple-element.190), channel_id=1, source_target_pairs={{0,8},{2,10},{4,12},{6,14},{8,0},{10,2},{12,4},{14,6},{16,24},{18,... | collective-permute-start | bytes 442376 | tf_op jit(solution)/shard_map/ppermute | solution.py:644
  123.1 4.8 %copy-start.18 = (bf16[392,384]{1,0:T(8,128)(2,1)S(1)}, bf16[392,384]{1,0:T(8,128)(2,1)}, u32[]{:S(2)}) copy-start(bf16[392,384]{1,0:T(8,128)(2,1)} %get-tuple-element.96.refs_1_) | copy-start | bytes 903172
  123.1 4.8 %copy-start.20 = (bf16[768,392]{1,0:T(8,128)(2,1)S(1)}, bf16[768,392]{1,0:T(8,128)(2,1)}, u32[]{:S(2)}) copy-start(bf16[768,392]{1,0:T(8,128)(2,1)} %get-tuple-element.142.refs_0_) | copy-start | bytes 1806340
  123.1 4.8 %copy-start.21 = (bf16[768,392]{1,0:T(8,128)(2,1)S(1)}, bf16[768,392]{1,0:T(8,128)(2,1)}, u32[]{:S(2)}) copy-start(bf16[768,392]{1,0:T(8,128)(2,1)} %get-tuple-element.148.refs_7_) | copy-start | bytes 1806340
  123.3 10.4 %collective-permute-start.20 = (bf16[96,768]{1,0:T(8,128)(2,1)S(1)}, bf16[96,768]{1,0:T(8,128)(2,1)S(1)}, u32[]{:S(2)}, u32[]{:S(2)}) collective-permute-start(bf16[96,768]{1,0:T(8,128)(2,1)S(1)} %get-tuple-element.185), channel_id=1, source_target_pairs={{0,24},{2,26},{4,28},{6,30},{8,16},{10,18},{12,20},{14,22},{16,8},... | collective-permute-start | bytes 442376 | tf_op jit(solution)/shard_map/ppermute | solution.py:644
  127.0 9.5 %collective-permute-start.19 = (bf16[96,768]{1,0:T(8,128)(2,1)S(1)}, bf16[96,768]{1,0:T(8,128)(2,1)S(1)}, u32[]{:S(2)}, u32[]{:S(2)}) collective-permute-start(bf16[96,768]{1,0:T(8,128)(2,1)S(1)} %get-tuple-element.186), channel_id=1, source_target_pairs={{0,16},{2,18},{4,20},{6,22},{8,24},{10,26},{12,28},{14,30},{16,0},... | collective-permute-start | bytes 442376 | tf_op jit(solution)/shard_map/ppermute | solution.py:644
  127.0 9.5 %collective-permute-start.18 = (bf16[96,768]{1,0:T(8,128)(2,1)S(1)}, bf16[96,768]{1,0:T(8,128)(2,1)S(1)}, u32[]{:S(2)}, u32[]{:S(2)}) collective-permute-start(bf16[96,768]{1,0:T(8,128)(2,1)S(1)} %get-tuple-element.187), channel_id=1, source_target_pairs={{0,8},{2,10},{4,12},{6,14},{8,0},{10,2},{12,4},{14,6},{16,24},{18,... | collective-permute-start | bytes 442376 | tf_op jit(solution)/shard_map/ppermute | solution.py:644
  136.6 2.9 %collective-permute-start.22 = (bf16[2,4,96,768]{3,2,1,0:T(8,128)(2,1)S(1)}, bf16[2,4,96,768]{3,2,1,0:T(8,128)(2,1)S(1)}, u32[]{:S(2)}, u32[]{:S(2)}) collective-permute-start(bf16[2,4,96,768]{3,2,1,0:T(8,128)(2,1)S(1)} %get-tuple-element.159), channel_id=1, source_target_pairs={{0,2},{2,0},{4,6},{6,4},{8,10},{10,8},{12,14},{14,12},{16,18},{18,... | collective-permute-start | bytes 3538952 | tf_op jit(solution)/shard_map/ppermute | solution.py:644
  136.7 21.6 %collective-permute-start.13 = (bf16[392,768]{1,0:T(8,128)(2,1)S(1)}, bf16[392,768]{1,0:T(8,128)(2,1)S(1)}, u32[]{:S(2)}, u32[]{:S(2)}) collective-permute-start(bf16[392,768]{1,0:T(8,128)(2,1)S(1)} %get-tuple-element.135), channel_id=1, source_target_pairs={{0,1},{1,0},{2,3},{3,2},{4,5},{5,4},{6,7},{7,6},{8,9},{9,8},{10,11... | collective-permute-start | bytes 1806344 | tf_op jit(solution)/shard_map/ppermute | solution.py:640
  139.7 18.6 %collective-permute-start.23 = (bf16[4,96,768]{2,1,0:T(8,128)(2,1)S(1)}, bf16[4,96,768]{2,1,0:T(8,128)(2,1)S(1)}, u32[]{:S(2)}, u32[]{:S(2)}) collective-permute-start(bf16[4,96,768]{2,1,0:T(8,128)(2,1)S(1)} %fusion.2), channel_id=1, source_target_pairs={{0,4},{2,6},{4,0},{6,2},{8,12},{10,14},{12,8},{14,10},{16,20},{18,... | collective-permute-start | bytes 1769480 | tf_op jit(solution)/shard_map/ppermute | solution.py:644
  141.3 17.0 %collective-permute-start.25 = (bf16[208,768]{1,0:T(8,128)(2,1)S(1)}, bf16[208,768]{1,0:T(8,128)(2,1)S(1)}, u32[]{:S(2)}, u32[]{:S(2)}) collective-permute-start(bf16[208,768]{1,0:T(8,128)(2,1)S(1)} %get-tuple-element.192), channel_id=1, source_target_pairs={{0,16},{2,18},{4,20},{6,22},{8,24},{10,26},{12,28},{14,30},{16,0},... | collective-permute-start | bytes 958472 | tf_op jit(solution)/shard_map/ppermute | solution.py:644
  141.4 29.4 %collective-permute-start.21 = (bf16[208,768]{1,0:T(8,128)(2,1)S(1)}, bf16[208,768]{1,0:T(8,128)(2,1)S(1)}, u32[]{:S(2)}, u32[]{:S(2)}) collective-permute-start(bf16[208,768]{1,0:T(8,128)(2,1)S(1)} %get-tuple-element.192), channel_id=1, source_target_pairs={{0,8},{2,10},{4,12},{6,14},{8,0},{10,2},{12,4},{14,6},{16,24},{18,... | collective-permute-start | bytes 958472 | tf_op jit(solution)/shard_map/ppermute | solution.py:644
  158.3 10.4 %collective-permute-start.26 = (bf16[208,768]{1,0:T(8,128)(2,1)S(1)}, bf16[208,768]{1,0:T(8,128)(2,1)S(1)}, u32[]{:S(2)}, u32[]{:S(2)}) collective-permute-start(bf16[208,768]{1,0:T(8,128)(2,1)S(1)} %collective-permute-done.25), channel_id=1, source_target_pairs={{0,8},{2,10},{4,12},{6,14},{8,0},{10,2},{12,4},{14,6},{16,24},{18,... | collective-permute-start | bytes 958472 | tf_op jit(solution)/shard_map/ppermute | solution.py:644
  158.3 12.5 %collective-permute-start.24 = (bf16[96,768]{1,0:T(8,128)(2,1)S(1)}, bf16[96,768]{1,0:T(8,128)(2,1)S(1)}, u32[]{:S(2)}, u32[]{:S(2)}) collective-permute-start(bf16[96,768]{1,0:T(8,128)(2,1)S(1)} %fusion.8), channel_id=1, source_target_pairs={{0,8},{2,10},{4,12},{6,14},{8,0},{10,2},{12,4},{14,6},{16,24},{18,... | collective-permute-start | bytes 442376 | tf_op jit(solution)/shard_map/ppermute | solution.py:644
  171.0 29.1 %collective-permute-start.27 = (bf16[4,208,768]{2,1,0:T(8,128)(2,1)S(1)}, bf16[4,208,768]{2,1,0:T(8,128)(2,1)S(1)}, u32[]{:S(2)}, u32[]{:S(2)}) collective-permute-start(bf16[4,208,768]{2,1,0:T(8,128)(2,1)S(1)} %pad_maximum_fusion.refs_0_), channel_id=1, source_target_pairs={{0,4},{2,6},{4,0},{6,2},{8,12},{10,14},{12,8},{14,10},{16,20},{18,... | collective-permute-start | bytes 3833864 | tf_op jit(solution)/shard_map/ppermute | solution.py:644
  171.7 6.9 %collective-permute-start.28 = (bf16[96,768]{1,0:T(8,128)(2,1)S(1)}, bf16[96,768]{1,0:T(8,128)(2,1)S(1)}, u32[]{:S(2)}, u32[]{:S(2)}) collective-permute-start(bf16[96,768]{1,0:T(8,128)(2,1)S(1)} %get-tuple-element.183), channel_id=1, source_target_pairs={{0,8},{2,10},{4,12},{6,14},{8,0},{10,2},{12,4},{14,6},{16,24},{18,... | collective-permute-start | bytes 442376 | tf_op jit(solution)/shard_map/ppermute | solution.py:644
  172.1 8.8 %collective-permute-start.29 = (bf16[96,768]{1,0:T(8,128)(2,1)S(1)}, bf16[96,768]{1,0:T(8,128)(2,1)S(1)}, u32[]{:S(2)}, u32[]{:S(2)}) collective-permute-start(bf16[96,768]{1,0:T(8,128)(2,1)S(1)} %get-tuple-element.184), channel_id=1, source_target_pairs={{0,16},{2,18},{4,20},{6,22},{8,24},{10,26},{12,28},{14,30},{16,0},... | collective-permute-start | bytes 442376 | tf_op jit(solution)/shard_map/ppermute | solution.py:644
  181.0 7.3 %collective-permute-start.31 = (bf16[96,768]{1,0:T(8,128)(2,1)S(1)}, bf16[96,768]{1,0:T(8,128)(2,1)S(1)}, u32[]{:S(2)}, u32[]{:S(2)}) collective-permute-start(bf16[96,768]{1,0:T(8,128)(2,1)S(1)} %fusion.7), channel_id=1, source_target_pairs={{0,16},{2,18},{4,20},{6,22},{8,24},{10,26},{12,28},{14,30},{16,0},... | collective-permute-start | bytes 442376 | tf_op jit(solution)/shard_map/ppermute | solution.py:644
  181.2 8.0 %collective-permute-start.30 = (bf16[96,768]{1,0:T(8,128)(2,1)S(1)}, bf16[96,768]{1,0:T(8,128)(2,1)S(1)}, u32[]{:S(2)}, u32[]{:S(2)}) collective-permute-start(bf16[96,768]{1,0:T(8,128)(2,1)S(1)} %fusion.7), channel_id=1, source_target_pairs={{0,8},{2,10},{4,12},{6,14},{8,0},{10,2},{12,4},{14,6},{16,24},{18,... | collective-permute-start | bytes 442376 | tf_op jit(solution)/shard_map/ppermute | solution.py:644
  188.3 5.1 %collective-permute-start.32 = (bf16[96,768]{1,0:T(8,128)(2,1)S(1)}, bf16[96,768]{1,0:T(8,128)(2,1)S(1)}, u32[]{:S(2)}, u32[]{:S(2)}) collective-permute-start(bf16[96,768]{1,0:T(8,128)(2,1)S(1)} %collective-permute-done.31), channel_id=1, source_target_pairs={{0,8},{2,10},{4,12},{6,14},{8,0},{10,2},{12,4},{14,6},{16,24},{18,... | collective-permute-start | bytes 442376 | tf_op jit(solution)/shard_map/ppermute | solution.py:644
  188.3 12.9 %collective-permute-start.33 = (bf16[4,208,768]{2,1,0:T(8,128)(2,1)S(1)}, bf16[4,208,768]{2,1,0:T(8,128)(2,1)S(1)}, u32[]{:S(2)}, u32[]{:S(2)}) collective-permute-start(bf16[4,208,768]{2,1,0:T(8,128)(2,1)S(1)} %pad_maximum_fusion.refs_0_), channel_id=1, source_target_pairs={{0,2},{2,0},{4,6},{6,4},{8,10},{10,8},{12,14},{14,12},{16,18},{18,... | collective-permute-start | bytes 3833864 | tf_op jit(solution)/shard_map/ppermute | solution.py:644
  200.2 3.0 %collective-permute-start.34 = (bf16[4,208,768]{2,1,0:T(8,128)(2,1)S(1)}, bf16[4,208,768]{2,1,0:T(8,128)(2,1)S(1)}, u32[]{:S(2)}, u32[]{:S(2)}) collective-permute-start(bf16[4,208,768]{2,1,0:T(8,128)(2,1)S(1)} %collective-permute-done.27.refs_1_), channel_id=1, source_target_pairs={{0,2},{2,0},{4,6},{6,4},{8,10},{10,8},{12,14},{14,12},{16,18},{18,... | collective-permute-start | bytes 3833864 | tf_op jit(solution)/shard_map/ppermute | solution.py:644
  200.2 9.1 %collective-permute-start.37 = (bf16[4,96,768]{2,1,0:T(8,128)(2,1)S(1)}, bf16[4,96,768]{2,1,0:T(8,128)(2,1)S(1)}, u32[]{:S(2)}, u32[]{:S(2)}) collective-permute-start(bf16[4,96,768]{2,1,0:T(8,128)(2,1)S(1)} %pad_maximum_fusion.1.refs_0_), channel_id=1, source_target_pairs={{0,2},{2,0},{4,6},{6,4},{8,10},{10,8},{12,14},{14,12},{16,18},{18,... | collective-permute-start | bytes 1769480 | tf_op jit(solution)/shard_map/ppermute | solution.py:644
  200.7 15.2 %collective-permute-start.36 = (bf16[4,96,768]{2,1,0:T(8,128)(2,1)S(1)}, bf16[4,96,768]{2,1,0:T(8,128)(2,1)S(1)}, u32[]{:S(2)}, u32[]{:S(2)}) collective-permute-start(bf16[4,96,768]{2,1,0:T(8,128)(2,1)S(1)} %pad_maximum_fusion.1.refs_0_), channel_id=1, source_target_pairs={{0,4},{2,6},{4,0},{6,2},{8,12},{10,14},{12,8},{14,10},{16,20},{18,... | collective-permute-start | bytes 1769480 | tf_op jit(solution)/shard_map/ppermute | solution.py:644
  208.6 3.9 %collective-permute-start.35 = (f32[6,768]{1,0:T(8,128)S(1)}, f32[6,768]{1,0:T(8,128)S(1)}, u32[]{:S(2)}, u32[]{:S(2)}) collective-permute-start(f32[6,768]{1,0:T(8,128)S(1)} %slice.210), channel_id=1, source_target_pairs={{0,1},{1,0},{2,3},{3,2},{4,5},{5,4},{6,7},{7,6},{8,9},{9,8},{10,11... | collective-permute-start | bytes 55304 | tf_op jit(solution)/shard_map/ppermute | solution.py:640
  215.9 2.0 collective-permute-start.38
  (24 other events, 48.1 us)

commit v7 on v6

--- a/solution.py
+++ b/solution.py
@@ -669,6 +669,11 @@
 
 def flip_line(pieces):
     return [flip(p, LINE * k) for k, p in zip((1, 2, 3), pieces)]
+
+
+def sum_line(sends):
+    near, far, both = sends
+    return [flip(near, LINE), flip(total_of([far, flip(both, LINE)]), 2 * LINE)]
 
 
 def gather_line(piece):
@@ -789,12 +794,11 @@
         piece2 = own_piece(keep2, got2, side2, line2)
         keep, send = g_attn
         got = flip(after(send, piece2), CORE)
-        side = after(flip(side_send(keep, got), SIDE), gnorms[1])
+        side = flip(side_send(keep, got), SIDE)
         fc = jnp.concatenate([piece1, piece2, small], axis=0)
-        near, far, both = line_sends(keep, got, side)
-        both = flip(both, LINE)
-        fc_quad = jnp.stack([fc] + [after(r, both) for r in gather_line(fc)])
-        line = [after(flip(near, LINE), output, gpatch), flip(total_of([far, both]), 2 * LINE)]
+        fc_quad = jnp.stack([fc] + [after(r, output, gpatch) for r in gather_line(fc)])
+        side = after(side, fc_quad, output, gpatch)
+        line = sum_line(line_sends(keep, got, side))
         piece = own_piece(keep, got, side, line)
         quad = jnp.stack([piece] + gather_line(piece))
         fc_pair = after(flip(fc_quad, SIDE), quad)

time: 220 us -> 215 us (0.977)
  waiting for transfers between devices: 72.2 us -> 68.6 us
    ppermute x28, waiting for transfers between devices: 59.2 us -> 56.2 us  [flip(): return lax.ppermute(v, 'dp', [(i, i ^ bits) for i in range(16)])]
    ppermute x28, starting transfers between devices: 24 us -> 21.6 us  [flip(): return lax.ppermute(v, 'dp', [(i, i ^ bits) for i in range(16)])]
  transfers between devices with their start and end apart: 39 -> 39, of which waited for: 20 -> 18; matrix products, arithmetic and copies ran while one was open for 4% -> 4% of each run, Pallas kernels for 35% -> 36%
where the time goes in v7:
time: 215 us
  Pallas kernels  90.7 us (42%)
  waiting for transfers between devices  68.6 us (32%)
  starting transfers between devices  33.2 us (15%)
  local copies, waits for them, and re-layouts  14.5 us (7%)
  other arithmetic  4.01 us (2%)
  matrix products  2.4 us (1%)
    pallas_call x15, Pallas kernels, call(): pl.pallas_call(kernel, out_shape=outs, in_specs=in_specs, out_specs=[spac...  90.7 us
    ppermute x28, waiting for transfers between devices, flip(): return lax.ppermute(v, 'dp', [(i, i ^ bits) for i in range(16)])  56.2 us
    ppermute x28, starting transfers between devices, flip(): return lax.ppermute(v, 'dp', [(i, i ^ bits) for i in range(16)])  21.6 us
    ppermute x11, waiting for transfers between devices, across(): return lax.ppermute(v, 'mp', [(0, 1), (1, 0)])  12.4 us
    unnamed x98, local copies, waits for them, and re-layouts  11.6 us
    ppermute x11, starting transfers between devices, across(): return lax.ppermute(v, 'mp', [(0, 1), (1, 0)])  11.6 us
  transfers between devices with their start and end apart: 39, of which 18 were waited for; matrix products, arithmetic and copies ran while one was open for 4% of the time, Pallas kernels for 36%

profile of v7, /device:TPU:0, one launch (start us, length us, event | category | flops | bytes accessed | tf_op | source)
XLA Modules:
  0.0 214.8 jit_solution(18073700292248581760)
XLA Ops:
  1.3 2.9 %collective-permute-start.1 = (f32[8,49]{1,0:T(8,128)S(1)}, f32[8,49]{1,0:T(8,128)S(1)}, u32[]{:S(2)}, u32[]{:S(2)}) collective-permute-start(f32[8,49]{1,0:T(8,128)S(1)} %convert_element_type.294.valid_ref), channel_id=1, source_target_pairs={{0,1},{1,0},{2,3},{3,2},{4,5},{5,4},{6,7},{7,6},{8,9},{9,8},{10,11... | collective-permute-start | bytes 4712 | tf_op jit(solution)/shard_map/ppermute | solution.py:640
  4.3 1.6 collective-permute-done.1.valid_ref
  5.9 2.0 collective-permute-start.2
  7.9 1.0 constant_dynamic-slice_fusion
  10.9 12.1 %attn_forward.2 = (bf16[8,3,64,256]{3,2,1,0:T(8,128)(2,1)}, bf16[8,64,384]{2,1,0:T(8,128)(2,1)}, bf16[8,64,384]{2,1,0:T(8,128)(2,1)}, bf16[8,64,384]{2,1,0:T(8,1...) custom-call(bf16[392,768]{1,0:T(8,128)(2,1)} %bitcast.102, f32[768]{0:T(1024)} %gain_ref.9, f32[768]{0:T(1024)} %shift_ref.4, ...), custom_call_target="tpu_custom_call" | custom-call | flops 1000000 | bytes 3906 | tf_op jit(solution)/shard_map/attn_forward/pallas_call | solution.py:519
  23.0 0.8 copy-done.11
  23.8 12.1 %attn_forward.3 = (bf16[8,3,64,256]{3,2,1,0:T(8,128)(2,1)}, bf16[8,64,384]{2,1,0:T(8,128)(2,1)}, bf16[8,64,384]{2,1,0:T(8,128)(2,1)}, bf16[8,64,384]{2,1,0:T(8,1...) custom-call(bf16[392,768]{1,0:T(8,128)(2,1)} %copy-done.11, f32[768]{0:T(1024)} %gain_ref.9, f32[768]{0:T(1024)} %shift_ref.4, ...), custom_call_target="tpu_custom_call" | custom-call | flops 1000000 | bytes 3906 | tf_op jit(solution)/shard_map/attn_forward/pallas_call | solution.py:519
  35.9 2.9 %collective-permute-done.3.refs_0_ = bf16[192,768]{1,0:T(8,128)(2,1)} collective-permute-done((bf16[192,768]{1,0:T(8,128)(2,1)S(1)}, bf16[192,768]{1,0:T(8,128)(2,1)}, u32[]{:S(2)}, u32[]{:S(2)}) %collective-permute-start.3) | collective-permute-done | bytes 294944 | tf_op jit(solution)/shard_map/ppermute | solution.py:640
  38.9 0.8 copy-done.7
  40.1 2.4 %convolution_convert_fusion.own_in = bf16[392,768]{1,0:T(8,128)(2,1)} fusion(bf16[392,384]{1,0:T(8,128)(2,1)} %get-tuple-element.95.refs_1_, bf16[384,768]{1,0:T(8,128)(2,1)S(1)} %copy-done.4), kind=kOutput, calls=%fused_computation | convolution fusion | flops 231512064 | bytes 1492992 | tf_op jit(solution)/shard_map/dot_general | solution.py:738
  42.5 5.1 %collective-permute-done.4.peer_in = bf16[392,384]{1,0:T(8,128)(2,1)S(1)} collective-permute-done((bf16[392,384]{1,0:T(8,128)(2,1)}, bf16[392,384]{1,0:T(8,128)(2,1)S(1)}, u32[]{:S(2)}, u32[]{:S(2)}) %collective-permute-start.4) | collective-permute-done | bytes 301088 | tf_op jit(solution)/shard_map/ppermute | solution.py:640
  47.6 0.7 copy-done.43
  48.3 3.8 %middle.1 = (f32[392,768]{1,0:T(8,128)}, bf16[392,768]{1,0:T(8,128)(2,1)}) custom-call(s32[1]{0:T(128)} %bitcast.me_ref, bf16[392,768]{1,0:T(8,128)(2,1)} %bitcast.103, bf16[392,768]{1,0:T(8,128)(2,1)} %convolution_convert_fusion.own_in, bf16[392,384]{1,0:T(8,128)(2,1)} %copy-done.43, f32[768]{0:T(1024)} %bias_ref.5, f32[768]{0:T(1024)} %gain_ref.8, ...), custom_call_target="tpu_custom_call" | custom-call | flops 1000000 | bytes 3906 | tf_op jit(solution)/shard_map/middle/pallas_call | solution.py:519
  52.2 0.8 collective-permute-start.6
  53.0 1.1 copy-done.9
  54.1 6.1 %mlp.2 = (bf16[392,1536]{1,0:T(8,128)(2,1)S(1)}, bf16[392,1536]{1,0:T(8,128)(2,1)S(1)}, bf16[392,768]{1,0:T(8,128)(2,1)S(1)}, bf16[392,768]{1,0:T(8,128)(2,1)S(1)}) custom-call(bf16[392,768]{1,0:T(8,128)(2,1)S(1)} %copy-done.9, bf16[392,768]{1,0:T(8,128)(2,1)S(1)} %bitcast.108, bf16[768,1536]{1,0:T(8,128)(2,1)S(1)} %copy-done.2, ...), custom_call_target="tpu_custom_call" | custom-call | flops 1000000 | bytes 3906 | tf_op jit(solution)/shard_map/mlp/pallas_call | solution.py:519
  60.2 1.0 copy-done.14
  61.2 0.8 copy-done.24
  62.0 0.8 copy-done.37
  62.9 2.8 %collective-permute-done.6.nm_ref.refs_4_ = bf16[392,768]{1,0:T(8,128)(2,1)S(1)} collective-permute-done((bf16[392,768]{1,0:T(8,128)(2,1)}, bf16[392,768]{1,0:T(8,128)(2,1)S(1)}, u32[]{:S(2)}, u32[]{:S(2)}) %collective-permute-start.6) | collective-permute-done | bytes 602144 | tf_op jit(solution)/shard_map/ppermute | solution.py:640
  65.7 6.9 %mlp.3 = (bf16[392,1536]{1,0:T(8,128)(2,1)S(1)}, bf16[392,1536]{1,0:T(8,128)(2,1)S(1)}, bf16[392,768]{1,0:T(8,128)(2,1)S(1)}, bf16[392,768]{1,0:T(8,128)(2,1)}) custom-call(bf16[392,768]{1,0:T(8,128)(2,1)S(1)} %collective-permute-done.6.nm_ref.refs_4_, bf16[392,768]{1,0:T(8,128)(2,1)S(1)} %copy-done.8, bf16[768,1536]{1,0:T(8,128)(2,1)S(1)} %copy-done.2, ...), custom_call_target="tpu_custom_call" | custom-call | flops 1000000 | bytes 3906 | tf_op jit(solution)/shard_map/mlp/pallas_call | solution.py:519
  72.6 1.0 copy-done.16
  73.6 1.0 copy-done.17
  74.6 1.1 collective-permute-start.8
  75.7 11.9 %mlp_weights.1 = (f32[1,1536]{1,0:T(1,128)}, bf16[2,4,96,768]{3,2,1,0:T(8,128)(2,1)}, bf16[2,4,96,768]{3,2,1,0:T(8,128)(2,1)}, bf16[2,4,96,768]{3,2,1,0:T(8,128)(2,1)}, bf16[2,4,96,768]{3,2,1,0:T(8,128)(2,1)}) custom-call(s32[1]{0:T(128)} %bitcast.me_ref, bf16[392,768]{1,0:T(8,128)(2,1)} %get-tuple-element.103.nm_ref.refs_0_, bf16[392,768]{1,0:T(8,128)(2,1)} %bitcast.107, ...), custom_call_target="tpu_custom_call" | custom-call | flops 1000000 | bytes 3906 | tf_op jit(solution)/shard_map/mlp_weights/pallas_call | solution.py:519
  88.2 0.8 copy-done.39
  89.0 1.1 copy-done.40
  90.1 1.1 middle_back.1
  91.2 1.0 collective-permute-start.11
  92.4 1.6 collective-permute-start.12
  94.7 1.1 collective-permute-start.7
  95.9 9.7 %attn_backward.2 = (bf16[3,392,384]{2,1,0:T(8,128)(2,1)S(1)}, f32[1,768]{1,0:T(1,128)S(1)}, f32[3,64,256]{2,1,0:T(8,128)S(1)}, bf16[392,768]{1,0:T(8,128)(2,1)S(1)}, f32[2,768]{1,0:T(2,128)S(1)}) custom-call(bf16[392,768]{1,0:T(8,128)(2,1)S(1)} %get-tuple-element.142.branch_ref.refs_2_, bf16[392,768]{1,0:T(8,128)(2,1)S(1)} %bitcast.104, ...), custom_call_target="tpu_custom_call" | custom-call | flops 1000000 | bytes 3906 | tf_op jit(solution)/shard_map/attn_backward/pallas_call | solution.py:519
  105.7 3.0 %collective-permute-done.12 = bf16[4,96,768]{2,1,0:T(8,128)(2,1)S(1)} collective-permute-done((bf16[4,96,768]{2,1,0:T(8,128)(2,1)S(1)}, bf16[4,96,768]{2,1,0:T(8,128)(2,1)S(1)}, u32[]{:S(2)}, u32[]{:S(2)}) %collective-permute-start.12) | collective-permute-done | bytes 589856 | tf_op jit(solution)/shard_map/ppermute | solution.py:644
  108.9 3.7 %collective-permute-start.16 = (bf16[96,768]{1,0:T(8,128)(2,1)S(1)}, bf16[96,768]{1,0:T(8,128)(2,1)S(1)}, u32[]{:S(2)}, u32[]{:S(2)}) collective-permute-start(bf16[96,768]{1,0:T(8,128)(2,1)S(1)} %get-tuple-element.186), channel_id=1, source_target_pairs={{0,24},{2,26},{4,28},{6,30},{8,16},{10,18},{12,20},{14,22},{16,8},... | collective-permute-start | bytes 442376 | tf_op jit(solution)/shard_map/ppermute | solution.py:644
  112.5 0.8 collective-permute-start.14
  113.4 9.7 %attn_backward.3 = (bf16[3,392,384]{2,1,0:T(8,128)(2,1)S(1)}, f32[1,768]{1,0:T(1,128)S(1)}, f32[3,64,256]{2,1,0:T(8,128)S(1)}, bf16[392,768]{1,0:T(8,128)(2,1)S(1)}, f32[2,768]{1,0:T(2,128)S(1)}) custom-call(bf16[392,768]{1,0:T(8,128)(2,1)S(1)} %collective-permute-done.11.branch_ref.refs_9_, bf16[392,768]{1,0:T(8,128)(2,1)S(1)} %copy-done.12, ...), custom_call_target="tpu_custom_call" | custom-call | flops 1000000 | bytes 3906 | tf_op jit(solution)/shard_map/attn_backward/pallas_call | solution.py:519
  123.3 3.7 %collective-permute-start.20 = (bf16[96,768]{1,0:T(8,128)(2,1)S(1)}, bf16[96,768]{1,0:T(8,128)(2,1)S(1)}, u32[]{:S(2)}, u32[]{:S(2)}) collective-permute-start(bf16[96,768]{1,0:T(8,128)(2,1)S(1)} %get-tuple-element.183), channel_id=1, source_target_pairs={{0,24},{2,26},{4,28},{6,30},{8,16},{10,18},{12,20},{14,22},{16,8},... | collective-permute-start | bytes 442376 | tf_op jit(solution)/shard_map/ppermute | solution.py:644
  127.0 0.8 collective-permute-start.18
  128.0 5.7 %attn_weights.1 = (bf16[2,4,96,768]{3,2,1,0:T(8,128)(2,1)S(1)}, bf16[2,4,96,768]{3,2,1,0:T(8,128)(2,1)S(1)}, bf16[16,768]{1,0:T(8,128)(2,1)S(1)}) custom-call(s32[1]{0:T(128)} %bitcast.me_ref, f32[4,768]{1,0:T(4,128)S(1)} %get-tuple-element.140.sums2_ref, f32[1,1536]{1,0:T(1,128)S(1)} %copy-done.35, bf16[768,392]{1,0:T(8,128)(2,1)S(1)} %copy-done.20, ...), custom_call_target="tpu_custom_call" | custom-call | flops 1000000 | bytes 3906 | tf_op jit(solution)/shard_map/attn_weights/pallas_call | solution.py:519
  133.8 2.7 %collective-permute-done.19 = bf16[96,768]{1,0:T(8,128)(2,1)S(1)} collective-permute-done((bf16[96,768]{1,0:T(8,128)(2,1)S(1)}, bf16[96,768]{1,0:T(8,128)(2,1)S(1)}, u32[]{:S(2)}, u32[]{:S(2)}) %collective-permute-start.19) | collective-permute-done | bytes 147488 | tf_op jit(solution)/shard_map/ppermute | solution.py:644
  136.7 0.7 collective-permute-start.13
  137.6 2.0 collective-permute-done.25
  139.7 1.6 collective-permute-start.26
  141.3 1.0 collective-permute-start.21
  142.3 12.5 %collective-permute-done.22 = bf16[208,768]{1,0:T(8,128)(2,1)S(1)} collective-permute-done((bf16[208,768]{1,0:T(8,128)(2,1)S(1)}, bf16[208,768]{1,0:T(8,128)(2,1)S(1)}, u32[]{:S(2)}, u32[]{:S(2)}) %collective-permute-start.22) | collective-permute-done | bytes 319520 | tf_op jit(solution)/shard_map/ppermute | solution.py:644
  154.8 1.1 add_convert_fusion
  155.9 1.7 input_back.1
  157.6 6.6 %collective-permute-done.23 = bf16[208,768]{1,0:T(8,128)(2,1)S(1)} collective-permute-done((bf16[208,768]{1,0:T(8,128)(2,1)S(1)}, bf16[208,768]{1,0:T(8,128)(2,1)S(1)}, u32[]{:S(2)}, u32[]{:S(2)}) %collective-permute-start.23) | collective-permute-done | bytes 319520 | tf_op jit(solution)/shard_map/ppermute | solution.py:644
  164.3 1.6 collective-permute-start.24
  166.4 1.7 collective-permute-start.27
  168.2 4.2 %collective-permute-done.28 = bf16[96,768]{1,0:T(8,128)(2,1)S(1)} collective-permute-done((bf16[96,768]{1,0:T(8,128)(2,1)S(1)}, bf16[96,768]{1,0:T(8,128)(2,1)S(1)}, u32[]{:S(2)}, u32[]{:S(2)}) %collective-permute-start.28) | collective-permute-done | bytes 147488 | tf_op jit(solution)/shard_map/ppermute | solution.py:644
  173.0 1.9 collective-permute-done.27
  175.0 7.6 %collective-permute-done.29 = bf16[96,768]{1,0:T(8,128)(2,1)S(1)} collective-permute-done((bf16[96,768]{1,0:T(8,128)(2,1)S(1)}, bf16[96,768]{1,0:T(8,128)(2,1)S(1)}, u32[]{:S(2)}, u32[]{:S(2)}) %collective-permute-start.29) | collective-permute-done | bytes 147488 | tf_op jit(solution)/shard_map/ppermute | solution.py:644
  182.8 1.6 collective-permute-start.30
  184.4 5.2 %collective-permute-done.31 = bf16[96,768]{1,0:T(8,128)(2,1)S(1)} collective-permute-done((bf16[96,768]{1,0:T(8,128)(2,1)S(1)}, bf16[96,768]{1,0:T(8,128)(2,1)S(1)}, u32[]{:S(2)}, u32[]{:S(2)}) %collective-permute-start.31) | collective-permute-done | bytes 147488 | tf_op jit(solution)/shard_map/ppermute | solution.py:644
  189.6 0.8 collective-permute-done.30
  190.4 4.3 %collective-permute-done.32 = bf16[96,768]{1,0:T(8,128)(2,1)S(1)} collective-permute-done((bf16[96,768]{1,0:T(8,128)(2,1)S(1)}, bf16[96,768]{1,0:T(8,128)(2,1)S(1)}, u32[]{:S(2)}, u32[]{:S(2)}) %collective-permute-start.32) | collective-permute-done | bytes 147488 | tf_op jit(solution)/shard_map/ppermute | solution.py:644
  195.4 0.7 collective-permute-start.36
  196.1 1.7 collective-permute-done.34.refs_3_
  197.9 5.4 %finish_mlp.1 = (f32[768,1536]{1,0:T(8,128)}, f32[1536,768]{1,0:T(8,128)}, f32[16,768]{1,0:T(8,128)S(1)}) custom-call(s32[1]{0:T(128)} %bitcast.me_ref, bf16[4,208,768]{2,1,0:T(8,128)(2,1)S(1)} %pad_maximum_fusion.refs_0_, bf16[4,208,768]{2,1,0:T(8,128)(2,1)S(1)} %collective-permute-done.24.refs_1_, ...), custom_call_target="tpu_custom_call" | custom-call | flops 1000000 | bytes 3906 | tf_op jit(solution)/shard_map/finish_mlp/pallas_call | solution.py:519
  203.3 1.4 collective-permute-start.35
  204.7 1.9 finish.2
  207.3 3.4 %collective-permute-done.36.refs_0_ = bf16[4,96,768]{2,1,0:T(8,128)(2,1)S(1)} collective-permute-done((bf16[4,96,768]{2,1,0:T(8,128)(2,1)S(1)}, bf16[4,96,768]{2,1,0:T(8,128)(2,1)S(1)}, u32[]{:S(2)}, u32[]{:S(2)}) %collective-permute-start.36) | collective-permute-done | bytes 589856 | tf_op jit(solution)/shard_map/ppermute | solution.py:644
  212.7 1.9 finish.3
  (155 shorter events, 10.5 us)
Async XLA Ops:
  1.3 9.6 %copy-start.45 = (f32[8,49]{1,0:T(8,128)}, f32[8,49]{1,0:T(8,128)S(1)}, u32[]{:S(2)}) copy-start(f32[8,49]{1,0:T(8,128)S(1)} %convert_element_type.294.valid_ref) | copy-start | bytes 4708
  1.3 4.5 %collective-permute-start.1 = (f32[8,49]{1,0:T(8,128)S(1)}, f32[8,49]{1,0:T(8,128)S(1)}, u32[]{:S(2)}, u32[]{:S(2)}) collective-permute-start(f32[8,49]{1,0:T(8,128)S(1)} %convert_element_type.294.valid_ref), channel_id=1, source_target_pairs={{0,1},{1,0},{2,3},{3,2},{4,5},{5,4},{6,7},{7,6},{8,9},{9,8},{10,11... | collective-permute-start | bytes 4712 | tf_op jit(solution)/shard_map/ppermute | solution.py:640
  4.3 18.7 %collective-permute-start = (bf16[392,768]{1,0:T(8,128)(2,1)}, bf16[392,768]{1,0:T(8,128)(2,1)S(1)}, u32[]{:S(2)}, u32[]{:S(2)}) collective-permute-start(bf16[392,768]{1,0:T(8,128)(2,1)} %bitcast.101), channel_id=1, source_target_pairs={{0,1},{1,0},{2,3},{3,2},{4,5},{5,4},{6,7},{7,6},{8,9},{9,8},{10,11... | collective-permute-start | bytes 1806344 | tf_op jit(solution)/shard_map/ppermute | solution.py:640
  5.9 17.1 %copy-start.48 = (f32[8,49]{1,0:T(8,128)}, f32[8,49]{1,0:T(8,128)S(1)}, u32[]{:S(2)}) copy-start(f32[8,49]{1,0:T(8,128)S(1)} %collective-permute-done.1.valid_ref) | copy-start | bytes 4708
  5.9 33.0 %collective-permute-start.2 = (bf16[392,768]{1,0:T(8,128)(2,1)}, bf16[392,768]{1,0:T(8,128)(2,1)S(1)}, u32[]{:S(2)}, u32[]{:S(2)}) collective-permute-start(bf16[392,768]{1,0:T(8,128)(2,1)} %bitcast.106), channel_id=1, source_target_pairs={{0,1},{1,0},{2,3},{3,2},{4,5},{5,4},{6,7},{7,6},{8,9},{9,8},{10,11... | collective-permute-start | bytes 1806344 | tf_op jit(solution)/shard_map/ppermute | solution.py:640
  8.9 30.0 %collective-permute-start.3 = (bf16[192,768]{1,0:T(8,128)(2,1)S(1)}, bf16[192,768]{1,0:T(8,128)(2,1)}, u32[]{:S(2)}, u32[]{:S(2)}) collective-permute-start(bf16[192,768]{1,0:T(8,128)(2,1)S(1)} %constant_dynamic-slice_fusion), channel_id=1, source_target_pairs={{0,1},{1,0},{2,3},{3,2},{4,5},{5,4},{6,7},{7,6},{8,9},{9,8},{10,11... | collective-permute-start | bytes 884744 | tf_op jit(solution)/shard_map/ppermute | solution.py:640
  10.9 29.2 %copy-start.4 = (bf16[384,768]{1,0:T(8,128)(2,1)S(1)}, bf16[384,768]{1,0:T(8,128)(2,1)}, u32[]{:S(2)}) copy-start(bf16[384,768]{1,0:T(8,128)(2,1)} %proj_ref.3) | copy-start | bytes 1769476
  23.8 29.2 %copy-start.3 = (bf16[1536,768]{1,0:T(8,128)(2,1)S(1)}, bf16[1536,768]{1,0:T(8,128)(2,1)}, u32[]{:S(2)}) copy-start(bf16[1536,768]{1,0:T(8,128)(2,1)} %fc2_ref.3) | copy-start | bytes 7077892
  39.7 7.9 %collective-permute-start.4 = (bf16[392,384]{1,0:T(8,128)(2,1)}, bf16[392,384]{1,0:T(8,128)(2,1)S(1)}, u32[]{:S(2)}, u32[]{:S(2)}) collective-permute-start(bf16[392,384]{1,0:T(8,128)(2,1)} %get-tuple-element.100.refs_8_), channel_id=1, source_target_pairs={{0,1},{1,0},{2,3},{3,2},{4,5},{5,4},{6,7},{7,6},{8,9},{9,8},{10,11... | collective-permute-start | bytes 903176 | tf_op jit(solution)/shard_map/ppermute | solution.py:640
  40.1 2.4 %collective-permute-start.5 = (bf16[192,768]{1,0:T(8,128)(2,1)}, bf16[192,768]{1,0:T(8,128)(2,1)S(1)}, u32[]{:S(2)}, u32[]{:S(2)}) collective-permute-start(bf16[192,768]{1,0:T(8,128)(2,1)} %collective-permute-done.3.refs_0_), channel_id=1, source_target_pairs={{0,2},{2,0},{4,6},{6,4},{8,10},{10,8},{12,14},{14,12},{16,18},{18,... | collective-permute-start | bytes 884744 | tf_op jit(solution)/shard_map/ppermute | solution.py:644
  40.1 12.9 %copy-start.2 = (bf16[768,1536]{1,0:T(8,128)(2,1)S(1)}, bf16[768,1536]{1,0:T(8,128)(2,1)}, u32[]{:S(2)}) copy-start(bf16[768,1536]{1,0:T(8,128)(2,1)} %fc1_ref.3) | copy-start | bytes 7077892
  42.5 10.5 %copy-start.46 = (f32[1536]{0:T(1024)S(1)}, f32[1536]{0:T(1024)}, u32[]{:S(2)}) copy-start(f32[1536]{0:T(1024)} %param.28) | copy-start | bytes 18436
  42.5 10.5 %copy-start.5 = (bf16[8,49,768]{2,0,1:T(8,128)(2,1)S(1)}, bf16[8,49,768]{2,0,1:T(8,128)(2,1)}, u32[]{:S(2)}) copy-start(bf16[8,49,768]{2,0,1:T(8,128)(2,1)} %param.31) | copy-start | bytes 1806340
  42.5 5.1 %copy-start.44 = (bf16[192,768]{1,0:T(8,128)(2,1)}, bf16[192,768]{1,0:T(8,128)(2,1)S(1)}, u32[]{:S(2)}) copy-start(bf16[192,768]{1,0:T(8,128)(2,1)S(1)} %collective-permute-done.5.refs_1_) | copy-start | bytes 884740
  52.2 13.5 %collective-permute-start.6 = (bf16[392,768]{1,0:T(8,128)(2,1)}, bf16[392,768]{1,0:T(8,128)(2,1)S(1)}, u32[]{:S(2)}, u32[]{:S(2)}) collective-permute-start(bf16[392,768]{1,0:T(8,128)(2,1)} %get-tuple-element.103.nm_ref.refs_0_), channel_id=1, source_target_pairs={{0,1},{1,0},{2,3},{3,2},{4,5},{5,4},{6,7},{7,6},{8,9},{9,8},{10,11... | collective-permute-start | bytes 1806344 | tf_op jit(solution)/shard_map/ppermute | solution.py:640
  54.1 11.6 %copy-start.8 = (bf16[392,768]{1,0:T(8,128)(2,1)S(1)}, bf16[392,768]{1,0:T(8,128)(2,1)}, u32[]{:S(2)}) copy-start(bf16[392,768]{1,0:T(8,128)(2,1)} %copy-done.7) | copy-start | bytes 1806340
  62.9 9.7 %copy-start.15 = (bf16[392,1536]{1,0:T(8,128)(2,1)}, bf16[392,1536]{1,0:T(8,128)(2,1)S(1)}, u32[]{:S(2)}) copy-start(bf16[392,1536]{1,0:T(8,128)(2,1)S(1)} %get-tuple-element.110.refs_3_) | copy-start | bytes 3612676
  65.7 6.9 %copy-start.10 = (bf16[392,768]{1,0:T(8,128)(2,1)}, bf16[392,768]{1,0:T(8,128)(2,1)S(1)}, u32[]{:S(2)}) copy-start(bf16[392,768]{1,0:T(8,128)(2,1)S(1)} %collective-permute-done.6.nm_ref.refs_4_) | copy-start | bytes 1806340
  74.6 13.6 %collective-permute-start.8 = (bf16[392,768]{1,0:T(8,128)(2,1)}, bf16[392,768]{1,0:T(8,128)(2,1)S(1)}, u32[]{:S(2)}, u32[]{:S(2)}) collective-permute-start(bf16[392,768]{1,0:T(8,128)(2,1)} %get-tuple-element.108), channel_id=1, source_target_pairs={{0,1},{1,0},{2,3},{3,2},{4,5},{5,4},{6,7},{7,6},{8,9},{9,8},{10,11... | collective-permute-start | bytes 1806344 | tf_op jit(solution)/shard_map/ppermute | solution.py:640
  75.7 13.3 %copy-start.6 = (bf16[8,49,768]{2,0,1:T(8,128)(2,1)S(1)}, bf16[8,49,768]{2,0,1:T(8,128)(2,1)}, u32[]{:S(2)}) copy-start(bf16[8,49,768]{2,0,1:T(8,128)(2,1)} %param.31) | copy-start | bytes 1806340
  75.7 13.3 %copy-start.19 = (f32[392,768]{1,0:T(8,128)S(1)}, f32[392,768]{1,0:T(8,128)}, u32[]{:S(2)}) copy-start(f32[392,768]{1,0:T(8,128)} %get-tuple-element.102.middle_ref) | copy-start | bytes 3612676
  75.7 13.3 %copy-start.36 = (f32[768]{0:T(1024)S(1)}, f32[768]{0:T(1024)}, u32[]{:S(2)}) copy-start(f32[768]{0:T(1024)} %gain_ref.8) | copy-start | bytes 9220
  75.7 13.3 %copy-start.38 = (bf16[392,768]{1,0:T(8,128)(2,1)S(1)}, bf16[392,768]{1,0:T(8,128)(2,1)}, u32[]{:S(2)}) copy-start(bf16[392,768]{1,0:T(8,128)(2,1)} %copy-done.37) | copy-start | bytes 1806340
  87.6 4.6 %collective-permute-start.9 = (bf16[2,4,96,768]{3,2,1,0:T(8,128)(2,1)}, bf16[2,4,96,768]{3,2,1,0:T(8,128)(2,1)S(1)}, u32[]{:S(2)}, u32[]{:S(2)}) collective-permute-start(bf16[2,4,96,768]{3,2,1,0:T(8,128)(2,1)} %get-tuple-element.117), channel_id=1, source_target_pairs={{0,2},{2,0},{4,6},{6,4},{8,10},{10,8},{12,14},{14,12},{16,18},{18,... | collective-permute-start | bytes 3538952 | tf_op jit(solution)/shard_map/ppermute | solution.py:644
  87.7 6.3 %collective-permute-start.10 = (bf16[2,4,96,768]{3,2,1,0:T(8,128)(2,1)}, bf16[2,4,96,768]{3,2,1,0:T(8,128)(2,1)S(1)}, u32[]{:S(2)}, u32[]{:S(2)}) collective-permute-start(bf16[2,4,96,768]{3,2,1,0:T(8,128)(2,1)} %get-tuple-element.120), channel_id=1, source_target_pairs={{0,2},{2,0},{4,6},{6,4},{8,10},{10,8},{12,14},{14,12},{16,18},{18,... | collective-permute-start | bytes 3538952 | tf_op jit(solution)/shard_map/ppermute | solution.py:644
  90.1 5.7 %copy-start.30 = (bf16[8,64,384]{2,1,0:T(8,128)(2,1)S(1)}, bf16[8,64,384]{2,1,0:T(8,128)(2,1)}, u32[]{:S(2)}) copy-start(bf16[8,64,384]{2,1,0:T(8,128)(2,1)} %get-tuple-element.125.k_ref) | copy-start | bytes 1179652
  90.1 5.7 %copy-start.31 = (bf16[8,64,384]{2,1,0:T(8,128)(2,1)S(1)}, bf16[8,64,384]{2,1,0:T(8,128)(2,1)}, u32[]{:S(2)}) copy-start(bf16[8,64,384]{2,1,0:T(8,128)(2,1)} %get-tuple-element.126.v_ref) | copy-start | bytes 1179652
  91.2 21.3 %collective-permute-start.11 = (bf16[392,768]{1,0:T(8,128)(2,1)S(1)}, bf16[392,768]{1,0:T(8,128)(2,1)S(1)}, u32[]{:S(2)}, u32[]{:S(2)}) collective-permute-start(bf16[392,768]{1,0:T(8,128)(2,1)S(1)} %get-tuple-element.142.branch_ref.refs_2_), channel_id=1, source_target_pairs={{0,1},{1,0},{2,3},{3,2},{4,5},{5,4},{6,7},{7,6},{8,9},{9,8},{10,11... | collective-permute-start | bytes 1806344 | tf_op jit(solution)/shard_map/ppermute | solution.py:640
  92.4 16.3 %collective-permute-start.12 = (bf16[4,96,768]{2,1,0:T(8,128)(2,1)S(1)}, bf16[4,96,768]{2,1,0:T(8,128)(2,1)S(1)}, u32[]{:S(2)}, u32[]{:S(2)}) collective-permute-start(bf16[4,96,768]{2,1,0:T(8,128)(2,1)S(1)} %fusion), channel_id=1, source_target_pairs={{0,4},{2,6},{4,0},{6,2},{8,12},{10,14},{12,8},{14,10},{16,20},{18,... | collective-permute-start | bytes 1769480 | tf_op jit(solution)/shard_map/ppermute | solution.py:644
  94.2 28.9 %collective-permute-start.17 = (bf16[4,96,768]{2,1,0:T(8,128)(2,1)S(1)}, bf16[4,96,768]{2,1,0:T(8,128)(2,1)S(1)}, u32[]{:S(2)}, u32[]{:S(2)}) collective-permute-start(bf16[4,96,768]{2,1,0:T(8,128)(2,1)S(1)} %fusion.1), channel_id=1, source_target_pairs={{0,4},{2,6},{4,0},{6,2},{8,12},{10,14},{12,8},{14,10},{16,20},{18,... | collective-permute-start | bytes 1769480 | tf_op jit(solution)/shard_map/ppermute | solution.py:644
  94.7 33.2 %collective-permute-start.7 = (bf16[392,768]{1,0:T(8,128)(2,1)S(1)}, bf16[392,768]{1,0:T(8,128)(2,1)S(1)}, u32[]{:S(2)}, u32[]{:S(2)}) collective-permute-start(bf16[392,768]{1,0:T(8,128)(2,1)S(1)} %get-tuple-element.107), channel_id=1, source_target_pairs={{0,1},{1,0},{2,3},{3,2},{4,5},{5,4},{6,7},{7,6},{8,9},{9,8},{10,11... | collective-permute-start | bytes 1806344 | tf_op jit(solution)/shard_map/ppermute | solution.py:640
  95.9 17.5 %copy-start.27 = (bf16[8,64,384]{2,1,0:T(8,128)(2,1)S(1)}, bf16[8,64,384]{2,1,0:T(8,128)(2,1)}, u32[]{:S(2)}) copy-start(bf16[8,64,384]{2,1,0:T(8,128)(2,1)} %get-tuple-element.132.k_ref) | copy-start | bytes 1179652
  95.9 17.5 %copy-start.28 = (bf16[8,64,384]{2,1,0:T(8,128)(2,1)S(1)}, bf16[8,64,384]{2,1,0:T(8,128)(2,1)}, u32[]{:S(2)}) copy-start(bf16[8,64,384]{2,1,0:T(8,128)(2,1)} %get-tuple-element.133.v_ref) | copy-start | bytes 1179652
  105.6 7.7 %copy-start.12 = (bf16[392,768]{1,0:T(8,128)(2,1)S(1)}, bf16[392,768]{1,0:T(8,128)(2,1)}, u32[]{:S(2)}) copy-start(bf16[392,768]{1,0:T(8,128)(2,1)} %copy-done.11) | copy-start | bytes 1806340
  105.6 7.7 %copy-start.22 = (bf16[8,3,64,256]{3,2,1,0:T(8,128)(2,1)S(1)}, bf16[8,3,64,256]{3,2,1,0:T(8,128)(2,1)}, u32[]{:S(2)}) copy-start(bf16[8,3,64,256]{3,2,1,0:T(8,128)(2,1)} %get-tuple-element.130.prob_ref) | copy-start | bytes 2359300
  105.6 7.7 %copy-start.26 = (bf16[8,64,384]{2,1,0:T(8,128)(2,1)S(1)}, bf16[8,64,384]{2,1,0:T(8,128)(2,1)}, u32[]{:S(2)}) copy-start(bf16[8,64,384]{2,1,0:T(8,128)(2,1)} %get-tuple-element.131.q_ref) | copy-start | bytes 1179652
  108.9 18.1 %collective-permute-start.16 = (bf16[96,768]{1,0:T(8,128)(2,1)S(1)}, bf16[96,768]{1,0:T(8,128)(2,1)S(1)}, u32[]{:S(2)}, u32[]{:S(2)}) collective-permute-start(bf16[96,768]{1,0:T(8,128)(2,1)S(1)} %get-tuple-element.186), channel_id=1, source_target_pairs={{0,24},{2,26},{4,28},{6,30},{8,16},{10,18},{12,20},{14,22},{16,8},... | collective-permute-start | bytes 442376 | tf_op jit(solution)/shard_map/ppermute | solution.py:644
  112.5 14.5 %collective-permute-start.15 = (bf16[96,768]{1,0:T(8,128)(2,1)S(1)}, bf16[96,768]{1,0:T(8,128)(2,1)S(1)}, u32[]{:S(2)}, u32[]{:S(2)}) collective-permute-start(bf16[96,768]{1,0:T(8,128)(2,1)S(1)} %get-tuple-element.187), channel_id=1, source_target_pairs={{0,16},{2,18},{4,20},{6,22},{8,24},{10,26},{12,28},{14,30},{16,0},... | collective-permute-start | bytes 442376 | tf_op jit(solution)/shard_map/ppermute | solution.py:644
  112.5 15.2 %collective-permute-start.14 = (bf16[96,768]{1,0:T(8,128)(2,1)S(1)}, bf16[96,768]{1,0:T(8,128)(2,1)S(1)}, u32[]{:S(2)}, u32[]{:S(2)}) collective-permute-start(bf16[96,768]{1,0:T(8,128)(2,1)S(1)} %get-tuple-element.188), channel_id=1, source_target_pairs={{0,8},{2,10},{4,12},{6,14},{8,0},{10,2},{12,4},{14,6},{16,24},{18,... | collective-permute-start | bytes 442376 | tf_op jit(solution)/shard_map/ppermute | solution.py:644
  123.1 4.8 %copy-start.18 = (bf16[392,384]{1,0:T(8,128)(2,1)S(1)}, bf16[392,384]{1,0:T(8,128)(2,1)}, u32[]{:S(2)}) copy-start(bf16[392,384]{1,0:T(8,128)(2,1)} %get-tuple-element.95.refs_1_) | copy-start | bytes 903172
  123.3 10.4 %collective-permute-start.20 = (bf16[96,768]{1,0:T(8,128)(2,1)S(1)}, bf16[96,768]{1,0:T(8,128)(2,1)S(1)}, u32[]{:S(2)}, u32[]{:S(2)}) collective-permute-start(bf16[96,768]{1,0:T(8,128)(2,1)S(1)} %get-tuple-element.183), channel_id=1, source_target_pairs={{0,24},{2,26},{4,28},{6,30},{8,16},{10,18},{12,20},{14,22},{16,8},... | collective-permute-start | bytes 442376 | tf_op jit(solution)/shard_map/ppermute | solution.py:644
  127.0 9.5 %collective-permute-start.19 = (bf16[96,768]{1,0:T(8,128)(2,1)S(1)}, bf16[96,768]{1,0:T(8,128)(2,1)S(1)}, u32[]{:S(2)}, u32[]{:S(2)}) collective-permute-start(bf16[96,768]{1,0:T(8,128)(2,1)S(1)} %get-tuple-element.184), channel_id=1, source_target_pairs={{0,16},{2,18},{4,20},{6,22},{8,24},{10,26},{12,28},{14,30},{16,0},... | collective-permute-start | bytes 442376 | tf_op jit(solution)/shard_map/ppermute | solution.py:644
  127.0 9.5 %collective-permute-start.18 = (bf16[96,768]{1,0:T(8,128)(2,1)S(1)}, bf16[96,768]{1,0:T(8,128)(2,1)S(1)}, u32[]{:S(2)}, u32[]{:S(2)}) collective-permute-start(bf16[96,768]{1,0:T(8,128)(2,1)S(1)} %get-tuple-element.185), channel_id=1, source_target_pairs={{0,8},{2,10},{4,12},{6,14},{8,0},{10,2},{12,4},{14,6},{16,24},{18,... | collective-permute-start | bytes 442376 | tf_op jit(solution)/shard_map/ppermute | solution.py:644
  136.6 18.2 %copy-start.25 = (bf16[392,768]{1,0:T(8,128)(2,1)S(1)}, bf16[392,768]{1,0:T(8,128)(2,1)}, u32[]{:S(2)}) copy-start(bf16[392,768]{1,0:T(8,128)(2,1)} %copy-done.24) | copy-start | bytes 1806340
  136.6 18.1 %copy-start.47 = (f32[768]{0:T(1024)S(1)}, f32[768]{0:T(1024)}, u32[]{:S(2)}) copy-start(f32[768]{0:T(1024)} %param.30) | copy-start | bytes 9220
  136.6 2.9 %collective-permute-start.25 = (bf16[2,4,96,768]{3,2,1,0:T(8,128)(2,1)S(1)}, bf16[2,4,96,768]{3,2,1,0:T(8,128)(2,1)S(1)}, u32[]{:S(2)}, u32[]{:S(2)}) collective-permute-start(bf16[2,4,96,768]{3,2,1,0:T(8,128)(2,1)S(1)} %get-tuple-element.161), channel_id=1, source_target_pairs={{0,2},{2,0},{4,6},{6,4},{8,10},{10,8},{12,14},{14,12},{16,18},{18,... | collective-permute-start | bytes 3538952 | tf_op jit(solution)/shard_map/ppermute | solution.py:644
  136.7 19.2 %collective-permute-start.13 = (bf16[392,768]{1,0:T(8,128)(2,1)S(1)}, bf16[392,768]{1,0:T(8,128)(2,1)S(1)}, u32[]{:S(2)}, u32[]{:S(2)}) collective-permute-start(bf16[392,768]{1,0:T(8,128)(2,1)S(1)} %get-tuple-element.134), channel_id=1, source_target_pairs={{0,1},{1,0},{2,3},{3,2},{4,5},{5,4},{6,7},{7,6},{8,9},{9,8},{10,11... | collective-permute-start | bytes 1806344 | tf_op jit(solution)/shard_map/ppermute | solution.py:640
  137.5 17.3 %collective-permute-start.22 = (bf16[208,768]{1,0:T(8,128)(2,1)S(1)}, bf16[208,768]{1,0:T(8,128)(2,1)S(1)}, u32[]{:S(2)}, u32[]{:S(2)}) collective-permute-start(bf16[208,768]{1,0:T(8,128)(2,1)S(1)} %get-tuple-element.190), channel_id=1, source_target_pairs={{0,16},{2,18},{4,20},{6,22},{8,24},{10,26},{12,28},{14,30},{16,0},... | collective-permute-start | bytes 958472 | tf_op jit(solution)/shard_map/ppermute | solution.py:644
  139.7 26.2 %collective-permute-start.26 = (bf16[4,96,768]{2,1,0:T(8,128)(2,1)S(1)}, bf16[4,96,768]{2,1,0:T(8,128)(2,1)S(1)}, u32[]{:S(2)}, u32[]{:S(2)}) collective-permute-start(bf16[4,96,768]{2,1,0:T(8,128)(2,1)S(1)} %fusion.2), channel_id=1, source_target_pairs={{0,4},{2,6},{4,0},{6,2},{8,12},{10,14},{12,8},{14,10},{16,20},{18,... | collective-permute-start | bytes 1769480 | tf_op jit(solution)/shard_map/ppermute | solution.py:644
  141.3 16.3 %collective-permute-start.21 = (bf16[208,768]{1,0:T(8,128)(2,1)S(1)}, bf16[208,768]{1,0:T(8,128)(2,1)S(1)}, u32[]{:S(2)}, u32[]{:S(2)}) collective-permute-start(bf16[208,768]{1,0:T(8,128)(2,1)S(1)} %get-tuple-element.190), channel_id=1, source_target_pairs={{0,8},{2,10},{4,12},{6,14},{8,0},{10,2},{12,4},{14,6},{16,24},{18,... | collective-permute-start | bytes 958472 | tf_op jit(solution)/shard_map/ppermute | solution.py:644
  154.8 9.4 %collective-permute-start.23 = (bf16[208,768]{1,0:T(8,128)(2,1)S(1)}, bf16[208,768]{1,0:T(8,128)(2,1)S(1)}, u32[]{:S(2)}, u32[]{:S(2)}) collective-permute-start(bf16[208,768]{1,0:T(8,128)(2,1)S(1)} %collective-permute-done.22), channel_id=1, source_target_pairs={{0,8},{2,10},{4,12},{6,14},{8,0},{10,2},{12,4},{14,6},{16,24},{18,... | collective-permute-start | bytes 958472 | tf_op jit(solution)/shard_map/ppermute | solution.py:644
  164.3 30.4 %collective-permute-start.24 = (bf16[4,208,768]{2,1,0:T(8,128)(2,1)S(1)}, bf16[4,208,768]{2,1,0:T(8,128)(2,1)S(1)}, u32[]{:S(2)}, u32[]{:S(2)}) collective-permute-start(bf16[4,208,768]{2,1,0:T(8,128)(2,1)S(1)} %pad_maximum_fusion.refs_0_), channel_id=1, source_target_pairs={{0,4},{2,6},{4,0},{6,2},{8,12},{10,14},{12,8},{14,10},{16,20},{18,... | collective-permute-start | bytes 3833864 | tf_op jit(solution)/shard_map/ppermute | solution.py:644
  166.1 6.2 %collective-permute-start.28 = (bf16[96,768]{1,0:T(8,128)(2,1)S(1)}, bf16[96,768]{1,0:T(8,128)(2,1)S(1)}, u32[]{:S(2)}, u32[]{:S(2)}) collective-permute-start(bf16[96,768]{1,0:T(8,128)(2,1)S(1)} %get-tuple-element.182), channel_id=1, source_target_pairs={{0,8},{2,10},{4,12},{6,14},{8,0},{10,2},{12,4},{14,6},{16,24},{18,... | collective-permute-start | bytes 442376 | tf_op jit(solution)/shard_map/ppermute | solution.py:644
  166.4 8.6 %collective-permute-start.27 = (bf16[96,768]{1,0:T(8,128)(2,1)S(1)}, bf16[96,768]{1,0:T(8,128)(2,1)S(1)}, u32[]{:S(2)}, u32[]{:S(2)}) collective-permute-start(bf16[96,768]{1,0:T(8,128)(2,1)S(1)} %get-tuple-element.181), channel_id=1, source_target_pairs={{0,8},{2,10},{4,12},{6,14},{8,0},{10,2},{12,4},{14,6},{16,24},{18,... | collective-permute-start | bytes 442376 | tf_op jit(solution)/shard_map/ppermute | solution.py:644
  172.4 10.2 %collective-permute-start.29 = (bf16[96,768]{1,0:T(8,128)(2,1)S(1)}, bf16[96,768]{1,0:T(8,128)(2,1)S(1)}, u32[]{:S(2)}, u32[]{:S(2)}) collective-permute-start(bf16[96,768]{1,0:T(8,128)(2,1)S(1)} %add_convert_fusion.4), channel_id=1, source_target_pairs={{0,16},{2,18},{4,20},{6,22},{8,24},{10,26},{12,28},{14,30},{16,0},... | collective-permute-start | bytes 442376 | tf_op jit(solution)/shard_map/ppermute | solution.py:644
  182.7 6.8 %collective-permute-start.31 = (bf16[96,768]{1,0:T(8,128)(2,1)S(1)}, bf16[96,768]{1,0:T(8,128)(2,1)S(1)}, u32[]{:S(2)}, u32[]{:S(2)}) collective-permute-start(bf16[96,768]{1,0:T(8,128)(2,1)S(1)} %fusion.8), channel_id=1, source_target_pairs={{0,16},{2,18},{4,20},{6,22},{8,24},{10,26},{12,28},{14,30},{16,0},... | collective-permute-start | bytes 442376 | tf_op jit(solution)/shard_map/ppermute | solution.py:644
  182.8 7.6 %collective-permute-start.30 = (bf16[96,768]{1,0:T(8,128)(2,1)S(1)}, bf16[96,768]{1,0:T(8,128)(2,1)S(1)}, u32[]{:S(2)}, u32[]{:S(2)}) collective-permute-start(bf16[96,768]{1,0:T(8,128)(2,1)S(1)} %fusion.8), channel_id=1, source_target_pairs={{0,8},{2,10},{4,12},{6,14},{8,0},{10,2},{12,4},{14,6},{16,24},{18,... | collective-permute-start | bytes 442376 | tf_op jit(solution)/shard_map/ppermute | solution.py:644
  189.6 5.1 %collective-permute-start.32 = (bf16[96,768]{1,0:T(8,128)(2,1)S(1)}, bf16[96,768]{1,0:T(8,128)(2,1)S(1)}, u32[]{:S(2)}, u32[]{:S(2)}) collective-permute-start(bf16[96,768]{1,0:T(8,128)(2,1)S(1)} %collective-permute-done.31), channel_id=1, source_target_pairs={{0,8},{2,10},{4,12},{6,14},{8,0},{10,2},{12,4},{14,6},{16,24},{18,... | collective-permute-start | bytes 442376 | tf_op jit(solution)/shard_map/ppermute | solution.py:644
  189.6 6.6 %collective-permute-start.33 = (bf16[4,208,768]{2,1,0:T(8,128)(2,1)S(1)}, bf16[4,208,768]{2,1,0:T(8,128)(2,1)S(1)}, u32[]{:S(2)}, u32[]{:S(2)}) collective-permute-start(bf16[4,208,768]{2,1,0:T(8,128)(2,1)S(1)} %pad_maximum_fusion.refs_0_), channel_id=1, source_target_pairs={{0,2},{2,0},{4,6},{6,4},{8,10},{10,8},{12,14},{14,12},{16,18},{18,... | collective-permute-start | bytes 3833864 | tf_op jit(solution)/shard_map/ppermute | solution.py:644
  194.8 3.1 %collective-permute-start.34 = (bf16[4,208,768]{2,1,0:T(8,128)(2,1)S(1)}, bf16[4,208,768]{2,1,0:T(8,128)(2,1)S(1)}, u32[]{:S(2)}, u32[]{:S(2)}) collective-permute-start(bf16[4,208,768]{2,1,0:T(8,128)(2,1)S(1)} %collective-permute-done.24.refs_1_), channel_id=1, source_target_pairs={{0,2},{2,0},{4,6},{6,4},{8,10},{10,8},{12,14},{14,12},{16,18},{18,... | collective-permute-start | bytes 3833864 | tf_op jit(solution)/shard_map/ppermute | solution.py:644
  194.9 9.8 %collective-permute-start.37 = (bf16[4,96,768]{2,1,0:T(8,128)(2,1)S(1)}, bf16[4,96,768]{2,1,0:T(8,128)(2,1)S(1)}, u32[]{:S(2)}, u32[]{:S(2)}) collective-permute-start(bf16[4,96,768]{2,1,0:T(8,128)(2,1)S(1)} %pad_maximum_fusion.1.refs_0_), channel_id=1, source_target_pairs={{0,2},{2,0},{4,6},{6,4},{8,10},{10,8},{12,14},{14,12},{16,18},{18,... | collective-permute-start | bytes 1769480 | tf_op jit(solution)/shard_map/ppermute | solution.py:644
  195.4 15.3 %collective-permute-start.36 = (bf16[4,96,768]{2,1,0:T(8,128)(2,1)S(1)}, bf16[4,96,768]{2,1,0:T(8,128)(2,1)S(1)}, u32[]{:S(2)}, u32[]{:S(2)}) collective-permute-start(bf16[4,96,768]{2,1,0:T(8,128)(2,1)S(1)} %pad_maximum_fusion.1.refs_0_), channel_id=1, source_target_pairs={{0,4},{2,6},{4,0},{6,2},{8,12},{10,14},{12,8},{14,10},{16,20},{18,... | collective-permute-start | bytes 1769480 | tf_op jit(solution)/shard_map/ppermute | solution.py:644
  203.3 4.0 %collective-permute-start.35 = (f32[6,768]{1,0:T(8,128)S(1)}, f32[6,768]{1,0:T(8,128)S(1)}, u32[]{:S(2)}, u32[]{:S(2)}) collective-permute-start(f32[6,768]{1,0:T(8,128)S(1)} %slice.210), channel_id=1, source_target_pairs={{0,1},{1,0},{2,3},{3,2},{4,5},{5,4},{6,7},{7,6},{8,9},{9,8},{10,11... | collective-permute-start | bytes 55304 | tf_op jit(solution)/shard_map/ppermute | solution.py:640
  210.7 2.0 collective-permute-start.38
  (24 other events, 52.3 us)

commit v8 on v7

--- a/solution.py
+++ b/solution.py
@@ -128,10 +128,10 @@
         copy.wait()
 
 
-def attn_forward_kernel(windows, x_in, gain_ref, shift_ref, w_in, bias_ref, pos_ref, valid_ref,
+def attn_forward_kernel(windows, x_in, gain_ref, shift_ref, w_in, bias_in, pos_ref, valid_ref,
                         prob_ref, q_ref, k_ref, v_ref, mixed_ref, normed_t_ref,
-                        mask_s, q_s, k_s, v_s, mixed_s, x_ref, w_ref, in_sems):
-    copies = begin(in_sems, (x_in, x_ref), *[(w_in.at[p], w_ref.at[p]) for p in range(3)])
+                        mask_s, q_s, k_s, v_s, mixed_s, x_ref, w_ref, bias_ref, in_sems):
+    copies = begin(in_sems, (x_in, x_ref), *[(w_in.at[p], w_ref.at[p]) for p in range(3)], (bias_in, bias_ref))
     mask_s[...] = jnp.zeros(mask_s.shape, F32)
     for h in range(GROUP):
         mask_s[:, h * SLOT : h * SLOT + WIN] = valid_ref[...].astype(F32)
@@ -139,6 +139,7 @@
     ones = block_ones()
     low_half = lax.broadcasted_iota(jnp.int32, (SLOT, LANES), 1) < SLOT
     copies[0].wait()
+    copies[4].wait()
     x = x_ref[...].astype(F32)
     rows = x.shape[0]
     groups = q_s.shape[0]
@@ -555,9 +556,9 @@
     outs = [shape_of(windows, groups, SLOT, GROUP * SLOT, dtype=BF), tile, tile, tile, shape_of(rows, width, dtype=BF),
             shape_of(features, rows, dtype=BF)]
     scratch = [pltpu.VMEM((windows, GROUP * SLOT), F32)] + [pltpu.VMEM((groups, SLOT * (windows + 1), LANES), F32)] * 4
-    scratch += like(x, qkv) + dma(4)
+    scratch += like(x, qkv, qv_bias) + dma(5)
     return call(functools.partial(attn_forward_kernel, windows), outs, scratch, "attn_forward", SMALL, (),
-                x, *ln1, qkv, qv_bias, pos, mask, far=(0, 3), limit=ALL_VMEM)
+                x, *ln1, qkv, qv_bias, pos, mask, far=(0, 3, 4), limit=ALL_VMEM)
 
 
 def middle_norm(me, x, own, peer, bias, ln2, halves):
@@ -738,8 +739,8 @@
     project = lambda mixed, weight: jnp.dot(mixed, weight, preferred_element_type=F32).astype(BF)
     if fast:
         core = index & 1
-        half = across(lax.dynamic_slice_in_dim(after(proj, valids[1]), core * (width // 2), width // 2, 0))
-        cots = [cot, across(after(cot, valids[1]))]
+        half = across(lax.dynamic_slice_in_dim(after(proj, valids[1], pos), core * (width // 2), width // 2, 0))
+        cots = [cot, across(after(cot, valids[1], pos))]
         mixed = across(after(kept[1][4], cots[1], half))
         half = after(half, kept[1][4])
         rest = flip(half, CORE)

time: 215 us -> 215 us (level)
  transfers between devices with their start and end apart: 39 -> 39, of which waited for: 18 -> 17; matrix products, arithmetic and copies ran while one was open for 4% -> 4% of each run, Pallas kernels for 36% -> 37%
where the time goes in v8:
time: 215 us
  Pallas kernels  91.4 us (43%)
  waiting for transfers between devices  67.9 us (32%)
  starting transfers between devices  33.2 us (15%)
  local copies, waits for them, and re-layouts  14.5 us (7%)
  other arithmetic  4.01 us (2%)
  matrix products  2.4 us (1%)
    pallas_call x15, Pallas kernels, call(): pl.pallas_call(kernel, out_shape=outs, in_specs=in_specs, out_specs=[spac...  91.4 us
    ppermute x28, waiting for transfers between devices, flip(): return lax.ppermute(v, 'dp', [(i, i ^ bits) for i in range(16)])  56.2 us
    ppermute x28, starting transfers between devices, flip(): return lax.ppermute(v, 'dp', [(i, i ^ bits) for i in range(16)])  21.6 us
    ppermute x11, waiting for transfers between devices, across(): return lax.ppermute(v, 'mp', [(0, 1), (1, 0)])  11.7 us
    unnamed x98, local copies, waits for them, and re-layouts  11.6 us
    ppermute x11, starting transfers between devices, across(): return lax.ppermute(v, 'mp', [(0, 1), (1, 0)])  11.5 us
  transfers between devices with their start and end apart: 39, of which 17 were waited for; matrix products, arithmetic and copies ran while one was open for 4% of the time, Pallas kernels for 37%

profile of v8, /device:TPU:0, one launch (start us, length us, event | category | flops | bytes accessed | tf_op | source)
XLA Modules:
  0.0 214.8 jit_solution(17837723178158494656)
XLA Ops:
  1.3 2.9 %collective-permute-start.1 = (f32[8,49]{1,0:T(8,128)S(1)}, f32[8,49]{1,0:T(8,128)S(1)}, u32[]{:S(2)}, u32[]{:S(2)}) collective-permute-start(f32[8,49]{1,0:T(8,128)S(1)} %convert_element_type.294.valid_ref), channel_id=1, source_target_pairs={{0,1},{1,0},{2,3},{3,2},{4,5},{5,4},{6,7},{7,6},{8,9},{9,8},{10,11... | collective-permute-start | bytes 4712 | tf_op jit(solution)/shard_map/ppermute | solution.py:641
  4.3 0.7 copy-done.34
  6.2 2.0 collective-permute-start.2
  8.2 1.0 constant_dynamic-slice_fusion
  9.3 12.4 %attn_forward.2 = (bf16[8,3,64,256]{3,2,1,0:T(8,128)(2,1)}, bf16[8,64,384]{2,1,0:T(8,128)(2,1)}, bf16[8,64,384]{2,1,0:T(8,128)(2,1)}, bf16[8,64,384]{2,1,0:T(8,1...) custom-call(bf16[392,768]{1,0:T(8,128)(2,1)} %bitcast.102, f32[768]{0:T(1024)} %gain_ref.9, f32[768]{0:T(1024)} %shift_ref.4, ...), custom_call_target="tpu_custom_call" | custom-call | flops 1000000 | bytes 3906 | tf_op jit(solution)/shard_map/attn_forward/pallas_call | solution.py:520
  21.8 0.8 copy-done.11
  22.6 12.5 %attn_forward.3 = (bf16[8,3,64,256]{3,2,1,0:T(8,128)(2,1)}, bf16[8,64,384]{2,1,0:T(8,128)(2,1)}, bf16[8,64,384]{2,1,0:T(8,128)(2,1)}, bf16[8,64,384]{2,1,0:T(8,1...) custom-call(bf16[392,768]{1,0:T(8,128)(2,1)} %copy-done.11, f32[768]{0:T(1024)} %gain_ref.9, f32[768]{0:T(1024)} %shift_ref.4, ...), custom_call_target="tpu_custom_call" | custom-call | flops 1000000 | bytes 3906 | tf_op jit(solution)/shard_map/attn_forward/pallas_call | solution.py:520
  35.1 3.8 %collective-permute-done.3.refs_0_ = bf16[192,768]{1,0:T(8,128)(2,1)} collective-permute-done((bf16[192,768]{1,0:T(8,128)(2,1)S(1)}, bf16[192,768]{1,0:T(8,128)(2,1)}, u32[]{:S(2)}, u32[]{:S(2)}) %collective-permute-start.3) | collective-permute-done | bytes 294944 | tf_op jit(solution)/shard_map/ppermute | solution.py:641
  38.9 0.8 copy-done.7
  40.1 2.4 %convolution_convert_fusion.own_in = bf16[392,768]{1,0:T(8,128)(2,1)} fusion(bf16[392,384]{1,0:T(8,128)(2,1)} %get-tuple-element.95.refs_1_, bf16[384,768]{1,0:T(8,128)(2,1)S(1)} %copy-done.4), kind=kOutput, calls=%fused_computation | convolution fusion | flops 231512064 | bytes 1492992 | tf_op jit(solution)/shard_map/dot_general | solution.py:739
  42.5 5.1 %collective-permute-done.4.peer_in = bf16[392,384]{1,0:T(8,128)(2,1)S(1)} collective-permute-done((bf16[392,384]{1,0:T(8,128)(2,1)}, bf16[392,384]{1,0:T(8,128)(2,1)S(1)}, u32[]{:S(2)}, u32[]{:S(2)}) %collective-permute-start.4) | collective-permute-done | bytes 301088 | tf_op jit(solution)/shard_map/ppermute | solution.py:641
  47.6 0.7 copy-done.43
  48.3 3.8 %middle.1 = (f32[392,768]{1,0:T(8,128)}, bf16[392,768]{1,0:T(8,128)(2,1)}) custom-call(s32[1]{0:T(128)} %bitcast.me_ref, bf16[392,768]{1,0:T(8,128)(2,1)} %bitcast.103, bf16[392,768]{1,0:T(8,128)(2,1)} %convolution_convert_fusion.own_in, bf16[392,384]{1,0:T(8,128)(2,1)} %copy-done.43, f32[768]{0:T(1024)} %bias_ref.1, f32[768]{0:T(1024)} %gain_ref.8, ...), custom_call_target="tpu_custom_call" | custom-call | flops 1000000 | bytes 3906 | tf_op jit(solution)/shard_map/middle/pallas_call | solution.py:520
  52.2 0.8 collective-permute-start.6
  53.0 1.1 copy-done.9
  54.1 6.1 %mlp.2 = (bf16[392,1536]{1,0:T(8,128)(2,1)S(1)}, bf16[392,1536]{1,0:T(8,128)(2,1)S(1)}, bf16[392,768]{1,0:T(8,128)(2,1)S(1)}, bf16[392,768]{1,0:T(8,128)(2,1)S(1)}) custom-call(bf16[392,768]{1,0:T(8,128)(2,1)S(1)} %copy-done.9, bf16[392,768]{1,0:T(8,128)(2,1)S(1)} %bitcast.108, bf16[768,1536]{1,0:T(8,128)(2,1)S(1)} %copy-done.2, ...), custom_call_target="tpu_custom_call" | custom-call | flops 1000000 | bytes 3906 | tf_op jit(solution)/shard_map/mlp/pallas_call | solution.py:520
  60.2 1.0 copy-done.14
  61.2 0.8 copy-done.24
  62.0 0.8 copy-done.37
  62.9 2.8 %collective-permute-done.6.nm_ref.refs_4_ = bf16[392,768]{1,0:T(8,128)(2,1)S(1)} collective-permute-done((bf16[392,768]{1,0:T(8,128)(2,1)}, bf16[392,768]{1,0:T(8,128)(2,1)S(1)}, u32[]{:S(2)}, u32[]{:S(2)}) %collective-permute-start.6) | collective-permute-done | bytes 602144 | tf_op jit(solution)/shard_map/ppermute | solution.py:641
  65.7 6.9 %mlp.3 = (bf16[392,1536]{1,0:T(8,128)(2,1)S(1)}, bf16[392,1536]{1,0:T(8,128)(2,1)S(1)}, bf16[392,768]{1,0:T(8,128)(2,1)S(1)}, bf16[392,768]{1,0:T(8,128)(2,1)}) custom-call(bf16[392,768]{1,0:T(8,128)(2,1)S(1)} %collective-permute-done.6.nm_ref.refs_4_, bf16[392,768]{1,0:T(8,128)(2,1)S(1)} %copy-done.8, bf16[768,1536]{1,0:T(8,128)(2,1)S(1)} %copy-done.2, ...), custom_call_target="tpu_custom_call" | custom-call | flops 1000000 | bytes 3906 | tf_op jit(solution)/shard_map/mlp/pallas_call | solution.py:520
  72.6 1.0 copy-done.16
  73.6 1.0 copy-done.17
  74.6 1.1 collective-permute-start.8
  75.7 11.9 %mlp_weights.1 = (f32[1,1536]{1,0:T(1,128)}, bf16[2,4,96,768]{3,2,1,0:T(8,128)(2,1)}, bf16[2,4,96,768]{3,2,1,0:T(8,128)(2,1)}, bf16[2,4,96,768]{3,2,1,0:T(8,128)(2,1)}, bf16[2,4,96,768]{3,2,1,0:T(8,128)(2,1)}) custom-call(s32[1]{0:T(128)} %bitcast.me_ref, bf16[392,768]{1,0:T(8,128)(2,1)} %get-tuple-element.103.nm_ref.refs_0_, bf16[392,768]{1,0:T(8,128)(2,1)} %bitcast.107, ...), custom_call_target="tpu_custom_call" | custom-call | flops 1000000 | bytes 3906 | tf_op jit(solution)/shard_map/mlp_weights/pallas_call | solution.py:520
  88.2 0.8 copy-done.39
  89.0 1.1 copy-done.40
  90.1 1.1 middle_back.1
  91.2 1.0 collective-permute-start.11
  92.4 1.6 collective-permute-start.12
  94.7 1.1 collective-permute-start.7
  95.9 9.7 %attn_backward.2 = (bf16[3,392,384]{2,1,0:T(8,128)(2,1)S(1)}, f32[1,768]{1,0:T(1,128)S(1)}, f32[3,64,256]{2,1,0:T(8,128)S(1)}, bf16[392,768]{1,0:T(8,128)(2,1)S(1)}, f32[2,768]{1,0:T(2,128)S(1)}) custom-call(bf16[392,768]{1,0:T(8,128)(2,1)S(1)} %get-tuple-element.142.branch_ref.refs_2_, bf16[392,768]{1,0:T(8,128)(2,1)S(1)} %bitcast.104, ...), custom_call_target="tpu_custom_call" | custom-call | flops 1000000 | bytes 3906 | tf_op jit(solution)/shard_map/attn_backward/pallas_call | solution.py:520
  105.7 3.0 %collective-permute-done.12 = bf16[4,96,768]{2,1,0:T(8,128)(2,1)S(1)} collective-permute-done((bf16[4,96,768]{2,1,0:T(8,128)(2,1)S(1)}, bf16[4,96,768]{2,1,0:T(8,128)(2,1)S(1)}, u32[]{:S(2)}, u32[]{:S(2)}) %collective-permute-start.12) | collective-permute-done | bytes 589856 | tf_op jit(solution)/shard_map/ppermute | solution.py:645
  108.9 3.7 %collective-permute-start.16 = (bf16[96,768]{1,0:T(8,128)(2,1)S(1)}, bf16[96,768]{1,0:T(8,128)(2,1)S(1)}, u32[]{:S(2)}, u32[]{:S(2)}) collective-permute-start(bf16[96,768]{1,0:T(8,128)(2,1)S(1)} %get-tuple-element.186), channel_id=1, source_target_pairs={{0,24},{2,26},{4,28},{6,30},{8,16},{10,18},{12,20},{14,22},{16,8},... | collective-permute-start | bytes 442376 | tf_op jit(solution)/shard_map/ppermute | solution.py:645
  112.5 0.8 collective-permute-start.14
  113.4 9.7 %attn_backward.3 = (bf16[3,392,384]{2,1,0:T(8,128)(2,1)S(1)}, f32[1,768]{1,0:T(1,128)S(1)}, f32[3,64,256]{2,1,0:T(8,128)S(1)}, bf16[392,768]{1,0:T(8,128)(2,1)S(1)}, f32[2,768]{1,0:T(2,128)S(1)}) custom-call(bf16[392,768]{1,0:T(8,128)(2,1)S(1)} %collective-permute-done.11.branch_ref.refs_9_, bf16[392,768]{1,0:T(8,128)(2,1)S(1)} %copy-done.12, ...), custom_call_target="tpu_custom_call" | custom-call | flops 1000000 | bytes 3906 | tf_op jit(solution)/shard_map/attn_backward/pallas_call | solution.py:520
  123.3 3.7 %collective-permute-start.20 = (bf16[96,768]{1,0:T(8,128)(2,1)S(1)}, bf16[96,768]{1,0:T(8,128)(2,1)S(1)}, u32[]{:S(2)}, u32[]{:S(2)}) collective-permute-start(bf16[96,768]{1,0:T(8,128)(2,1)S(1)} %get-tuple-element.183), channel_id=1, source_target_pairs={{0,24},{2,26},{4,28},{6,30},{8,16},{10,18},{12,20},{14,22},{16,8},... | collective-permute-start | bytes 442376 | tf_op jit(solution)/shard_map/ppermute | solution.py:645
  127.0 0.8 collective-permute-start.18
  128.0 5.7 %attn_weights.1 = (bf16[2,4,96,768]{3,2,1,0:T(8,128)(2,1)S(1)}, bf16[2,4,96,768]{3,2,1,0:T(8,128)(2,1)S(1)}, bf16[16,768]{1,0:T(8,128)(2,1)S(1)}) custom-call(s32[1]{0:T(128)} %bitcast.me_ref, f32[4,768]{1,0:T(4,128)S(1)} %get-tuple-element.140.sums2_ref, f32[1,1536]{1,0:T(1,128)S(1)} %copy-done.35, bf16[768,392]{1,0:T(8,128)(2,1)S(1)} %copy-done.20, ...), custom_call_target="tpu_custom_call" | custom-call | flops 1000000 | bytes 3906 | tf_op jit(solution)/shard_map/attn_weights/pallas_call | solution.py:520
  133.8 2.7 %collective-permute-done.19 = bf16[96,768]{1,0:T(8,128)(2,1)S(1)} collective-permute-done((bf16[96,768]{1,0:T(8,128)(2,1)S(1)}, bf16[96,768]{1,0:T(8,128)(2,1)S(1)}, u32[]{:S(2)}, u32[]{:S(2)}) %collective-permute-start.19) | collective-permute-done | bytes 147488 | tf_op jit(solution)/shard_map/ppermute | solution.py:645
  136.7 0.7 collective-permute-start.13
  137.6 2.0 collective-permute-done.25
  139.7 1.6 collective-permute-start.26
  141.3 1.0 collective-permute-start.21
  142.3 12.5 %collective-permute-done.22 = bf16[208,768]{1,0:T(8,128)(2,1)S(1)} collective-permute-done((bf16[208,768]{1,0:T(8,128)(2,1)S(1)}, bf16[208,768]{1,0:T(8,128)(2,1)S(1)}, u32[]{:S(2)}, u32[]{:S(2)}) %collective-permute-start.22) | collective-permute-done | bytes 319520 | tf_op jit(solution)/shard_map/ppermute | solution.py:645
  154.8 1.1 add_convert_fusion
  155.9 1.7 input_back.1
  157.6 6.6 %collective-permute-done.23 = bf16[208,768]{1,0:T(8,128)(2,1)S(1)} collective-permute-done((bf16[208,768]{1,0:T(8,128)(2,1)S(1)}, bf16[208,768]{1,0:T(8,128)(2,1)S(1)}, u32[]{:S(2)}, u32[]{:S(2)}) %collective-permute-start.23) | collective-permute-done | bytes 319520 | tf_op jit(solution)/shard_map/ppermute | solution.py:645
  164.3 1.6 collective-permute-start.24
  166.4 1.7 collective-permute-start.27
  168.2 4.2 %collective-permute-done.28 = bf16[96,768]{1,0:T(8,128)(2,1)S(1)} collective-permute-done((bf16[96,768]{1,0:T(8,128)(2,1)S(1)}, bf16[96,768]{1,0:T(8,128)(2,1)S(1)}, u32[]{:S(2)}, u32[]{:S(2)}) %collective-permute-start.28) | collective-permute-done | bytes 147488 | tf_op jit(solution)/shard_map/ppermute | solution.py:645
  173.0 1.9 collective-permute-done.27
  175.0 7.6 %collective-permute-done.29 = bf16[96,768]{1,0:T(8,128)(2,1)S(1)} collective-permute-done((bf16[96,768]{1,0:T(8,128)(2,1)S(1)}, bf16[96,768]{1,0:T(8,128)(2,1)S(1)}, u32[]{:S(2)}, u32[]{:S(2)}) %collective-permute-start.29) | collective-permute-done | bytes 147488 | tf_op jit(solution)/shard_map/ppermute | solution.py:645
  182.8 1.6 collective-permute-start.30
  184.4 5.2 %collective-permute-done.31 = bf16[96,768]{1,0:T(8,128)(2,1)S(1)} collective-permute-done((bf16[96,768]{1,0:T(8,128)(2,1)S(1)}, bf16[96,768]{1,0:T(8,128)(2,1)S(1)}, u32[]{:S(2)}, u32[]{:S(2)}) %collective-permute-start.31) | collective-permute-done | bytes 147488 | tf_op jit(solution)/shard_map/ppermute | solution.py:645
  189.6 0.8 collective-permute-done.30
  190.4 4.3 %collective-permute-done.32 = bf16[96,768]{1,0:T(8,128)(2,1)S(1)} collective-permute-done((bf16[96,768]{1,0:T(8,128)(2,1)S(1)}, bf16[96,768]{1,0:T(8,128)(2,1)S(1)}, u32[]{:S(2)}, u32[]{:S(2)}) %collective-permute-start.32) | collective-permute-done | bytes 147488 | tf_op jit(solution)/shard_map/ppermute | solution.py:645
  195.4 0.7 collective-permute-start.36
  196.1 1.7 collective-permute-done.34.refs_3_
  197.9 5.4 %finish_mlp.1 = (f32[768,1536]{1,0:T(8,128)}, f32[1536,768]{1,0:T(8,128)}, f32[16,768]{1,0:T(8,128)S(1)}) custom-call(s32[1]{0:T(128)} %bitcast.me_ref, bf16[4,208,768]{2,1,0:T(8,128)(2,1)S(1)} %pad_maximum_fusion.refs_0_, bf16[4,208,768]{2,1,0:T(8,128)(2,1)S(1)} %collective-permute-done.24.refs_1_, ...), custom_call_target="tpu_custom_call" | custom-call | flops 1000000 | bytes 3906 | tf_op jit(solution)/shard_map/finish_mlp/pallas_call | solution.py:520
  203.3 1.4 collective-permute-start.35
  204.7 1.9 finish.2
  207.3 3.4 %collective-permute-done.36.refs_0_ = bf16[4,96,768]{2,1,0:T(8,128)(2,1)S(1)} collective-permute-done((bf16[4,96,768]{2,1,0:T(8,128)(2,1)S(1)}, bf16[4,96,768]{2,1,0:T(8,128)(2,1)S(1)}, u32[]{:S(2)}, u32[]{:S(2)}) %collective-permute-start.36) | collective-permute-done | bytes 589856 | tf_op jit(solution)/shard_map/ppermute | solution.py:645
  212.7 1.9 finish.3
  (155 shorter events, 9.8 us)
Async XLA Ops:
  1.3 8.0 %copy-start.45 = (f32[8,49]{1,0:T(8,128)}, f32[8,49]{1,0:T(8,128)S(1)}, u32[]{:S(2)}) copy-start(f32[8,49]{1,0:T(8,128)S(1)} %convert_element_type.294.valid_ref) | copy-start | bytes 4708
  1.3 4.9 %collective-permute-start.1 = (f32[8,49]{1,0:T(8,128)S(1)}, f32[8,49]{1,0:T(8,128)S(1)}, u32[]{:S(2)}, u32[]{:S(2)}) collective-permute-start(f32[8,49]{1,0:T(8,128)S(1)} %convert_element_type.294.valid_ref), channel_id=1, source_target_pairs={{0,1},{1,0},{2,3},{3,2},{4,5},{5,4},{6,7},{7,6},{8,9},{9,8},{10,11... | collective-permute-start | bytes 4712 | tf_op jit(solution)/shard_map/ppermute | solution.py:641
  4.3 17.5 %collective-permute-start = (bf16[392,768]{1,0:T(8,128)(2,1)}, bf16[392,768]{1,0:T(8,128)(2,1)S(1)}, u32[]{:S(2)}, u32[]{:S(2)}) collective-permute-start(bf16[392,768]{1,0:T(8,128)(2,1)} %bitcast.101), channel_id=1, source_target_pairs={{0,1},{1,0},{2,3},{3,2},{4,5},{5,4},{6,7},{7,6},{8,9},{9,8},{10,11... | collective-permute-start | bytes 1806344 | tf_op jit(solution)/shard_map/ppermute | solution.py:641
  6.2 15.5 %copy-start.48 = (f32[8,49]{1,0:T(8,128)}, f32[8,49]{1,0:T(8,128)S(1)}, u32[]{:S(2)}) copy-start(f32[8,49]{1,0:T(8,128)S(1)} %collective-permute-done.1.valid_ref) | copy-start | bytes 4708
  6.2 32.6 %collective-permute-start.2 = (bf16[392,768]{1,0:T(8,128)(2,1)}, bf16[392,768]{1,0:T(8,128)(2,1)S(1)}, u32[]{:S(2)}, u32[]{:S(2)}) collective-permute-start(bf16[392,768]{1,0:T(8,128)(2,1)} %bitcast.106), channel_id=1, source_target_pairs={{0,1},{1,0},{2,3},{3,2},{4,5},{5,4},{6,7},{7,6},{8,9},{9,8},{10,11... | collective-permute-start | bytes 1806344 | tf_op jit(solution)/shard_map/ppermute | solution.py:641
  9.2 29.6 %collective-permute-start.3 = (bf16[192,768]{1,0:T(8,128)(2,1)S(1)}, bf16[192,768]{1,0:T(8,128)(2,1)}, u32[]{:S(2)}, u32[]{:S(2)}) collective-permute-start(bf16[192,768]{1,0:T(8,128)(2,1)S(1)} %constant_dynamic-slice_fusion), channel_id=1, source_target_pairs={{0,1},{1,0},{2,3},{3,2},{4,5},{5,4},{6,7},{7,6},{8,9},{9,8},{10,11... | collective-permute-start | bytes 884744 | tf_op jit(solution)/shard_map/ppermute | solution.py:641
  9.3 30.8 %copy-start.4 = (bf16[384,768]{1,0:T(8,128)(2,1)S(1)}, bf16[384,768]{1,0:T(8,128)(2,1)}, u32[]{:S(2)}) copy-start(bf16[384,768]{1,0:T(8,128)(2,1)} %proj_ref.3) | copy-start | bytes 1769476
  22.6 30.3 %copy-start.3 = (bf16[1536,768]{1,0:T(8,128)(2,1)S(1)}, bf16[1536,768]{1,0:T(8,128)(2,1)}, u32[]{:S(2)}) copy-start(bf16[1536,768]{1,0:T(8,128)(2,1)} %fc2_ref.3) | copy-start | bytes 7077892
  39.7 7.9 %collective-permute-start.4 = (bf16[392,384]{1,0:T(8,128)(2,1)}, bf16[392,384]{1,0:T(8,128)(2,1)S(1)}, u32[]{:S(2)}, u32[]{:S(2)}) collective-permute-start(bf16[392,384]{1,0:T(8,128)(2,1)} %get-tuple-element.100.refs_8_), channel_id=1, source_target_pairs={{0,1},{1,0},{2,3},{3,2},{4,5},{5,4},{6,7},{7,6},{8,9},{9,8},{10,11... | collective-permute-start | bytes 903176 | tf_op jit(solution)/shard_map/ppermute | solution.py:641
  40.1 2.4 %collective-permute-start.5 = (bf16[192,768]{1,0:T(8,128)(2,1)}, bf16[192,768]{1,0:T(8,128)(2,1)S(1)}, u32[]{:S(2)}, u32[]{:S(2)}) collective-permute-start(bf16[192,768]{1,0:T(8,128)(2,1)} %collective-permute-done.3.refs_0_), channel_id=1, source_target_pairs={{0,2},{2,0},{4,6},{6,4},{8,10},{10,8},{12,14},{14,12},{16,18},{18,... | collective-permute-start | bytes 884744 | tf_op jit(solution)/shard_map/ppermute | solution.py:645
  40.1 12.9 %copy-start.2 = (bf16[768,1536]{1,0:T(8,128)(2,1)S(1)}, bf16[768,1536]{1,0:T(8,128)(2,1)}, u32[]{:S(2)}) copy-start(bf16[768,1536]{1,0:T(8,128)(2,1)} %fc1_ref.3) | copy-start | bytes 7077892
  42.5 10.5 %copy-start.46 = (f32[1536]{0:T(1024)S(1)}, f32[1536]{0:T(1024)}, u32[]{:S(2)}) copy-start(f32[1536]{0:T(1024)} %param.28) | copy-start | bytes 18436
  42.5 10.5 %copy-start.5 = (bf16[8,49,768]{2,0,1:T(8,128)(2,1)S(1)}, bf16[8,49,768]{2,0,1:T(8,128)(2,1)}, u32[]{:S(2)}) copy-start(bf16[8,49,768]{2,0,1:T(8,128)(2,1)} %param.31) | copy-start | bytes 1806340
  42.5 5.1 %copy-start.44 = (bf16[192,768]{1,0:T(8,128)(2,1)}, bf16[192,768]{1,0:T(8,128)(2,1)S(1)}, u32[]{:S(2)}) copy-start(bf16[192,768]{1,0:T(8,128)(2,1)S(1)} %collective-permute-done.5.refs_1_) | copy-start | bytes 884740
  52.2 13.5 %collective-permute-start.6 = (bf16[392,768]{1,0:T(8,128)(2,1)}, bf16[392,768]{1,0:T(8,128)(2,1)S(1)}, u32[]{:S(2)}, u32[]{:S(2)}) collective-permute-start(bf16[392,768]{1,0:T(8,128)(2,1)} %get-tuple-element.103.nm_ref.refs_0_), channel_id=1, source_target_pairs={{0,1},{1,0},{2,3},{3,2},{4,5},{5,4},{6,7},{7,6},{8,9},{9,8},{10,11... | collective-permute-start | bytes 1806344 | tf_op jit(solution)/shard_map/ppermute | solution.py:641
  54.1 11.6 %copy-start.8 = (bf16[392,768]{1,0:T(8,128)(2,1)S(1)}, bf16[392,768]{1,0:T(8,128)(2,1)}, u32[]{:S(2)}) copy-start(bf16[392,768]{1,0:T(8,128)(2,1)} %copy-done.7) | copy-start | bytes 1806340
  62.9 9.7 %copy-start.15 = (bf16[392,1536]{1,0:T(8,128)(2,1)}, bf16[392,1536]{1,0:T(8,128)(2,1)S(1)}, u32[]{:S(2)}) copy-start(bf16[392,1536]{1,0:T(8,128)(2,1)S(1)} %get-tuple-element.110.refs_3_) | copy-start | bytes 3612676
  65.7 6.9 %copy-start.10 = (bf16[392,768]{1,0:T(8,128)(2,1)}, bf16[392,768]{1,0:T(8,128)(2,1)S(1)}, u32[]{:S(2)}) copy-start(bf16[392,768]{1,0:T(8,128)(2,1)S(1)} %collective-permute-done.6.nm_ref.refs_4_) | copy-start | bytes 1806340
  74.6 13.6 %collective-permute-start.8 = (bf16[392,768]{1,0:T(8,128)(2,1)}, bf16[392,768]{1,0:T(8,128)(2,1)S(1)}, u32[]{:S(2)}, u32[]{:S(2)}) collective-permute-start(bf16[392,768]{1,0:T(8,128)(2,1)} %get-tuple-element.108), channel_id=1, source_target_pairs={{0,1},{1,0},{2,3},{3,2},{4,5},{5,4},{6,7},{7,6},{8,9},{9,8},{10,11... | collective-permute-start | bytes 1806344 | tf_op jit(solution)/shard_map/ppermute | solution.py:641
  75.7 13.3 %copy-start.6 = (bf16[8,49,768]{2,0,1:T(8,128)(2,1)S(1)}, bf16[8,49,768]{2,0,1:T(8,128)(2,1)}, u32[]{:S(2)}) copy-start(bf16[8,49,768]{2,0,1:T(8,128)(2,1)} %param.31) | copy-start | bytes 1806340
  75.7 13.3 %copy-start.19 = (f32[392,768]{1,0:T(8,128)S(1)}, f32[392,768]{1,0:T(8,128)}, u32[]{:S(2)}) copy-start(f32[392,768]{1,0:T(8,128)} %get-tuple-element.102.middle_ref) | copy-start | bytes 3612676
  75.7 13.3 %copy-start.36 = (f32[768]{0:T(1024)S(1)}, f32[768]{0:T(1024)}, u32[]{:S(2)}) copy-start(f32[768]{0:T(1024)} %gain_ref.8) | copy-start | bytes 9220
  75.7 13.3 %copy-start.38 = (bf16[392,768]{1,0:T(8,128)(2,1)S(1)}, bf16[392,768]{1,0:T(8,128)(2,1)}, u32[]{:S(2)}) copy-start(bf16[392,768]{1,0:T(8,128)(2,1)} %copy-done.37) | copy-start | bytes 1806340
  87.6 4.6 %collective-permute-start.9 = (bf16[2,4,96,768]{3,2,1,0:T(8,128)(2,1)}, bf16[2,4,96,768]{3,2,1,0:T(8,128)(2,1)S(1)}, u32[]{:S(2)}, u32[]{:S(2)}) collective-permute-start(bf16[2,4,96,768]{3,2,1,0:T(8,128)(2,1)} %get-tuple-element.117), channel_id=1, source_target_pairs={{0,2},{2,0},{4,6},{6,4},{8,10},{10,8},{12,14},{14,12},{16,18},{18,... | collective-permute-start | bytes 3538952 | tf_op jit(solution)/shard_map/ppermute | solution.py:645
  87.7 6.3 %collective-permute-start.10 = (bf16[2,4,96,768]{3,2,1,0:T(8,128)(2,1)}, bf16[2,4,96,768]{3,2,1,0:T(8,128)(2,1)S(1)}, u32[]{:S(2)}, u32[]{:S(2)}) collective-permute-start(bf16[2,4,96,768]{3,2,1,0:T(8,128)(2,1)} %get-tuple-element.120), channel_id=1, source_target_pairs={{0,2},{2,0},{4,6},{6,4},{8,10},{10,8},{12,14},{14,12},{16,18},{18,... | collective-permute-start | bytes 3538952 | tf_op jit(solution)/shard_map/ppermute | solution.py:645
  90.1 5.7 %copy-start.30 = (bf16[8,64,384]{2,1,0:T(8,128)(2,1)S(1)}, bf16[8,64,384]{2,1,0:T(8,128)(2,1)}, u32[]{:S(2)}) copy-start(bf16[8,64,384]{2,1,0:T(8,128)(2,1)} %get-tuple-element.125.k_ref) | copy-start | bytes 1179652
  90.1 5.7 %copy-start.31 = (bf16[8,64,384]{2,1,0:T(8,128)(2,1)S(1)}, bf16[8,64,384]{2,1,0:T(8,128)(2,1)}, u32[]{:S(2)}) copy-start(bf16[8,64,384]{2,1,0:T(8,128)(2,1)} %get-tuple-element.126.v_ref) | copy-start | bytes 1179652
  91.2 21.3 %collective-permute-start.11 = (bf16[392,768]{1,0:T(8,128)(2,1)S(1)}, bf16[392,768]{1,0:T(8,128)(2,1)S(1)}, u32[]{:S(2)}, u32[]{:S(2)}) collective-permute-start(bf16[392,768]{1,0:T(8,128)(2,1)S(1)} %get-tuple-element.142.branch_ref.refs_2_), channel_id=1, source_target_pairs={{0,1},{1,0},{2,3},{3,2},{4,5},{5,4},{6,7},{7,6},{8,9},{9,8},{10,11... | collective-permute-start | bytes 1806344 | tf_op jit(solution)/shard_map/ppermute | solution.py:641
  92.4 16.3 %collective-permute-start.12 = (bf16[4,96,768]{2,1,0:T(8,128)(2,1)S(1)}, bf16[4,96,768]{2,1,0:T(8,128)(2,1)S(1)}, u32[]{:S(2)}, u32[]{:S(2)}) collective-permute-start(bf16[4,96,768]{2,1,0:T(8,128)(2,1)S(1)} %fusion), channel_id=1, source_target_pairs={{0,4},{2,6},{4,0},{6,2},{8,12},{10,14},{12,8},{14,10},{16,20},{18,... | collective-permute-start | bytes 1769480 | tf_op jit(solution)/shard_map/ppermute | solution.py:645
  94.2 28.9 %collective-permute-start.17 = (bf16[4,96,768]{2,1,0:T(8,128)(2,1)S(1)}, bf16[4,96,768]{2,1,0:T(8,128)(2,1)S(1)}, u32[]{:S(2)}, u32[]{:S(2)}) collective-permute-start(bf16[4,96,768]{2,1,0:T(8,128)(2,1)S(1)} %fusion.1), channel_id=1, source_target_pairs={{0,4},{2,6},{4,0},{6,2},{8,12},{10,14},{12,8},{14,10},{16,20},{18,... | collective-permute-start | bytes 1769480 | tf_op jit(solution)/shard_map/ppermute | solution.py:645
  94.7 33.2 %collective-permute-start.7 = (bf16[392,768]{1,0:T(8,128)(2,1)S(1)}, bf16[392,768]{1,0:T(8,128)(2,1)S(1)}, u32[]{:S(2)}, u32[]{:S(2)}) collective-permute-start(bf16[392,768]{1,0:T(8,128)(2,1)S(1)} %get-tuple-element.107), channel_id=1, source_target_pairs={{0,1},{1,0},{2,3},{3,2},{4,5},{5,4},{6,7},{7,6},{8,9},{9,8},{10,11... | collective-permute-start | bytes 1806344 | tf_op jit(solution)/shard_map/ppermute | solution.py:641
  95.9 17.5 %copy-start.27 = (bf16[8,64,384]{2,1,0:T(8,128)(2,1)S(1)}, bf16[8,64,384]{2,1,0:T(8,128)(2,1)}, u32[]{:S(2)}) copy-start(bf16[8,64,384]{2,1,0:T(8,128)(2,1)} %get-tuple-element.132.k_ref) | copy-start | bytes 1179652
  95.9 17.5 %copy-start.28 = (bf16[8,64,384]{2,1,0:T(8,128)(2,1)S(1)}, bf16[8,64,384]{2,1,0:T(8,128)(2,1)}, u32[]{:S(2)}) copy-start(bf16[8,64,384]{2,1,0:T(8,128)(2,1)} %get-tuple-element.133.v_ref) | copy-start | bytes 1179652
  105.6 7.7 %copy-start.12 = (bf16[392,768]{1,0:T(8,128)(2,1)S(1)}, bf16[392,768]{1,0:T(8,128)(2,1)}, u32[]{:S(2)}) copy-start(bf16[392,768]{1,0:T(8,128)(2,1)} %copy-done.11) | copy-start | bytes 1806340
  105.6 7.7 %copy-start.22 = (bf16[8,3,64,256]{3,2,1,0:T(8,128)(2,1)S(1)}, bf16[8,3,64,256]{3,2,1,0:T(8,128)(2,1)}, u32[]{:S(2)}) copy-start(bf16[8,3,64,256]{3,2,1,0:T(8,128)(2,1)} %get-tuple-element.130.prob_ref) | copy-start | bytes 2359300
  105.6 7.7 %copy-start.26 = (bf16[8,64,384]{2,1,0:T(8,128)(2,1)S(1)}, bf16[8,64,384]{2,1,0:T(8,128)(2,1)}, u32[]{:S(2)}) copy-start(bf16[8,64,384]{2,1,0:T(8,128)(2,1)} %get-tuple-element.131.q_ref) | copy-start | bytes 1179652
  108.9 18.1 %collective-permute-start.16 = (bf16[96,768]{1,0:T(8,128)(2,1)S(1)}, bf16[96,768]{1,0:T(8,128)(2,1)S(1)}, u32[]{:S(2)}, u32[]{:S(2)}) collective-permute-start(bf16[96,768]{1,0:T(8,128)(2,1)S(1)} %get-tuple-element.186), channel_id=1, source_target_pairs={{0,24},{2,26},{4,28},{6,30},{8,16},{10,18},{12,20},{14,22},{16,8},... | collective-permute-start | bytes 442376 | tf_op jit(solution)/shard_map/ppermute | solution.py:645
  112.5 14.5 %collective-permute-start.15 = (bf16[96,768]{1,0:T(8,128)(2,1)S(1)}, bf16[96,768]{1,0:T(8,128)(2,1)S(1)}, u32[]{:S(2)}, u32[]{:S(2)}) collective-permute-start(bf16[96,768]{1,0:T(8,128)(2,1)S(1)} %get-tuple-element.187), channel_id=1, source_target_pairs={{0,16},{2,18},{4,20},{6,22},{8,24},{10,26},{12,28},{14,30},{16,0},... | collective-permute-start | bytes 442376 | tf_op jit(solution)/shard_map/ppermute | solution.py:645
  112.5 15.2 %collective-permute-start.14 = (bf16[96,768]{1,0:T(8,128)(2,1)S(1)}, bf16[96,768]{1,0:T(8,128)(2,1)S(1)}, u32[]{:S(2)}, u32[]{:S(2)}) collective-permute-start(bf16[96,768]{1,0:T(8,128)(2,1)S(1)} %get-tuple-element.188), channel_id=1, source_target_pairs={{0,8},{2,10},{4,12},{6,14},{8,0},{10,2},{12,4},{14,6},{16,24},{18,... | collective-permute-start | bytes 442376 | tf_op jit(solution)/shard_map/ppermute | solution.py:645
  123.1 4.8 %copy-start.18 = (bf16[392,384]{1,0:T(8,128)(2,1)S(1)}, bf16[392,384]{1,0:T(8,128)(2,1)}, u32[]{:S(2)}) copy-start(bf16[392,384]{1,0:T(8,128)(2,1)} %get-tuple-element.95.refs_1_) | copy-start | bytes 903172
  123.3 10.4 %collective-permute-start.20 = (bf16[96,768]{1,0:T(8,128)(2,1)S(1)}, bf16[96,768]{1,0:T(8,128)(2,1)S(1)}, u32[]{:S(2)}, u32[]{:S(2)}) collective-permute-start(bf16[96,768]{1,0:T(8,128)(2,1)S(1)} %get-tuple-element.183), channel_id=1, source_target_pairs={{0,24},{2,26},{4,28},{6,30},{8,16},{10,18},{12,20},{14,22},{16,8},... | collective-permute-start | bytes 442376 | tf_op jit(solution)/shard_map/ppermute | solution.py:645
  127.0 9.5 %collective-permute-start.19 = (bf16[96,768]{1,0:T(8,128)(2,1)S(1)}, bf16[96,768]{1,0:T(8,128)(2,1)S(1)}, u32[]{:S(2)}, u32[]{:S(2)}) collective-permute-start(bf16[96,768]{1,0:T(8,128)(2,1)S(1)} %get-tuple-element.184), channel_id=1, source_target_pairs={{0,16},{2,18},{4,20},{6,22},{8,24},{10,26},{12,28},{14,30},{16,0},... | collective-permute-start | bytes 442376 | tf_op jit(solution)/shard_map/ppermute | solution.py:645
  127.0 9.5 %collective-permute-start.18 = (bf16[96,768]{1,0:T(8,128)(2,1)S(1)}, bf16[96,768]{1,0:T(8,128)(2,1)S(1)}, u32[]{:S(2)}, u32[]{:S(2)}) collective-permute-start(bf16[96,768]{1,0:T(8,128)(2,1)S(1)} %get-tuple-element.185), channel_id=1, source_target_pairs={{0,8},{2,10},{4,12},{6,14},{8,0},{10,2},{12,4},{14,6},{16,24},{18,... | collective-permute-start | bytes 442376 | tf_op jit(solution)/shard_map/ppermute | solution.py:645
  136.6 18.2 %copy-start.25 = (bf16[392,768]{1,0:T(8,128)(2,1)S(1)}, bf16[392,768]{1,0:T(8,128)(2,1)}, u32[]{:S(2)}) copy-start(bf16[392,768]{1,0:T(8,128)(2,1)} %copy-done.24) | copy-start | bytes 1806340
  136.6 18.1 %copy-start.47 = (f32[768]{0:T(1024)S(1)}, f32[768]{0:T(1024)}, u32[]{:S(2)}) copy-start(f32[768]{0:T(1024)} %param.30) | copy-start | bytes 9220
  136.6 2.9 %collective-permute-start.25 = (bf16[2,4,96,768]{3,2,1,0:T(8,128)(2,1)S(1)}, bf16[2,4,96,768]{3,2,1,0:T(8,128)(2,1)S(1)}, u32[]{:S(2)}, u32[]{:S(2)}) collective-permute-start(bf16[2,4,96,768]{3,2,1,0:T(8,128)(2,1)S(1)} %get-tuple-element.161), channel_id=1, source_target_pairs={{0,2},{2,0},{4,6},{6,4},{8,10},{10,8},{12,14},{14,12},{16,18},{18,... | collective-permute-start | bytes 3538952 | tf_op jit(solution)/shard_map/ppermute | solution.py:645
  136.7 19.2 %collective-permute-start.13 = (bf16[392,768]{1,0:T(8,128)(2,1)S(1)}, bf16[392,768]{1,0:T(8,128)(2,1)S(1)}, u32[]{:S(2)}, u32[]{:S(2)}) collective-permute-start(bf16[392,768]{1,0:T(8,128)(2,1)S(1)} %get-tuple-element.134), channel_id=1, source_target_pairs={{0,1},{1,0},{2,3},{3,2},{4,5},{5,4},{6,7},{7,6},{8,9},{9,8},{10,11... | collective-permute-start | bytes 1806344 | tf_op jit(solution)/shard_map/ppermute | solution.py:641
  137.5 17.3 %collective-permute-start.22 = (bf16[208,768]{1,0:T(8,128)(2,1)S(1)}, bf16[208,768]{1,0:T(8,128)(2,1)S(1)}, u32[]{:S(2)}, u32[]{:S(2)}) collective-permute-start(bf16[208,768]{1,0:T(8,128)(2,1)S(1)} %get-tuple-element.190), channel_id=1, source_target_pairs={{0,16},{2,18},{4,20},{6,22},{8,24},{10,26},{12,28},{14,30},{16,0},... | collective-permute-start | bytes 958472 | tf_op jit(solution)/shard_map/ppermute | solution.py:645
  139.7 26.2 %collective-permute-start.26 = (bf16[4,96,768]{2,1,0:T(8,128)(2,1)S(1)}, bf16[4,96,768]{2,1,0:T(8,128)(2,1)S(1)}, u32[]{:S(2)}, u32[]{:S(2)}) collective-permute-start(bf16[4,96,768]{2,1,0:T(8,128)(2,1)S(1)} %fusion.2), channel_id=1, source_target_pairs={{0,4},{2,6},{4,0},{6,2},{8,12},{10,14},{12,8},{14,10},{16,20},{18,... | collective-permute-start | bytes 1769480 | tf_op jit(solution)/shard_map/ppermute | solution.py:645
  141.3 16.3 %collective-permute-start.21 = (bf16[208,768]{1,0:T(8,128)(2,1)S(1)}, bf16[208,768]{1,0:T(8,128)(2,1)S(1)}, u32[]{:S(2)}, u32[]{:S(2)}) collective-permute-start(bf16[208,768]{1,0:T(8,128)(2,1)S(1)} %get-tuple-element.190), channel_id=1, source_target_pairs={{0,8},{2,10},{4,12},{6,14},{8,0},{10,2},{12,4},{14,6},{16,24},{18,... | collective-permute-start | bytes 958472 | tf_op jit(solution)/shard_map/ppermute | solution.py:645
  154.8 9.4 %collective-permute-start.23 = (bf16[208,768]{1,0:T(8,128)(2,1)S(1)}, bf16[208,768]{1,0:T(8,128)(2,1)S(1)}, u32[]{:S(2)}, u32[]{:S(2)}) collective-permute-start(bf16[208,768]{1,0:T(8,128)(2,1)S(1)} %collective-permute-done.22), channel_id=1, source_target_pairs={{0,8},{2,10},{4,12},{6,14},{8,0},{10,2},{12,4},{14,6},{16,24},{18,... | collective-permute-start | bytes 958472 | tf_op jit(solution)/shard_map/ppermute | solution.py:645
  164.3 30.4 %collective-permute-start.24 = (bf16[4,208,768]{2,1,0:T(8,128)(2,1)S(1)}, bf16[4,208,768]{2,1,0:T(8,128)(2,1)S(1)}, u32[]{:S(2)}, u32[]{:S(2)}) collective-permute-start(bf16[4,208,768]{2,1,0:T(8,128)(2,1)S(1)} %pad_maximum_fusion.refs_0_), channel_id=1, source_target_pairs={{0,4},{2,6},{4,0},{6,2},{8,12},{10,14},{12,8},{14,10},{16,20},{18,... | collective-permute-start | bytes 3833864 | tf_op jit(solution)/shard_map/ppermute | solution.py:645
  166.1 6.2 %collective-permute-start.28 = (bf16[96,768]{1,0:T(8,128)(2,1)S(1)}, bf16[96,768]{1,0:T(8,128)(2,1)S(1)}, u32[]{:S(2)}, u32[]{:S(2)}) collective-permute-start(bf16[96,768]{1,0:T(8,128)(2,1)S(1)} %get-tuple-element.182), channel_id=1, source_target_pairs={{0,8},{2,10},{4,12},{6,14},{8,0},{10,2},{12,4},{14,6},{16,24},{18,... | collective-permute-start | bytes 442376 | tf_op jit(solution)/shard_map/ppermute | solution.py:645
  166.4 8.6 %collective-permute-start.27 = (bf16[96,768]{1,0:T(8,128)(2,1)S(1)}, bf16[96,768]{1,0:T(8,128)(2,1)S(1)}, u32[]{:S(2)}, u32[]{:S(2)}) collective-permute-start(bf16[96,768]{1,0:T(8,128)(2,1)S(1)} %get-tuple-element.181), channel_id=1, source_target_pairs={{0,8},{2,10},{4,12},{6,14},{8,0},{10,2},{12,4},{14,6},{16,24},{18,... | collective-permute-start | bytes 442376 | tf_op jit(solution)/shard_map/ppermute | solution.py:645
  172.4 10.2 %collective-permute-start.29 = (bf16[96,768]{1,0:T(8,128)(2,1)S(1)}, bf16[96,768]{1,0:T(8,128)(2,1)S(1)}, u32[]{:S(2)}, u32[]{:S(2)}) collective-permute-start(bf16[96,768]{1,0:T(8,128)(2,1)S(1)} %add_convert_fusion.4), channel_id=1, source_target_pairs={{0,16},{2,18},{4,20},{6,22},{8,24},{10,26},{12,28},{14,30},{16,0},... | collective-permute-start | bytes 442376 | tf_op jit(solution)/shard_map/ppermute | solution.py:645
  182.7 6.8 %collective-permute-start.31 = (bf16[96,768]{1,0:T(8,128)(2,1)S(1)}, bf16[96,768]{1,0:T(8,128)(2,1)S(1)}, u32[]{:S(2)}, u32[]{:S(2)}) collective-permute-start(bf16[96,768]{1,0:T(8,128)(2,1)S(1)} %fusion.8), channel_id=1, source_target_pairs={{0,16},{2,18},{4,20},{6,22},{8,24},{10,26},{12,28},{14,30},{16,0},... | collective-permute-start | bytes 442376 | tf_op jit(solution)/shard_map/ppermute | solution.py:645
  182.8 7.6 %collective-permute-start.30 = (bf16[96,768]{1,0:T(8,128)(2,1)S(1)}, bf16[96,768]{1,0:T(8,128)(2,1)S(1)}, u32[]{:S(2)}, u32[]{:S(2)}) collective-permute-start(bf16[96,768]{1,0:T(8,128)(2,1)S(1)} %fusion.8), channel_id=1, source_target_pairs={{0,8},{2,10},{4,12},{6,14},{8,0},{10,2},{12,4},{14,6},{16,24},{18,... | collective-permute-start | bytes 442376 | tf_op jit(solution)/shard_map/ppermute | solution.py:645
  189.6 5.1 %collective-permute-start.32 = (bf16[96,768]{1,0:T(8,128)(2,1)S(1)}, bf16[96,768]{1,0:T(8,128)(2,1)S(1)}, u32[]{:S(2)}, u32[]{:S(2)}) collective-permute-start(bf16[96,768]{1,0:T(8,128)(2,1)S(1)} %collective-permute-done.31), channel_id=1, source_target_pairs={{0,8},{2,10},{4,12},{6,14},{8,0},{10,2},{12,4},{14,6},{16,24},{18,... | collective-permute-start | bytes 442376 | tf_op jit(solution)/shard_map/ppermute | solution.py:645
  189.6 6.6 %collective-permute-start.33 = (bf16[4,208,768]{2,1,0:T(8,128)(2,1)S(1)}, bf16[4,208,768]{2,1,0:T(8,128)(2,1)S(1)}, u32[]{:S(2)}, u32[]{:S(2)}) collective-permute-start(bf16[4,208,768]{2,1,0:T(8,128)(2,1)S(1)} %pad_maximum_fusion.refs_0_), channel_id=1, source_target_pairs={{0,2},{2,0},{4,6},{6,4},{8,10},{10,8},{12,14},{14,12},{16,18},{18,... | collective-permute-start | bytes 3833864 | tf_op jit(solution)/shard_map/ppermute | solution.py:645
  194.8 3.1 %collective-permute-start.34 = (bf16[4,208,768]{2,1,0:T(8,128)(2,1)S(1)}, bf16[4,208,768]{2,1,0:T(8,128)(2,1)S(1)}, u32[]{:S(2)}, u32[]{:S(2)}) collective-permute-start(bf16[4,208,768]{2,1,0:T(8,128)(2,1)S(1)} %collective-permute-done.24.refs_1_), channel_id=1, source_target_pairs={{0,2},{2,0},{4,6},{6,4},{8,10},{10,8},{12,14},{14,12},{16,18},{18,... | collective-permute-start | bytes 3833864 | tf_op jit(solution)/shard_map/ppermute | solution.py:645
  194.9 9.8 %collective-permute-start.37 = (bf16[4,96,768]{2,1,0:T(8,128)(2,1)S(1)}, bf16[4,96,768]{2,1,0:T(8,128)(2,1)S(1)}, u32[]{:S(2)}, u32[]{:S(2)}) collective-permute-start(bf16[4,96,768]{2,1,0:T(8,128)(2,1)S(1)} %pad_maximum_fusion.1.refs_0_), channel_id=1, source_target_pairs={{0,2},{2,0},{4,6},{6,4},{8,10},{10,8},{12,14},{14,12},{16,18},{18,... | collective-permute-start | bytes 1769480 | tf_op jit(solution)/shard_map/ppermute | solution.py:645
  195.4 15.3 %collective-permute-start.36 = (bf16[4,96,768]{2,1,0:T(8,128)(2,1)S(1)}, bf16[4,96,768]{2,1,0:T(8,128)(2,1)S(1)}, u32[]{:S(2)}, u32[]{:S(2)}) collective-permute-start(bf16[4,96,768]{2,1,0:T(8,128)(2,1)S(1)} %pad_maximum_fusion.1.refs_0_), channel_id=1, source_target_pairs={{0,4},{2,6},{4,0},{6,2},{8,12},{10,14},{12,8},{14,10},{16,20},{18,... | collective-permute-start | bytes 1769480 | tf_op jit(solution)/shard_map/ppermute | solution.py:645
  203.3 4.0 %collective-permute-start.35 = (f32[6,768]{1,0:T(8,128)S(1)}, f32[6,768]{1,0:T(8,128)S(1)}, u32[]{:S(2)}, u32[]{:S(2)}) collective-permute-start(f32[6,768]{1,0:T(8,128)S(1)} %slice.210), channel_id=1, source_target_pairs={{0,1},{1,0},{2,3},{3,2},{4,5},{5,4},{6,7},{7,6},{8,9},{9,8},{10,11... | collective-permute-start | bytes 55304 | tf_op jit(solution)/shard_map/ppermute | solution.py:641
  210.7 2.0 collective-permute-start.38
  (24 other events, 52.2 us)

commit v9 on v8

--- a/solution.py
+++ b/solution.py
@@ -731,7 +731,7 @@
     me = index.reshape(1)
     valids = blocks_of(valid)
     kept, xs = [], []
-    for x_b, valid_b in zip(blocks_of(x), valids):
+    for x_b, valid_b in zip([x, across(after(x, valids[1]))] if fast else blocks_of(x), valids):
         if kept:
             x_b = after(x_b, kept[0][4])
         xs.append(x_b)
@@ -741,10 +741,10 @@
         core = index & 1
         half = across(lax.dynamic_slice_in_dim(after(proj, valids[1], pos), core * (width // 2), width // 2, 0))
         cots = [cot, across(after(cot, valids[1], pos))]
-        mixed = across(after(kept[1][4], cots[1], half))
+        mixed = across(kept[1][4])
         half = after(half, kept[1][4])
         rest = flip(half, CORE)
-        parts, halves = (project(kept[0][4], proj), mixed), (half, rest)
+        parts, halves = (project(after(kept[0][4], cots[1], half), proj), mixed), (half, rest)
     else:
         parts, halves = own_sums([project(k[4], proj) for k in kept]), ()
         cots = blocks_of(cot)

time: 215 us -> 217 us (level)
  starting transfers between devices: 33.2 us -> 38.4 us
  waiting for transfers between devices: 67.9 us -> 64 us
    ppermute x11, starting transfers between devices: 11.5 us -> 15.9 us  [across(): return lax.ppermute(v, 'mp', [(0, 1), (1, 0)])]
    ppermute x28, waiting for transfers between devices: 56.2 us -> 53.6 us  [flip(): return lax.ppermute(v, 'dp', [(i, i ^ bits) for i in range(16)])]
  transfers between devices with their start and end apart: 39 -> 39, of which waited for: 17 -> 19; matrix products, arithmetic and copies ran while one was open for 4% -> 4% of each run, Pallas kernels for 37% -> 36%
where the time goes in v9:
time: 217 us; the launch traced here: 216 us
  Pallas kernels  91.4 us (42%)
  waiting for transfers between devices  64 us (29%)
  starting transfers between devices  38.4 us (18%)
  local copies, waits for them, and re-layouts  14.5 us (7%)
  other arithmetic  4.01 us (2%)
  matrix products  2.4 us (1%)
    pallas_call x15, Pallas kernels, call(): pl.pallas_call(kernel, out_shape=outs, in_specs=in_specs, out_specs=[spac...  91.4 us
    ppermute x28, waiting for transfers between devices, flip(): return lax.ppermute(v, 'dp', [(i, i ^ bits) for i in range(16)])  53.6 us
    ppermute x28, starting transfers between devices, flip(): return lax.ppermute(v, 'dp', [(i, i ^ bits) for i in range(16)])  22.5 us
    ppermute x11, starting transfers between devices, across(): return lax.ppermute(v, 'mp', [(0, 1), (1, 0)])  15.9 us
    unnamed x98, local copies, waits for them, and re-layouts  11.6 us
    ppermute x11, waiting for transfers between devices, across(): return lax.ppermute(v, 'mp', [(0, 1), (1, 0)])  10.4 us
  transfers between devices with their start and end apart: 39, of which 19 were waited for; matrix products, arithmetic and copies ran while one was open for 4% of the time, Pallas kernels for 36%

profile of v9, /device:TPU:0, one launch (start us, length us, event | category | flops | bytes accessed | tf_op | source)
XLA Modules:
  0.0 216.1 jit_solution(9225414681009533297)
XLA Ops:
  1.3 2.9 %collective-permute-start = (f32[8,49]{1,0:T(8,128)S(1)}, f32[8,49]{1,0:T(8,128)S(1)}, u32[]{:S(2)}, u32[]{:S(2)}) collective-permute-start(f32[8,49]{1,0:T(8,128)S(1)} %convert_element_type.294.valid_ref), channel_id=1, source_target_pairs={{0,1},{1,0},{2,3},{3,2},{4,5},{5,4},{6,7},{7,6},{8,9},{9,8},{10,11... | collective-permute-start | bytes 4712 | tf_op jit(solution)/shard_map/ppermute | solution.py:641
  4.3 1.6 collective-permute-done.valid_ref
  5.9 2.0 collective-permute-start.3
  7.9 0.7 copy-done.34
  9.8 1.0 constant_dynamic-slice_fusion
  10.8 2.1 collective-permute-start.2
  12.9 12.4 %attn_forward.2 = (bf16[8,3,64,256]{3,2,1,0:T(8,128)(2,1)}, bf16[8,64,384]{2,1,0:T(8,128)(2,1)}, bf16[8,64,384]{2,1,0:T(8,128)(2,1)}, bf16[8,64,384]{2,1,0:T(8,1...) custom-call(bf16[392,768]{1,0:T(8,128)(2,1)} %bitcast.102, f32[768]{0:T(1024)} %gain_ref.9, f32[768]{0:T(1024)} %shift_ref.4, ...), custom_call_target="tpu_custom_call" | custom-call | flops 1000000 | bytes 3906 | tf_op jit(solution)/shard_map/attn_forward/pallas_call | solution.py:520
  25.4 0.8 copy-done.11
  26.2 12.5 %attn_forward.3 = (bf16[8,3,64,256]{3,2,1,0:T(8,128)(2,1)}, bf16[8,64,384]{2,1,0:T(8,128)(2,1)}, bf16[8,64,384]{2,1,0:T(8,128)(2,1)}, bf16[8,64,384]{2,1,0:T(8,1...) custom-call(bf16[392,768]{1,0:T(8,128)(2,1)} %copy-done.11, f32[768]{0:T(1024)} %gain_ref.9, f32[768]{0:T(1024)} %shift_ref.4, ...), custom_call_target="tpu_custom_call" | custom-call | flops 1000000 | bytes 3906 | tf_op jit(solution)/shard_map/attn_forward/pallas_call | solution.py:520
  38.8 2.0 collective-permute-done.2.refs_0_
  40.8 0.8 copy-done.7
  41.6 2.4 %convolution_convert_fusion.own_in = bf16[392,768]{1,0:T(8,128)(2,1)} fusion(bf16[392,384]{1,0:T(8,128)(2,1)} %get-tuple-element.103.refs_1_, bf16[384,768]{1,0:T(8,128)(2,1)S(1)} %copy-done.4), kind=kOutput, calls=%fused_computation | convolution fusion | flops 231512064 | bytes 1492992 | tf_op jit(solution)/shard_map/dot_general | solution.py:739
  44.0 2.2 %collective-permute-done.4.peer_in = bf16[392,384]{1,0:T(8,128)(2,1)S(1)} collective-permute-done((bf16[392,384]{1,0:T(8,128)(2,1)}, bf16[392,384]{1,0:T(8,128)(2,1)S(1)}, u32[]{:S(2)}, u32[]{:S(2)}) %collective-permute-start.4) | collective-permute-done | bytes 301088 | tf_op jit(solution)/shard_map/ppermute | solution.py:641
  46.2 0.7 copy-done.43
  46.9 3.8 %middle.1 = (f32[392,768]{1,0:T(8,128)}, bf16[392,768]{1,0:T(8,128)(2,1)}) custom-call(s32[1]{0:T(128)} %bitcast.me_ref, bf16[392,768]{1,0:T(8,128)(2,1)} %bitcast.103, bf16[392,768]{1,0:T(8,128)(2,1)} %convolution_convert_fusion.own_in, bf16[392,384]{1,0:T(8,128)(2,1)} %copy-done.43, f32[768]{0:T(1024)} %bias_ref.1, f32[768]{0:T(1024)} %gain_ref.8, ...), custom_call_target="tpu_custom_call" | custom-call | flops 1000000 | bytes 3906 | tf_op jit(solution)/shard_map/middle/pallas_call | solution.py:520
  50.8 1.8 collective-permute-start.6
  52.6 1.1 copy-done.9
  53.7 6.1 %mlp.2 = (bf16[392,1536]{1,0:T(8,128)(2,1)S(1)}, bf16[392,1536]{1,0:T(8,128)(2,1)S(1)}, bf16[392,768]{1,0:T(8,128)(2,1)S(1)}, bf16[392,768]{1,0:T(8,128)(2,1)S(1)}) custom-call(bf16[392,768]{1,0:T(8,128)(2,1)S(1)} %copy-done.9, bf16[392,768]{1,0:T(8,128)(2,1)S(1)} %bitcast.108, bf16[768,1536]{1,0:T(8,128)(2,1)S(1)} %copy-done.2, ...), custom_call_target="tpu_custom_call" | custom-call | flops 1000000 | bytes 3906 | tf_op jit(solution)/shard_map/mlp/pallas_call | solution.py:520
  59.8 1.0 copy-done.14
  60.8 0.8 copy-done.24
  61.7 0.8 copy-done.37
  62.5 3.9 %collective-permute-done.6.nm_ref.refs_4_ = bf16[392,768]{1,0:T(8,128)(2,1)S(1)} collective-permute-done((bf16[392,768]{1,0:T(8,128)(2,1)}, bf16[392,768]{1,0:T(8,128)(2,1)S(1)}, u32[]{:S(2)}, u32[]{:S(2)}) %collective-permute-start.6) | collective-permute-done | bytes 602144 | tf_op jit(solution)/shard_map/ppermute | solution.py:641
  66.4 6.9 %mlp.3 = (bf16[392,1536]{1,0:T(8,128)(2,1)S(1)}, bf16[392,1536]{1,0:T(8,128)(2,1)S(1)}, bf16[392,768]{1,0:T(8,128)(2,1)S(1)}, bf16[392,768]{1,0:T(8,128)(2,1)}) custom-call(bf16[392,768]{1,0:T(8,128)(2,1)S(1)} %collective-permute-done.6.nm_ref.refs_4_, bf16[392,768]{1,0:T(8,128)(2,1)S(1)} %copy-done.8, bf16[768,1536]{1,0:T(8,128)(2,1)S(1)} %copy-done.2, ...), custom_call_target="tpu_custom_call" | custom-call | flops 1000000 | bytes 3906 | tf_op jit(solution)/shard_map/mlp/pallas_call | solution.py:520
  73.3 1.0 copy-done.16
  74.3 1.0 copy-done.17
  75.4 1.7 collective-permute-start.8
  77.1 11.9 %mlp_weights.1 = (f32[1,1536]{1,0:T(1,128)}, bf16[2,4,96,768]{3,2,1,0:T(8,128)(2,1)}, bf16[2,4,96,768]{3,2,1,0:T(8,128)(2,1)}, bf16[2,4,96,768]{3,2,1,0:T(8,128)(2,1)}, bf16[2,4,96,768]{3,2,1,0:T(8,128)(2,1)}) custom-call(s32[1]{0:T(128)} %bitcast.me_ref, bf16[392,768]{1,0:T(8,128)(2,1)} %get-tuple-element.105.nm_ref.refs_0_, bf16[392,768]{1,0:T(8,128)(2,1)} %bitcast.107, ...), custom_call_target="tpu_custom_call" | custom-call | flops 1000000 | bytes 3906 | tf_op jit(solution)/shard_map/mlp_weights/pallas_call | solution.py:520
  90.1 0.8 copy-done.39
  90.9 1.1 copy-done.40
  92.0 1.1 middle_back.1
  93.1 1.8 collective-permute-start.11
  95.1 1.1 collective-permute-start.12
  96.4 1.0 collective-permute-start.17
  97.8 9.7 %attn_backward.2 = (bf16[3,392,384]{2,1,0:T(8,128)(2,1)S(1)}, f32[1,768]{1,0:T(1,128)S(1)}, f32[3,64,256]{2,1,0:T(8,128)S(1)}, bf16[392,768]{1,0:T(8,128)(2,1)S(1)}, f32[2,768]{1,0:T(2,128)S(1)}) custom-call(bf16[392,768]{1,0:T(8,128)(2,1)S(1)} %get-tuple-element.144.branch_ref.refs_2_, bf16[392,768]{1,0:T(8,128)(2,1)S(1)} %bitcast.104, ...), custom_call_target="tpu_custom_call" | custom-call | flops 1000000 | bytes 3906 | tf_op jit(solution)/shard_map/attn_backward/pallas_call | solution.py:520
  107.6 3.9 %collective-permute-done.12 = bf16[4,96,768]{2,1,0:T(8,128)(2,1)S(1)} collective-permute-done((bf16[4,96,768]{2,1,0:T(8,128)(2,1)S(1)}, bf16[4,96,768]{2,1,0:T(8,128)(2,1)S(1)}, u32[]{:S(2)}, u32[]{:S(2)}) %collective-permute-start.12) | collective-permute-done | bytes 589856 | tf_op jit(solution)/shard_map/ppermute | solution.py:645
  111.6 3.2 %collective-permute-start.16 = (bf16[96,768]{1,0:T(8,128)(2,1)S(1)}, bf16[96,768]{1,0:T(8,128)(2,1)S(1)}, u32[]{:S(2)}, u32[]{:S(2)}) collective-permute-start(bf16[96,768]{1,0:T(8,128)(2,1)S(1)} %get-tuple-element.188), channel_id=1, source_target_pairs={{0,24},{2,26},{4,28},{6,30},{8,16},{10,18},{12,20},{14,22},{16,8},... | collective-permute-start | bytes 442376 | tf_op jit(solution)/shard_map/ppermute | solution.py:645
  114.8 1.3 collective-permute-start.14
  116.1 9.7 %attn_backward.3 = (bf16[3,392,384]{2,1,0:T(8,128)(2,1)S(1)}, f32[1,768]{1,0:T(1,128)S(1)}, f32[3,64,256]{2,1,0:T(8,128)S(1)}, bf16[392,768]{1,0:T(8,128)(2,1)S(1)}, f32[2,768]{1,0:T(2,128)S(1)}) custom-call(bf16[392,768]{1,0:T(8,128)(2,1)S(1)} %collective-permute-done.11.branch_ref.refs_9_, bf16[392,768]{1,0:T(8,128)(2,1)S(1)} %copy-done.12, ...), custom_call_target="tpu_custom_call" | custom-call | flops 1000000 | bytes 3906 | tf_op jit(solution)/shard_map/attn_backward/pallas_call | solution.py:520
  126.1 3.2 %collective-permute-start.20 = (bf16[96,768]{1,0:T(8,128)(2,1)S(1)}, bf16[96,768]{1,0:T(8,128)(2,1)S(1)}, u32[]{:S(2)}, u32[]{:S(2)}) collective-permute-start(bf16[96,768]{1,0:T(8,128)(2,1)S(1)} %get-tuple-element.185), channel_id=1, source_target_pairs={{0,24},{2,26},{4,28},{6,30},{8,16},{10,18},{12,20},{14,22},{16,8},... | collective-permute-start | bytes 442376 | tf_op jit(solution)/shard_map/ppermute | solution.py:645
  129.3 1.3 collective-permute-start.18
  130.8 5.8 %attn_weights.1 = (bf16[2,4,96,768]{3,2,1,0:T(8,128)(2,1)S(1)}, bf16[2,4,96,768]{3,2,1,0:T(8,128)(2,1)S(1)}, bf16[16,768]{1,0:T(8,128)(2,1)S(1)}) custom-call(s32[1]{0:T(128)} %bitcast.me_ref, f32[4,768]{1,0:T(4,128)S(1)} %get-tuple-element.142.sums2_ref, f32[1,1536]{1,0:T(1,128)S(1)} %copy-done.35, bf16[768,392]{1,0:T(8,128)(2,1)S(1)} %copy-done.20, ...), custom_call_target="tpu_custom_call" | custom-call | flops 1000000 | bytes 3906 | tf_op jit(solution)/shard_map/attn_weights/pallas_call | solution.py:520
  136.8 2.0 collective-permute-start.13
  138.9 0.7 collective-permute-done.25
  139.8 1.3 collective-permute-start.26
  141.0 2.5 %collective-permute-start.21 = (bf16[208,768]{1,0:T(8,128)(2,1)S(1)}, bf16[208,768]{1,0:T(8,128)(2,1)S(1)}, u32[]{:S(2)}, u32[]{:S(2)}) collective-permute-start(bf16[208,768]{1,0:T(8,128)(2,1)S(1)} %get-tuple-element.192), channel_id=1, source_target_pairs={{0,8},{2,10},{4,12},{6,14},{8,0},{10,2},{12,4},{14,6},{16,24},{18,... | collective-permute-start | bytes 958472 | tf_op jit(solution)/shard_map/ppermute | solution.py:645
  143.6 12.5 %collective-permute-done.22 = bf16[208,768]{1,0:T(8,128)(2,1)S(1)} collective-permute-done((bf16[208,768]{1,0:T(8,128)(2,1)S(1)}, bf16[208,768]{1,0:T(8,128)(2,1)S(1)}, u32[]{:S(2)}, u32[]{:S(2)}) %collective-permute-start.22) | collective-permute-done | bytes 319520 | tf_op jit(solution)/shard_map/ppermute | solution.py:645
  156.1 1.1 add_convert_fusion
  157.2 1.7 input_back.1
  158.9 6.6 %collective-permute-done.23 = bf16[208,768]{1,0:T(8,128)(2,1)S(1)} collective-permute-done((bf16[208,768]{1,0:T(8,128)(2,1)S(1)}, bf16[208,768]{1,0:T(8,128)(2,1)S(1)}, u32[]{:S(2)}, u32[]{:S(2)}) %collective-permute-start.23) | collective-permute-done | bytes 319520 | tf_op jit(solution)/shard_map/ppermute | solution.py:645
  165.7 1.6 collective-permute-start.24
  167.7 1.7 collective-permute-start.27
  169.5 4.2 %collective-permute-done.28 = bf16[96,768]{1,0:T(8,128)(2,1)S(1)} collective-permute-done((bf16[96,768]{1,0:T(8,128)(2,1)S(1)}, bf16[96,768]{1,0:T(8,128)(2,1)S(1)}, u32[]{:S(2)}, u32[]{:S(2)}) %collective-permute-start.28) | collective-permute-done | bytes 147488 | tf_op jit(solution)/shard_map/ppermute | solution.py:645
  174.4 1.9 collective-permute-done.27
  176.3 7.6 %collective-permute-done.29 = bf16[96,768]{1,0:T(8,128)(2,1)S(1)} collective-permute-done((bf16[96,768]{1,0:T(8,128)(2,1)S(1)}, bf16[96,768]{1,0:T(8,128)(2,1)S(1)}, u32[]{:S(2)}, u32[]{:S(2)}) %collective-permute-start.29) | collective-permute-done | bytes 147488 | tf_op jit(solution)/shard_map/ppermute | solution.py:645
  184.1 1.6 collective-permute-start.30
  185.7 5.2 %collective-permute-done.31 = bf16[96,768]{1,0:T(8,128)(2,1)S(1)} collective-permute-done((bf16[96,768]{1,0:T(8,128)(2,1)S(1)}, bf16[96,768]{1,0:T(8,128)(2,1)S(1)}, u32[]{:S(2)}, u32[]{:S(2)}) %collective-permute-start.31) | collective-permute-done | bytes 147488 | tf_op jit(solution)/shard_map/ppermute | solution.py:645
  190.9 0.8 collective-permute-done.30
  191.7 4.3 %collective-permute-done.32 = bf16[96,768]{1,0:T(8,128)(2,1)S(1)} collective-permute-done((bf16[96,768]{1,0:T(8,128)(2,1)S(1)}, bf16[96,768]{1,0:T(8,128)(2,1)S(1)}, u32[]{:S(2)}, u32[]{:S(2)}) %collective-permute-start.32) | collective-permute-done | bytes 147488 | tf_op jit(solution)/shard_map/ppermute | solution.py:645
  197.1 2.1 collective-permute-done.34.refs_3_
  199.2 5.4 %finish_mlp.1 = (f32[768,1536]{1,0:T(8,128)}, f32[1536,768]{1,0:T(8,128)}, f32[16,768]{1,0:T(8,128)S(1)}) custom-call(s32[1]{0:T(128)} %bitcast.me_ref, bf16[4,208,768]{2,1,0:T(8,128)(2,1)S(1)} %pad_maximum_fusion.refs_0_, bf16[4,208,768]{2,1,0:T(8,128)(2,1)S(1)} %collective-permute-done.24.refs_1_, ...), custom_call_target="tpu_custom_call" | custom-call | flops 1000000 | bytes 3906 | tf_op jit(solution)/shard_map/finish_mlp/pallas_call | solution.py:520
  204.6 1.1 collective-permute-start.35
  205.7 1.9 finish.2
  208.5 3.5 %collective-permute-done.36.refs_0_ = bf16[4,96,768]{2,1,0:T(8,128)(2,1)S(1)} collective-permute-done((bf16[4,96,768]{2,1,0:T(8,128)(2,1)S(1)}, bf16[4,96,768]{2,1,0:T(8,128)(2,1)S(1)}, u32[]{:S(2)}, u32[]{:S(2)}) %collective-permute-start.36) | collective-permute-done | bytes 589856 | tf_op jit(solution)/shard_map/ppermute | solution.py:645
  214.0 1.9 finish.3
  (155 shorter events, 10.2 us)
Async XLA Ops:
  1.3 11.5 %copy-start.45 = (f32[8,49]{1,0:T(8,128)}, f32[8,49]{1,0:T(8,128)S(1)}, u32[]{:S(2)}) copy-start(f32[8,49]{1,0:T(8,128)S(1)} %convert_element_type.294.valid_ref) | copy-start | bytes 4708
  1.3 4.5 %collective-permute-start = (f32[8,49]{1,0:T(8,128)S(1)}, f32[8,49]{1,0:T(8,128)S(1)}, u32[]{:S(2)}, u32[]{:S(2)}) collective-permute-start(f32[8,49]{1,0:T(8,128)S(1)} %convert_element_type.294.valid_ref), channel_id=1, source_target_pairs={{0,1},{1,0},{2,3},{3,2},{4,5},{5,4},{6,7},{7,6},{8,9},{9,8},{10,11... | collective-permute-start | bytes 4712 | tf_op jit(solution)/shard_map/ppermute | solution.py:641
  5.9 19.5 %copy-start.48 = (f32[8,49]{1,0:T(8,128)}, f32[8,49]{1,0:T(8,128)S(1)}, u32[]{:S(2)}) copy-start(f32[8,49]{1,0:T(8,128)S(1)} %collective-permute-done.valid_ref) | copy-start | bytes 4708
  5.9 19.5 %collective-permute-start.3 = (bf16[392,768]{1,0:T(8,128)(2,1)}, bf16[392,768]{1,0:T(8,128)(2,1)S(1)}, u32[]{:S(2)}, u32[]{:S(2)}) collective-permute-start(bf16[392,768]{1,0:T(8,128)(2,1)} %bitcast.101), channel_id=1, source_target_pairs={{0,1},{1,0},{2,3},{3,2},{4,5},{5,4},{6,7},{7,6},{8,9},{9,8},{10,11... | collective-permute-start | bytes 1806344 | tf_op jit(solution)/shard_map/ppermute | solution.py:641
  9.8 31.0 %collective-permute-start.1 = (bf16[392,768]{1,0:T(8,128)(2,1)}, bf16[392,768]{1,0:T(8,128)(2,1)S(1)}, u32[]{:S(2)}, u32[]{:S(2)}) collective-permute-start(bf16[392,768]{1,0:T(8,128)(2,1)} %bitcast.106), channel_id=1, source_target_pairs={{0,1},{1,0},{2,3},{3,2},{4,5},{5,4},{6,7},{7,6},{8,9},{9,8},{10,11... | collective-permute-start | bytes 1806344 | tf_op jit(solution)/shard_map/ppermute | solution.py:641
  10.8 30.0 %collective-permute-start.2 = (bf16[192,768]{1,0:T(8,128)(2,1)S(1)}, bf16[192,768]{1,0:T(8,128)(2,1)}, u32[]{:S(2)}, u32[]{:S(2)}) collective-permute-start(bf16[192,768]{1,0:T(8,128)(2,1)S(1)} %constant_dynamic-slice_fusion), channel_id=1, source_target_pairs={{0,1},{1,0},{2,3},{3,2},{4,5},{5,4},{6,7},{7,6},{8,9},{9,8},{10,11... | collective-permute-start | bytes 884744 | tf_op jit(solution)/shard_map/ppermute | solution.py:641
  12.9 28.7 %copy-start.4 = (bf16[384,768]{1,0:T(8,128)(2,1)S(1)}, bf16[384,768]{1,0:T(8,128)(2,1)}, u32[]{:S(2)}) copy-start(bf16[384,768]{1,0:T(8,128)(2,1)} %proj_ref.3) | copy-start | bytes 1769476
  26.2 26.4 %copy-start.3 = (bf16[1536,768]{1,0:T(8,128)(2,1)S(1)}, bf16[1536,768]{1,0:T(8,128)(2,1)}, u32[]{:S(2)}) copy-start(bf16[1536,768]{1,0:T(8,128)(2,1)} %fc2_ref.3) | copy-start | bytes 7077892
  38.7 7.6 %collective-permute-start.4 = (bf16[392,384]{1,0:T(8,128)(2,1)}, bf16[392,384]{1,0:T(8,128)(2,1)S(1)}, u32[]{:S(2)}, u32[]{:S(2)}) collective-permute-start(bf16[392,384]{1,0:T(8,128)(2,1)} %get-tuple-element.101.refs_8_), channel_id=1, source_target_pairs={{0,1},{1,0},{2,3},{3,2},{4,5},{5,4},{6,7},{7,6},{8,9},{9,8},{10,11... | collective-permute-start | bytes 903176 | tf_op jit(solution)/shard_map/ppermute | solution.py:641
  40.8 3.3 %collective-permute-start.5 = (bf16[192,768]{1,0:T(8,128)(2,1)}, bf16[192,768]{1,0:T(8,128)(2,1)S(1)}, u32[]{:S(2)}, u32[]{:S(2)}) collective-permute-start(bf16[192,768]{1,0:T(8,128)(2,1)} %collective-permute-done.2.refs_0_), channel_id=1, source_target_pairs={{0,2},{2,0},{4,6},{6,4},{8,10},{10,8},{12,14},{14,12},{16,18},{18,... | collective-permute-start | bytes 884744 | tf_op jit(solution)/shard_map/ppermute | solution.py:645
  41.6 11.0 %copy-start.2 = (bf16[768,1536]{1,0:T(8,128)(2,1)S(1)}, bf16[768,1536]{1,0:T(8,128)(2,1)}, u32[]{:S(2)}) copy-start(bf16[768,1536]{1,0:T(8,128)(2,1)} %fc1_ref.3) | copy-start | bytes 7077892
  44.0 8.6 %copy-start.46 = (f32[1536]{0:T(1024)S(1)}, f32[1536]{0:T(1024)}, u32[]{:S(2)}) copy-start(f32[1536]{0:T(1024)} %param.28) | copy-start | bytes 18436
  44.0 8.6 %copy-start.5 = (bf16[8,49,768]{2,0,1:T(8,128)(2,1)S(1)}, bf16[8,49,768]{2,0,1:T(8,128)(2,1)}, u32[]{:S(2)}) copy-start(bf16[8,49,768]{2,0,1:T(8,128)(2,1)} %param.31) | copy-start | bytes 1806340
  50.8 15.6 %collective-permute-start.6 = (bf16[392,768]{1,0:T(8,128)(2,1)}, bf16[392,768]{1,0:T(8,128)(2,1)S(1)}, u32[]{:S(2)}, u32[]{:S(2)}) collective-permute-start(bf16[392,768]{1,0:T(8,128)(2,1)} %get-tuple-element.105.nm_ref.refs_0_), channel_id=1, source_target_pairs={{0,1},{1,0},{2,3},{3,2},{4,5},{5,4},{6,7},{7,6},{8,9},{9,8},{10,11... | collective-permute-start | bytes 1806344 | tf_op jit(solution)/shard_map/ppermute | solution.py:641
  53.7 12.7 %copy-start.8 = (bf16[392,768]{1,0:T(8,128)(2,1)S(1)}, bf16[392,768]{1,0:T(8,128)(2,1)}, u32[]{:S(2)}) copy-start(bf16[392,768]{1,0:T(8,128)(2,1)} %copy-done.7) | copy-start | bytes 1806340
  62.5 10.8 %copy-start.15 = (bf16[392,1536]{1,0:T(8,128)(2,1)}, bf16[392,1536]{1,0:T(8,128)(2,1)S(1)}, u32[]{:S(2)}) copy-start(bf16[392,1536]{1,0:T(8,128)(2,1)S(1)} %get-tuple-element.112.refs_3_) | copy-start | bytes 3612676
  66.4 6.9 %copy-start.10 = (bf16[392,768]{1,0:T(8,128)(2,1)}, bf16[392,768]{1,0:T(8,128)(2,1)S(1)}, u32[]{:S(2)}) copy-start(bf16[392,768]{1,0:T(8,128)(2,1)S(1)} %collective-permute-done.6.nm_ref.refs_4_) | copy-start | bytes 1806340
  75.4 14.7 %collective-permute-start.8 = (bf16[392,768]{1,0:T(8,128)(2,1)}, bf16[392,768]{1,0:T(8,128)(2,1)S(1)}, u32[]{:S(2)}, u32[]{:S(2)}) collective-permute-start(bf16[392,768]{1,0:T(8,128)(2,1)} %get-tuple-element.110), channel_id=1, source_target_pairs={{0,1},{1,0},{2,3},{3,2},{4,5},{5,4},{6,7},{7,6},{8,9},{9,8},{10,11... | collective-permute-start | bytes 1806344 | tf_op jit(solution)/shard_map/ppermute | solution.py:641
  77.1 13.8 %copy-start.6 = (bf16[8,49,768]{2,0,1:T(8,128)(2,1)S(1)}, bf16[8,49,768]{2,0,1:T(8,128)(2,1)}, u32[]{:S(2)}) copy-start(bf16[8,49,768]{2,0,1:T(8,128)(2,1)} %param.31) | copy-start | bytes 1806340
  77.1 13.8 %copy-start.19 = (f32[392,768]{1,0:T(8,128)S(1)}, f32[392,768]{1,0:T(8,128)}, u32[]{:S(2)}) copy-start(f32[392,768]{1,0:T(8,128)} %get-tuple-element.104.middle_ref) | copy-start | bytes 3612676
  77.1 13.8 %copy-start.36 = (f32[768]{0:T(1024)S(1)}, f32[768]{0:T(1024)}, u32[]{:S(2)}) copy-start(f32[768]{0:T(1024)} %gain_ref.8) | copy-start | bytes 9220
  77.1 13.8 %copy-start.38 = (bf16[392,768]{1,0:T(8,128)(2,1)S(1)}, bf16[392,768]{1,0:T(8,128)(2,1)}, u32[]{:S(2)}) copy-start(bf16[392,768]{1,0:T(8,128)(2,1)} %copy-done.37) | copy-start | bytes 1806340
  89.0 5.9 %collective-permute-start.9 = (bf16[2,4,96,768]{3,2,1,0:T(8,128)(2,1)}, bf16[2,4,96,768]{3,2,1,0:T(8,128)(2,1)S(1)}, u32[]{:S(2)}, u32[]{:S(2)}) collective-permute-start(bf16[2,4,96,768]{3,2,1,0:T(8,128)(2,1)} %get-tuple-element.119), channel_id=1, source_target_pairs={{0,2},{2,0},{4,6},{6,4},{8,10},{10,8},{12,14},{14,12},{16,18},{18,... | collective-permute-start | bytes 3538952 | tf_op jit(solution)/shard_map/ppermute | solution.py:645
  89.1 7.2 %collective-permute-start.10 = (bf16[2,4,96,768]{3,2,1,0:T(8,128)(2,1)}, bf16[2,4,96,768]{3,2,1,0:T(8,128)(2,1)S(1)}, u32[]{:S(2)}, u32[]{:S(2)}) collective-permute-start(bf16[2,4,96,768]{3,2,1,0:T(8,128)(2,1)} %get-tuple-element.122), channel_id=1, source_target_pairs={{0,2},{2,0},{4,6},{6,4},{8,10},{10,8},{12,14},{14,12},{16,18},{18,... | collective-permute-start | bytes 3538952 | tf_op jit(solution)/shard_map/ppermute | solution.py:645
  92.0 5.7 %copy-start.30 = (bf16[8,64,384]{2,1,0:T(8,128)(2,1)S(1)}, bf16[8,64,384]{2,1,0:T(8,128)(2,1)}, u32[]{:S(2)}) copy-start(bf16[8,64,384]{2,1,0:T(8,128)(2,1)} %get-tuple-element.127.k_ref) | copy-start | bytes 1179652
  92.0 5.7 %copy-start.31 = (bf16[8,64,384]{2,1,0:T(8,128)(2,1)S(1)}, bf16[8,64,384]{2,1,0:T(8,128)(2,1)}, u32[]{:S(2)}) copy-start(bf16[8,64,384]{2,1,0:T(8,128)(2,1)} %get-tuple-element.128.v_ref) | copy-start | bytes 1179652
  93.1 21.7 %collective-permute-start.11 = (bf16[392,768]{1,0:T(8,128)(2,1)S(1)}, bf16[392,768]{1,0:T(8,128)(2,1)S(1)}, u32[]{:S(2)}, u32[]{:S(2)}) collective-permute-start(bf16[392,768]{1,0:T(8,128)(2,1)S(1)} %get-tuple-element.144.branch_ref.refs_2_), channel_id=1, source_target_pairs={{0,1},{1,0},{2,3},{3,2},{4,5},{5,4},{6,7},{7,6},{8,9},{9,8},{10,11... | collective-permute-start | bytes 1806344 | tf_op jit(solution)/shard_map/ppermute | solution.py:641
  95.1 16.3 %collective-permute-start.12 = (bf16[4,96,768]{2,1,0:T(8,128)(2,1)S(1)}, bf16[4,96,768]{2,1,0:T(8,128)(2,1)S(1)}, u32[]{:S(2)}, u32[]{:S(2)}) collective-permute-start(bf16[4,96,768]{2,1,0:T(8,128)(2,1)S(1)} %fusion), channel_id=1, source_target_pairs={{0,4},{2,6},{4,0},{6,2},{8,12},{10,14},{12,8},{14,10},{16,20},{18,... | collective-permute-start | bytes 1769480 | tf_op jit(solution)/shard_map/ppermute | solution.py:645
  96.4 29.5 %collective-permute-start.17 = (bf16[4,96,768]{2,1,0:T(8,128)(2,1)S(1)}, bf16[4,96,768]{2,1,0:T(8,128)(2,1)S(1)}, u32[]{:S(2)}, u32[]{:S(2)}) collective-permute-start(bf16[4,96,768]{2,1,0:T(8,128)(2,1)S(1)} %fusion.1), channel_id=1, source_target_pairs={{0,4},{2,6},{4,0},{6,2},{8,12},{10,14},{12,8},{14,10},{16,20},{18,... | collective-permute-start | bytes 1769480 | tf_op jit(solution)/shard_map/ppermute | solution.py:645
  97.4 33.3 %collective-permute-start.7 = (bf16[392,768]{1,0:T(8,128)(2,1)S(1)}, bf16[392,768]{1,0:T(8,128)(2,1)S(1)}, u32[]{:S(2)}, u32[]{:S(2)}) collective-permute-start(bf16[392,768]{1,0:T(8,128)(2,1)S(1)} %get-tuple-element.109), channel_id=1, source_target_pairs={{0,1},{1,0},{2,3},{3,2},{4,5},{5,4},{6,7},{7,6},{8,9},{9,8},{10,11... | collective-permute-start | bytes 1806344 | tf_op jit(solution)/shard_map/ppermute | solution.py:641
  97.8 18.3 %copy-start.27 = (bf16[8,64,384]{2,1,0:T(8,128)(2,1)S(1)}, bf16[8,64,384]{2,1,0:T(8,128)(2,1)}, u32[]{:S(2)}) copy-start(bf16[8,64,384]{2,1,0:T(8,128)(2,1)} %get-tuple-element.134.k_ref) | copy-start | bytes 1179652
  97.8 18.3 %copy-start.28 = (bf16[8,64,384]{2,1,0:T(8,128)(2,1)S(1)}, bf16[8,64,384]{2,1,0:T(8,128)(2,1)}, u32[]{:S(2)}) copy-start(bf16[8,64,384]{2,1,0:T(8,128)(2,1)} %get-tuple-element.135.v_ref) | copy-start | bytes 1179652
  107.5 8.6 %copy-start.12 = (bf16[392,768]{1,0:T(8,128)(2,1)S(1)}, bf16[392,768]{1,0:T(8,128)(2,1)}, u32[]{:S(2)}) copy-start(bf16[392,768]{1,0:T(8,128)(2,1)} %copy-done.11) | copy-start | bytes 1806340
  107.5 8.6 %copy-start.22 = (bf16[8,3,64,256]{3,2,1,0:T(8,128)(2,1)S(1)}, bf16[8,3,64,256]{3,2,1,0:T(8,128)(2,1)}, u32[]{:S(2)}) copy-start(bf16[8,3,64,256]{3,2,1,0:T(8,128)(2,1)} %get-tuple-element.132.prob_ref) | copy-start | bytes 2359300
  107.6 8.6 %copy-start.26 = (bf16[8,64,384]{2,1,0:T(8,128)(2,1)S(1)}, bf16[8,64,384]{2,1,0:T(8,128)(2,1)}, u32[]{:S(2)}) copy-start(bf16[8,64,384]{2,1,0:T(8,128)(2,1)} %get-tuple-element.133.q_ref) | copy-start | bytes 1179652
  111.6 17.7 %collective-permute-start.16 = (bf16[96,768]{1,0:T(8,128)(2,1)S(1)}, bf16[96,768]{1,0:T(8,128)(2,1)S(1)}, u32[]{:S(2)}, u32[]{:S(2)}) collective-permute-start(bf16[96,768]{1,0:T(8,128)(2,1)S(1)} %get-tuple-element.188), channel_id=1, source_target_pairs={{0,24},{2,26},{4,28},{6,30},{8,16},{10,18},{12,20},{14,22},{16,8},... | collective-permute-start | bytes 442376 | tf_op jit(solution)/shard_map/ppermute | solution.py:645
  114.8 14.5 %collective-permute-start.15 = (bf16[96,768]{1,0:T(8,128)(2,1)S(1)}, bf16[96,768]{1,0:T(8,128)(2,1)S(1)}, u32[]{:S(2)}, u32[]{:S(2)}) collective-permute-start(bf16[96,768]{1,0:T(8,128)(2,1)S(1)} %get-tuple-element.189), channel_id=1, source_target_pairs={{0,16},{2,18},{4,20},{6,22},{8,24},{10,26},{12,28},{14,30},{16,0},... | collective-permute-start | bytes 442376 | tf_op jit(solution)/shard_map/ppermute | solution.py:645
  114.8 15.7 %collective-permute-start.14 = (bf16[96,768]{1,0:T(8,128)(2,1)S(1)}, bf16[96,768]{1,0:T(8,128)(2,1)S(1)}, u32[]{:S(2)}, u32[]{:S(2)}) collective-permute-start(bf16[96,768]{1,0:T(8,128)(2,1)S(1)} %get-tuple-element.190), channel_id=1, source_target_pairs={{0,8},{2,10},{4,12},{6,14},{8,0},{10,2},{12,4},{14,6},{16,24},{18,... | collective-permute-start | bytes 442376 | tf_op jit(solution)/shard_map/ppermute | solution.py:645
  125.9 4.8 %copy-start.18 = (bf16[392,384]{1,0:T(8,128)(2,1)S(1)}, bf16[392,384]{1,0:T(8,128)(2,1)}, u32[]{:S(2)}) copy-start(bf16[392,384]{1,0:T(8,128)(2,1)} %get-tuple-element.103.refs_1_) | copy-start | bytes 903172
  125.9 4.8 %copy-start.20 = (bf16[768,392]{1,0:T(8,128)(2,1)S(1)}, bf16[768,392]{1,0:T(8,128)(2,1)}, u32[]{:S(2)}) copy-start(bf16[768,392]{1,0:T(8,128)(2,1)} %get-tuple-element.143.refs_0_) | copy-start | bytes 1806340
  126.1 10.4 %collective-permute-start.20 = (bf16[96,768]{1,0:T(8,128)(2,1)S(1)}, bf16[96,768]{1,0:T(8,128)(2,1)S(1)}, u32[]{:S(2)}, u32[]{:S(2)}) collective-permute-start(bf16[96,768]{1,0:T(8,128)(2,1)S(1)} %get-tuple-element.185), channel_id=1, source_target_pairs={{0,24},{2,26},{4,28},{6,30},{8,16},{10,18},{12,20},{14,22},{16,8},... | collective-permute-start | bytes 442376 | tf_op jit(solution)/shard_map/ppermute | solution.py:645
  129.3 7.3 %collective-permute-start.19 = (bf16[96,768]{1,0:T(8,128)(2,1)S(1)}, bf16[96,768]{1,0:T(8,128)(2,1)S(1)}, u32[]{:S(2)}, u32[]{:S(2)}) collective-permute-start(bf16[96,768]{1,0:T(8,128)(2,1)S(1)} %get-tuple-element.186), channel_id=1, source_target_pairs={{0,16},{2,18},{4,20},{6,22},{8,24},{10,26},{12,28},{14,30},{16,0},... | collective-permute-start | bytes 442376 | tf_op jit(solution)/shard_map/ppermute | solution.py:645
  129.3 7.3 %collective-permute-start.18 = (bf16[96,768]{1,0:T(8,128)(2,1)S(1)}, bf16[96,768]{1,0:T(8,128)(2,1)S(1)}, u32[]{:S(2)}, u32[]{:S(2)}) collective-permute-start(bf16[96,768]{1,0:T(8,128)(2,1)S(1)} %get-tuple-element.187), channel_id=1, source_target_pairs={{0,8},{2,10},{4,12},{6,14},{8,0},{10,2},{12,4},{14,6},{16,24},{18,... | collective-permute-start | bytes 442376 | tf_op jit(solution)/shard_map/ppermute | solution.py:645
  136.7 19.4 %copy-start.25 = (bf16[392,768]{1,0:T(8,128)(2,1)S(1)}, bf16[392,768]{1,0:T(8,128)(2,1)}, u32[]{:S(2)}) copy-start(bf16[392,768]{1,0:T(8,128)(2,1)} %copy-done.24) | copy-start | bytes 1806340
  136.7 19.4 %copy-start.47 = (f32[768]{0:T(1024)S(1)}, f32[768]{0:T(1024)}, u32[]{:S(2)}) copy-start(f32[768]{0:T(1024)} %param.30) | copy-start | bytes 9220
  136.7 2.9 %collective-permute-start.25 = (bf16[2,4,96,768]{3,2,1,0:T(8,128)(2,1)S(1)}, bf16[2,4,96,768]{3,2,1,0:T(8,128)(2,1)S(1)}, u32[]{:S(2)}, u32[]{:S(2)}) collective-permute-start(bf16[2,4,96,768]{3,2,1,0:T(8,128)(2,1)S(1)} %get-tuple-element.163), channel_id=1, source_target_pairs={{0,2},{2,0},{4,6},{6,4},{8,10},{10,8},{12,14},{14,12},{16,18},{18,... | collective-permute-start | bytes 3538952 | tf_op jit(solution)/shard_map/ppermute | solution.py:645
  136.8 20.4 %collective-permute-start.13 = (bf16[392,768]{1,0:T(8,128)(2,1)S(1)}, bf16[392,768]{1,0:T(8,128)(2,1)S(1)}, u32[]{:S(2)}, u32[]{:S(2)}) collective-permute-start(bf16[392,768]{1,0:T(8,128)(2,1)S(1)} %get-tuple-element.136), channel_id=1, source_target_pairs={{0,1},{1,0},{2,3},{3,2},{4,5},{5,4},{6,7},{7,6},{8,9},{9,8},{10,11... | collective-permute-start | bytes 1806344 | tf_op jit(solution)/shard_map/ppermute | solution.py:641
  138.8 17.3 %collective-permute-start.22 = (bf16[208,768]{1,0:T(8,128)(2,1)S(1)}, bf16[208,768]{1,0:T(8,128)(2,1)S(1)}, u32[]{:S(2)}, u32[]{:S(2)}) collective-permute-start(bf16[208,768]{1,0:T(8,128)(2,1)S(1)} %get-tuple-element.192), channel_id=1, source_target_pairs={{0,16},{2,18},{4,20},{6,22},{8,24},{10,26},{12,28},{14,30},{16,0},... | collective-permute-start | bytes 958472 | tf_op jit(solution)/shard_map/ppermute | solution.py:645
  139.8 27.5 %collective-permute-start.26 = (bf16[4,96,768]{2,1,0:T(8,128)(2,1)S(1)}, bf16[4,96,768]{2,1,0:T(8,128)(2,1)S(1)}, u32[]{:S(2)}, u32[]{:S(2)}) collective-permute-start(bf16[4,96,768]{2,1,0:T(8,128)(2,1)S(1)} %fusion.2), channel_id=1, source_target_pairs={{0,4},{2,6},{4,0},{6,2},{8,12},{10,14},{12,8},{14,10},{16,20},{18,... | collective-permute-start | bytes 1769480 | tf_op jit(solution)/shard_map/ppermute | solution.py:645
  141.0 17.9 %collective-permute-start.21 = (bf16[208,768]{1,0:T(8,128)(2,1)S(1)}, bf16[208,768]{1,0:T(8,128)(2,1)S(1)}, u32[]{:S(2)}, u32[]{:S(2)}) collective-permute-start(bf16[208,768]{1,0:T(8,128)(2,1)S(1)} %get-tuple-element.192), channel_id=1, source_target_pairs={{0,8},{2,10},{4,12},{6,14},{8,0},{10,2},{12,4},{14,6},{16,24},{18,... | collective-permute-start | bytes 958472 | tf_op jit(solution)/shard_map/ppermute | solution.py:645
  156.1 9.4 %collective-permute-start.23 = (bf16[208,768]{1,0:T(8,128)(2,1)S(1)}, bf16[208,768]{1,0:T(8,128)(2,1)S(1)}, u32[]{:S(2)}, u32[]{:S(2)}) collective-permute-start(bf16[208,768]{1,0:T(8,128)(2,1)S(1)} %collective-permute-done.22), channel_id=1, source_target_pairs={{0,8},{2,10},{4,12},{6,14},{8,0},{10,2},{12,4},{14,6},{16,24},{18,... | collective-permute-start | bytes 958472 | tf_op jit(solution)/shard_map/ppermute | solution.py:645
  165.7 30.5 %collective-permute-start.24 = (bf16[4,208,768]{2,1,0:T(8,128)(2,1)S(1)}, bf16[4,208,768]{2,1,0:T(8,128)(2,1)S(1)}, u32[]{:S(2)}, u32[]{:S(2)}) collective-permute-start(bf16[4,208,768]{2,1,0:T(8,128)(2,1)S(1)} %pad_maximum_fusion.refs_0_), channel_id=1, source_target_pairs={{0,4},{2,6},{4,0},{6,2},{8,12},{10,14},{12,8},{14,10},{16,20},{18,... | collective-permute-start | bytes 3833864 | tf_op jit(solution)/shard_map/ppermute | solution.py:645
  167.4 6.2 %collective-permute-start.28 = (bf16[96,768]{1,0:T(8,128)(2,1)S(1)}, bf16[96,768]{1,0:T(8,128)(2,1)S(1)}, u32[]{:S(2)}, u32[]{:S(2)}) collective-permute-start(bf16[96,768]{1,0:T(8,128)(2,1)S(1)} %get-tuple-element.184), channel_id=1, source_target_pairs={{0,8},{2,10},{4,12},{6,14},{8,0},{10,2},{12,4},{14,6},{16,24},{18,... | collective-permute-start | bytes 442376 | tf_op jit(solution)/shard_map/ppermute | solution.py:645
  167.7 8.6 %collective-permute-start.27 = (bf16[96,768]{1,0:T(8,128)(2,1)S(1)}, bf16[96,768]{1,0:T(8,128)(2,1)S(1)}, u32[]{:S(2)}, u32[]{:S(2)}) collective-permute-start(bf16[96,768]{1,0:T(8,128)(2,1)S(1)} %get-tuple-element.183), channel_id=1, source_target_pairs={{0,8},{2,10},{4,12},{6,14},{8,0},{10,2},{12,4},{14,6},{16,24},{18,... | collective-permute-start | bytes 442376 | tf_op jit(solution)/shard_map/ppermute | solution.py:645
  173.7 10.2 %collective-permute-start.29 = (bf16[96,768]{1,0:T(8,128)(2,1)S(1)}, bf16[96,768]{1,0:T(8,128)(2,1)S(1)}, u32[]{:S(2)}, u32[]{:S(2)}) collective-permute-start(bf16[96,768]{1,0:T(8,128)(2,1)S(1)} %add_convert_fusion.4), channel_id=1, source_target_pairs={{0,16},{2,18},{4,20},{6,22},{8,24},{10,26},{12,28},{14,30},{16,0},... | collective-permute-start | bytes 442376 | tf_op jit(solution)/shard_map/ppermute | solution.py:645
  184.0 6.8 %collective-permute-start.31 = (bf16[96,768]{1,0:T(8,128)(2,1)S(1)}, bf16[96,768]{1,0:T(8,128)(2,1)S(1)}, u32[]{:S(2)}, u32[]{:S(2)}) collective-permute-start(bf16[96,768]{1,0:T(8,128)(2,1)S(1)} %fusion.8), channel_id=1, source_target_pairs={{0,16},{2,18},{4,20},{6,22},{8,24},{10,26},{12,28},{14,30},{16,0},... | collective-permute-start | bytes 442376 | tf_op jit(solution)/shard_map/ppermute | solution.py:645
  184.1 7.6 %collective-permute-start.30 = (bf16[96,768]{1,0:T(8,128)(2,1)S(1)}, bf16[96,768]{1,0:T(8,128)(2,1)S(1)}, u32[]{:S(2)}, u32[]{:S(2)}) collective-permute-start(bf16[96,768]{1,0:T(8,128)(2,1)S(1)} %fusion.8), channel_id=1, source_target_pairs={{0,8},{2,10},{4,12},{6,14},{8,0},{10,2},{12,4},{14,6},{16,24},{18,... | collective-permute-start | bytes 442376 | tf_op jit(solution)/shard_map/ppermute | solution.py:645
  190.9 5.1 %collective-permute-start.32 = (bf16[96,768]{1,0:T(8,128)(2,1)S(1)}, bf16[96,768]{1,0:T(8,128)(2,1)S(1)}, u32[]{:S(2)}, u32[]{:S(2)}) collective-permute-start(bf16[96,768]{1,0:T(8,128)(2,1)S(1)} %collective-permute-done.31), channel_id=1, source_target_pairs={{0,8},{2,10},{4,12},{6,14},{8,0},{10,2},{12,4},{14,6},{16,24},{18,... | collective-permute-start | bytes 442376 | tf_op jit(solution)/shard_map/ppermute | solution.py:645
  190.9 6.2 %collective-permute-start.33 = (bf16[4,208,768]{2,1,0:T(8,128)(2,1)S(1)}, bf16[4,208,768]{2,1,0:T(8,128)(2,1)S(1)}, u32[]{:S(2)}, u32[]{:S(2)}) collective-permute-start(bf16[4,208,768]{2,1,0:T(8,128)(2,1)S(1)} %pad_maximum_fusion.refs_0_), channel_id=1, source_target_pairs={{0,2},{2,0},{4,6},{6,4},{8,10},{10,8},{12,14},{14,12},{16,18},{18,... | collective-permute-start | bytes 3833864 | tf_op jit(solution)/shard_map/ppermute | solution.py:645
  196.1 3.1 %collective-permute-start.34 = (bf16[4,208,768]{2,1,0:T(8,128)(2,1)S(1)}, bf16[4,208,768]{2,1,0:T(8,128)(2,1)S(1)}, u32[]{:S(2)}, u32[]{:S(2)}) collective-permute-start(bf16[4,208,768]{2,1,0:T(8,128)(2,1)S(1)} %collective-permute-done.24.refs_1_), channel_id=1, source_target_pairs={{0,2},{2,0},{4,6},{6,4},{8,10},{10,8},{12,14},{14,12},{16,18},{18,... | collective-permute-start | bytes 3833864 | tf_op jit(solution)/shard_map/ppermute | solution.py:645
  196.2 9.5 %collective-permute-start.37 = (bf16[4,96,768]{2,1,0:T(8,128)(2,1)S(1)}, bf16[4,96,768]{2,1,0:T(8,128)(2,1)S(1)}, u32[]{:S(2)}, u32[]{:S(2)}) collective-permute-start(bf16[4,96,768]{2,1,0:T(8,128)(2,1)S(1)} %pad_maximum_fusion.1.refs_0_), channel_id=1, source_target_pairs={{0,2},{2,0},{4,6},{6,4},{8,10},{10,8},{12,14},{14,12},{16,18},{18,... | collective-permute-start | bytes 1769480 | tf_op jit(solution)/shard_map/ppermute | solution.py:645
  196.7 15.3 %collective-permute-start.36 = (bf16[4,96,768]{2,1,0:T(8,128)(2,1)S(1)}, bf16[4,96,768]{2,1,0:T(8,128)(2,1)S(1)}, u32[]{:S(2)}, u32[]{:S(2)}) collective-permute-start(bf16[4,96,768]{2,1,0:T(8,128)(2,1)S(1)} %pad_maximum_fusion.1.refs_0_), channel_id=1, source_target_pairs={{0,4},{2,6},{4,0},{6,2},{8,12},{10,14},{12,8},{14,10},{16,20},{18,... | collective-permute-start | bytes 1769480 | tf_op jit(solution)/shard_map/ppermute | solution.py:645
  204.6 3.9 %collective-permute-start.35 = (f32[6,768]{1,0:T(8,128)S(1)}, f32[6,768]{1,0:T(8,128)S(1)}, u32[]{:S(2)}, u32[]{:S(2)}) collective-permute-start(f32[6,768]{1,0:T(8,128)S(1)} %slice.210), channel_id=1, source_target_pairs={{0,1},{1,0},{2,3},{3,2},{4,5},{5,4},{6,7},{7,6},{8,9},{9,8},{10,11... | collective-permute-start | bytes 55304 | tf_op jit(solution)/shard_map/ppermute | solution.py:641
  212.0 2.0 collective-permute-start.38
  (24 other events, 47.5 us)
